TPU v7x, 32 devices: a whole 2x2x4 slice. The times are simulated.
32 devices in a mesh: grp: 2 (over y), slab: 8 (over z, x), col: 2 (over core).
Axes of the slice: x: 2, y: 2, z: 4, core: 2. Of those that a mesh axis runs over, the one named last changes fastest.
Arguments:
- states: float32 [4, 64, 128, 1024], P(None, ('grp', 'slab'), 'col'), parts along dimension 1, may hold values from 0 to 1.4, as said below
- cond: float32 [6, 16, 32, 256], P(None, ('grp', 'slab'), 'col'), parts along dimension 1, may hold values from -0.025 to 0.15, as said below
- tension: float32 [32, 64, 512], P(('grp', 'slab'), 'col'), parts along dimension 0, may hold values from 0 to 1
- fiber: int32 [16, 32, 256], P(('grp', 'slab'), 'col'), parts along dimension 0, may hold values from 0 to 63
- disp: float32 [3, 16, 32, 256], P(None, ('grp', 'slab'), 'col'), parts along dimension 1, may hold values from -0.12 to 0.12
Outputs:
- states_next: float32 [4, 64, 128, 1024], P(None, ('grp', 'slab'), 'col'), parts along dimension 1
- tension_next: float32 [32, 64, 512], P(('grp', 'slab'), 'col'), parts along dimension 0
- disp_next: float32 [3, 16, 32, 256], P(None, ('grp', 'slab'), 'col'), parts along dimension 1
- cond_next: float32 [6, 16, 32, 256], P(None, ('grp', 'slab'), 'col'), parts along dimension 1
There are 2 independent parts, one for each index of `grp`. A program takes and returns all parts, laid end to end along the dimension named above; each array names one. Nothing has to cross between parts.
Inputs may be any that keep to these rules, and one draw needn't show every extreme that they name: `states`: component 0 lies in 0 to 1.4, components 1 to 3 in 0 to 1. `cond`: components 0 to 2 lie in 0.05 to 0.15, components 3 to 5 in -0.025 to 0.025.
All inputs are finite; a program needn't handle non-finite values.
Results may differ from a plain program's by a relative error of at most 0.0003.
Values sent between devices are 32-bit elements; how exact they have to be, the bound alone decides.
No kernel may reach another device: no remote copies, remote signals or barrier semaphores. Data moves between devices by JAX's collectives and lax.ppermute only.
A program may use at most 192 MiB of HBM per device.

v0:
```python
import jax
import jax.numpy as jnp
from jax import lax
from jax.sharding import PartitionSpec as P

SUB = 4
MECH_STEPS = 2
NFIB = 64


SHARP = 50.0
STEP_TIME = 0.05
LAME_FIRST = 1.0
SHEAR = 0.5
ACTIVE_GAIN = 0.5
MECH_RATE = 0.15
SIGMA_LONG = 0.16
SIGMA_TRANS = 0.04
SMOOTH_WEIGHTS = (0.125, 0.75, 0.125)
SLOPE_WEIGHTS = (-0.5, 0.0, 0.5)
PAIRS = ((0, 0), (1, 1), (2, 2), (0, 1), (0, 2), (1, 2))


def extended(array, sides, width):
    for axis, dim in sides:
        devices, length = (lax.axis_size(axis), array.shape[dim])
        up = [(i, (i + 1) % devices) for i in range(devices - 1)]
        down = [(j, i) for i, j in up]
        last = lax.slice_in_dim(array, length - width, length, axis=dim)
        initial = lax.slice_in_dim(array, 0, width, axis=dim)
        before = lax.ppermute(last, axis, up)
        after = lax.ppermute(initial, axis, down)
        array = jnp.concatenate([before, array, after], axis=dim)
    return array


def switch(value):
    return 0.5 * (1.0 + jnp.tanh(SHARP * value))


def ionic_rates(volt, gate_v, gate_w, gate_s):
    high_v = switch(volt - 0.3)
    high_w = switch(volt - 0.13)
    high_o = switch(volt - 0.006)
    tau_vminus = (1.0 - high_o) * 60.0 + high_o * 1150.0
    tau_wminus = 60.0 + (15.0 - 60.0) * 0.5 * (1.0 + jnp.tanh(65.0 * (volt - 0.03)))
    tau_soft = 30.0181 + (0.9957 - 30.0181) * 0.5 * (1.0 + jnp.tanh(2.0458 * (volt - 0.65)))
    tau_slow = (1.0 - high_w) * 2.7342 + high_w * 16.0
    tau_open = (1.0 - high_o) * 400.0 + high_o * 6.0
    v_inf = 1.0 - high_o
    w_inf = (1.0 - high_o) * (1.0 - volt / 0.07) + high_o * 0.94
    fast_current = -gate_v * high_v * (volt - 0.3) * (1.55 - volt) / 0.11
    outward = volt * (1.0 - high_w) / tau_open + high_w / tau_soft
    slow_current = -high_w * gate_w * gate_s / 1.8875
    rate_v = (1.0 - high_v) * (v_inf - gate_v) / tau_vminus - high_v * gate_v / 1.4506
    rate_w = (1.0 - high_w) * (w_inf - gate_w) / tau_wminus - high_w * gate_w / 200.0
    rate_s = (0.5 * (1.0 + jnp.tanh(2.0994 * (volt - 0.9087))) - gate_s) / tau_slow
    return (-(fast_current + outward + slow_current), rate_v, rate_w, rate_s)


def diffusion(padded, coeff):
    centre = padded[1:-1, 1:-1, 1:-1]
    along_z = padded[2:, 1:-1, 1:-1] + padded[:-2, 1:-1, 1:-1] - 2.0 * centre
    along_y = padded[1:-1, 2:, 1:-1] + padded[1:-1, :-2, 1:-1] - 2.0 * centre
    along_x = padded[1:-1, 1:-1, 2:] + padded[1:-1, 1:-1, :-2] - 2.0 * centre
    cross_zy = 0.25 * (
        padded[2:, 2:, 1:-1]
        - padded[2:, :-2, 1:-1]
        - padded[:-2, 2:, 1:-1]
        + padded[:-2, :-2, 1:-1]
    )
    cross_zx = 0.25 * (
        padded[2:, 1:-1, 2:]
        - padded[2:, 1:-1, :-2]
        - padded[:-2, 1:-1, 2:]
        + padded[:-2, 1:-1, :-2]
    )
    cross_yx = 0.25 * (
        padded[1:-1, 2:, 2:]
        - padded[1:-1, 2:, :-2]
        - padded[1:-1, :-2, 2:]
        + padded[1:-1, :-2, :-2]
    )
    return (
        coeff[0] * along_z
        + coeff[1] * along_y
        + coeff[2] * along_x
        + 2.0 * (coeff[3] * cross_zy + coeff[4] * cross_zx + coeff[5] * cross_yx)
    )


def excite_step(padded, volt, gate_v, gate_w, gate_s, coeff):
    ion, rate_v, rate_w, rate_s = ionic_rates(volt, gate_v, gate_w, gate_s)
    new_volt = volt + diffusion(padded, coeff) + STEP_TIME * ion
    return (
        new_volt,
        gate_v + STEP_TIME * rate_v,
        gate_w + STEP_TIME * rate_w,
        gate_s + STEP_TIME * rate_s,
    )


def upsample(cond):
    return jnp.repeat(jnp.repeat(jnp.repeat(cond, 4, axis=1), 4, axis=2), 4, axis=3)


def coarsen(field):
    shaped = field.reshape(field.shape[0] // 2, 2, field.shape[1] // 2, 2, field.shape[2] // 2, 2)
    return jnp.mean(shaped, axis=(1, 3, 5))


def fiber_dir(fiber):
    block_index = fiber.astype(jnp.float32)
    theta = -1.0 + 2.0 * block_index / (NFIB - 1)
    tilt = 0.3 * jnp.sin(3.0 * block_index)
    return jnp.stack(
        [jnp.sin(tilt), jnp.cos(tilt) * jnp.sin(theta), jnp.cos(tilt) * jnp.cos(theta)]
    )


def along(field, axis_pos, weights):
    count = field.shape[axis_pos] - 2
    total = weights[0] * lax.slice_in_dim(field, 0, count, axis=axis_pos)
    total = total + weights[1] * lax.slice_in_dim(field, 1, count + 1, axis=axis_pos)
    return total + weights[2] * lax.slice_in_dim(field, 2, count + 2, axis=axis_pos)


def spline_op(padded, direction):
    result = padded
    for dim_pos in range(3):
        result = along(
            result, dim_pos + 1, SLOPE_WEIGHTS if dim_pos == direction else SMOOTH_WEIGHTS
        )
    return result


def deformation(padded_disp):
    grads = [spline_op(padded_disp, direction) for direction in range(3)]
    return [
        [grads[col_pos][row_pos] + (1.0 if row_pos == col_pos else 0.0) for col_pos in range(3)]
        for row_pos in range(3)
    ]


def first_piola(deform, active, fdir):
    right = [
        [
            deform[0][a_pos] * deform[0][b_pos]
            + deform[1][a_pos] * deform[1][b_pos]
            + deform[2][a_pos] * deform[2][b_pos]
            for b_pos in range(3)
        ]
        for a_pos in range(3)
    ]
    strain = [
        [0.5 * (right[a_pos][b_pos] - (1.0 if a_pos == b_pos else 0.0)) for b_pos in range(3)]
        for a_pos in range(3)
    ]
    trace_e = strain[0][0] + strain[1][1] + strain[2][2]
    second = []
    for a_pos in range(3):
        row_list = []
        for b_pos in range(3):
            entry = (
                2.0 * SHEAR * strain[a_pos][b_pos]
                + ACTIVE_GAIN * active * fdir[a_pos] * fdir[b_pos]
            )
            if a_pos == b_pos:
                entry = LAME_FIRST * trace_e + entry
            row_list.append(entry)
        second.append(row_list)
    pieces = []
    for a_pos in range(3):
        for i_pos in range(3):
            pieces.append(
                deform[i_pos][0] * second[0][a_pos]
                + deform[i_pos][1] * second[1][a_pos]
                + deform[i_pos][2] * second[2][a_pos]
            )
    return jnp.stack(pieces)


def forces(padded_piola):
    total = spline_op(padded_piola[0:3], 0)
    total = total + spline_op(padded_piola[3:6], 1)
    return total + spline_op(padded_piola[6:9], 2)


def metric(deform, fdir):
    det_f = (
        deform[0][0] * (deform[1][1] * deform[2][2] - deform[1][2] * deform[2][1])
        - deform[0][1] * (deform[1][0] * deform[2][2] - deform[1][2] * deform[2][0])
        + deform[0][2] * (deform[1][0] * deform[2][1] - deform[1][1] * deform[2][0])
    )
    inverse = [[None, None, None] for row_pos in range(3)]
    for i_pos in range(3):
        for j_pos in range(3):
            cofac = (
                deform[(i_pos + 1) % 3][(j_pos + 1) % 3] * deform[(i_pos + 2) % 3][(j_pos + 2) % 3]
                - deform[(i_pos + 1) % 3][(j_pos + 2) % 3]
                * deform[(i_pos + 2) % 3][(j_pos + 1) % 3]
            )
            inverse[j_pos][i_pos] = cofac / det_f
    along_fiber = [
        inverse[a_pos][0] * fdir[0] + inverse[a_pos][1] * fdir[1] + inverse[a_pos][2] * fdir[2]
        for a_pos in range(3)
    ]
    comps = []
    for a_pos, b_pos in PAIRS:
        inv_metric = (
            inverse[a_pos][0] * inverse[b_pos][0]
            + inverse[a_pos][1] * inverse[b_pos][1]
            + inverse[a_pos][2] * inverse[b_pos][2]
        )
        comps.append(
            SIGMA_TRANS * inv_metric
            + (SIGMA_LONG - SIGMA_TRANS) * along_fiber[a_pos] * along_fiber[b_pos]
        )
    return jnp.stack(comps)


def mechanics(disp, active, fdir, extend):
    for turn_index in range(MECH_STEPS):
        deform = deformation(extend(disp))
        piola = first_piola(deform, active, fdir)
        disp = disp + MECH_RATE * forces(extend(piola))
    deform = deformation(extend(disp))
    return (disp, metric(deform, fdir))


def pad_last(field):
    return jnp.pad(field, [(0, 0)] * (field.ndim - 1) + [(1, 1)])


def extend_spread(field):
    return pad_last(extended(field, (("slab", 1), ("col", 2)), 1))


def on_device(states, cond, tension, fiber, disp):
    volt, gate_v, gate_w, gate_s = (states[0], states[1], states[2], states[3])
    coeff = upsample(cond)
    for turn_index in range(SUB):
        padded = pad_last(extended(volt, (("slab", 0), ("col", 1)), 1))
        volt, gate_v, gate_w, gate_s = excite_step(padded, volt, gate_v, gate_w, gate_s, coeff)
    states_next = jnp.stack([volt, gate_v, gate_w, gate_s])
    tension_next = tension + 0.5 * (coarsen(volt) - tension)
    active = coarsen(tension_next)
    fdir = fiber_dir(fiber)
    disp_next, cond_next = mechanics(disp, active, fdir, extend_spread)
    return (states_next, tension_next, disp_next, cond_next)


def solution(mesh):
    in_specs = (
        P(None, ("grp", "slab"), "col", None),
        P(None, ("grp", "slab"), "col", None),
        P(("grp", "slab"), "col", None),
        P(("grp", "slab"), "col", None),
        P(None, ("grp", "slab"), "col", None),
    )
    out_specs = (
        P(None, ("grp", "slab"), "col", None),
        P(("grp", "slab"), "col", None),
        P(None, ("grp", "slab"), "col", None),
        P(None, ("grp", "slab"), "col", None),
    )
    return jax.shard_map(
        on_device, mesh=mesh, in_specs=in_specs, out_specs=out_specs, check_vma=False
    )
```

profile of v0, /device:TPU:0, one launch (start us, length us, event | category | flops | bytes accessed | tf_op | source)
XLA Modules:
  0.0 313.0 jit_solution(10889490930675842464)
XLA Ops:
  0.6 5.5 %collective-permute-start.16 = (f32[3,1,16,256]{3,2,1,0:T(8,128)}, f32[3,1,16,256]{3,2,1,0:T(8,128)}, u32[]{:S(2)}, u32[]{:S(2)}) collective-permute-start(f32[3,1,16,256]{3,2,1,0:T(8,128)} %param.9), channel_id=1, source_target_pairs={{0,2},{2,4},{4,6},{6,8},{8,10},{10,12},{12,14},{1,3},{3,5},{5,7},{... | collective-permute-start | bytes 147464 | tf_op jit(solution)/shard_map/ppermute | solution.py:31
  9.9 5.2 %collective-permute-start.1 = (f32[1,64,1024]{2,1,0:T(8,128)S(1)}, f32[1,64,1024]{2,1,0:T(8,128)S(1)}, u32[]{:S(2)}, u32[]{:S(2)}) collective-permute-start(f32[1,64,1024]{2,1,0:T(8,128)S(1)} %get-tuple-element.53), channel_id=1, source_target_pairs={{0,2},{2,4},{4,6},{6,8},{8,10},{10,12},{12,14},{1,3},{3,5},{5,7},{... | collective-permute-start | bytes 786440 | tf_op jit(solution)/shard_map/ppermute | solution.py:31
  18.9 5.8 %collective-permute-done.1 = f32[1,64,1024]{2,1,0:T(8,128)S(1)} collective-permute-done((f32[1,64,1024]{2,1,0:T(8,128)S(1)}, f32[1,64,1024]{2,1,0:T(8,128)S(1)}, u32[]{:S(2)}, u32[]{:S(2)}) %collective-permute-start.1) | collective-permute-done | bytes 262176 | tf_op jit(solution)/shard_map/ppermute | solution.py:31
  40.7 4.5 %fusion.57 = f32[4,64,1024]{2,1,0:T(8,128)S(1)} fusion(f32[4,64,1024]{2,1,0:T(8,128)S(1)} %slice_bitcast_fusion, f32[6,66,1026]{2,1,0:T(8,128)S(1)} %select_maximum_fusion.12, f32[6,65,1024]{2,1,0:T(8,128)S(1)} %get-tuple-element.68, f32[6,65,1024]{2,1,0:T(8,128)S(1)} %get-tuple-element.67, f32[1,64,1024]{2,1,0:T(8,128)S(1)} %collective-permute-done.1, ...), kind=kLoop, calls=%fused_computation.129 | loop fusion | flops 18874368 | bytes 24117248 | tf_op jit(solution)/shard_map/add | solution.py:94
  46.6 5.0 %collective-permute-start.5 = (f32[1,64,1024]{2,1,0:T(8,128)S(1)}, f32[1,64,1024]{2,1,0:T(8,128)S(1)}, u32[]{:S(2)}, u32[]{:S(2)}) collective-permute-start(f32[1,64,1024]{2,1,0:T(8,128)S(1)} %get-tuple-element.78), channel_id=1, source_target_pairs={{0,2},{2,4},{4,6},{6,8},{8,10},{10,12},{12,14},{1,3},{3,5},{5,7},{... | collective-permute-start | bytes 786440 | tf_op jit(solution)/shard_map/ppermute | solution.py:31
  55.5 5.8 %collective-permute-done.5 = f32[1,64,1024]{2,1,0:T(8,128)S(1)} collective-permute-done((f32[1,64,1024]{2,1,0:T(8,128)S(1)}, f32[1,64,1024]{2,1,0:T(8,128)S(1)}, u32[]{:S(2)}, u32[]{:S(2)}) %collective-permute-start.5) | collective-permute-done | bytes 262176 | tf_op jit(solution)/shard_map/ppermute | solution.py:31
  71.2 6.3 %fusion.40 = f32[4,64,1024]{2,1,0:T(8,128)S(1)} fusion(f32[4,64,1024]{2,1,0:T(8,128)S(1)} %fusion.57, f32[6,66,1026]{2,1,0:T(8,128)S(1)} %select_maximum_fusion.8, f32[6,65,1024]{2,1,0:T(8,128)S(1)} %get-tuple-element.64, f32[6,65,1024]{2,1,0:T(8,128)S(1)} %get-tuple-element.63, f32[1,64,1024]{2,1,0:T(8,128)S(1)} %collective-permute-done.5, ...), kind=kLoop, calls=%fused_computation.98 | loop fusion | flops 33292288 | bytes 25165824 | tf_op jit(solution)/shard_map/add | solution.py:94
  78.8 5.0 %collective-permute-start.9 = (f32[1,64,1024]{2,1,0:T(8,128)S(1)}, f32[1,64,1024]{2,1,0:T(8,128)S(1)}, u32[]{:S(2)}, u32[]{:S(2)}) collective-permute-start(f32[1,64,1024]{2,1,0:T(8,128)S(1)} %get-tuple-element.76), channel_id=1, source_target_pairs={{0,2},{2,4},{4,6},{6,8},{8,10},{10,12},{12,14},{1,3},{3,5},{5,7},{... | collective-permute-start | bytes 786440 | tf_op jit(solution)/shard_map/ppermute | solution.py:31
  84.1 3.6 %collective-permute-done.8 = f32[1,64,1024]{2,1,0:T(8,128)S(1)} collective-permute-done((f32[1,64,1024]{2,1,0:T(8,128)S(1)}, f32[1,64,1024]{2,1,0:T(8,128)S(1)}, u32[]{:S(2)}, u32[]{:S(2)}) %collective-permute-start.8) | collective-permute-done | bytes 262176 | tf_op jit(solution)/shard_map/ppermute | solution.py:32
  87.7 5.8 %collective-permute-done.9 = f32[1,64,1024]{2,1,0:T(8,128)S(1)} collective-permute-done((f32[1,64,1024]{2,1,0:T(8,128)S(1)}, f32[1,64,1024]{2,1,0:T(8,128)S(1)}, u32[]{:S(2)}, u32[]{:S(2)}) %collective-permute-start.9) | collective-permute-done | bytes 262176 | tf_op jit(solution)/shard_map/ppermute | solution.py:31
  99.8 8.4 %fusion.23 = f32[4,64,1024]{2,1,0:T(8,128)S(1)} fusion(f32[4,64,1024]{2,1,0:T(8,128)S(1)} %fusion.40, f32[6,66,1026]{2,1,0:T(8,128)S(1)} %select_maximum_fusion.4, f32[6,65,1024]{2,1,0:T(8,128)S(1)} %get-tuple-element.60, f32[6,65,1024]{2,1,0:T(8,128)S(1)} %get-tuple-element.59, f32[1,64,1024]{2,1,0:T(8,128)S(1)} %collective-permute-done.9, ...), kind=kLoop, calls=%fused_computation.67 | loop fusion | flops 47710208 | bytes 26214400 | tf_op jit(solution)/shard_map/add | solution.py:94
  109.6 5.0 %collective-permute-start.13 = (f32[1,64,1024]{2,1,0:T(8,128)S(1)}, f32[1,64,1024]{2,1,0:T(8,128)S(1)}, u32[]{:S(2)}, u32[]{:S(2)}) collective-permute-start(f32[1,64,1024]{2,1,0:T(8,128)S(1)} %get-tuple-element.74), channel_id=1, source_target_pairs={{0,2},{2,4},{4,6},{6,8},{8,10},{10,12},{12,14},{1,3},{3,5},{5,7},{... | collective-permute-start | bytes 786440 | tf_op jit(solution)/shard_map/ppermute | solution.py:31
  114.9 4.7 %collective-permute-done.12 = f32[1,64,1024]{2,1,0:T(8,128)S(1)} collective-permute-done((f32[1,64,1024]{2,1,0:T(8,128)S(1)}, f32[1,64,1024]{2,1,0:T(8,128)S(1)}, u32[]{:S(2)}, u32[]{:S(2)}) %collective-permute-start.12) | collective-permute-done | bytes 262176 | tf_op jit(solution)/shard_map/ppermute | solution.py:32
  119.5 5.8 %collective-permute-done.13 = f32[1,64,1024]{2,1,0:T(8,128)S(1)} collective-permute-done((f32[1,64,1024]{2,1,0:T(8,128)S(1)}, f32[1,64,1024]{2,1,0:T(8,128)S(1)}, u32[]{:S(2)}, u32[]{:S(2)}) %collective-permute-start.13) | collective-permute-done | bytes 262176 | tf_op jit(solution)/shard_map/ppermute | solution.py:31
  132.2 11.5 %fusion.6 = (f32[4,64,1024]{2,1,0:T(8,128)S(1)}, f32[4,64,1024]{2,1,0:T(8,128)}, f32[4,64,1024]{2,1,0:T(8,128)}, f32[4,64,1024]{2,1,0:T(8,128)}) fusion(f32[4,64,1024]{2,1,0:T(8,128)S(1)} %fusion.23, f32[6,66,1026]{2,1,0:T(8,128)S(1)} %select_maximum_fusion, f32[6,65,1024]{2,1,0:T(8,128)S(1)} %get-tuple-element.56, f32[6,65,1024]{2,1,0:T(8,128)S(1)} %get-tuple-element.55, ...), kind=kLoop, calls=%fused_computation.36 | loop fusion | flops 62128128 | bytes 30408704 | tf_op jit(solution)/shard_map/add | solution.py:94
  143.7 68.4 %reshape.2435 = f32[2,2,32,2,512,2]{5,4,3,2,1,0:T(8,128)} reshape(f32[4,64,1024]{2,1,0:T(8,128)S(1)} %get-tuple-element.49) | data formatting | bytes 2097152 | tf_op jit(solution)/shard_map/reshape | solution.py:108
  212.1 20.8 %reduce_sum.21 = f32[2,32,512]{2,1,0:T(8,128)S(1)} reduce(f32[2,2,32,2,512,2]{5,4,3,2,1,0:T(8,128)} %reshape.2435, f32[]{:T(128)} %constant.134.clone.1), dimensions={1,3,5}, to_apply=%region_0.1 | reduce | flops 229376 | bytes 1179652 | tf_op jit(solution)/shard_map/reduce_sum | solution.py:109
  233.6 5.5 %reduce_sum.27 = f32[16,2,256,2]{3,2,1,0:T(8,128)} reshape(f32[32,512]{1,0:T(8,128)S(1)} %get-tuple-element.47) | data formatting | bytes 131072 | tf_op jit(solution)/shard_map/reduce_sum | solution.py:109
  244.2 5.0 %collective-permute-start.20 = (f32[9,1,16,256]{3,2,1,0:T(8,128)S(1)}, f32[9,1,16,256]{3,2,1,0:T(8,128)S(1)}, u32[]{:S(2)}, u32[]{:S(2)}) collective-permute-start(f32[9,1,16,256]{3,2,1,0:T(8,128)S(1)} %constant_dynamic-update-slice_fusion.3), channel_id=1, source_target_pairs={{0,2},{2,4},{4,6},{6,8},{8,10},{10,12},{12,14},{1,3},{3,5},{5,7},{... | collective-permute-start | bytes 442376 | tf_op jit(solution)/shard_map/ppermute | solution.py:31
  251.6 3.3 %collective-permute-done.20 = f32[9,1,16,256]{3,2,1,0:T(8,128)S(1)} collective-permute-done((f32[9,1,16,256]{3,2,1,0:T(8,128)S(1)}, f32[9,1,16,256]{3,2,1,0:T(8,128)S(1)}, u32[]{:S(2)}, u32[]{:S(2)}) %collective-permute-start.20) | collective-permute-done | bytes 147488 | tf_op jit(solution)/shard_map/ppermute | solution.py:31
  262.3 5.0 %collective-permute-start.24 = (f32[3,1,16,256]{3,2,1,0:T(8,128)S(1)}, f32[3,1,16,256]{3,2,1,0:T(8,128)S(1)}, u32[]{:S(2)}, u32[]{:S(2)}) collective-permute-start(f32[3,1,16,256]{3,2,1,0:T(8,128)S(1)} %fusion.155), channel_id=1, source_target_pairs={{0,2},{2,4},{4,6},{6,8},{8,10},{10,12},{12,14},{1,3},{3,5},{5,7},{... | collective-permute-start | bytes 147464 | tf_op jit(solution)/shard_map/ppermute | solution.py:31
  276.9 5.5 %collective-permute-start.28 = (f32[9,1,16,256]{3,2,1,0:T(8,128)S(1)}, f32[9,1,16,256]{3,2,1,0:T(8,128)S(1)}, u32[]{:S(2)}, u32[]{:S(2)}) collective-permute-start(f32[9,1,16,256]{3,2,1,0:T(8,128)S(1)} %constant_dynamic-update-slice_fusion.12), channel_id=1, source_target_pairs={{0,2},{2,4},{4,6},{6,8},{8,10},{10,12},{12,14},{1,3},{3,5},{5,7},{... | collective-permute-start | bytes 442376 | tf_op jit(solution)/shard_map/ppermute | solution.py:31
  284.8 3.9 %collective-permute-done.28 = f32[9,1,16,256]{3,2,1,0:T(8,128)S(1)} collective-permute-done((f32[9,1,16,256]{3,2,1,0:T(8,128)S(1)}, f32[9,1,16,256]{3,2,1,0:T(8,128)S(1)}, u32[]{:S(2)}, u32[]{:S(2)}) %collective-permute-start.28) | collective-permute-done | bytes 147488 | tf_op jit(solution)/shard_map/ppermute | solution.py:31
  296.4 5.0 %collective-permute-start.32 = (f32[3,1,16,256]{3,2,1,0:T(8,128)S(1)}, f32[3,1,16,256]{3,2,1,0:T(8,128)S(1)}, u32[]{:S(2)}, u32[]{:S(2)}) collective-permute-start(f32[3,1,16,256]{3,2,1,0:T(8,128)S(1)} %fusion.139), channel_id=1, source_target_pairs={{0,2},{2,4},{4,6},{6,8},{8,10},{10,12},{12,14},{1,3},{3,5},{5,7},{... | collective-permute-start | bytes 147464 | tf_op jit(solution)/shard_map/ppermute | solution.py:31
  (199 shorter events, 100.9 us)
Async XLA Ops:
  0.6 51.0 %collective-permute-start.16 = (f32[3,1,16,256]{3,2,1,0:T(8,128)}, f32[3,1,16,256]{3,2,1,0:T(8,128)}, u32[]{:S(2)}, u32[]{:S(2)}) collective-permute-start(f32[3,1,16,256]{3,2,1,0:T(8,128)} %param.9), channel_id=1, source_target_pairs={{0,2},{2,4},{4,6},{6,8},{8,10},{10,12},{12,14},{1,3},{3,5},{5,7},{... | collective-permute-start | bytes 147464 | tf_op jit(solution)/shard_map/ppermute | solution.py:31
  6.1 46.4 %collective-permute-start.17 = (f32[3,1,16,256]{3,2,1,0:T(8,128)}, f32[3,1,16,256]{3,2,1,0:T(8,128)S(1)}, u32[]{:S(2)}, u32[]{:S(2)}) collective-permute-start(f32[3,1,16,256]{3,2,1,0:T(8,128)} %param.9), channel_id=1, source_target_pairs={{2,0},{4,2},{6,4},{8,6},{10,8},{12,10},{14,12},{3,1},{5,3},{7,5},{... | collective-permute-start | bytes 147464 | tf_op jit(solution)/shard_map/ppermute | solution.py:32
  8.5 10.4 %collective-permute-start = (f32[1,64,1024]{2,1,0:T(8,128)S(1)}, f32[1,64,1024]{2,1,0:T(8,128)S(1)}, u32[]{:S(2)}, u32[]{:S(2)}) collective-permute-start(f32[1,64,1024]{2,1,0:T(8,128)S(1)} %get-tuple-element.54), channel_id=1, source_target_pairs={{2,0},{4,2},{6,4},{8,6},{10,8},{12,10},{14,12},{3,1},{5,3},{7,5},{... | collective-permute-start | bytes 786440 | tf_op jit(solution)/shard_map/ppermute | solution.py:32
  9.9 14.8 %collective-permute-start.1 = (f32[1,64,1024]{2,1,0:T(8,128)S(1)}, f32[1,64,1024]{2,1,0:T(8,128)S(1)}, u32[]{:S(2)}, u32[]{:S(2)}) collective-permute-start(f32[1,64,1024]{2,1,0:T(8,128)S(1)} %get-tuple-element.53), channel_id=1, source_target_pairs={{0,2},{2,4},{4,6},{6,8},{8,10},{10,12},{12,14},{1,3},{3,5},{5,7},{... | collective-permute-start | bytes 786440 | tf_op jit(solution)/shard_map/ppermute | solution.py:31
  25.3 12.5 %collective-permute-start.2 = (f32[6,1,1024]{2,1,0:T(1,128)}, f32[6,1,1024]{2,1,0:T(1,128)S(1)}, u32[]{:S(2)}, u32[]{:S(2)}) collective-permute-start(f32[6,1,1024]{2,1,0:T(1,128)} %get-tuple-element.70), channel_id=1, source_target_pairs={{1,0},{3,2},{5,4},{7,6},{9,8},{11,10},{13,12},{15,14},{17,16},{19,... | collective-permute-start | bytes 73736 | tf_op jit(solution)/shard_map/ppermute | solution.py:32
  26.6 11.2 %collective-permute-start.3 = (f32[6,1,1024]{2,1,0:T(1,128)}, f32[6,1,1024]{2,1,0:T(1,128)S(1)}, u32[]{:S(2)}, u32[]{:S(2)}) collective-permute-start(f32[6,1,1024]{2,1,0:T(1,128)} %get-tuple-element.69), channel_id=1, source_target_pairs={{0,1},{2,3},{4,5},{6,7},{8,9},{10,11},{12,13},{14,15},{16,17},{18,... | collective-permute-start | bytes 73736 | tf_op jit(solution)/shard_map/ppermute | solution.py:31
  45.3 10.2 %collective-permute-start.4 = (f32[1,64,1024]{2,1,0:T(8,128)S(1)}, f32[1,64,1024]{2,1,0:T(8,128)S(1)}, u32[]{:S(2)}, u32[]{:S(2)}) collective-permute-start(f32[1,64,1024]{2,1,0:T(8,128)S(1)} %get-tuple-element.79), channel_id=1, source_target_pairs={{2,0},{4,2},{6,4},{8,6},{10,8},{12,10},{14,12},{3,1},{5,3},{7,5},{... | collective-permute-start | bytes 786440 | tf_op jit(solution)/shard_map/ppermute | solution.py:32
  46.6 14.7 %collective-permute-start.5 = (f32[1,64,1024]{2,1,0:T(8,128)S(1)}, f32[1,64,1024]{2,1,0:T(8,128)S(1)}, u32[]{:S(2)}, u32[]{:S(2)}) collective-permute-start(f32[1,64,1024]{2,1,0:T(8,128)S(1)} %get-tuple-element.78), channel_id=1, source_target_pairs={{0,2},{2,4},{4,6},{6,8},{8,10},{10,12},{12,14},{1,3},{3,5},{5,7},{... | collective-permute-start | bytes 786440 | tf_op jit(solution)/shard_map/ppermute | solution.py:31
  61.3 8.7 %collective-permute-start.6 = (f32[6,1,1024]{2,1,0:T(1,128)S(1)}, f32[6,1,1024]{2,1,0:T(1,128)S(1)}, u32[]{:S(2)}, u32[]{:S(2)}) collective-permute-start(f32[6,1,1024]{2,1,0:T(1,128)S(1)} %get-tuple-element.66), channel_id=1, source_target_pairs={{1,0},{3,2},{5,4},{7,6},{9,8},{11,10},{13,12},{15,14},{17,16},{19,... | collective-permute-start | bytes 73736 | tf_op jit(solution)/shard_map/ppermute | solution.py:32
  62.6 7.4 %collective-permute-start.7 = (f32[6,1,1024]{2,1,0:T(1,128)S(1)}, f32[6,1,1024]{2,1,0:T(1,128)S(1)}, u32[]{:S(2)}, u32[]{:S(2)}) collective-permute-start(f32[6,1,1024]{2,1,0:T(1,128)S(1)} %get-tuple-element.65), channel_id=1, source_target_pairs={{0,1},{2,3},{4,5},{6,7},{8,9},{10,11},{12,13},{14,15},{16,17},{18,... | collective-permute-start | bytes 73736 | tf_op jit(solution)/shard_map/ppermute | solution.py:31
  65.7 18.2 %collective-permute-start.19 = (f32[3,3,1,256]{3,2,1,0:T(1,128)S(1)}, f32[3,3,1,256]{3,2,1,0:T(1,128)S(1)}, u32[]{:S(2)}, u32[]{:S(2)}) collective-permute-start(f32[3,3,1,256]{3,2,1,0:T(1,128)S(1)} %get-tuple-element.101), channel_id=1, source_target_pairs={{1,0},{3,2},{5,4},{7,6},{9,8},{11,10},{13,12},{15,14},{17,16},{19,... | collective-permute-start | bytes 27656 | tf_op jit(solution)/shard_map/ppermute | solution.py:32
  67.0 16.9 %collective-permute-start.18 = (f32[3,3,1,256]{3,2,1,0:T(1,128)S(1)}, f32[3,3,1,256]{3,2,1,0:T(1,128)S(1)}, u32[]{:S(2)}, u32[]{:S(2)}) collective-permute-start(f32[3,3,1,256]{3,2,1,0:T(1,128)S(1)} %get-tuple-element.100), channel_id=1, source_target_pairs={{0,1},{2,3},{4,5},{6,7},{8,9},{10,11},{12,13},{14,15},{16,17},{18,... | collective-permute-start | bytes 27656 | tf_op jit(solution)/shard_map/ppermute | solution.py:31
  77.5 10.2 %collective-permute-start.8 = (f32[1,64,1024]{2,1,0:T(8,128)S(1)}, f32[1,64,1024]{2,1,0:T(8,128)S(1)}, u32[]{:S(2)}, u32[]{:S(2)}) collective-permute-start(f32[1,64,1024]{2,1,0:T(8,128)S(1)} %get-tuple-element.77), channel_id=1, source_target_pairs={{2,0},{4,2},{6,4},{8,6},{10,8},{12,10},{14,12},{3,1},{5,3},{7,5},{... | collective-permute-start | bytes 786440 | tf_op jit(solution)/shard_map/ppermute | solution.py:32
  78.8 14.7 %collective-permute-start.9 = (f32[1,64,1024]{2,1,0:T(8,128)S(1)}, f32[1,64,1024]{2,1,0:T(8,128)S(1)}, u32[]{:S(2)}, u32[]{:S(2)}) collective-permute-start(f32[1,64,1024]{2,1,0:T(8,128)S(1)} %get-tuple-element.76), channel_id=1, source_target_pairs={{0,2},{2,4},{4,6},{6,8},{8,10},{10,12},{12,14},{1,3},{3,5},{5,7},{... | collective-permute-start | bytes 786440 | tf_op jit(solution)/shard_map/ppermute | solution.py:31
  108.3 11.2 %collective-permute-start.12 = (f32[1,64,1024]{2,1,0:T(8,128)S(1)}, f32[1,64,1024]{2,1,0:T(8,128)S(1)}, u32[]{:S(2)}, u32[]{:S(2)}) collective-permute-start(f32[1,64,1024]{2,1,0:T(8,128)S(1)} %get-tuple-element.75), channel_id=1, source_target_pairs={{2,0},{4,2},{6,4},{8,6},{10,8},{12,10},{14,12},{3,1},{5,3},{7,5},{... | collective-permute-start | bytes 786440 | tf_op jit(solution)/shard_map/ppermute | solution.py:32
  109.6 15.7 %collective-permute-start.13 = (f32[1,64,1024]{2,1,0:T(8,128)S(1)}, f32[1,64,1024]{2,1,0:T(8,128)S(1)}, u32[]{:S(2)}, u32[]{:S(2)}) collective-permute-start(f32[1,64,1024]{2,1,0:T(8,128)S(1)} %get-tuple-element.74), channel_id=1, source_target_pairs={{0,2},{2,4},{4,6},{6,8},{8,10},{10,12},{12,14},{1,3},{3,5},{5,7},{... | collective-permute-start | bytes 786440 | tf_op jit(solution)/shard_map/ppermute | solution.py:31
  242.7 8.9 %collective-permute-start.21 = (f32[9,1,16,256]{3,2,1,0:T(8,128)S(1)}, f32[9,1,16,256]{3,2,1,0:T(8,128)S(1)}, u32[]{:S(2)}, u32[]{:S(2)}) collective-permute-start(f32[9,1,16,256]{3,2,1,0:T(8,128)S(1)} %constant_dynamic-update-slice_fusion.3), channel_id=1, source_target_pairs={{2,0},{4,2},{6,4},{8,6},{10,8},{12,10},{14,12},{3,1},{5,3},{7,5},{... | collective-permute-start | bytes 442376 | tf_op jit(solution)/shard_map/ppermute | solution.py:32
  244.2 10.8 %collective-permute-start.20 = (f32[9,1,16,256]{3,2,1,0:T(8,128)S(1)}, f32[9,1,16,256]{3,2,1,0:T(8,128)S(1)}, u32[]{:S(2)}, u32[]{:S(2)}) collective-permute-start(f32[9,1,16,256]{3,2,1,0:T(8,128)S(1)} %constant_dynamic-update-slice_fusion.3), channel_id=1, source_target_pairs={{0,2},{2,4},{4,6},{6,8},{8,10},{10,12},{12,14},{1,3},{3,5},{5,7},{... | collective-permute-start | bytes 442376 | tf_op jit(solution)/shard_map/ppermute | solution.py:31
  262.3 6.7 %collective-permute-start.24 = (f32[3,1,16,256]{3,2,1,0:T(8,128)S(1)}, f32[3,1,16,256]{3,2,1,0:T(8,128)S(1)}, u32[]{:S(2)}, u32[]{:S(2)}) collective-permute-start(f32[3,1,16,256]{3,2,1,0:T(8,128)S(1)} %fusion.155), channel_id=1, source_target_pairs={{0,2},{2,4},{4,6},{6,8},{8,10},{10,12},{12,14},{1,3},{3,5},{5,7},{... | collective-permute-start | bytes 147464 | tf_op jit(solution)/shard_map/ppermute | solution.py:31
  275.6 9.2 %collective-permute-start.29 = (f32[9,1,16,256]{3,2,1,0:T(8,128)S(1)}, f32[9,1,16,256]{3,2,1,0:T(8,128)S(1)}, u32[]{:S(2)}, u32[]{:S(2)}) collective-permute-start(f32[9,1,16,256]{3,2,1,0:T(8,128)S(1)} %constant_dynamic-update-slice_fusion.12), channel_id=1, source_target_pairs={{2,0},{4,2},{6,4},{8,6},{10,8},{12,10},{14,12},{3,1},{5,3},{7,5},{... | collective-permute-start | bytes 442376 | tf_op jit(solution)/shard_map/ppermute | solution.py:32
  276.9 11.8 %collective-permute-start.28 = (f32[9,1,16,256]{3,2,1,0:T(8,128)S(1)}, f32[9,1,16,256]{3,2,1,0:T(8,128)S(1)}, u32[]{:S(2)}, u32[]{:S(2)}) collective-permute-start(f32[9,1,16,256]{3,2,1,0:T(8,128)S(1)} %constant_dynamic-update-slice_fusion.12), channel_id=1, source_target_pairs={{0,2},{2,4},{4,6},{6,8},{8,10},{10,12},{12,14},{1,3},{3,5},{5,7},{... | collective-permute-start | bytes 442376 | tf_op jit(solution)/shard_map/ppermute | solution.py:31
  295.1 8.5 %collective-permute-start.33 = (f32[3,1,16,256]{3,2,1,0:T(8,128)S(1)}, f32[3,1,16,256]{3,2,1,0:T(8,128)S(1)}, u32[]{:S(2)}, u32[]{:S(2)}) collective-permute-start(f32[3,1,16,256]{3,2,1,0:T(8,128)S(1)} %fusion.139), channel_id=1, source_target_pairs={{2,0},{4,2},{6,4},{8,6},{10,8},{12,10},{14,12},{3,1},{5,3},{7,5},{... | collective-permute-start | bytes 147464 | tf_op jit(solution)/shard_map/ppermute | solution.py:32
  296.4 7.2 %collective-permute-start.32 = (f32[3,1,16,256]{3,2,1,0:T(8,128)S(1)}, f32[3,1,16,256]{3,2,1,0:T(8,128)S(1)}, u32[]{:S(2)}, u32[]{:S(2)}) collective-permute-start(f32[3,1,16,256]{3,2,1,0:T(8,128)S(1)} %fusion.139), channel_id=1, source_target_pairs={{0,2},{2,4},{4,6},{6,8},{8,10},{10,12},{12,14},{1,3},{3,5},{5,7},{... | collective-permute-start | bytes 147464 | tf_op jit(solution)/shard_map/ppermute | solution.py:31
  303.7 6.7 %collective-permute-start.35 = (f32[3,3,1,256]{3,2,1,0:T(1,128)S(1)}, f32[3,3,1,256]{3,2,1,0:T(1,128)S(1)}, u32[]{:S(2)}, u32[]{:S(2)}) collective-permute-start(f32[3,3,1,256]{3,2,1,0:T(1,128)S(1)} %get-tuple-element.97), channel_id=1, source_target_pairs={{1,0},{3,2},{5,4},{7,6},{9,8},{11,10},{13,12},{15,14},{17,16},{19,... | collective-permute-start | bytes 27656 | tf_op jit(solution)/shard_map/ppermute | solution.py:32
  (26 other events, 247.5 us)
where the time goes:
time: 315 us; the launch traced here: 313 us
  starting transfers between devices  97.6 us (31%)
  local copies, waits for them, and re-layouts  88.1 us (28%)
  other arithmetic  71.7 us (23%)
  waiting for transfers between devices  53.7 us (17%)
    ppermute x18, starting transfers between devices, extended(): before = lax.ppermute(last, axis, up)  74.1 us
    reshape x1, local copies, waits for them, and re-layouts, coarsen(): field.reshape(field.shape[0] // 2, 2, field.shape[1] // 2, 2, field.shape...  68.4 us
    ppermute x18, waiting for transfers between devices, extended(): before = lax.ppermute(last, axis, up)  34.7 us
    add x4, other arithmetic, excite_step(): new_volt = volt + diffusion(padded, coeff) + STEP_TIME * ion  30.7 us
    reduce_sum x3, other arithmetic, coarsen(): return jnp.mean(shaped, axis=(1, 3, 5))  24.3 us
    ppermute x18, starting transfers between devices, extended(): after = lax.ppermute(initial, axis, down)  23.5 us
    ppermute x18, waiting for transfers between devices, extended(): after = lax.ppermute(initial, axis, down)  19 us
    concatenate x17, other arithmetic, extended(): array = jnp.concatenate([before, array, after], axis=dim)  6.91 us
  transfers between devices with their start and end apart: 36, of which 19 were waited for; matrix products, arithmetic and copies ran while one was open for 10% of the time, Pallas kernels for 0%

commit v1 on v0

v1 whole, which is shorter than its diff:
```python
import functools

import jax
import jax.numpy as jnp
from jax import lax
from jax.experimental import pallas as pl
from jax.experimental.pallas import tpu as pltpu
from jax.sharding import PartitionSpec as P

SUB = 4
MECH_STEPS = 2
NFIB = 64

STEP_TIME = 0.05
LAME_FIRST = 1.0
SHEAR = 0.5
ACTIVE_GAIN = 0.5
MECH_RATE = 0.15
SIGMA_LONG = 0.16
SIGMA_TRANS = 0.04
PAIRS = ((0, 0), (1, 1), (2, 2), (0, 1), (0, 2), (1, 2))

C_ZZ, C_ZY, C_ZXR, C_ZXL, C_MID, C_YY, C_XXR, C_YXR, C_XXL, C_YXL = range(10)

HIGHEST = lax.Precision.HIGHEST
LIMIT = 40 * 1024 * 1024


def params(**kwargs):
    return pltpu.CompilerParams(vmem_limit_bytes=LIMIT, **kwargs)


def cost(flops, nbytes, trans=0):
    return pl.CostEstimate(flops=flops, bytes_accessed=nbytes, transcendentals=trans)


def row_iota():
    return lax.broadcasted_iota(jnp.int32, (8, 1024), 0)


def next_row(cur, nxt, sub):
    return pltpu.roll(jnp.where(sub == 0, nxt, cur), 7, 0)


def prev_row(cur, prv, sub):
    return pltpu.roll(jnp.where(sub == 7, prv, cur), 1, 0)


def left(val):
    return pltpu.roll(val, val.shape[-1] - 1, val.ndim - 1)


def right(val):
    return pltpu.roll(val, 1, val.ndim - 1)


def edge_masks(tile, side, own):
    before = jnp.where((tile == 0) & (side == 0), 0.0, 1.0)
    after = jnp.where((tile == own - 1) & (side == 1), 0.0, 1.0)
    return before, after


def ring_neighbours(tile, tiles):
    before = jnp.where(tile == 0, tiles - 1, tile - 1)
    after = jnp.where(tile == tiles - 1, 0, tile + 1)
    return before, after


def coeff_kernel(cond_ref, out_ref):
    six, rows, width = cond_ref.shape
    fine = 4 * width
    mech = lax.broadcasted_iota(jnp.int32, (width, fine), 0)
    cell = lax.broadcasted_iota(jnp.int32, (width, fine), 1)
    tiles = rows // 2
    sub = lax.broadcasted_iota(jnp.int32, (8, fine), 0)

    def spread(comps, shift):
        pick = jnp.where(mech == ((cell + shift) >> 2), 1.0, 0.0)
        flat = jnp.concatenate([cond_ref[comp] for comp in comps], axis=0)
        wide = jnp.dot(flat, pick, precision=HIGHEST, preferred_element_type=jnp.float32)
        return [wide[pos * rows : (pos + 1) * rows] for pos in range(len(comps))]

    def store(index, wide):
        for tile in range(tiles):
            upper = jnp.broadcast_to(wide[2 * tile : 2 * tile + 1], (8, fine))
            lower = jnp.broadcast_to(wide[2 * tile + 1 : 2 * tile + 2], (8, fine))
            out_ref[index, tile] = jnp.where(sub < 4, upper, lower)

    zz, yy, xx, zy = spread((0, 1, 2, 3), 0)
    store(C_ZZ, zz)
    store(C_YY, yy)
    store(C_MID, -2.0 * (zz + yy + xx))
    store(C_ZY, 0.5 * zy)
    xx, zx, yx = spread((2, 4, 5), -1)
    store(C_XXR, xx)
    store(C_ZXR, 0.5 * zx)
    store(C_YXR, 0.5 * yx)
    xx, zx, yx = spread((2, 4, 5), 1)
    store(C_XXL, xx)
    store(C_ZXL, 0.5 * zx)
    store(C_YXL, 0.5 * yx)


def fine_coeffs(cond_rows):
    six, rows, width = cond_rows.shape
    return pl.pallas_call(
        coeff_kernel,
        out_shape=jax.ShapeDtypeStruct((10, rows // 2, 8, 4 * width), jnp.float32),
        compiler_params=params(),
        cost_estimate=cost(2_000_000, 3_200_000),
        name="coeffs",
    )(cond_rows)


def inverse(val):
    guess = pl.reciprocal(val, approx=True)
    return guess * (2.0 - val * guess)


def ionic(u, v, w, s):
    t_v = jnp.tanh(50.0 * u - 15.0)
    t_w = jnp.tanh(50.0 * u - 6.5)
    t_o = jnp.tanh(50.0 * u - 0.3)
    t_m = jnp.tanh(65.0 * u - 65.0 * 0.03)
    t_f = jnp.tanh(2.0458 * u - 2.0458 * 0.65)
    t_s = jnp.tanh(2.0994 * u - 2.0994 * 0.9087)
    hv = 0.5 + 0.5 * t_v
    hw = 0.5 + 0.5 * t_w
    ho = 0.5 + 0.5 * t_o
    nv = 1.0 - hv
    nw = 1.0 - hw
    no = 1.0 - ho
    r_vm = inverse(605.0 + 545.0 * t_o)
    r_wm = inverse(37.5 - 22.5 * t_m)
    half_so = 0.5 * (30.0181 - 0.9957)
    r_so = inverse((30.0181 - half_so) - half_so * t_f)
    r_s = inverse(9.3671 + 6.6329 * t_w)
    r_o = inverse(203.0 - 197.0 * t_o)
    w_inf = no * (1.0 - u * (1.0 / 0.07)) + 0.94 * ho
    hvv = hv * v
    hww = hw * w
    fast = hvv * ((u - 0.3) * (1.55 - u)) * (STEP_TIME / 0.11)
    out = (u * nw) * r_o + hw * r_so
    slow = hww * s * (STEP_TIME / 1.8875)
    u_add = fast + slow - STEP_TIME * out
    v_new = v + (nv * (no - v)) * (STEP_TIME * r_vm) - hvv * (STEP_TIME / 1.4506)
    w_new = w + (nw * (w_inf - w)) * (STEP_TIME * r_wm) - hww * (STEP_TIME / 200.0)
    s_new = s + ((0.5 + 0.5 * t_s) - s) * (STEP_TIME * r_s)
    return u_add, v_new, w_new, s_new


def local_kernel(last, tiles, per_block, side_ref, lo_ref, mid_ref, hi_ref, gate_ref, coeff_ref, *outs):
    side = side_ref[0]
    sub = row_iota()
    own = tiles - 1
    refs = [lambda t: lo_ref[t], lambda t: mid_ref[0, t], lambda t: mid_ref[1, t], lambda t: hi_ref[t]]
    planes = len(refs)

    def one(local_tile, carry):
        tile = pl.program_id(0) * per_block + local_tile
        before, after = ring_neighbours(tile, tiles)
        mask_before, mask_after = edge_masks(tile, side, own)
        cur = [ref(tile) for ref in refs]
        prv = [ref(before) * mask_before for ref in refs]
        nxt = [ref(after) * mask_after for ref in refs]

        def coeff(index):
            return coeff_ref[index, local_tile]

        for plane in range(planes):
            u = cur[plane]

            def slope(field):
                if plane == 0:
                    return field[1]
                if plane == planes - 1:
                    return -field[plane - 1]
                return field[plane + 1] - field[plane - 1]

            if plane == 0:
                around = cur[1]
            elif plane == planes - 1:
                around = cur[plane - 1]
            else:
                around = cur[plane + 1] + cur[plane - 1]
            wide = slope(cur)
            u_next = next_row(u, nxt[plane], sub)
            u_prev = prev_row(u, prv[plane], sub)
            w_next = next_row(wide, slope(nxt), sub)
            w_prev = prev_row(wide, slope(prv), sub)
            tall = u_next - u_prev
            diff = coeff(C_MID) * u + coeff(C_ZZ) * around
            diff += coeff(C_YY) * (u_next + u_prev) + coeff(C_ZY) * (w_next - w_prev)
            diff += left(coeff(C_XXR) * u + coeff(C_ZXR) * wide + coeff(C_YXR) * tall)
            diff += right(coeff(C_XXL) * u - coeff(C_ZXL) * wide - coeff(C_YXL) * tall)
            base = u + diff
            chunk = 256
            for start in range(0, 1024, chunk):
                lanes = slice(start, start + chunk)
                u_add, v_new, w_new, s_new = ionic(
                    u[:, lanes],
                    gate_ref[0, plane, local_tile, :, lanes],
                    gate_ref[1, plane, local_tile, :, lanes],
                    gate_ref[2, plane, local_tile, :, lanes],
                )
                u_new = base[:, lanes] + u_add
                if last:
                    outs[0][0, plane, local_tile, :, lanes] = u_new
                    outs[0][1, plane, local_tile, :, lanes] = v_new
                    outs[0][2, plane, local_tile, :, lanes] = w_new
                    outs[0][3, plane, local_tile, :, lanes] = s_new
                else:
                    if plane == 0:
                        outs[0][local_tile, :, lanes] = u_new
                    elif plane == planes - 1:
                        outs[2][local_tile, :, lanes] = u_new
                    else:
                        outs[1][plane - 1, local_tile, :, lanes] = u_new
                    outs[3][0, plane, local_tile, :, lanes] = v_new
                    outs[3][1, plane, local_tile, :, lanes] = w_new
                    outs[3][2, plane, local_tile, :, lanes] = s_new
        return carry

    lax.fori_loop(0, per_block, one, 0)


def local_step(side, lo, mid, hi, gates, coeffs, last):
    tiles, _, width = lo.shape
    per_block = 2 if last else 3
    blocks = (tiles - 1) // per_block if last else tiles // per_block
    whole3 = pl.BlockSpec((tiles, 8, width), lambda i: (0, 0, 0))
    whole4 = pl.BlockSpec((2, tiles, 8, width), lambda i: (0, 0, 0, 0))
    in_specs = [
        pl.BlockSpec(memory_space=pltpu.SMEM),
        whole3,
        whole4,
        whole3,
        pl.BlockSpec((3, 4, per_block, 8, width), lambda i: (0, 0, i, 0, 0)),
        pl.BlockSpec((10, per_block, 8, width), lambda i: (0, i, 0, 0)),
    ]
    if last:
        out_shape = jax.ShapeDtypeStruct((4, 4, tiles - 1, 8, width), jnp.float32)
        out_specs = pl.BlockSpec((4, 4, per_block, 8, width), lambda i: (0, 0, i, 0, 0))
    else:
        out_shape = [
            jax.ShapeDtypeStruct(lo.shape, jnp.float32),
            jax.ShapeDtypeStruct(mid.shape, jnp.float32),
            jax.ShapeDtypeStruct(hi.shape, jnp.float32),
            jax.ShapeDtypeStruct(gates.shape, jnp.float32),
        ]
        out_specs = [
            pl.BlockSpec((per_block, 8, width), lambda i: (i, 0, 0)),
            pl.BlockSpec((2, per_block, 8, width), lambda i: (0, i, 0, 0)),
            pl.BlockSpec((per_block, 8, width), lambda i: (i, 0, 0)),
            pl.BlockSpec((3, 4, per_block, 8, width), lambda i: (0, 0, i, 0, 0)),
        ]
    cells = 4 * tiles * 8 * width
    return pl.pallas_call(
        functools.partial(local_kernel, last, tiles, per_block),
        grid=(blocks,),
        in_specs=in_specs,
        out_specs=out_specs,
        out_shape=out_shape,
        compiler_params=params(),
        cost_estimate=cost(150 * cells, 40 * cells, 11 * cells),
        name="local_last" if last else "local",
    )(side, lo, mid, hi, gates, coeffs)


def halo_terms(halo_ref, coeff_ref, tile, tiles, side, sub, sign):
    before, after = ring_neighbours(tile, tiles)
    mask_before, mask_after = edge_masks(tile, side, tiles - 1)
    cur = halo_ref[tile]
    up = next_row(cur, halo_ref[after] * mask_after, sub)
    down = prev_row(cur, halo_ref[before] * mask_before, sub)
    cross = coeff_ref[C_ZY, tile] * (up - down)
    cross += left(coeff_ref[C_ZXR, tile] * cur) - right(coeff_ref[C_ZXL, tile] * cur)
    total = coeff_ref[C_ZZ, tile] * cur
    return total + cross if sign > 0 else total - cross


def halo_kernel(tiles, side_ref, lo_ref, hi_ref, below_ref, above_ref, coeff_ref, lo_out, hi_out):
    side = side_ref[0]
    sub = row_iota()

    def one(tile, carry):
        lo_out[tile] = lo_ref[tile] + halo_terms(below_ref, coeff_ref, tile, tiles, side, sub, -1)
        hi_out[tile] = hi_ref[tile] + halo_terms(above_ref, coeff_ref, tile, tiles, side, sub, 1)
        return carry

    lax.fori_loop(0, tiles, one, 0)


def halo_step(side, lo, hi, below, above, coeffs):
    tiles, _, width = lo.shape
    whole = pl.BlockSpec((tiles, 8, width), lambda i: (0, 0, 0))
    cells = 2 * tiles * 8 * width
    return pl.pallas_call(
        functools.partial(halo_kernel, tiles),
        grid=(1,),
        in_specs=[pl.BlockSpec(memory_space=pltpu.SMEM)]
        + [whole] * 4
        + [pl.BlockSpec((4, tiles, 8, width), lambda i: (0, 0, 0, 0))],
        out_specs=[whole, whole],
        out_shape=[jax.ShapeDtypeStruct(lo.shape, jnp.float32)] * 2,
        compiler_params=params(),
        cost_estimate=cost(15 * cells, 20 * cells),
        name="halo",
    )(side, lo, hi, below, above, coeffs)


def pair_matrix(width, scale):
    fine = lax.broadcasted_iota(jnp.int32, (width, width // 2), 0)
    coarse = lax.broadcasted_iota(jnp.int32, (width, width // 2), 1)
    return jnp.where((fine >> 1) == coarse, scale, 0.0)


def row_pairs(count, scale):
    coarse = lax.broadcasted_iota(jnp.int32, (count // 2, count), 0)
    fine = lax.broadcasted_iota(jnp.int32, (count // 2, count), 1)
    return jnp.where((fine >> 1) == coarse, scale, 0.0)


def dot(a, b):
    return jnp.dot(a, b, precision=HIGHEST, preferred_element_type=jnp.float32)


def pooled(field):
    rows, lanes = field.shape
    few = dot(row_pairs(rows, 0.5), field)
    pick = pair_matrix(256, 0.5)
    return jnp.concatenate([dot(few[:, at : at + 256], pick) for at in range(0, lanes, 256)], axis=1)


def finish_kernel(tiles, side_ref, part_ref, below_ref, above_ref, coeff_ref, tension_ref, out_ref, tension_out, active_out):
    side = side_ref[0]
    sub = row_iota()
    own = tiles - 1
    planes = part_ref.shape[1]

    def one(tile, carry):
        out_ref[0, 0, tile] = part_ref[0, 0, tile] + halo_terms(below_ref, coeff_ref, tile, tiles, side, sub, -1)
        for plane in range(1, planes - 1):
            out_ref[0, plane, tile] = part_ref[0, plane, tile]
        out_ref[0, planes - 1, tile] = part_ref[0, planes - 1, tile] + halo_terms(
            above_ref, coeff_ref, tile, tiles, side, sub, 1
        )
        return carry

    lax.fori_loop(0, own, one, 0)
    width = part_ref.shape[-1]
    total = None
    for layer in range(planes // 2):
        both = 0.5 * (out_ref[0, 2 * layer] + out_ref[0, 2 * layer + 1])
        mean = pooled(both.reshape(own * 8, width))
        old = tension_ref[layer]
        new = old + 0.5 * (mean - old)
        tension_out[layer] = new
        total = new if total is None else total + new
    active_out[...] = pooled(0.5 * total)


def finish_step(side, part, below, above, coeffs, tension):
    tiles, _, width = below.shape
    own = tiles - 1
    planes = part.shape[1]
    halo_spec = pl.BlockSpec((tiles, 8, width), lambda i: (0, 0, 0))
    u_spec = pl.BlockSpec((1, planes, own, 8, width), lambda i: (0, 0, 0, 0, 0))
    tension_spec = pl.BlockSpec(tension.shape, lambda i: (0, 0, 0))
    active_shape = (own * 2, width // 4)
    cells = planes * own * 8 * width
    return pl.pallas_call(
        functools.partial(finish_kernel, tiles),
        grid=(1,),
        in_specs=[
            pl.BlockSpec(memory_space=pltpu.SMEM),
            u_spec,
            halo_spec,
            halo_spec,
            pl.BlockSpec((4, tiles, 8, width), lambda i: (0, 0, 0, 0)),
            tension_spec,
        ],
        out_specs=[u_spec, tension_spec, pl.BlockSpec(active_shape, lambda i: (0, 0))],
        out_shape=[
            jax.ShapeDtypeStruct(part.shape, jnp.float32),
            jax.ShapeDtypeStruct(tension.shape, jnp.float32),
            jax.ShapeDtypeStruct(active_shape, jnp.float32),
        ],
        input_output_aliases={1: 0},
        compiler_params=params(),
        cost_estimate=cost(20 * cells, 20 * cells),
        name="finish",
    )(side, part, below, above, coeffs, tension)


REACH = 4
ROWS = 24


class Weights:
    def __init__(self, side, own, width):
        row = lax.broadcasted_iota(jnp.int32, (ROWS, width), 0)
        lane = lax.broadcasted_iota(jnp.int32, (ROWS, width), 1)
        self.next_y = jnp.where((row == own - 1) & (side == 1), 0.0, 1.0)
        self.prev_y = jnp.where((row == 0) & (side == 0), 0.0, 1.0)
        self.next_x = jnp.where(lane == width - 1, 0.0, 1.0)
        self.prev_x = jnp.where(lane == 0, 0.0, 1.0)


def up_y(val):
    return pltpu.roll(val, ROWS - 1, 0)


def down_y(val):
    return pltpu.roll(val, 1, 0)


def slope_z(below, mid, above):
    return 0.5 * (above - below)


def smooth_z(below, mid, above):
    return 0.75 * mid + 0.125 * (above + below)


def gradients(below, mid, above, k):
    slope = slope_z(below, mid, above)
    smooth = smooth_z(below, mid, above)
    slope_s = 0.75 * slope + 0.125 * (up_y(slope) * k.next_y + down_y(slope) * k.prev_y)
    ahead = up_y(smooth) * k.next_y
    behind = down_y(smooth) * k.prev_y
    smooth_s = 0.75 * smooth + 0.125 * (ahead + behind)
    smooth_d = 0.5 * (ahead - behind)

    def smooth_x(val):
        return 0.75 * val + 0.125 * (left(val) * k.next_x + right(val) * k.prev_x)

    return (
        smooth_x(slope_s),
        smooth_x(smooth_d),
        0.5 * (left(smooth_s) * k.next_x - right(smooth_s) * k.prev_x),
    )


def force(below, mid, above, k):
    p_z = slope_z(below[0], mid[0], above[0])
    p_y = smooth_z(below[1], mid[1], above[1])
    p_x = smooth_z(below[2], mid[2], above[2])
    small, half = 0.125 * p_z, 0.5 * p_y
    both = 0.75 * p_z + up_y(small + half) * k.next_y + down_y(small - half) * k.prev_y
    p_x = 0.75 * p_x + 0.125 * (up_y(p_x) * k.next_y + down_y(p_x) * k.prev_y)
    small, half = 0.125 * both, 0.5 * p_x
    return 0.75 * both + left(small + half) * k.next_x + right(small - half) * k.prev_x


def deformation(below, mid, above, k):
    deform = []
    for comp in range(3):
        row = list(gradients(below[comp], mid[comp], above[comp], k))
        row[comp] = row[comp] + 1.0
        deform.append(row)
    return deform


def passive_stress(deform):
    right_c = {}
    for a_pos, b_pos in PAIRS:
        right_c[a_pos, b_pos] = sum(deform[i_pos][a_pos] * deform[i_pos][b_pos] for i_pos in range(3))
    strain = {}
    for a_pos, b_pos in PAIRS:
        strain[a_pos, b_pos] = 0.5 * (right_c[a_pos, b_pos] - (1.0 if a_pos == b_pos else 0.0))
    trace = strain[0, 0] + strain[1, 1] + strain[2, 2]
    second = {}
    for a_pos, b_pos in PAIRS:
        entry = (2.0 * SHEAR) * strain[a_pos, b_pos]
        if a_pos == b_pos:
            entry = entry + LAME_FIRST * trace
        second[a_pos, b_pos] = entry
        second[b_pos, a_pos] = entry
    return second


def times(deform, second):
    return [
        [sum(deform[i_pos][b_pos] * second[b_pos, a_pos] for b_pos in range(3)) for a_pos in range(3)]
        for i_pos in range(3)
    ]


def metric(deform, fdir):
    def cofactor(i_pos, j_pos):
        i_next, i_last = (i_pos + 1) % 3, (i_pos + 2) % 3
        j_next, j_last = (j_pos + 1) % 3, (j_pos + 2) % 3
        return deform[i_next][j_next] * deform[i_last][j_last] - deform[i_next][j_last] * deform[i_last][j_next]

    cof = [[cofactor(i_pos, j_pos) for j_pos in range(3)] for i_pos in range(3)]
    det = deform[0][0] * cof[0][0] + deform[0][1] * cof[0][1] + deform[0][2] * cof[0][2]
    scale = 1.0 / det
    inv = [[cof[i_pos][j_pos] * scale for i_pos in range(3)] for j_pos in range(3)]
    along = [sum(inv[a_pos][i_pos] * fdir[i_pos] for i_pos in range(3)) for a_pos in range(3)]
    comps = []
    for a_pos, b_pos in PAIRS:
        inner = sum(inv[a_pos][i_pos] * inv[b_pos][i_pos] for i_pos in range(3))
        comps.append(SIGMA_TRANS * inner + (SIGMA_LONG - SIGMA_TRANS) * along[a_pos] * along[b_pos])
    return comps


def window_plane(ref, comp, place, offset):
    slab, side, slabs = place
    spot = jnp.clip(slab + offset, 0, slabs - 1)
    own = ref[spot, side, comp]
    first = pl.multiple_of(8 * side, 8)
    strip = ref[spot, 1 - side, comp, pl.ds(first, 8), :]
    return jnp.concatenate([own, strip], axis=0)


def inside(place, offset):
    slab, _, slabs = place
    spot = slab + offset
    return jnp.where((spot >= 0) & (spot < slabs), 1.0, 0.0)


def passive_kernel(place_ref, field_ref, disp_out, stress_out, pull_out, fdir_out):
    slabs, _, _, own, width = field_ref.shape
    place = (place_ref[0], place_ref[1], slabs)
    k = Weights(place[1], own, width)

    def disp_at(offset):
        factor = inside(place, offset)
        return [window_plane(field_ref, comp, place, offset) * factor for comp in range(3)]

    def one(step, carry):
        offset = step - REACH
        below, mid, above = (disp_at(offset - 1), disp_at(offset), disp_at(offset + 1))
        factor = inside(place, offset)
        deform = deformation(below, mid, above, k)
        stress = times(deform, passive_stress(deform))
        fdir = [window_plane(field_ref, 3 + comp, place, offset) for comp in range(3)]
        for i_pos in range(3):
            pull = (ACTIVE_GAIN * factor) * sum(deform[i_pos][b_pos] * fdir[b_pos] for b_pos in range(3))
            for a_pos in range(3):
                stress_out[3 * i_pos + a_pos, step] = stress[i_pos][a_pos] * factor
                pull_out[3 * i_pos + a_pos, step] = pull * fdir[a_pos]
            disp_out[i_pos, step] = mid[i_pos]
            fdir_out[i_pos, step] = fdir[i_pos]
        return carry

    lax.fori_loop(0, 2 * REACH + 1, one, 0)


def passive_step(place, field):
    slabs, _, _, own, width = field.shape
    planes = 2 * REACH + 1
    shapes = [(3, planes), (9, planes), (9, planes), (3, planes)]
    return pl.pallas_call(
        passive_kernel,
        in_specs=[pl.BlockSpec(memory_space=pltpu.SMEM), pl.BlockSpec(memory_space=pltpu.VMEM)],
        out_shape=[jax.ShapeDtypeStruct((a, b, ROWS, width), jnp.float32) for a, b in shapes],
        compiler_params=params(),
        cost_estimate=cost(400 * planes * ROWS * width, 5_000_000),
        name="passive",
    )(place, field)


def mechanics_kernel(place_ref, active_ref, disp_ref, stress_ref, pull_ref, fdir_ref, disp_out, cond_out, d_one, p_two):
    slabs, _, own, width = active_ref.shape
    slab, side = place_ref[0], place_ref[1]
    place = (slab, side, slabs)
    k = Weights(side, own, width)

    def active_at(step):
        spot = jnp.clip(slab + step - REACH, 0, slabs - 1)
        first = pl.multiple_of(8 * side, 8)
        return jnp.concatenate([active_ref[spot, side], active_ref[spot, 1 - side, pl.ds(first, 8), :]], axis=0)

    def first_force(step, carry):
        act = [active_at(step + shift) for shift in (-1, 0, 1)]
        factor = inside(place, step - REACH)
        for i_pos in range(3):
            stress = [
                [stress_ref[3 * i_pos + a_pos, step + shift] + act[shift + 1] * pull_ref[3 * i_pos + a_pos, step + shift] for a_pos in range(3)]
                for shift in (-1, 0, 1)
            ]
            moved = disp_ref[i_pos, step] + MECH_RATE * force(stress[0], stress[1], stress[2], k)
            d_one[i_pos, step] = moved * factor
        return carry

    lax.fori_loop(1, 2 * REACH, first_force, 0)

    def second_stress(step, carry):
        planes = [[d_one[comp, step + shift] for comp in range(3)] for shift in (-1, 0, 1)]
        deform = deformation(planes[0], planes[1], planes[2], k)
        second = passive_stress(deform)
        fdir = [fdir_ref[comp, step] for comp in range(3)]
        gain = ACTIVE_GAIN * active_at(step)
        for a_pos, b_pos in PAIRS:
            entry = second[a_pos, b_pos] + gain * fdir[a_pos] * fdir[b_pos]
            second[a_pos, b_pos] = entry
            second[b_pos, a_pos] = entry
        stress = times(deform, second)
        factor = inside(place, step - REACH)
        for i_pos in range(3):
            for a_pos in range(3):
                p_two[3 * i_pos + a_pos, step] = stress[i_pos][a_pos] * factor
        return carry

    lax.fori_loop(2, 2 * REACH - 1, second_stress, 0)

    last = []
    for step in (REACH - 1, REACH, REACH + 1):
        factor = inside(place, step - REACH)
        row = []
        for i_pos in range(3):
            stress = [[p_two[3 * i_pos + a_pos, step + shift] for a_pos in range(3)] for shift in (-1, 0, 1)]
            moved = d_one[i_pos, step] + MECH_RATE * force(stress[0], stress[1], stress[2], k)
            row.append(moved * factor)
        last.append(row)
    deform = deformation(last[0], last[1], last[2], k)
    comps = metric(deform, [fdir_ref[comp, REACH] for comp in range(3)])
    for i_pos in range(3):
        disp_out[i_pos, 0] = last[1][i_pos][:own]
    for pos, comp in enumerate(comps):
        cond_out[pos, 0] = comp[:own]


def mechanics_step(place, active, window):
    slabs, _, own, width = active.shape
    planes = 2 * REACH + 1
    vmem = pl.BlockSpec(memory_space=pltpu.VMEM)
    return pl.pallas_call(
        mechanics_kernel,
        in_specs=[pl.BlockSpec(memory_space=pltpu.SMEM)] + [vmem] * 5,
        out_shape=[
            jax.ShapeDtypeStruct((3, 1, own, width), jnp.float32),
            jax.ShapeDtypeStruct((6, 1, own, width), jnp.float32),
        ],
        scratch_shapes=[
            pltpu.VMEM((3, planes, ROWS, width), jnp.float32),
            pltpu.VMEM((9, planes, ROWS, width), jnp.float32),
        ],
        compiler_params=params(),
        cost_estimate=cost(400 * planes * ROWS * width, 5_000_000),
        name="mechanics",
    )(place, active, *window)


def fiber_dir(fiber):
    block_index = fiber.astype(jnp.float32)
    theta = -1.0 + 2.0 * block_index / (NFIB - 1)
    tilt = 0.3 * jnp.sin(3.0 * block_index)
    return jnp.stack([jnp.sin(tilt), jnp.cos(tilt) * jnp.sin(theta), jnp.cos(tilt) * jnp.cos(theta)])


def on_device(states, cond, tension, fiber, disp):
    slabs = lax.axis_size("slab")
    slab, col = lax.axis_index("slab"), lax.axis_index("col")
    _, planes, rows, width = states.shape
    own = rows // 8
    up = [(i, i + 1) for i in range(slabs - 1)]
    down = [(i + 1, i) for i in range(slabs - 1)]
    up_cross = [(2 * i + c, 2 * i + 3 - c) for i in range(slabs - 1) for c in range(2)]
    down_cross = [(dst, src) for src, dst in up_cross]
    swap = [(0, 1), (1, 0)]
    side = col.astype(jnp.int32).reshape(1)
    place = jnp.stack([slab, col]).astype(jnp.int32)

    tiled = states.reshape(4, planes, own, 8, width)
    below_own = lax.ppermute(tiled[0, planes - 1], "slab", up)
    above_own = lax.ppermute(tiled[0, 0], "slab", down)

    facing = jnp.where(col == 0, tiled[:, :, own - 1], tiled[:, :, 0])
    cond_facing = jnp.where(col == 0, cond[:, 0, -2:], cond[:, 0, :2])
    strip = lax.ppermute(facing, "col", swap)
    cond_strip = lax.ppermute(cond_facing, "col", swap)
    below_strip = lax.ppermute(facing[0, planes - 1], ("slab", "col"), up_cross)
    above_strip = lax.ppermute(facing[0, 0], ("slab", "col"), down_cross)

    field = jnp.concatenate([disp[:, 0], fiber_dir(fiber)[:, 0]], axis=0)
    field = lax.all_gather(field, ("slab", "col")).reshape((slabs, 2) + field.shape)

    coeffs = fine_coeffs(jnp.concatenate([cond[:, 0], cond_strip], axis=1))
    wide = jnp.concatenate([tiled, strip[:, :, None]], axis=2)
    lo, mid, hi, gates = wide[0, 0], wide[0, 1:-1], wide[0, -1], wide[1:]
    below = jnp.concatenate([below_own, below_strip[None]], axis=0)
    above = jnp.concatenate([above_own, above_strip[None]], axis=0)
    window = None
    for turn_index in range(SUB):
        last = turn_index == SUB - 1
        result = local_step(side, lo, mid, hi, gates, coeffs, last)
        if turn_index == 1:
            window = passive_step(place, field)
        if last:
            part = result
        else:
            lo, mid, hi, gates = result
            lo, hi = halo_step(side, lo, hi, below, above, coeffs)
            below = lax.ppermute(hi, "slab", up)
            above = lax.ppermute(lo, "slab", down)
    states_next, tension_next, active = finish_step(side, part, below, above, coeffs, tension)
    active = lax.all_gather(active, ("slab", "col")).reshape((slabs, 2) + active.shape)
    disp_next, cond_next = mechanics_step(place, active, window)
    return (states_next.reshape(states.shape), tension_next, disp_next, cond_next)


def solution(mesh):
    in_specs = (
        P(None, ("grp", "slab"), "col", None),
        P(None, ("grp", "slab"), "col", None),
        P(("grp", "slab"), "col", None),
        P(("grp", "slab"), "col", None),
        P(None, ("grp", "slab"), "col", None),
    )
    out_specs = (
        P(None, ("grp", "slab"), "col", None),
        P(("grp", "slab"), "col", None),
        P(None, ("grp", "slab"), "col", None),
        P(None, ("grp", "slab"), "col", None),
    )
    return jax.shard_map(
        on_device, mesh=mesh, in_specs=in_specs, out_specs=out_specs, check_vma=False
    )
```

time: 315 us -> 142 us (0.45)
  local copies, waits for them, and re-layouts: 88.1 us -> 6.28 us
  starting transfers between devices: 97.6 us -> 29.2 us
  other arithmetic: 71.7 us -> 6.2 us
  Pallas kernels: 0 us -> 43.9 us
  waiting for transfers between devices: 53.7 us -> 17 us
  blocking collectives: 0 us -> 24.4 us
  between operations: 1.88 us -> 14.3 us
    ppermute x36 -> x12, starting transfers between devices: 97.6 us -> 29.1 us  [the longest x3 13.5 us: on_device(): below = lax.ppermute(hi, 'slab', up)]
    reshape x1 -> x0, local copies, waits for them, and re-layouts: 68.4 us -> none  [coarsen(): field.reshape(field.shape[0] // 2, 2, field.shape[1] // 2, 2, field.shape...]
    pallas_call x0 -> x11, Pallas kernels: none -> 43.9 us  [the longest x4 25.9 us: local_step(): pl.pallas_call(functools.partial(local_kernel, last, tiles, per_block), g...]
    ppermute x36 -> x12, waiting for transfers between devices: 53.7 us -> 17 us  [the longest x3 11.3 us: on_device(): below = lax.ppermute(hi, 'slab', up)]
    add x31 -> x0, other arithmetic: 33 us -> none  [the longest x4 30.7 us: excite_step(): new_volt = volt + diffusion(padded, coeff) + STEP_TIME * ion]
    all_gather x0 -> x1, blocking collectives: none -> 24.4 us  [on_device(): lax.all_gather(active, ('slab', 'col')).reshape((slabs, 2) + active.shape)]
    reduce_sum x3 -> x0, other arithmetic: 24.3 us -> none  [coarsen(): return jnp.mean(shaped, axis=(1, 3, 5))]
    broadcast_in_dim x21 -> x0, local copies, waits for them, and re-layouts: 7.03 us -> none  [the longest x9 6.6 us: upsample(): jnp.repeat(jnp.repeat(jnp.repeat(cond, 4, axis=1), 4, axis=2), 4, axis=3)]
  transfers between devices with their start and end apart: 36 -> 13, of which waited for: 19 -> 4; matrix products, arithmetic and copies ran while one was open for 10% -> 3% of each run, Pallas kernels for 0% -> 25%
where the time goes in v1:
time: 142 us; the launch traced here: 141 us
  Pallas kernels  43.9 us (31%)
  starting transfers between devices  29.2 us (21%)
  blocking collectives  24.4 us (17%)
  waiting for transfers between devices  17 us (12%)
  between operations  14.3 us (10%)
  local copies, waits for them, and re-layouts  6.28 us (4%)
  other arithmetic  6.2 us (4%)
    pallas_call x4, Pallas kernels, local_step(): pl.pallas_call(functools.partial(local_kernel, last, tiles, per_block), g...  25.9 us
    all_gather x1, blocking collectives, on_device(): lax.all_gather(active, ('slab', 'col')).reshape((slabs, 2) + active.shape)  24.4 us
    ppermute x3, starting transfers between devices, on_device(): below = lax.ppermute(hi, 'slab', up)  13.5 us
    ppermute x3, waiting for transfers between devices, on_device(): below = lax.ppermute(hi, 'slab', up)  11.3 us
    unnamed x10, local copies, waits for them, and re-layouts  5.21 us
    ppermute x1, starting transfers between devices, on_device(): below_own = lax.ppermute(tiled[0, planes - 1], 'slab', up)  4.84 us
    pallas_call x1, Pallas kernels, mechanics_step(): pl.pallas_call(mechanics_kernel, in_specs=[pl.BlockSpec(memory_space=pltp...  4.84 us
    ppermute x1, waiting for transfers between devices, on_device(): below_strip = lax.ppermute(facing[0, planes - 1], ('slab', 'col'), up_cross)  4.19 us
  transfers between devices with their start and end apart: 13, of which 4 were waited for; matrix products, arithmetic and copies ran while one was open for 3% of the time, Pallas kernels for 25%

profile of v1, /device:TPU:0, one launch (start us, length us, event | category | flops | bytes accessed | tf_op | source)
XLA Modules:
  0.0 141.3 jit_solution(17217766365611186156)
XLA Ops:
  8.1 1.4 %pad_maximum_fusion.4 = f32[6,16,256]{2,1,0:T(8,128)} fusion(f32[3,16,256]{2,1,0:T(8,128)S(1)} %maximum_bitcast_fusion.3, f32[3,16,256]{2,1,0:T(8,128)} %bitcast.67), kind=kLoop, calls=%fused_computation.13 | loop fusion | flops 24576 | bytes 196608 | tf_op jit(solution)/shard_map/concatenate | solution.py:678
  9.6 1.4 %fusion.1 = f32[4,4,8,1024]{3,2,1,0:T(8,128)S(1)} fusion(f32[4,4,8,8,1024]{4,3,2,1,0:T(8,128)} %bitcast.56, pred[]{:T(512)S(6)} %eq.4), kind=kLoop, calls=%fused_computation.4 | loop fusion | flops 131072 | bytes 1572865 | tf_op jit(solution)/shard_map/jit(_where)/select_n | solution.py:671
  13.6 4.8 %collective-permute-start.2 = (f32[8,8,1024]{2,1,0:T(8,128)S(1)}, f32[8,8,1024]{2,1,0:T(8,128)S(1)}, u32[]{:S(2)}, u32[]{:S(2)}) collective-permute-start(f32[8,8,1024]{2,1,0:T(8,128)S(1)} %get-tuple-element.61), channel_id=1, source_target_pairs={{0,2},{2,4},{4,6},{6,8},{8,10},{10,12},{12,14},{1,3},{3,5},{5,7},{... | collective-permute-start | bytes 786440 | tf_op jit(solution)/shard_map/ppermute | solution.py:668
  19.8 3.7 %collective-permute-start.3 = (f32[8,1024]{1,0:T(8,128)S(1)}, f32[8,1024]{1,0:T(8,128)S(1)}, u32[]{:S(2)}, u32[]{:S(2)}) collective-permute-start(f32[8,1024]{1,0:T(8,128)S(1)} %get-tuple-element.63), channel_id=1, source_target_pairs={{0,3},{1,2},{2,5},{3,4},{4,7},{5,6},{6,9},{7,8},{8,11},{9,10},{10,... | collective-permute-start | bytes 98312 | tf_op jit(solution)/shard_map/ppermute | solution.py:675
  25.7 2.4 %coeffs.1.coeff_ref = f32[10,9,8,1024]{3,2,1,0:T(8,128)S(1)} custom-call(f32[6,18,256]{2,1,0:T(8,128)S(1)} %pad_maximum_fusion.3.cond_ref), custom_call_target="tpu_custom_call" | custom-call | flops 2000000 | bytes 3200000 | tf_op jit(solution)/shard_map/coeffs/pallas_call | solution.py:106
  28.1 4.2 %collective-permute-done.3 = f32[8,1024]{1,0:T(8,128)S(1)} collective-permute-done((f32[8,1024]{1,0:T(8,128)S(1)}, f32[8,1024]{1,0:T(8,128)S(1)}, u32[]{:S(2)}, u32[]{:S(2)}) %collective-permute-start.3) | collective-permute-done | bytes 32800 | tf_op jit(solution)/shard_map/ppermute | solution.py:675
  33.0 6.2 %local.3 = (f32[9,8,1024]{2,1,0:T(8,128)S(1)}, f32[2,9,8,1024]{3,2,1,0:T(8,128)S(1)}, f32[9,8,1024]{2,1,0:T(8,128)S(1)}, f32[3,4,9,8,1024]{4,3,2,1,0:T(8,128)S(1)}) custom-call(s32[1]{0:T(128)} %bitcast.side_ref, f32[9,8,1024]{2,1,0:T(8,128)S(1)} %get-tuple-element.59.lo_ref, f32[2,9,8,1024]{3,2,1,0:T(8,128)S(1)} %maximum_bitcast_fusion.mid_ref, ...), custom_call_target="tpu_custom_call" | custom-call | flops 44236800 | bytes 11796480 | tf_op jit(solution)/shard_map/local/pallas_call | solution.py:258
  40.2 4.0 %collective-permute-start.6 = (f32[9,8,1024]{2,1,0:T(8,128)S(1)}, f32[9,8,1024]{2,1,0:T(8,128)S(1)}, u32[]{:S(2)}, u32[]{:S(2)}) collective-permute-start(f32[9,8,1024]{2,1,0:T(8,128)S(1)} %get-tuple-element.35.hi_ref), channel_id=1, source_target_pairs={{0,2},{2,4},{4,6},{6,8},{8,10},{10,12},{12,14},{1,3},{3,5},{5,7},{... | collective-permute-start | bytes 884744 | tf_op jit(solution)/shard_map/ppermute | solution.py:697
  45.6 6.2 %local.4 = (f32[9,8,1024]{2,1,0:T(8,128)S(1)}, f32[2,9,8,1024]{3,2,1,0:T(8,128)S(1)}, f32[9,8,1024]{2,1,0:T(8,128)S(1)}, f32[3,4,9,8,1024]{4,3,2,1,0:T(8,128)S(1)}) custom-call(s32[1]{0:T(128)} %bitcast.side_ref, f32[9,8,1024]{2,1,0:T(8,128)S(1)} %get-tuple-element.33.lo_ref, f32[2,9,8,1024]{3,2,1,0:T(8,128)S(1)} %get-tuple-element.34.mid_ref, ...), custom_call_target="tpu_custom_call" | custom-call | flops 44236800 | bytes 11796480 | tf_op jit(solution)/shard_map/local/pallas_call | solution.py:258
  51.8 8.1 %collective-permute-done.6.below_ref = f32[9,8,1024]{2,1,0:T(8,128)S(1)} collective-permute-done((f32[9,8,1024]{2,1,0:T(8,128)S(1)}, f32[9,8,1024]{2,1,0:T(8,128)S(1)}, u32[]{:S(2)}, u32[]{:S(2)}) %collective-permute-start.6) | collective-permute-done | bytes 294944 | tf_op jit(solution)/shard_map/ppermute | solution.py:697
  60.9 4.4 %collective-permute-start.8 = (f32[9,8,1024]{2,1,0:T(8,128)S(1)}, f32[9,8,1024]{2,1,0:T(8,128)S(1)}, u32[]{:S(2)}, u32[]{:S(2)}) collective-permute-start(f32[9,8,1024]{2,1,0:T(8,128)S(1)} %get-tuple-element.41.hi_ref), channel_id=1, source_target_pairs={{0,2},{2,4},{4,6},{6,8},{8,10},{10,12},{12,14},{1,3},{3,5},{5,7},{... | collective-permute-start | bytes 884744 | tf_op jit(solution)/shard_map/ppermute | solution.py:697
  66.5 6.2 %local.5 = (f32[9,8,1024]{2,1,0:T(8,128)S(1)}, f32[2,9,8,1024]{3,2,1,0:T(8,128)S(1)}, f32[9,8,1024]{2,1,0:T(8,128)S(1)}, f32[3,4,9,8,1024]{4,3,2,1,0:T(8,128)S(1)}) custom-call(s32[1]{0:T(128)} %bitcast.side_ref, f32[9,8,1024]{2,1,0:T(8,128)S(1)} %get-tuple-element.39.lo_ref, f32[2,9,8,1024]{3,2,1,0:T(8,128)S(1)} %get-tuple-element.40.mid_ref, ...), custom_call_target="tpu_custom_call" | custom-call | flops 44236800 | bytes 11796480 | tf_op jit(solution)/shard_map/local/pallas_call | solution.py:258
  72.8 1.8 %copy-done = f32[3,4,9,8,1024]{4,3,2,1,0:T(8,128)} copy-done((f32[3,4,9,8,1024]{4,3,2,1,0:T(8,128)}, f32[3,4,9,8,1024]{4,3,2,1,0:T(8,128)S(1)}, u32[]{:S(2)}) %copy-start) | copy-done | bytes 3538968
  74.6 3.2 %collective-permute-done.8.below_ref = f32[9,8,1024]{2,1,0:T(8,128)S(1)} collective-permute-done((f32[9,8,1024]{2,1,0:T(8,128)S(1)}, f32[9,8,1024]{2,1,0:T(8,128)S(1)}, u32[]{:S(2)}, u32[]{:S(2)}) %collective-permute-start.8) | collective-permute-done | bytes 294944 | tf_op jit(solution)/shard_map/ppermute | solution.py:697
  77.8 1.8 %halo.5 = (f32[9,8,1024]{2,1,0:T(8,128)}, f32[9,8,1024]{2,1,0:T(8,128)}) custom-call(s32[1]{0:T(128)} %bitcast.side_ref, f32[9,8,1024]{2,1,0:T(8,128)S(1)} %get-tuple-element.43.lo_ref, f32[9,8,1024]{2,1,0:T(8,128)S(1)} %get-tuple-element.44.hi_ref, f32[9,8,1024]{2,1,0:T(8,128)S(1)} %collective-permute-done.8.below_ref, ...), custom_call_target="tpu_custom_call" | custom-call | flops 2211840 | bytes 2949120 | tf_op jit(solution)/shard_map/halo/pallas_call | solution.py:298
  79.6 5.1 %collective-permute-start.10 = (f32[9,8,1024]{2,1,0:T(8,128)}, f32[9,8,1024]{2,1,0:T(8,128)}, u32[]{:S(2)}, u32[]{:S(2)}) collective-permute-start(f32[9,8,1024]{2,1,0:T(8,128)} %get-tuple-element.47.hi_ref), channel_id=1, source_target_pairs={{0,2},{2,4},{4,6},{6,8},{8,10},{10,12},{12,14},{1,3},{3,5},{5,7},{... | collective-permute-start | bytes 884744 | tf_op jit(solution)/shard_map/ppermute | solution.py:697
  86.0 2.0 %copy-done.1 = f32[3,4,9,8,1024]{4,3,2,1,0:T(8,128)S(1)} copy-done((f32[3,4,9,8,1024]{4,3,2,1,0:T(8,128)S(1)}, f32[3,4,9,8,1024]{4,3,2,1,0:T(8,128)}, u32[]{:S(2)}) %copy-start.1) | copy-done | bytes 3538968
  88.0 7.2 %local_last.1.part_ref = f32[4,4,8,8,1024]{4,3,2,1,0:T(8,128)} custom-call(s32[1]{0:T(128)} %bitcast.side_ref, f32[9,8,1024]{2,1,0:T(8,128)} %get-tuple-element.45.lo_ref, f32[2,9,8,1024]{3,2,1,0:T(8,128)S(1)} %get-tuple-element.46.mid_ref, f32[9,8,1024]{2,1,0:T(8,128)} %get-tuple-element.47.hi_ref, f32[3,4,9,8,1024]{4,3,2,1,0:T(8,128)S(1)} %copy-done.1, ...), custom_call_target="tpu_custom_call" | custom-call | flops 44236800 | bytes 11796480 | tf_op jit(solution)/shard_map/local_last/pallas_call | solution.py:258
  95.3 1.5 %collective-permute-done.11.above_ref = f32[9,8,1024]{2,1,0:T(8,128)} collective-permute-done((f32[9,8,1024]{2,1,0:T(8,128)}, f32[9,8,1024]{2,1,0:T(8,128)}, u32[]{:S(2)}, u32[]{:S(2)}) %collective-permute-start.11) | collective-permute-done | bytes 294944 | tf_op jit(solution)/shard_map/ppermute | solution.py:698
  96.8 3.8 %finish.1 = (f32[4,4,8,8,1024]{4,3,2,1,0:T(8,128)}, f32[2,32,512]{2,1,0:T(8,128)}, f32[16,256]{1,0:T(8,128)S(1)}) custom-call(s32[1]{0:T(128)} %bitcast.side_ref, f32[4,4,8,8,1024]{4,3,2,1,0:T(8,128)} %local_last.1.part_ref, f32[9,8,1024]{2,1,0:T(8,128)} %collective-permute-done.10.below_ref, ...), custom_call_target="tpu_custom_call", output_to_operand_aliasing={{0}: (1, {})} | custom-call | flops 5242880 | bytes 5242880 | tf_op jit(solution)/shard_map/finish/pallas_call | solution.py:372
  100.6 24.4 %all-gather = f32[256,256]{1,0:T(8,128)S(1)} all-gather(f32[16,256]{1,0:T(8,128)S(1)} %get-tuple-element.51), channel_id=2, replica_groups=mesh['grp'=2,'slab'=8,'col'=2] {'slab','col'}, dimensions={0}, use_global_device_ids=true | all-gather | bytes 278528 | tf_op jit(solution)/shard_map/all_gather | solution.py:700
  125.0 1.4 copy-done.2
  126.4 3.2 %passive.1 = (f32[3,9,24,256]{3,2,1,0:T(8,128)S(1)}, f32[9,9,24,256]{3,2,1,0:T(8,128)S(1)}, f32[9,9,24,256]{3,2,1,0:T(8,128)S(1)}, f32[3,9,24,256]{3,2,1,0:T(8,128)S(1)}) custom-call(s32[2]{0:T(128)S(1)} %pad_add_fusion.place_ref, f32[8,2,6,16,256]{4,3,2,1,0:T(8,128)S(1)} %bitcast.54), custom_call_target="tpu_custom_call" | custom-call | flops 22118400 | bytes 5000000 | tf_op jit(solution)/shard_map/passive/pallas_call | solution.py:555
  129.6 4.8 %mechanics.1 = (f32[3,1,16,256]{3,2,1,0:T(8,128)}, f32[6,1,16,256]{3,2,1,0:T(8,128)}) custom-call(s32[2]{0:T(128)S(1)} %pad_add_fusion.place_ref, f32[8,2,16,256]{3,2,1,0:T(8,128)S(1)} %bitcast.55, f32[3,9,24,256]{3,2,1,0:T(8,128)S(1)} %get-tuple-element.52.disp_ref, f32[9,9,24,256]{3,2,1,0:T(8,128)S(1)} %get-tuple-element.53.stress_ref, ...), custom_call_target="tpu_custom_call" | custom-call | flops 22118400 | bytes 5000000 | tf_op jit(solution)/shard_map/mechanics/pallas_call | solution.py:630
  (39 shorter events, 13.6 us)
Async XLA Ops:
  7.2 117.9 %all-gather.4.cloned.1.call-start = ((), (), s32[]{:S(2)}) async-start(), calls=%async_computation | async-start | bytes 1671168 | tf_op jit(solution)/shard_map/all_gather | solution.py:679
  9.6 22.8 %copy-start.4 = (f32[4,4,64,1024]{3,2,1,0:T(8,128)S(1)}, f32[4,4,64,1024]{3,2,1,0:T(8,128)}, u32[]{:S(2)}) copy-start(f32[4,4,64,1024]{3,2,1,0:T(8,128)} %param.5) | copy-start | bytes 12582916
  11.0 21.4 %collective-permute-start = (f32[4,4,8,1024]{3,2,1,0:T(8,128)S(1)}, f32[4,4,8,1024]{3,2,1,0:T(8,128)S(1)}, u32[]{:S(2)}, u32[]{:S(2)}) collective-permute-start(f32[4,4,8,1024]{3,2,1,0:T(8,128)S(1)} %fusion.1), channel_id=1, source_target_pairs={{0,1},{1,0},{2,3},{3,2},{4,5},{5,4},{6,7},{7,6},{8,9},{9,8},{10,11... | collective-permute-start | bytes 1572872 | tf_op jit(solution)/shard_map/ppermute | solution.py:673
  12.4 11.1 %collective-permute-start.1 = (f32[6,2,256]{2,1,0:T(2,128)S(1)}, f32[6,2,256]{2,1,0:T(2,128)S(1)}, u32[]{:S(2)}, u32[]{:S(2)}) collective-permute-start(f32[6,2,256]{2,1,0:T(2,128)S(1)} %fusion.3), channel_id=1, source_target_pairs={{0,1},{1,0},{2,3},{3,2},{4,5},{5,4},{6,7},{7,6},{8,9},{9,8},{10,11... | collective-permute-start | bytes 36872 | tf_op jit(solution)/shard_map/ppermute | solution.py:674
  13.6 18.7 %collective-permute-start.2 = (f32[8,8,1024]{2,1,0:T(8,128)S(1)}, f32[8,8,1024]{2,1,0:T(8,128)S(1)}, u32[]{:S(2)}, u32[]{:S(2)}) collective-permute-start(f32[8,8,1024]{2,1,0:T(8,128)S(1)} %get-tuple-element.61), channel_id=1, source_target_pairs={{0,2},{2,4},{4,6},{6,8},{8,10},{10,12},{12,14},{1,3},{3,5},{5,7},{... | collective-permute-start | bytes 786440 | tf_op jit(solution)/shard_map/ppermute | solution.py:668
  18.5 13.9 %collective-permute-start.4 = (f32[8,8,1024]{2,1,0:T(8,128)S(1)}, f32[8,8,1024]{2,1,0:T(8,128)S(1)}, u32[]{:S(2)}, u32[]{:S(2)}) collective-permute-start(f32[8,8,1024]{2,1,0:T(8,128)S(1)} %get-tuple-element.60), channel_id=1, source_target_pairs={{2,0},{4,2},{6,4},{8,6},{10,8},{12,10},{14,12},{3,1},{5,3},{7,5},{... | collective-permute-start | bytes 786440 | tf_op jit(solution)/shard_map/ppermute | solution.py:669
  19.8 12.5 %collective-permute-start.3 = (f32[8,1024]{1,0:T(8,128)S(1)}, f32[8,1024]{1,0:T(8,128)S(1)}, u32[]{:S(2)}, u32[]{:S(2)}) collective-permute-start(f32[8,1024]{1,0:T(8,128)S(1)} %get-tuple-element.63), channel_id=1, source_target_pairs={{0,3},{1,2},{2,5},{3,4},{4,7},{5,6},{6,9},{7,8},{8,11},{9,10},{10,... | collective-permute-start | bytes 98312 | tf_op jit(solution)/shard_map/ppermute | solution.py:675
  23.5 8.9 %collective-permute-start.5 = (f32[8,1024]{1,0:T(8,128)S(1)}, f32[8,1024]{1,0:T(8,128)S(1)}, u32[]{:S(2)}, u32[]{:S(2)}) collective-permute-start(f32[8,1024]{1,0:T(8,128)S(1)} %get-tuple-element.62), channel_id=1, source_target_pairs={{3,0},{2,1},{5,2},{4,3},{7,4},{6,5},{9,6},{8,7},{11,8},{10,9},{13,... | collective-permute-start | bytes 98312 | tf_op jit(solution)/shard_map/ppermute | solution.py:676
  40.2 19.7 %collective-permute-start.6 = (f32[9,8,1024]{2,1,0:T(8,128)S(1)}, f32[9,8,1024]{2,1,0:T(8,128)S(1)}, u32[]{:S(2)}, u32[]{:S(2)}) collective-permute-start(f32[9,8,1024]{2,1,0:T(8,128)S(1)} %get-tuple-element.35.hi_ref), channel_id=1, source_target_pairs={{0,2},{2,4},{4,6},{6,8},{8,10},{10,12},{12,14},{1,3},{3,5},{5,7},{... | collective-permute-start | bytes 884744 | tf_op jit(solution)/shard_map/ppermute | solution.py:697
  44.3 15.6 %collective-permute-start.7 = (f32[9,8,1024]{2,1,0:T(8,128)S(1)}, f32[9,8,1024]{2,1,0:T(8,128)S(1)}, u32[]{:S(2)}, u32[]{:S(2)}) collective-permute-start(f32[9,8,1024]{2,1,0:T(8,128)S(1)} %get-tuple-element.33.lo_ref), channel_id=1, source_target_pairs={{2,0},{4,2},{6,4},{8,6},{10,8},{12,10},{14,12},{3,1},{5,3},{7,5},{... | collective-permute-start | bytes 884744 | tf_op jit(solution)/shard_map/ppermute | solution.py:698
  60.9 16.9 %collective-permute-start.8 = (f32[9,8,1024]{2,1,0:T(8,128)S(1)}, f32[9,8,1024]{2,1,0:T(8,128)S(1)}, u32[]{:S(2)}, u32[]{:S(2)}) collective-permute-start(f32[9,8,1024]{2,1,0:T(8,128)S(1)} %get-tuple-element.41.hi_ref), channel_id=1, source_target_pairs={{0,2},{2,4},{4,6},{6,8},{8,10},{10,12},{12,14},{1,3},{3,5},{5,7},{... | collective-permute-start | bytes 884744 | tf_op jit(solution)/shard_map/ppermute | solution.py:697
  65.2 12.5 %collective-permute-start.9 = (f32[9,8,1024]{2,1,0:T(8,128)S(1)}, f32[9,8,1024]{2,1,0:T(8,128)S(1)}, u32[]{:S(2)}, u32[]{:S(2)}) collective-permute-start(f32[9,8,1024]{2,1,0:T(8,128)S(1)} %get-tuple-element.39.lo_ref), channel_id=1, source_target_pairs={{2,0},{4,2},{6,4},{8,6},{10,8},{12,10},{14,12},{3,1},{5,3},{7,5},{... | collective-permute-start | bytes 884744 | tf_op jit(solution)/shard_map/ppermute | solution.py:698
  72.8 1.8 %copy-start = (f32[3,4,9,8,1024]{4,3,2,1,0:T(8,128)}, f32[3,4,9,8,1024]{4,3,2,1,0:T(8,128)S(1)}, u32[]{:S(2)}) copy-start(f32[3,4,9,8,1024]{4,3,2,1,0:T(8,128)S(1)} %get-tuple-element.48.gate_ref) | copy-start | bytes 10616836
  79.6 15.7 %collective-permute-start.10 = (f32[9,8,1024]{2,1,0:T(8,128)}, f32[9,8,1024]{2,1,0:T(8,128)}, u32[]{:S(2)}, u32[]{:S(2)}) collective-permute-start(f32[9,8,1024]{2,1,0:T(8,128)} %get-tuple-element.47.hi_ref), channel_id=1, source_target_pairs={{0,2},{2,4},{4,6},{6,8},{8,10},{10,12},{12,14},{1,3},{3,5},{5,7},{... | collective-permute-start | bytes 884744 | tf_op jit(solution)/shard_map/ppermute | solution.py:697
  84.7 12.1 %collective-permute-start.11 = (f32[9,8,1024]{2,1,0:T(8,128)}, f32[9,8,1024]{2,1,0:T(8,128)}, u32[]{:S(2)}, u32[]{:S(2)}) collective-permute-start(f32[9,8,1024]{2,1,0:T(8,128)} %get-tuple-element.45.lo_ref), channel_id=1, source_target_pairs={{2,0},{4,2},{6,4},{8,6},{10,8},{12,10},{14,12},{3,1},{5,3},{7,5},{... | collective-permute-start | bytes 884744 | tf_op jit(solution)/shard_map/ppermute | solution.py:698
  86.0 2.0 %copy-start.1 = (f32[3,4,9,8,1024]{4,3,2,1,0:T(8,128)S(1)}, f32[3,4,9,8,1024]{4,3,2,1,0:T(8,128)}, u32[]{:S(2)}) copy-start(f32[3,4,9,8,1024]{4,3,2,1,0:T(8,128)} %copy-done) | copy-start | bytes 10616836
  88.0 8.8 %copy-start.3 = (f32[2,32,512]{2,1,0:T(8,128)S(1)}, f32[2,32,512]{2,1,0:T(8,128)}, u32[]{:S(2)}) copy-start(f32[2,32,512]{2,1,0:T(8,128)} %tension_ref.1) | copy-start | bytes 393220
  125.0 1.4 copy-start.2
Sparse Core Ops, SparseCore 0:
  10.9 51.0 all-gather.3

commit v2 on v1

--- a/solution.py
+++ b/solution.py
@@ -22,6 +22,8 @@
 
 C_ZZ, C_ZY, C_ZXR, C_ZXL, C_MID, C_YY, C_XXR, C_YXR, C_XXL, C_YXL = range(10)
 
+SLAB, SIDE, FLIP, FAR = range(4)
+
 HIGHEST = lax.Precision.HIGHEST
 LIMIT = 40 * 1024 * 1024
 
@@ -66,8 +68,9 @@
     return before, after
 
 
-def coeff_kernel(cond_ref, out_ref):
+def coeff_kernel(info_ref, cond_ref, out_ref):
     six, rows, width = cond_ref.shape
+    turn = jnp.where(info_ref[FLIP] == 1, -0.5, 0.5)
     fine = 4 * width
     mech = lax.broadcasted_iota(jnp.int32, (width, fine), 0)
     cell = lax.broadcasted_iota(jnp.int32, (width, fine), 1)
@@ -90,26 +93,27 @@
     store(C_ZZ, zz)
     store(C_YY, yy)
     store(C_MID, -2.0 * (zz + yy + xx))
-    store(C_ZY, 0.5 * zy)
+    store(C_ZY, turn * zy)
     xx, zx, yx = spread((2, 4, 5), -1)
     store(C_XXR, xx)
-    store(C_ZXR, 0.5 * zx)
+    store(C_ZXR, turn * zx)
     store(C_YXR, 0.5 * yx)
     xx, zx, yx = spread((2, 4, 5), 1)
     store(C_XXL, xx)
-    store(C_ZXL, 0.5 * zx)
+    store(C_ZXL, turn * zx)
     store(C_YXL, 0.5 * yx)
 
 
-def fine_coeffs(cond_rows):
+def fine_coeffs(info, cond_rows):
     six, rows, width = cond_rows.shape
     return pl.pallas_call(
         coeff_kernel,
+        in_specs=[pl.BlockSpec(memory_space=pltpu.SMEM), pl.BlockSpec(memory_space=pltpu.VMEM)],
         out_shape=jax.ShapeDtypeStruct((10, rows // 2, 8, 4 * width), jnp.float32),
         compiler_params=params(),
         cost_estimate=cost(2_000_000, 3_200_000),
         name="coeffs",
-    )(cond_rows)
+    )(info, cond_rows)
 
 
 def inverse(val):
@@ -149,20 +153,28 @@
     return u_add, v_new, w_new, s_new
 
 
-def local_kernel(last, tiles, per_block, side_ref, lo_ref, mid_ref, hi_ref, gate_ref, coeff_ref, *outs):
-    side = side_ref[0]
+def local_kernel(first, last, tiles, per_block, info_ref, *refs):
+    side, flip = info_ref[SIDE], info_ref[FLIP]
     sub = row_iota()
     own = tiles - 1
-    refs = [lambda t: lo_ref[t], lambda t: mid_ref[0, t], lambda t: mid_ref[1, t], lambda t: hi_ref[t]]
-    planes = len(refs)
+    planes = 4
+    place = [plane + flip * (planes - 1 - 2 * plane) for plane in range(planes)]
+    if first:
+        u_ref, gate_ref, coeff_ref, *outs = refs
+        reads = [lambda t, p=p: u_ref[p, t] for p in place]
+        gate_place = place
+    else:
+        far_ref, mid_ref, near_ref, gate_ref, coeff_ref, *outs = refs
+        reads = [lambda t: far_ref[t], lambda t: mid_ref[0, t], lambda t: mid_ref[1, t], lambda t: near_ref[t]]
+        gate_place = list(range(planes))
 
     def one(local_tile, carry):
         tile = pl.program_id(0) * per_block + local_tile
         before, after = ring_neighbours(tile, tiles)
         mask_before, mask_after = edge_masks(tile, side, own)
-        cur = [ref(tile) for ref in refs]
-        prv = [ref(before) * mask_before for ref in refs]
-        nxt = [ref(after) * mask_after for ref in refs]
+        cur = [read(tile) for read in reads]
+        prv = [read(before) * mask_before for read in reads]
+        nxt = [read(after) * mask_after for read in reads]
 
         def coeff(index):
             return coeff_ref[index, local_tile]
@@ -197,18 +209,12 @@
             chunk = 256
             for start in range(0, 1024, chunk):
                 lanes = slice(start, start + chunk)
-                u_add, v_new, w_new, s_new = ionic(
-                    u[:, lanes],
-                    gate_ref[0, plane, local_tile, :, lanes],
-                    gate_ref[1, plane, local_tile, :, lanes],
-                    gate_ref[2, plane, local_tile, :, lanes],
-                )
+                gates = [gate_ref[g, gate_place[plane], local_tile, :, lanes] for g in range(3)]
+                u_add, v_new, w_new, s_new = ionic(u[:, lanes], *gates)
                 u_new = base[:, lanes] + u_add
                 if last:
-                    outs[0][0, plane, local_tile, :, lanes] = u_new
-                    outs[0][1, plane, local_tile, :, lanes] = v_new
-                    outs[0][2, plane, local_tile, :, lanes] = w_new
-                    outs[0][3, plane, local_tile, :, lanes] = s_new
+                    for comp, value in enumerate((u_new, v_new, w_new, s_new)):
+                        outs[0][comp, place[plane], local_tile, :, lanes] = value
                 else:
                     if plane == 0:
                         outs[0][local_tile, :, lanes] = u_new
@@ -216,55 +222,52 @@
                         outs[2][local_tile, :, lanes] = u_new
                     else:
                         outs[1][plane - 1, local_tile, :, lanes] = u_new
-                    outs[3][0, plane, local_tile, :, lanes] = v_new
-                    outs[3][1, plane, local_tile, :, lanes] = w_new
-                    outs[3][2, plane, local_tile, :, lanes] = s_new
+                    for comp, value in enumerate((v_new, w_new, s_new)):
+                        outs[3][comp, plane, local_tile, :, lanes] = value
         return carry
 
     lax.fori_loop(0, per_block, one, 0)
 
 
-def local_step(side, lo, mid, hi, gates, coeffs, last):
-    tiles, _, width = lo.shape
+def local_step(info, u_parts, gates, coeffs, last):
+    first = len(u_parts) == 1
+    _, planes, tiles, _, width = gates.shape
     per_block = 2 if last else 3
     blocks = (tiles - 1) // per_block if last else tiles // per_block
-    whole3 = pl.BlockSpec((tiles, 8, width), lambda i: (0, 0, 0))
-    whole4 = pl.BlockSpec((2, tiles, 8, width), lambda i: (0, 0, 0, 0))
-    in_specs = [
-        pl.BlockSpec(memory_space=pltpu.SMEM),
-        whole3,
-        whole4,
-        whole3,
-        pl.BlockSpec((3, 4, per_block, 8, width), lambda i: (0, 0, i, 0, 0)),
+    plane_shape, mid_shape = (tiles, 8, width), (planes - 2, tiles, 8, width)
+    in_specs = [pl.BlockSpec(memory_space=pltpu.SMEM)]
+    in_specs += [pl.BlockSpec(part.shape, lambda i, n=part.ndim: (0,) * n) for part in u_parts]
+    in_specs += [
+        pl.BlockSpec((3, planes, per_block, 8, width), lambda i: (0, 0, i, 0, 0)),
         pl.BlockSpec((10, per_block, 8, width), lambda i: (0, i, 0, 0)),
     ]
     if last:
-        out_shape = jax.ShapeDtypeStruct((4, 4, tiles - 1, 8, width), jnp.float32)
-        out_specs = pl.BlockSpec((4, 4, per_block, 8, width), lambda i: (0, 0, i, 0, 0))
+        out_shape = jax.ShapeDtypeStruct((4, planes, tiles - 1, 8, width), jnp.float32)
+        out_specs = pl.BlockSpec((4, planes, per_block, 8, width), lambda i: (0, 0, i, 0, 0))
     else:
         out_shape = [
-            jax.ShapeDtypeStruct(lo.shape, jnp.float32),
-            jax.ShapeDtypeStruct(mid.shape, jnp.float32),
-            jax.ShapeDtypeStruct(hi.shape, jnp.float32),
+            jax.ShapeDtypeStruct(plane_shape, jnp.float32),
+            jax.ShapeDtypeStruct(mid_shape, jnp.float32),
+            jax.ShapeDtypeStruct(plane_shape, jnp.float32),
             jax.ShapeDtypeStruct(gates.shape, jnp.float32),
         ]
         out_specs = [
             pl.BlockSpec((per_block, 8, width), lambda i: (i, 0, 0)),
-            pl.BlockSpec((2, per_block, 8, width), lambda i: (0, i, 0, 0)),
+            pl.BlockSpec((planes - 2, per_block, 8, width), lambda i: (0, i, 0, 0)),
             pl.BlockSpec((per_block, 8, width), lambda i: (i, 0, 0)),
-            pl.BlockSpec((3, 4, per_block, 8, width), lambda i: (0, 0, i, 0, 0)),
+            pl.BlockSpec((3, planes, per_block, 8, width), lambda i: (0, 0, i, 0, 0)),
         ]
-    cells = 4 * tiles * 8 * width
+    cells = planes * tiles * 8 * width
     return pl.pallas_call(
-        functools.partial(local_kernel, last, tiles, per_block),
+        functools.partial(local_kernel, first, last, tiles, per_block),
         grid=(blocks,),
         in_specs=in_specs,
         out_specs=out_specs,
         out_shape=out_shape,
         compiler_params=params(),
         cost_estimate=cost(150 * cells, 40 * cells, 11 * cells),
-        name="local_last" if last else "local",
-    )(side, lo, mid, hi, gates, coeffs)
+        name="local_first" if first else "local_last" if last else "local",
+    )(info, *u_parts, gates, coeffs)
 
 
 def halo_terms(halo_ref, coeff_ref, tile, tiles, side, sub, sign):
@@ -279,20 +282,21 @@
     return total + cross if sign > 0 else total - cross
 
 
-def halo_kernel(tiles, side_ref, lo_ref, hi_ref, below_ref, above_ref, coeff_ref, lo_out, hi_out):
-    side = side_ref[0]
+def halo_kernel(tiles, info_ref, far_ref, near_ref, beyond_ref, pair_ref, coeff_ref, far_out, near_out):
+    side = info_ref[SIDE]
+    exists = info_ref[FAR].astype(jnp.float32)
     sub = row_iota()
 
     def one(tile, carry):
-        lo_out[tile] = lo_ref[tile] + halo_terms(below_ref, coeff_ref, tile, tiles, side, sub, -1)
-        hi_out[tile] = hi_ref[tile] + halo_terms(above_ref, coeff_ref, tile, tiles, side, sub, 1)
+        near_out[tile] = near_ref[tile] + halo_terms(pair_ref, coeff_ref, tile, tiles, side, sub, 1)
+        far_out[tile] = far_ref[tile] + exists * halo_terms(beyond_ref, coeff_ref, tile, tiles, side, sub, -1)
         return carry
 
     lax.fori_loop(0, tiles, one, 0)
 
 
-def halo_step(side, lo, hi, below, above, coeffs):
-    tiles, _, width = lo.shape
+def halo_step(info, far, near, beyond, pair, coeffs):
+    tiles, _, width = far.shape
     whole = pl.BlockSpec((tiles, 8, width), lambda i: (0, 0, 0))
     cells = 2 * tiles * 8 * width
     return pl.pallas_call(
@@ -302,11 +306,11 @@
         + [whole] * 4
         + [pl.BlockSpec((4, tiles, 8, width), lambda i: (0, 0, 0, 0))],
         out_specs=[whole, whole],
-        out_shape=[jax.ShapeDtypeStruct(lo.shape, jnp.float32)] * 2,
+        out_shape=[jax.ShapeDtypeStruct(far.shape, jnp.float32)] * 2,
         compiler_params=params(),
         cost_estimate=cost(15 * cells, 20 * cells),
         name="halo",
-    )(side, lo, hi, below, above, coeffs)
+    )(info, far, near, beyond, pair, coeffs)
 
 
 def pair_matrix(width, scale):
@@ -332,18 +336,20 @@
     return jnp.concatenate([dot(few[:, at : at + 256], pick) for at in range(0, lanes, 256)], axis=1)
 
 
-def finish_kernel(tiles, side_ref, part_ref, below_ref, above_ref, coeff_ref, tension_ref, out_ref, tension_out, active_out):
-    side = side_ref[0]
+def finish_kernel(tiles, info_ref, part_ref, beyond_ref, pair_ref, coeff_ref, tension_ref, out_ref, tension_out, active_out, facing_out):
+    side, flip = info_ref[SIDE], info_ref[FLIP]
+    exists = info_ref[FAR].astype(jnp.float32)
     sub = row_iota()
     own = tiles - 1
     planes = part_ref.shape[1]
+    far, near = flip * (planes - 1), (1 - flip) * (planes - 1)
 
     def one(tile, carry):
-        out_ref[0, 0, tile] = part_ref[0, 0, tile] + halo_terms(below_ref, coeff_ref, tile, tiles, side, sub, -1)
+        out_ref[0, near, tile] = part_ref[0, near, tile] + halo_terms(pair_ref, coeff_ref, tile, tiles, side, sub, 1)
         for plane in range(1, planes - 1):
             out_ref[0, plane, tile] = part_ref[0, plane, tile]
-        out_ref[0, planes - 1, tile] = part_ref[0, planes - 1, tile] + halo_terms(
-            above_ref, coeff_ref, tile, tiles, side, sub, 1
+        out_ref[0, far, tile] = part_ref[0, far, tile] + exists * halo_terms(
+            beyond_ref, coeff_ref, tile, tiles, side, sub, -1
         )
         return carry
 
@@ -358,10 +364,11 @@
         tension_out[layer] = new
         total = new if total is None else total + new
     active_out[...] = pooled(0.5 * total)
-
-
-def finish_step(side, part, below, above, coeffs, tension):
-    tiles, _, width = below.shape
+    facing_out[...] = active_out[pl.ds(pl.multiple_of(8 * (1 - side), 8), 8), :]
+
+
+def finish_step(info, part, beyond, pair, coeffs, tension):
+    tiles, _, width = pair.shape
     own = tiles - 1
     planes = part.shape[1]
     halo_spec = pl.BlockSpec((tiles, 8, width), lambda i: (0, 0, 0))
@@ -380,17 +387,18 @@
             pl.BlockSpec((4, tiles, 8, width), lambda i: (0, 0, 0, 0)),
             tension_spec,
         ],
-        out_specs=[u_spec, tension_spec, pl.BlockSpec(active_shape, lambda i: (0, 0))],
+        out_specs=[u_spec, tension_spec, pl.BlockSpec(active_shape, lambda i: (0, 0)), pl.BlockSpec((8, width // 4), lambda i: (0, 0))],
         out_shape=[
             jax.ShapeDtypeStruct(part.shape, jnp.float32),
             jax.ShapeDtypeStruct(tension.shape, jnp.float32),
             jax.ShapeDtypeStruct(active_shape, jnp.float32),
+            jax.ShapeDtypeStruct((8, width // 4), jnp.float32),
         ],
         input_output_aliases={1: 0},
         compiler_params=params(),
         cost_estimate=cost(20 * cells, 20 * cells),
         name="finish",
-    )(side, part, below, above, coeffs, tension)
+    )(info, part, beyond, pair, coeffs, tension)
 
 
 REACH = 4
@@ -505,77 +513,124 @@
     return comps
 
 
-def window_plane(ref, comp, place, offset):
-    slab, side, slabs = place
-    spot = jnp.clip(slab + offset, 0, slabs - 1)
-    own = ref[spot, side, comp]
-    first = pl.multiple_of(8 * side, 8)
-    strip = ref[spot, 1 - side, comp, pl.ds(first, 8), :]
-    return jnp.concatenate([own, strip], axis=0)
-
-
-def inside(place, offset):
-    slab, _, slabs = place
+def inside(slab, slabs, offset):
     spot = slab + offset
     return jnp.where((spot >= 0) & (spot < slabs), 1.0, 0.0)
 
 
-def passive_kernel(place_ref, field_ref, disp_out, stress_out, pull_out, fdir_out):
-    slabs, _, _, own, width = field_ref.shape
-    place = (place_ref[0], place_ref[1], slabs)
-    k = Weights(place[1], own, width)
-
-    def disp_at(offset):
-        factor = inside(place, offset)
-        return [window_plane(field_ref, comp, place, offset) * factor for comp in range(3)]
-
-    def one(step, carry):
+def gather_planes(field, slabs, reach):
+    planes = {0: field}
+    for offset in range(1, reach + 1):
+        for shift in (offset % slabs, -offset % slabs):
+            if shift not in planes:
+                perm = [((i + shift) % slabs, i) for i in range(slabs)]
+                planes[shift] = lax.ppermute(field, "slab", perm)
+    return planes
+
+
+def fiber_table():
+    index = jnp.arange(128, dtype=jnp.float32)
+    theta = -1.0 + 2.0 * index / (NFIB - 1)
+    tilt = 0.3 * jnp.sin(3.0 * index)
+    return jnp.stack([jnp.sin(tilt), jnp.cos(tilt) * jnp.sin(theta), jnp.cos(tilt) * jnp.cos(theta)])
+
+
+def facing_kernel(info_ref, *refs):
+    out_ref = refs[-1]
+    first = pl.multiple_of(8 * (1 - info_ref[SIDE]), 8)
+    for pos, ref in enumerate(refs[:-1]):
+        for comp in range(ref.shape[0]):
+            out_ref[pos, comp] = ref[comp, pl.ds(first, 8), :]
+
+
+def facing_rows(info, fields):
+    comps, _, width = fields[0].shape
+    vmem = pl.BlockSpec(memory_space=pltpu.VMEM)
+    return pl.pallas_call(
+        facing_kernel,
+        in_specs=[pl.BlockSpec(memory_space=pltpu.SMEM)] + [vmem] * len(fields),
+        out_shape=jax.ShapeDtypeStruct((len(fields), comps, 8, width), jnp.float32),
+        compiler_params=params(),
+        cost_estimate=cost(0, 600_000),
+        name="facing",
+    )(info, *fields)
+
+
+def passive_kernel(slabs, shifts, info_ref, table_ref, strip_ref, *refs):
+    own_refs, (disp_out, stress_out, pull_out, disp_all) = refs[:-4], refs[-4:]
+    slab = info_ref[SLAB]
+    own, width = own_refs[0].shape[-2:]
+    k = Weights(info_ref[SIDE], own, width)
+    reach = REACH + 1
+
+    def plane(comp, offset):
+        spot = shifts.index(offset % slabs)
+        return jnp.concatenate([own_refs[spot][comp], strip_ref[spot, comp]], axis=0)
+
+    for offset in range(-reach, reach + 1):
+        factor = inside(slab, slabs, offset)
+        for comp in range(3):
+            disp_all[comp, offset + reach] = plane(comp, offset) * factor
+
+    tables = [jnp.broadcast_to(table_ref[comp : comp + 1], (8, 128)) for comp in range(3)]
+
+    def direction(index, comp):
+        index = index.astype(jnp.int32)
+        rows = []
+        for top in range(0, ROWS, 8):
+            parts = [
+                jnp.take_along_axis(tables[comp], index[top : top + 8, at : at + 128], axis=1, mode="promise_in_bounds")
+                for at in range(0, width, 128)
+            ]
+            rows.append(jnp.concatenate(parts, axis=1))
+        return jnp.concatenate(rows, axis=0)
+
+    for step in range(2 * REACH + 1):
         offset = step - REACH
-        below, mid, above = (disp_at(offset - 1), disp_at(offset), disp_at(offset + 1))
-        factor = inside(place, offset)
+        below, mid, above = ([disp_all[comp, step + shift] for comp in range(3)] for shift in range(3))
+        factor = inside(slab, slabs, offset)
         deform = deformation(below, mid, above, k)
         stress = times(deform, passive_stress(deform))
-        fdir = [window_plane(field_ref, 3 + comp, place, offset) for comp in range(3)]
+        index = plane(3, offset)
+        fdir = [direction(index, comp) for comp in range(3)]
         for i_pos in range(3):
             pull = (ACTIVE_GAIN * factor) * sum(deform[i_pos][b_pos] * fdir[b_pos] for b_pos in range(3))
             for a_pos in range(3):
                 stress_out[3 * i_pos + a_pos, step] = stress[i_pos][a_pos] * factor
                 pull_out[3 * i_pos + a_pos, step] = pull * fdir[a_pos]
             disp_out[i_pos, step] = mid[i_pos]
-            fdir_out[i_pos, step] = fdir[i_pos]
-        return carry
-
-    lax.fori_loop(0, 2 * REACH + 1, one, 0)
-
-
-def passive_step(place, field):
-    slabs, _, _, own, width = field.shape
+            disp_out[3 + i_pos, step] = fdir[i_pos]
+
+
+def passive_step(info, slabs, fields, strips):
+    shifts = sorted(fields)
+    width = strips.shape[-1]
     planes = 2 * REACH + 1
-    shapes = [(3, planes), (9, planes), (9, planes), (3, planes)]
+    shapes = [(6, planes), (9, planes), (9, planes)]
+    vmem = pl.BlockSpec(memory_space=pltpu.VMEM)
     return pl.pallas_call(
-        passive_kernel,
-        in_specs=[pl.BlockSpec(memory_space=pltpu.SMEM), pl.BlockSpec(memory_space=pltpu.VMEM)],
+        functools.partial(passive_kernel, slabs, shifts),
+        in_specs=[pl.BlockSpec(memory_space=pltpu.SMEM)] + [vmem] * (2 + len(shifts)),
         out_shape=[jax.ShapeDtypeStruct((a, b, ROWS, width), jnp.float32) for a, b in shapes],
+        scratch_shapes=[pltpu.VMEM((3, planes + 2, ROWS, width), jnp.float32)],
         compiler_params=params(),
         cost_estimate=cost(400 * planes * ROWS * width, 5_000_000),
         name="passive",
-    )(place, field)
-
-
-def mechanics_kernel(place_ref, active_ref, disp_ref, stress_ref, pull_ref, fdir_ref, disp_out, cond_out, d_one, p_two):
-    slabs, _, own, width = active_ref.shape
-    slab, side = place_ref[0], place_ref[1]
-    place = (slab, side, slabs)
+    )(info, fiber_table(), strips, *[fields[shift] for shift in shifts])
+
+
+def mechanics_kernel(slabs, shifts, info_ref, disp_ref, stress_ref, pull_ref, *rest):
+    active_refs, (disp_out, cond_out, d_one, p_two) = rest[:-4], rest[-4:]
+    slab, side = info_ref[SLAB], info_ref[SIDE]
+    own, width = disp_out.shape[-2:]
     k = Weights(side, own, width)
 
     def active_at(step):
-        spot = jnp.clip(slab + step - REACH, 0, slabs - 1)
-        first = pl.multiple_of(8 * side, 8)
-        return jnp.concatenate([active_ref[spot, side], active_ref[spot, 1 - side, pl.ds(first, 8), :]], axis=0)
-
-    def first_force(step, carry):
+        return active_refs[shifts.index((step - REACH) % slabs)][...]
+
+    for step in range(1, 2 * REACH):
         act = [active_at(step + shift) for shift in (-1, 0, 1)]
-        factor = inside(place, step - REACH)
+        factor = inside(slab, slabs, step - REACH)
         for i_pos in range(3):
             stress = [
                 [stress_ref[3 * i_pos + a_pos, step + shift] + act[shift + 1] * pull_ref[3 * i_pos + a_pos, step + shift] for a_pos in range(3)]
@@ -583,32 +638,26 @@
             ]
             moved = disp_ref[i_pos, step] + MECH_RATE * force(stress[0], stress[1], stress[2], k)
             d_one[i_pos, step] = moved * factor
-        return carry
-
-    lax.fori_loop(1, 2 * REACH, first_force, 0)
-
-    def second_stress(step, carry):
+
+    for step in range(2, 2 * REACH - 1):
         planes = [[d_one[comp, step + shift] for comp in range(3)] for shift in (-1, 0, 1)]
         deform = deformation(planes[0], planes[1], planes[2], k)
         second = passive_stress(deform)
-        fdir = [fdir_ref[comp, step] for comp in range(3)]
+        fdir = [disp_ref[3 + comp, step] for comp in range(3)]
         gain = ACTIVE_GAIN * active_at(step)
         for a_pos, b_pos in PAIRS:
             entry = second[a_pos, b_pos] + gain * fdir[a_pos] * fdir[b_pos]
             second[a_pos, b_pos] = entry
             second[b_pos, a_pos] = entry
         stress = times(deform, second)
-        factor = inside(place, step - REACH)
+        factor = inside(slab, slabs, step - REACH)
         for i_pos in range(3):
             for a_pos in range(3):
                 p_two[3 * i_pos + a_pos, step] = stress[i_pos][a_pos] * factor
-        return carry
-
-    lax.fori_loop(2, 2 * REACH - 1, second_stress, 0)
 
     last = []
     for step in (REACH - 1, REACH, REACH + 1):
-        factor = inside(place, step - REACH)
+        factor = inside(slab, slabs, step - REACH)
         row = []
         for i_pos in range(3):
             stress = [[p_two[3 * i_pos + a_pos, step + shift] for a_pos in range(3)] for shift in (-1, 0, 1)]
@@ -616,20 +665,21 @@
             row.append(moved * factor)
         last.append(row)
     deform = deformation(last[0], last[1], last[2], k)
-    comps = metric(deform, [fdir_ref[comp, REACH] for comp in range(3)])
+    comps = metric(deform, [disp_ref[3 + comp, REACH] for comp in range(3)])
     for i_pos in range(3):
         disp_out[i_pos, 0] = last[1][i_pos][:own]
     for pos, comp in enumerate(comps):
         cond_out[pos, 0] = comp[:own]
 
 
-def mechanics_step(place, active, window):
-    slabs, _, own, width = active.shape
+def mechanics_step(info, slabs, own, active, window):
+    shifts = sorted(active)
+    width = active[0].shape[-1]
     planes = 2 * REACH + 1
     vmem = pl.BlockSpec(memory_space=pltpu.VMEM)
     return pl.pallas_call(
-        mechanics_kernel,
-        in_specs=[pl.BlockSpec(memory_space=pltpu.SMEM)] + [vmem] * 5,
+        functools.partial(mechanics_kernel, slabs, shifts),
+        in_specs=[pl.BlockSpec(memory_space=pltpu.SMEM)] + [vmem] * (3 + len(shifts)),
         out_shape=[
             jax.ShapeDtypeStruct((3, 1, own, width), jnp.float32),
             jax.ShapeDtypeStruct((6, 1, own, width), jnp.float32),
@@ -641,14 +691,7 @@
         compiler_params=params(),
         cost_estimate=cost(400 * planes * ROWS * width, 5_000_000),
         name="mechanics",
-    )(place, active, *window)
-
-
-def fiber_dir(fiber):
-    block_index = fiber.astype(jnp.float32)
-    theta = -1.0 + 2.0 * block_index / (NFIB - 1)
-    tilt = 0.3 * jnp.sin(3.0 * block_index)
-    return jnp.stack([jnp.sin(tilt), jnp.cos(tilt) * jnp.sin(theta), jnp.cos(tilt) * jnp.cos(theta)])
+    )(info, *window, *[active[shift] for shift in shifts])
 
 
 def on_device(states, cond, tension, fiber, disp):
@@ -656,49 +699,60 @@
     slab, col = lax.axis_index("slab"), lax.axis_index("col")
     _, planes, rows, width = states.shape
     own = rows // 8
-    up = [(i, i + 1) for i in range(slabs - 1)]
-    down = [(i + 1, i) for i in range(slabs - 1)]
-    up_cross = [(2 * i + c, 2 * i + 3 - c) for i in range(slabs - 1) for c in range(2)]
-    down_cross = [(dst, src) for src, dst in up_cross]
+    flip = slab % 2
+    far_exists = (slab > 0) & (slab < slabs - 1)
+    info = jnp.stack([slab, col, flip, far_exists]).astype(jnp.int32)
+
+    partner = {i: i ^ 1 for i in range(slabs)}
+    other = {i: i if i in (0, slabs - 1) else ((i + 1) ^ 1) - 1 for i in range(slabs)}
+    to_pair = list(partner.items())
+    to_other = list(other.items())
+    cross_pair = [(2 * i + c, 2 * j + 1 - c) for i, j in to_pair for c in range(2)]
+    cross_other = [(2 * i + c, 2 * j + 1 - c) for i, j in to_other for c in range(2)]
     swap = [(0, 1), (1, 0)]
-    side = col.astype(jnp.int32).reshape(1)
-    place = jnp.stack([slab, col]).astype(jnp.int32)
 
     tiled = states.reshape(4, planes, own, 8, width)
-    below_own = lax.ppermute(tiled[0, planes - 1], "slab", up)
-    above_own = lax.ppermute(tiled[0, 0], "slab", down)
-
+    far_z, near_z = flip * (planes - 1), (1 - flip) * (planes - 1)
+    near = lax.dynamic_index_in_dim(tiled[0], near_z, 0, keepdims=False)
+    far = lax.dynamic_index_in_dim(tiled[0], far_z, 0, keepdims=False)
+    pair_own = lax.ppermute(near, "slab", to_pair)
+    beyond_own = lax.ppermute(far, "slab", to_other)
+
+    cond_strip = lax.ppermute(jnp.where(col == 0, cond[:, 0, -2:], cond[:, 0, :2]), "col", swap)
     facing = jnp.where(col == 0, tiled[:, :, own - 1], tiled[:, :, 0])
-    cond_facing = jnp.where(col == 0, cond[:, 0, -2:], cond[:, 0, :2])
     strip = lax.ppermute(facing, "col", swap)
-    cond_strip = lax.ppermute(cond_facing, "col", swap)
-    below_strip = lax.ppermute(facing[0, planes - 1], ("slab", "col"), up_cross)
-    above_strip = lax.ppermute(facing[0, 0], ("slab", "col"), down_cross)
-
-    field = jnp.concatenate([disp[:, 0], fiber_dir(fiber)[:, 0]], axis=0)
-    field = lax.all_gather(field, ("slab", "col")).reshape((slabs, 2) + field.shape)
-
-    coeffs = fine_coeffs(jnp.concatenate([cond[:, 0], cond_strip], axis=1))
-    wide = jnp.concatenate([tiled, strip[:, :, None]], axis=2)
-    lo, mid, hi, gates = wide[0, 0], wide[0, 1:-1], wide[0, -1], wide[1:]
-    below = jnp.concatenate([below_own, below_strip[None]], axis=0)
-    above = jnp.concatenate([above_own, above_strip[None]], axis=0)
+    facing_near = jnp.where(col == 0, near[own - 1], near[0])
+    facing_far = jnp.where(col == 0, far[own - 1], far[0])
+    pair_strip = lax.ppermute(facing_near, ("slab", "col"), cross_pair)
+    beyond_strip = lax.ppermute(facing_far, ("slab", "col"), cross_other)
+
+    field = jnp.concatenate([disp[:, 0], fiber.astype(jnp.float32)], axis=0)
+    fields = gather_planes(field, slabs, REACH + 1)
+    strips = lax.ppermute(facing_rows(info, [fields[shift] for shift in sorted(fields)]), "col", swap)
+
+    coeffs = fine_coeffs(info, jnp.concatenate([cond[:, 0], cond_strip], axis=1))
+    whole = jnp.concatenate([tiled, strip[:, :, None]], axis=2)
+    u_parts, gates = (whole[0],), whole[1:]
+    pair = jnp.concatenate([pair_own, pair_strip[None]], axis=0)
+    beyond = jnp.concatenate([beyond_own, beyond_strip[None]], axis=0)
     window = None
     for turn_index in range(SUB):
         last = turn_index == SUB - 1
-        result = local_step(side, lo, mid, hi, gates, coeffs, last)
+        result = local_step(info, u_parts, gates, coeffs, last)
         if turn_index == 1:
-            window = passive_step(place, field)
+            window = passive_step(info, slabs, fields, strips)
         if last:
             part = result
         else:
-            lo, mid, hi, gates = result
-            lo, hi = halo_step(side, lo, hi, below, above, coeffs)
-            below = lax.ppermute(hi, "slab", up)
-            above = lax.ppermute(lo, "slab", down)
-    states_next, tension_next, active = finish_step(side, part, below, above, coeffs, tension)
-    active = lax.all_gather(active, ("slab", "col")).reshape((slabs, 2) + active.shape)
-    disp_next, cond_next = mechanics_step(place, active, window)
+            far, mid, near, gates = result
+            far, near = halo_step(info, far, near, beyond, pair, coeffs)
+            pair = lax.ppermute(near, "slab", to_pair)
+            beyond = lax.ppermute(far, "slab", to_other)
+            u_parts = (far, mid, near)
+    states_next, tension_next, active, facing = finish_step(info, part, beyond, pair, coeffs, tension)
+    active_strip = lax.ppermute(facing, "col", swap)
+    active = gather_planes(jnp.concatenate([active, active_strip], axis=0), slabs, REACH)
+    disp_next, cond_next = mechanics_step(info, slabs, disp.shape[2], active, window)
     return (states_next.reshape(states.shape), tension_next, disp_next, cond_next)
 
 

time: 142 us -> 139 us (0.979)
  blocking collectives: 24.4 us -> 0 us
  waiting for transfers between devices: 17 us -> 37.5 us
  starting transfers between devices: 29.2 us -> 49.5 us
  between operations: 14.3 us -> 0.98 us
  local copies, waits for them, and re-layouts: 6.28 us -> 1.37 us
  other arithmetic: 6.2 us -> 3.05 us
  Pallas kernels: 43.9 us -> 46.5 us
    all_gather x1 -> x0, blocking collectives: 24.4 us -> none  [on_device(): lax.all_gather(active, ('slab', 'col')).reshape((slabs, 2) + active.shape)]
    ppermute x11 -> x27, starting transfers between devices: 28.6 us -> 49.4 us  [the longest x14 22.8 us: gather_planes(): planes[shift] = lax.ppermute(field, 'slab', perm)]
    ppermute x11 -> x27, waiting for transfers between devices: 17 us -> 37.5 us  [the longest x14 18.3 us: gather_planes(): planes[shift] = lax.ppermute(field, 'slab', perm)]
    unnamed x10 -> x11, local copies, waits for them, and re-layouts: 5.21 us -> 0.03 us
    concatenate x5, other arithmetic: 2.87 us -> 0.52 us  [the longest x1 0.46 us: on_device(): whole = jnp.concatenate([tiled, strip[:, :, None]], axis=2)]
    pallas_call x7 -> x8, Pallas kernels: 36.4 us -> 38.3 us  [the longest x4 27.6 us: local_step(): pl.pallas_call(functools.partial(local_kernel, first, last, tiles, per_bl...]
  transfers between devices with their start and end apart: 13 -> 28, of which waited for: 4 -> 9; matrix products, arithmetic and copies ran while one was open for 3% -> 2% of each run, Pallas kernels for 25% -> 22%
where the time goes in v2:
time: 139 us
  starting transfers between devices  49.5 us (36%)
  Pallas kernels  46.5 us (33%)
  waiting for transfers between devices  37.5 us (27%)
  other arithmetic  3.05 us (2%)
    pallas_call x4, Pallas kernels, local_step(): pl.pallas_call(functools.partial(local_kernel, first, last, tiles, per_bl...  27.6 us
    ppermute x14, starting transfers between devices, gather_planes(): planes[shift] = lax.ppermute(field, 'slab', perm)  22.8 us
    ppermute x14, waiting for transfers between devices, gather_planes(): planes[shift] = lax.ppermute(field, 'slab', perm)  18.3 us
    ppermute x3, starting transfers between devices, on_device(): pair = lax.ppermute(near, 'slab', to_pair)  15.9 us
    ppermute x3, waiting for transfers between devices, on_device(): pair = lax.ppermute(near, 'slab', to_pair)  10.5 us
    ppermute x1, waiting for transfers between devices, on_device(): pair_strip = lax.ppermute(facing_near, ('slab', 'col'), cross_pair)  7.79 us
    ppermute x1, starting transfers between devices, on_device(): pair_own = lax.ppermute(near, 'slab', to_pair)  6 us
    pallas_call x3, Pallas kernels, halo_step(): pl.pallas_call(functools.partial(halo_kernel, tiles), grid=(1,), in_specs...  4.52 us
  transfers between devices with their start and end apart: 28, of which 9 were waited for; matrix products, arithmetic and copies ran while one was open for 2% of the time, Pallas kernels for 22%

profile of v2, /device:TPU:0, one launch (start us, length us, event | category | flops | bytes accessed | tf_op | source)
XLA Modules:
  0.0 138.9 jit_solution(7365414745348464242)
XLA Ops:
  6.0 6.0 %collective-permute-start.4 = (f32[8,8,1024]{2,1,0:T(8,128)S(1)}, f32[8,8,1024]{2,1,0:T(8,128)S(1)}, u32[]{:S(2)}, u32[]{:S(2)}) collective-permute-start(f32[8,8,1024]{2,1,0:T(8,128)S(1)} %get-tuple-element.58), channel_id=1, source_target_pairs={{0,2},{2,0},{4,6},{6,4},{8,10},{10,8},{12,14},{14,12},{1,3},{3,1},... | collective-permute-start | bytes 786440 | tf_op jit(solution)/shard_map/ppermute | solution.py:718
  12.5 3.0 %coeffs.1.refs_2_.coeff_ref.refs_4_ = f32[10,9,8,1024]{3,2,1,0:T(8,128)S(1)} custom-call(s32[4]{0:T(128)S(1)} %pad_add_fusion.info_ref, f32[6,18,256]{2,1,0:T(8,128)S(1)} %pad_maximum_fusion.3.cond_ref), custom_call_target="tpu_custom_call" | custom-call | flops 2000000 | bytes 3200000 | tf_op jit(solution)/shard_map/coeffs/pallas_call | solution.py:109
  15.5 7.8 %collective-permute-done.5 = f32[8,1024]{1,0:T(8,128)S(1)} collective-permute-done((f32[8,1024]{1,0:T(8,128)S(1)}, f32[8,1024]{1,0:T(8,128)S(1)}, u32[]{:S(2)}, u32[]{:S(2)}) %collective-permute-start.5) | collective-permute-done | bytes 32800 | tf_op jit(solution)/shard_map/ppermute | solution.py:726
  24.0 7.0 %local_first.1 = (f32[9,8,1024]{2,1,0:T(8,128)S(1)}, f32[2,9,8,1024]{3,2,1,0:T(8,128)S(1)}, f32[9,8,1024]{2,1,0:T(8,128)S(1)}, f32[3,4,9,8,1024]{4,3,2,1,0:T(8,128)S(1)}) custom-call(s32[4]{0:T(128)S(1)} %pad_add_fusion.info_ref, f32[4,9,8,1024]{3,2,1,0:T(8,128)S(1)} %maximum_bitcast_fusion.refs_0_, f32[3,4,9,8,1024]{4,3,2,1,0:T(8,128)S(1)} %pad_maximum_fusion.refs_1_, ...), custom_call_target="tpu_custom_call" | custom-call | flops 44236800 | bytes 11796480 | tf_op jit(solution)/shard_map/local_first/pallas_call | solution.py:261
  33.1 5.3 %collective-permute-start.7 = (f32[9,8,1024]{2,1,0:T(8,128)S(1)}, f32[9,8,1024]{2,1,0:T(8,128)S(1)}, u32[]{:S(2)}, u32[]{:S(2)}) collective-permute-start(f32[9,8,1024]{2,1,0:T(8,128)S(1)} %get-tuple-element.35.refs_2_), channel_id=1, source_target_pairs={{0,2},{2,0},{4,6},{6,4},{8,10},{10,8},{12,14},{14,12},{1,3},{3,1},... | collective-permute-start | bytes 884744 | tf_op jit(solution)/shard_map/ppermute | solution.py:749
  38.4 6.8 %local.2 = (f32[9,8,1024]{2,1,0:T(8,128)S(1)}, f32[2,9,8,1024]{3,2,1,0:T(8,128)S(1)}, f32[9,8,1024]{2,1,0:T(8,128)S(1)}, f32[3,4,9,8,1024]{4,3,2,1,0:T(8,128)S(1)}) custom-call(s32[4]{0:T(128)S(1)} %pad_add_fusion.info_ref, f32[9,8,1024]{2,1,0:T(8,128)S(1)} %get-tuple-element.33.refs_0_, f32[2,9,8,1024]{3,2,1,0:T(8,128)S(1)} %get-tuple-element.34.refs_1_, ...), custom_call_target="tpu_custom_call" | custom-call | flops 44236800 | bytes 11796480 | tf_op jit(solution)/shard_map/local/pallas_call | solution.py:261
  45.3 5.3 %collective-permute-done.7.pair_ref = f32[9,8,1024]{2,1,0:T(8,128)S(1)} collective-permute-done((f32[9,8,1024]{2,1,0:T(8,128)S(1)}, f32[9,8,1024]{2,1,0:T(8,128)S(1)}, u32[]{:S(2)}, u32[]{:S(2)}) %collective-permute-start.7) | collective-permute-done | bytes 294944 | tf_op jit(solution)/shard_map/ppermute | solution.py:749
  52.8 5.3 %collective-permute-start.9 = (f32[9,8,1024]{2,1,0:T(8,128)S(1)}, f32[9,8,1024]{2,1,0:T(8,128)S(1)}, u32[]{:S(2)}, u32[]{:S(2)}) collective-permute-start(f32[9,8,1024]{2,1,0:T(8,128)S(1)} %get-tuple-element.41.refs_2_), channel_id=1, source_target_pairs={{0,2},{2,0},{4,6},{6,4},{8,10},{10,8},{12,14},{14,12},{1,3},{3,1},... | collective-permute-start | bytes 884744 | tf_op jit(solution)/shard_map/ppermute | solution.py:749
  58.1 6.8 %local.3 = (f32[9,8,1024]{2,1,0:T(8,128)S(1)}, f32[2,9,8,1024]{3,2,1,0:T(8,128)S(1)}, f32[9,8,1024]{2,1,0:T(8,128)S(1)}, f32[3,4,9,8,1024]{4,3,2,1,0:T(8,128)S(1)}) custom-call(s32[4]{0:T(128)S(1)} %pad_add_fusion.info_ref, f32[9,8,1024]{2,1,0:T(8,128)S(1)} %get-tuple-element.39.refs_0_, f32[2,9,8,1024]{3,2,1,0:T(8,128)S(1)} %get-tuple-element.40.refs_1_, ...), custom_call_target="tpu_custom_call" | custom-call | flops 44236800 | bytes 11796480 | tf_op jit(solution)/shard_map/local/pallas_call | solution.py:261
  64.9 5.2 %collective-permute-done.9.pair_ref = f32[9,8,1024]{2,1,0:T(8,128)S(1)} collective-permute-done((f32[9,8,1024]{2,1,0:T(8,128)S(1)}, f32[9,8,1024]{2,1,0:T(8,128)S(1)}, u32[]{:S(2)}, u32[]{:S(2)}) %collective-permute-start.9) | collective-permute-done | bytes 294944 | tf_op jit(solution)/shard_map/ppermute | solution.py:749
  72.3 5.3 %collective-permute-start.11 = (f32[9,8,1024]{2,1,0:T(8,128)S(1)}, f32[9,8,1024]{2,1,0:T(8,128)S(1)}, u32[]{:S(2)}, u32[]{:S(2)}) collective-permute-start(f32[9,8,1024]{2,1,0:T(8,128)S(1)} %get-tuple-element.47.refs_2_), channel_id=1, source_target_pairs={{0,2},{2,0},{4,6},{6,4},{8,10},{10,8},{12,14},{14,12},{1,3},{3,1},... | collective-permute-start | bytes 884744 | tf_op jit(solution)/shard_map/ppermute | solution.py:749
  77.7 3.5 %collective-permute-start.12 = (f32[4,16,256]{2,1,0:T(8,128)S(1)}, f32[4,16,256]{2,1,0:T(8,128)S(1)}, u32[]{:S(2)}, u32[]{:S(2)}) collective-permute-start(f32[4,16,256]{2,1,0:T(8,128)S(1)} %pad_maximum_fusion.4.refs_0_), channel_id=1, source_target_pairs={{2,0},{4,2},{6,4},{8,6},{10,8},{12,10},{14,12},{0,14},{3,1},{5,3},... | collective-permute-start | bytes 196616 | tf_op jit(solution)/shard_map/ppermute | solution.py:527
  82.2 5.2 %collective-permute-done.12.refs_1_ = f32[4,16,256]{2,1,0:T(8,128)S(1)} collective-permute-done((f32[4,16,256]{2,1,0:T(8,128)S(1)}, f32[4,16,256]{2,1,0:T(8,128)S(1)}, u32[]{:S(2)}, u32[]{:S(2)}) %collective-permute-start.12) | collective-permute-done | bytes 65568 | tf_op jit(solution)/shard_map/ppermute | solution.py:527
  87.4 8.7 %collective-permute-start.15 = (f32[4,16,256]{2,1,0:T(8,128)S(1)}, f32[4,16,256]{2,1,0:T(8,128)S(1)}, u32[]{:S(2)}, u32[]{:S(2)}) collective-permute-start(f32[4,16,256]{2,1,0:T(8,128)S(1)} %pad_maximum_fusion.4.refs_0_), channel_id=1, source_target_pairs={{8,0},{10,2},{12,4},{14,6},{0,8},{2,10},{4,12},{6,14},{9,1},{11,3}... | collective-permute-start | bytes 196616 | tf_op jit(solution)/shard_map/ppermute | solution.py:527
  97.7 4.1 %collective-permute-done.15.refs_4_ = f32[4,16,256]{2,1,0:T(8,128)S(1)} collective-permute-done((f32[4,16,256]{2,1,0:T(8,128)S(1)}, f32[4,16,256]{2,1,0:T(8,128)S(1)}, u32[]{:S(2)}, u32[]{:S(2)}) %collective-permute-start.15) | collective-permute-done | bytes 65568 | tf_op jit(solution)/shard_map/ppermute | solution.py:527
  101.9 3.5 %collective-permute-done.16.refs_5_ = f32[4,16,256]{2,1,0:T(8,128)S(1)} collective-permute-done((f32[4,16,256]{2,1,0:T(8,128)S(1)}, f32[4,16,256]{2,1,0:T(8,128)S(1)}, u32[]{:S(2)}, u32[]{:S(2)}) %collective-permute-start.16) | collective-permute-done | bytes 65568 | tf_op jit(solution)/shard_map/ppermute | solution.py:527
  105.4 3.4 %collective-permute-done.18.refs_7_ = f32[4,16,256]{2,1,0:T(8,128)S(1)} collective-permute-done((f32[4,16,256]{2,1,0:T(8,128)S(1)}, f32[4,16,256]{2,1,0:T(8,128)S(1)}, u32[]{:S(2)}, u32[]{:S(2)}) %collective-permute-start.18) | collective-permute-done | bytes 65568 | tf_op jit(solution)/shard_map/ppermute | solution.py:527
  109.5 7.0 %local_last.1.part_ref = f32[4,4,8,8,1024]{4,3,2,1,0:T(8,128)} custom-call(s32[4]{0:T(128)S(1)} %pad_add_fusion.info_ref, f32[9,8,1024]{2,1,0:T(8,128)S(1)} %get-tuple-element.45.refs_0_, f32[2,9,8,1024]{3,2,1,0:T(8,128)S(1)} %get-tuple-element.46.refs_1_, f32[9,8,1024]{2,1,0:T(8,128)S(1)} %get-tuple-element.47.refs_2_, ...), custom_call_target="tpu_custom_call" | custom-call | flops 44236800 | bytes 11796480 | tf_op jit(solution)/shard_map/local_last/pallas_call | solution.py:261
  116.5 3.7 %finish.1 = (f32[4,4,8,8,1024]{4,3,2,1,0:T(8,128)}, f32[2,32,512]{2,1,0:T(8,128)}, f32[16,256]{1,0:T(8,128)S(1)}, f32[8,256]{1,0:T(8,128)S(1)}) custom-call(s32[4]{0:T(128)S(1)} %pad_add_fusion.info_ref, f32[4,4,8,8,1024]{4,3,2,1,0:T(8,128)} %local_last.1.part_ref, ...), custom_call_target="tpu_custom_call", output_to_operand_aliasing={{0}: (1, {})} | custom-call | flops 5242880 | bytes 5242880 | tf_op jit(solution)/shard_map/finish/pallas_call | solution.py:379
  121.6 4.4 %collective-permute-start.24 = (f32[24,256]{1,0:T(8,128)S(1)}, f32[24,256]{1,0:T(8,128)S(1)}, u32[]{:S(2)}, u32[]{:S(2)}) collective-permute-start(f32[24,256]{1,0:T(8,128)S(1)} %constant_dynamic-update-slice_fusion.rest_0_), channel_id=1, source_target_pairs={{8,0},{10,2},{12,4},{14,6},{0,8},{2,10},{4,12},{6,14},{9,1},{11,3}... | collective-permute-start | bytes 73736 | tf_op jit(solution)/shard_map/ppermute | solution.py:527
  126.0 2.1 %collective-permute-start.26 = (f32[24,256]{1,0:T(8,128)S(1)}, f32[24,256]{1,0:T(8,128)S(1)}, u32[]{:S(2)}, u32[]{:S(2)}) collective-permute-start(f32[24,256]{1,0:T(8,128)S(1)} %constant_dynamic-update-slice_fusion.rest_0_), channel_id=1, source_target_pairs={{12,0},{14,2},{0,4},{2,6},{4,8},{6,10},{8,12},{10,14},{13,1},{15,3... | collective-permute-start | bytes 73736 | tf_op jit(solution)/shard_map/ppermute | solution.py:527
  129.5 2.9 %passive.1 = (f32[6,9,24,256]{3,2,1,0:T(8,128)S(1)}, f32[9,9,24,256]{3,2,1,0:T(8,128)S(1)}, f32[9,9,24,256]{3,2,1,0:T(8,128)S(1)}) custom-call(s32[4]{0:T(128)S(1)} %pad_add_fusion.info_ref, f32[3,128]{1,0:T(4,128)S(1)} %pad_maximum_fusion.5.table_ref, f32[8,4,8,256]{3,2,1,0:T(8,128)S(1)} %collective-permute-done.19.strip_ref, ...), custom_call_target="tpu_custom_call" | custom-call | flops 22118400 | bytes 5000000 | tf_op jit(solution)/shard_map/passive/pallas_call | solution.py:611
  132.5 2.1 %collective-permute-done.27.rest_7_ = f32[24,256]{1,0:T(8,128)S(1)} collective-permute-done((f32[24,256]{1,0:T(8,128)S(1)}, f32[24,256]{1,0:T(8,128)S(1)}, u32[]{:S(2)}, u32[]{:S(2)}) %collective-permute-start.27) | collective-permute-done | bytes 24608 | tf_op jit(solution)/shard_map/ppermute | solution.py:527
  134.6 4.3 %mechanics.1 = (f32[3,1,16,256]{3,2,1,0:T(8,128)}, f32[6,1,16,256]{3,2,1,0:T(8,128)}) custom-call(s32[4]{0:T(128)S(1)} %pad_add_fusion.info_ref, f32[6,9,24,256]{3,2,1,0:T(8,128)S(1)} %get-tuple-element.51.disp_ref, f32[9,9,24,256]{3,2,1,0:T(8,128)S(1)} %get-tuple-element.52.stress_ref, f32[9,9,24,256]{3,2,1,0:T(8,128)S(1)} %get-tuple-element.53.pull_ref, ...), custom_call_target="tpu_custom_call" | custom-call | flops 22118400 | bytes 5000000 | tf_op jit(solution)/shard_map/mechanics/pallas_call | solution.py:680
  (72 shorter events, 19.4 us)
Async XLA Ops:
  1.5 10.6 %collective-permute-start.1 = (f32[6,2,256]{2,1,0:T(2,128)S(1)}, f32[6,2,256]{2,1,0:T(2,128)S(1)}, u32[]{:S(2)}, u32[]{:S(2)}) collective-permute-start(f32[6,2,256]{2,1,0:T(2,128)S(1)} %fusion.4), channel_id=1, source_target_pairs={{0,1},{1,0},{2,3},{3,2},{4,5},{5,4},{6,7},{7,6},{8,9},{9,8},{10,11... | collective-permute-start | bytes 36872 | tf_op jit(solution)/shard_map/ppermute | solution.py:721
  3.3 20.1 %collective-permute-start = (f32[4,4,8,1024]{3,2,1,0:T(8,128)S(1)}, f32[4,4,8,1024]{3,2,1,0:T(8,128)S(1)}, u32[]{:S(2)}, u32[]{:S(2)}) collective-permute-start(f32[4,4,8,1024]{3,2,1,0:T(8,128)S(1)} %fusion.1), channel_id=1, source_target_pairs={{0,1},{1,0},{2,3},{3,2},{4,5},{5,4},{6,7},{7,6},{8,9},{9,8},{10,11... | collective-permute-start | bytes 1572872 | tf_op jit(solution)/shard_map/ppermute | solution.py:723
  4.8 10.7 %collective-permute-start.2 = (f32[8,8,1024]{2,1,0:T(8,128)S(1)}, f32[8,8,1024]{2,1,0:T(8,128)S(1)}, u32[]{:S(2)}, u32[]{:S(2)}) collective-permute-start(f32[8,8,1024]{2,1,0:T(8,128)S(1)} %get-tuple-element.59), channel_id=1, source_target_pairs={{0,0},{2,4},{4,2},{6,8},{8,6},{10,12},{12,10},{14,14},{1,1},{3,5},... | collective-permute-start | bytes 786440 | tf_op jit(solution)/shard_map/ppermute | solution.py:719
  5.5 10.0 %collective-permute-start.3 = (f32[8,1024]{1,0:T(8,128)S(1)}, f32[8,1024]{1,0:T(8,128)S(1)}, u32[]{:S(2)}, u32[]{:S(2)}) collective-permute-start(f32[8,1024]{1,0:T(8,128)S(1)} %get-tuple-element.61), channel_id=1, source_target_pairs={{0,1},{1,0},{2,5},{3,4},{4,3},{5,2},{6,9},{7,8},{8,7},{9,6},{10,13... | collective-permute-start | bytes 98312 | tf_op jit(solution)/shard_map/ppermute | solution.py:727
  6.0 17.3 %collective-permute-start.4 = (f32[8,8,1024]{2,1,0:T(8,128)S(1)}, f32[8,8,1024]{2,1,0:T(8,128)S(1)}, u32[]{:S(2)}, u32[]{:S(2)}) collective-permute-start(f32[8,8,1024]{2,1,0:T(8,128)S(1)} %get-tuple-element.58), channel_id=1, source_target_pairs={{0,2},{2,0},{4,6},{6,4},{8,10},{10,8},{12,14},{14,12},{1,3},{3,1},... | collective-permute-start | bytes 786440 | tf_op jit(solution)/shard_map/ppermute | solution.py:718
  12.1 11.2 %collective-permute-start.5 = (f32[8,1024]{1,0:T(8,128)S(1)}, f32[8,1024]{1,0:T(8,128)S(1)}, u32[]{:S(2)}, u32[]{:S(2)}) collective-permute-start(f32[8,1024]{1,0:T(8,128)S(1)} %get-tuple-element.60), channel_id=1, source_target_pairs={{0,3},{1,2},{2,1},{3,0},{4,7},{5,6},{6,5},{7,4},{8,11},{9,10},{10,... | collective-permute-start | bytes 98312 | tf_op jit(solution)/shard_map/ppermute | solution.py:726
  32.4 12.8 %collective-permute-start.6 = (f32[9,8,1024]{2,1,0:T(8,128)S(1)}, f32[9,8,1024]{2,1,0:T(8,128)S(1)}, u32[]{:S(2)}, u32[]{:S(2)}) collective-permute-start(f32[9,8,1024]{2,1,0:T(8,128)S(1)} %get-tuple-element.33.refs_0_), channel_id=1, source_target_pairs={{0,0},{2,4},{4,2},{6,8},{8,6},{10,12},{12,10},{14,14},{1,1},{3,5},... | collective-permute-start | bytes 884744 | tf_op jit(solution)/shard_map/ppermute | solution.py:750
  33.1 17.4 %collective-permute-start.7 = (f32[9,8,1024]{2,1,0:T(8,128)S(1)}, f32[9,8,1024]{2,1,0:T(8,128)S(1)}, u32[]{:S(2)}, u32[]{:S(2)}) collective-permute-start(f32[9,8,1024]{2,1,0:T(8,128)S(1)} %get-tuple-element.35.refs_2_), channel_id=1, source_target_pairs={{0,2},{2,0},{4,6},{6,4},{8,10},{10,8},{12,14},{14,12},{1,3},{3,1},... | collective-permute-start | bytes 884744 | tf_op jit(solution)/shard_map/ppermute | solution.py:749
  52.1 12.8 %collective-permute-start.8 = (f32[9,8,1024]{2,1,0:T(8,128)S(1)}, f32[9,8,1024]{2,1,0:T(8,128)S(1)}, u32[]{:S(2)}, u32[]{:S(2)}) collective-permute-start(f32[9,8,1024]{2,1,0:T(8,128)S(1)} %get-tuple-element.39.refs_0_), channel_id=1, source_target_pairs={{0,0},{2,4},{4,2},{6,8},{8,6},{10,12},{12,10},{14,14},{1,1},{3,5},... | collective-permute-start | bytes 884744 | tf_op jit(solution)/shard_map/ppermute | solution.py:750
  52.8 17.4 %collective-permute-start.9 = (f32[9,8,1024]{2,1,0:T(8,128)S(1)}, f32[9,8,1024]{2,1,0:T(8,128)S(1)}, u32[]{:S(2)}, u32[]{:S(2)}) collective-permute-start(f32[9,8,1024]{2,1,0:T(8,128)S(1)} %get-tuple-element.41.refs_2_), channel_id=1, source_target_pairs={{0,2},{2,0},{4,6},{6,4},{8,10},{10,8},{12,14},{14,12},{1,3},{3,1},... | collective-permute-start | bytes 884744 | tf_op jit(solution)/shard_map/ppermute | solution.py:749
  71.6 44.9 %collective-permute-start.10 = (f32[9,8,1024]{2,1,0:T(8,128)S(1)}, f32[9,8,1024]{2,1,0:T(8,128)S(1)}, u32[]{:S(2)}, u32[]{:S(2)}) collective-permute-start(f32[9,8,1024]{2,1,0:T(8,128)S(1)} %get-tuple-element.45.refs_0_), channel_id=1, source_target_pairs={{0,0},{2,4},{4,2},{6,8},{8,6},{10,12},{12,10},{14,14},{1,1},{3,5},... | collective-permute-start | bytes 884744 | tf_op jit(solution)/shard_map/ppermute | solution.py:750
  72.3 44.2 %collective-permute-start.11 = (f32[9,8,1024]{2,1,0:T(8,128)S(1)}, f32[9,8,1024]{2,1,0:T(8,128)S(1)}, u32[]{:S(2)}, u32[]{:S(2)}) collective-permute-start(f32[9,8,1024]{2,1,0:T(8,128)S(1)} %get-tuple-element.47.refs_2_), channel_id=1, source_target_pairs={{0,2},{2,0},{4,6},{6,4},{8,10},{10,8},{12,14},{14,12},{1,3},{3,1},... | collective-permute-start | bytes 884744 | tf_op jit(solution)/shard_map/ppermute | solution.py:749
  77.7 9.7 %collective-permute-start.12 = (f32[4,16,256]{2,1,0:T(8,128)S(1)}, f32[4,16,256]{2,1,0:T(8,128)S(1)}, u32[]{:S(2)}, u32[]{:S(2)}) collective-permute-start(f32[4,16,256]{2,1,0:T(8,128)S(1)} %pad_maximum_fusion.4.refs_0_), channel_id=1, source_target_pairs={{2,0},{4,2},{6,4},{8,6},{10,8},{12,10},{14,12},{0,14},{3,1},{5,3},... | collective-permute-start | bytes 196616 | tf_op jit(solution)/shard_map/ppermute | solution.py:527
  81.1 15.0 %collective-permute-start.13 = (f32[4,16,256]{2,1,0:T(8,128)S(1)}, f32[4,16,256]{2,1,0:T(8,128)S(1)}, u32[]{:S(2)}, u32[]{:S(2)}) collective-permute-start(f32[4,16,256]{2,1,0:T(8,128)S(1)} %pad_maximum_fusion.4.refs_0_), channel_id=1, source_target_pairs={{4,0},{6,2},{8,4},{10,6},{12,8},{14,10},{0,12},{2,14},{5,1},{7,3},... | collective-permute-start | bytes 196616 | tf_op jit(solution)/shard_map/ppermute | solution.py:527
  81.6 15.1 %collective-permute-start.14 = (f32[4,16,256]{2,1,0:T(8,128)S(1)}, f32[4,16,256]{2,1,0:T(8,128)S(1)}, u32[]{:S(2)}, u32[]{:S(2)}) collective-permute-start(f32[4,16,256]{2,1,0:T(8,128)S(1)} %pad_maximum_fusion.4.refs_0_), channel_id=1, source_target_pairs={{6,0},{8,2},{10,4},{12,6},{14,8},{0,10},{2,12},{4,14},{7,1},{9,3},... | collective-permute-start | bytes 196616 | tf_op jit(solution)/shard_map/ppermute | solution.py:527
  87.4 14.5 %collective-permute-start.15 = (f32[4,16,256]{2,1,0:T(8,128)S(1)}, f32[4,16,256]{2,1,0:T(8,128)S(1)}, u32[]{:S(2)}, u32[]{:S(2)}) collective-permute-start(f32[4,16,256]{2,1,0:T(8,128)S(1)} %pad_maximum_fusion.4.refs_0_), channel_id=1, source_target_pairs={{8,0},{10,2},{12,4},{14,6},{0,8},{2,10},{4,12},{6,14},{9,1},{11,3}... | collective-permute-start | bytes 196616 | tf_op jit(solution)/shard_map/ppermute | solution.py:527
  96.1 9.4 %collective-permute-start.16 = (f32[4,16,256]{2,1,0:T(8,128)S(1)}, f32[4,16,256]{2,1,0:T(8,128)S(1)}, u32[]{:S(2)}, u32[]{:S(2)}) collective-permute-start(f32[4,16,256]{2,1,0:T(8,128)S(1)} %pad_maximum_fusion.4.refs_0_), channel_id=1, source_target_pairs={{10,0},{12,2},{14,4},{0,6},{2,8},{4,10},{6,12},{8,14},{11,1},{13,3... | collective-permute-start | bytes 196616 | tf_op jit(solution)/shard_map/ppermute | solution.py:527
  96.6 8.8 %collective-permute-start.17 = (f32[4,16,256]{2,1,0:T(8,128)S(1)}, f32[4,16,256]{2,1,0:T(8,128)S(1)}, u32[]{:S(2)}, u32[]{:S(2)}) collective-permute-start(f32[4,16,256]{2,1,0:T(8,128)S(1)} %pad_maximum_fusion.4.refs_0_), channel_id=1, source_target_pairs={{12,0},{14,2},{0,4},{2,6},{4,8},{6,10},{8,12},{10,14},{13,1},{15,3... | collective-permute-start | bytes 196616 | tf_op jit(solution)/shard_map/ppermute | solution.py:527
  101.8 7.0 %collective-permute-start.18 = (f32[4,16,256]{2,1,0:T(8,128)S(1)}, f32[4,16,256]{2,1,0:T(8,128)S(1)}, u32[]{:S(2)}, u32[]{:S(2)}) collective-permute-start(f32[4,16,256]{2,1,0:T(8,128)S(1)} %pad_maximum_fusion.4.refs_0_), channel_id=1, source_target_pairs={{14,0},{0,2},{2,4},{4,6},{6,8},{8,10},{10,12},{12,14},{15,1},{1,3}... | collective-permute-start | bytes 196616 | tf_op jit(solution)/shard_map/ppermute | solution.py:527
  109.4 16.6 %collective-permute-start.19 = (f32[8,4,8,256]{3,2,1,0:T(8,128)S(1)}, f32[8,4,8,256]{3,2,1,0:T(8,128)S(1)}, u32[]{:S(2)}, u32[]{:S(2)}) collective-permute-start(f32[8,4,8,256]{3,2,1,0:T(8,128)S(1)} %facing.1), channel_id=1, source_target_pairs={{0,1},{1,0},{2,3},{3,2},{4,5},{5,4},{6,7},{7,6},{8,9},{9,8},{10,11... | collective-permute-start | bytes 786440 | tf_op jit(solution)/shard_map/ppermute | solution.py:731
  121.5 6.6 %collective-permute-start.22 = (f32[24,256]{1,0:T(8,128)S(1)}, f32[24,256]{1,0:T(8,128)S(1)}, u32[]{:S(2)}, u32[]{:S(2)}) collective-permute-start(f32[24,256]{1,0:T(8,128)S(1)} %constant_dynamic-update-slice_fusion.rest_0_), channel_id=1, source_target_pairs={{4,0},{6,2},{8,4},{10,6},{12,8},{14,10},{0,12},{2,14},{5,1},{7,3},... | collective-permute-start | bytes 73736 | tf_op jit(solution)/shard_map/ppermute | solution.py:527
  121.6 10.9 %collective-permute-start.23 = (f32[24,256]{1,0:T(8,128)S(1)}, f32[24,256]{1,0:T(8,128)S(1)}, u32[]{:S(2)}, u32[]{:S(2)}) collective-permute-start(f32[24,256]{1,0:T(8,128)S(1)} %constant_dynamic-update-slice_fusion.rest_0_), channel_id=1, source_target_pairs={{6,0},{8,2},{10,4},{12,6},{14,8},{0,10},{2,12},{4,14},{7,1},{9,3},... | collective-permute-start | bytes 73736 | tf_op jit(solution)/shard_map/ppermute | solution.py:527
  121.6 10.8 %collective-permute-start.24 = (f32[24,256]{1,0:T(8,128)S(1)}, f32[24,256]{1,0:T(8,128)S(1)}, u32[]{:S(2)}, u32[]{:S(2)}) collective-permute-start(f32[24,256]{1,0:T(8,128)S(1)} %constant_dynamic-update-slice_fusion.rest_0_), channel_id=1, source_target_pairs={{8,0},{10,2},{12,4},{14,6},{0,8},{2,10},{4,12},{6,14},{9,1},{11,3}... | collective-permute-start | bytes 73736 | tf_op jit(solution)/shard_map/ppermute | solution.py:527
  128.1 6.5 %collective-permute-start.27 = (f32[24,256]{1,0:T(8,128)S(1)}, f32[24,256]{1,0:T(8,128)S(1)}, u32[]{:S(2)}, u32[]{:S(2)}) collective-permute-start(f32[24,256]{1,0:T(8,128)S(1)} %constant_dynamic-update-slice_fusion.rest_0_), channel_id=1, source_target_pairs={{14,0},{0,2},{2,4},{4,6},{6,8},{8,10},{10,12},{12,14},{15,1},{1,3}... | collective-permute-start | bytes 73736 | tf_op jit(solution)/shard_map/ppermute | solution.py:527
  (9 other events, 74.6 us)

commit v3 on v2

v3 whole, which is shorter than its diff:
```python
import functools

import jax
import jax.numpy as jnp
from jax import lax
from jax.experimental import pallas as pl
from jax.experimental.pallas import tpu as pltpu
from jax.sharding import PartitionSpec as P

SUB = 4
MECH_STEPS = 2
NFIB = 64

STEP_TIME = 0.05
LAME_FIRST = 1.0
SHEAR = 0.5
ACTIVE_GAIN = 0.5
MECH_RATE = 0.15
SIGMA_LONG = 0.16
SIGMA_TRANS = 0.04
PAIRS = ((0, 0), (1, 1), (2, 2), (0, 1), (0, 2), (1, 2))

C_ZZ, C_ZY, C_ZXR, C_ZXL, C_MID, C_YY, C_XXR, C_YXR, C_XXL, C_YXL = range(10)

SLAB, SIDE, FLIP, FAR = range(4)

HIGHEST = lax.Precision.HIGHEST
LIMIT = 40 * 1024 * 1024


def params(**kwargs):
    return pltpu.CompilerParams(vmem_limit_bytes=LIMIT, **kwargs)


def cost(flops, nbytes, trans=0):
    return pl.CostEstimate(flops=flops, bytes_accessed=nbytes, transcendentals=trans)


def row_iota():
    return lax.broadcasted_iota(jnp.int32, (8, 1024), 0)


def next_row(cur, nxt, sub):
    return pltpu.roll(jnp.where(sub == 0, nxt, cur), 7, 0)


def prev_row(cur, prv, sub):
    return pltpu.roll(jnp.where(sub == 7, prv, cur), 1, 0)


def left(val):
    return pltpu.roll(val, val.shape[-1] - 1, val.ndim - 1)


def right(val):
    return pltpu.roll(val, 1, val.ndim - 1)


def edge_masks(tile, side, own):
    before = jnp.where((tile == 0) & (side == 0), 0.0, 1.0)
    after = jnp.where((tile == own - 1) & (side == 1), 0.0, 1.0)
    return before, after


def ring_neighbours(tile, tiles):
    before = jnp.where(tile == 0, tiles - 1, tile - 1)
    after = jnp.where(tile == tiles - 1, 0, tile + 1)
    return before, after


def coeff_kernel(info_ref, cond_ref, strip_ref, out_ref):
    rows, width = cond_ref.shape[-2:]
    turn = jnp.where(info_ref[FLIP] == 1, -0.5, 0.5)
    upper_side = info_ref[SIDE] == 0
    fine = 4 * width
    mech = lax.broadcasted_iota(jnp.int32, (width, fine), 0)
    cell = lax.broadcasted_iota(jnp.int32, (width, fine), 1)
    own = rows // 2
    block = rows + 8
    sub = lax.broadcasted_iota(jnp.int32, (8, fine), 0)

    def spread(comps, shift):
        pick = jnp.where(mech == ((cell + shift) >> 2), 1.0, 0.0)
        flat = jnp.concatenate([part for comp in comps for part in (cond_ref[comp, 0], strip_ref[comp])], axis=0)
        wide = jnp.dot(flat, pick, precision=HIGHEST, preferred_element_type=jnp.float32)
        return [wide[pos * block : (pos + 1) * block] for pos in range(len(comps))]

    def both(first, second):
        return jnp.where(sub < 4, jnp.broadcast_to(first, (8, fine)), jnp.broadcast_to(second, (8, fine)))

    def store(index, wide):
        for tile in range(own):
            out_ref[index, tile] = both(wide[2 * tile : 2 * tile + 1], wide[2 * tile + 1 : 2 * tile + 2])
        head = both(wide[rows : rows + 1], wide[rows + 1 : rows + 2])
        tail = both(wide[block - 2 : block - 1], wide[block - 1 : block])
        out_ref[index, own] = jnp.where(upper_side, head, tail)

    zz, yy, xx, zy = spread((0, 1, 2, 3), 0)
    store(C_ZZ, zz)
    store(C_YY, yy)
    store(C_MID, 1.0 - 2.0 * (zz + yy + xx))
    store(C_ZY, turn * zy)
    xx, zx, yx = spread((2, 4, 5), -1)
    store(C_XXR, xx)
    store(C_ZXR, turn * zx)
    store(C_YXR, 0.5 * yx)
    xx, zx, yx = spread((2, 4, 5), 1)
    store(C_XXL, xx)
    store(C_ZXL, turn * zx)
    store(C_YXL, 0.5 * yx)


def fine_coeffs(info, cond, strip):
    rows, width = cond.shape[-2:]
    vmem = pl.BlockSpec(memory_space=pltpu.VMEM)
    return pl.pallas_call(
        coeff_kernel,
        in_specs=[pl.BlockSpec(memory_space=pltpu.SMEM), vmem, vmem],
        out_shape=jax.ShapeDtypeStruct((10, rows // 2 + 1, 8, 4 * width), jnp.float32),
        compiler_params=params(),
        cost_estimate=cost(2_000_000, 3_200_000),
        name="coeffs",
    )(info, cond, strip)


def pack_kernel(info_ref, states_ref, cond_ref, far_ref, near_ref, facing_ref, far_rows, near_rows, cond_rows, sems):
    side, flip = info_ref[SIDE], info_ref[FLIP]
    planes, own = states_ref.shape[1:3]
    far, near = flip * (planes - 1), (1 - flip) * (planes - 1)
    edge = (1 - side) * (own - 1)
    half = pl.multiple_of(8 * (1 - side), 8)
    moves = [
        (states_ref.at[0, far], far_ref),
        (states_ref.at[0, near], near_ref),
        (states_ref.at[0, far, edge], far_rows),
        (states_ref.at[0, near, edge], near_rows),
        (states_ref.at[:, :, edge], facing_ref),
        (cond_ref.at[:, 0, pl.ds(half, 8), :], cond_rows),
    ]
    copies = [pltpu.make_async_copy(src, dst, sems.at[pos]) for pos, (src, dst) in enumerate(moves)]
    for copy in copies:
        copy.start()
    for copy in copies:
        copy.wait()


def pack(info, tiled, cond):
    comps, planes, own, _, width = tiled.shape
    shapes = [(own, 8, width), (own, 8, width), (comps, planes, 8, width), (8, width), (8, width)]
    shapes.append((cond.shape[0], 8, cond.shape[-1]))
    return pl.pallas_call(
        pack_kernel,
        in_specs=[pl.BlockSpec(memory_space=pltpu.SMEM)] + [pl.BlockSpec(memory_space=pltpu.HBM)] * 2,
        out_specs=[pl.BlockSpec(memory_space=pltpu.VMEM)] * len(shapes),
        out_shape=[jax.ShapeDtypeStruct(shape, jnp.float32) for shape in shapes],
        scratch_shapes=[pltpu.SemaphoreType.DMA((len(shapes),))],
        compiler_params=params(),
        cost_estimate=cost(0, 2_500_000),
        name="pack",
    )(info, tiled, cond)


def fraction(val):
    return pl.reciprocal(val, approx=True)


def ionic(u, v, w, s):
    dt = STEP_TIME
    steep = 50.0 * u
    t_v = jnp.tanh(steep - 15.0)
    t_w = jnp.tanh(steep - 6.5)
    t_o = jnp.tanh(steep - 0.3)
    t_m = jnp.tanh(65.0 * u - 65.0 * 0.03)
    t_f = jnp.tanh(2.0458 * u - 2.0458 * 0.65)
    t_s = jnp.tanh(2.0994 * u - 2.0994 * 0.9087)
    hv, nv = 1.0 + t_v, 1.0 - t_v
    hw, nw = 1.0 + t_w, 1.0 - t_w
    no = 0.5 - 0.5 * t_o
    half_so = 0.5 * (30.0181 - 0.9957)
    r_vm = fraction(2.0 / dt * 605.0 + (2.0 / dt * 545.0) * t_o)
    r_wm = fraction(2.0 / dt * 37.5 - (2.0 / dt * 22.5) * t_m)
    r_so = fraction(2.0 / dt * (30.0181 - half_so) - (2.0 / dt * half_so) * t_f)
    r_s = fraction(9.3671 / dt + (6.6329 / dt) * t_w)
    r_o = fraction(2.0 / dt * 203.0 - (2.0 / dt * 197.0) * t_o)
    w_inf = 0.94 + no * (0.06 - u * (1.0 / 0.07))
    hvv = hv * v
    hww = hw * w
    fast = hvv * ((u - 0.3) * (0.5 * dt / 0.11 * 1.55 - (0.5 * dt / 0.11) * u))
    out = (u * nw) * r_o + hw * r_so
    slow = hww * (s * (0.5 * dt / 1.8875))
    v_new = v + (nv * (no - v)) * r_vm - hvv * (0.5 * dt / 1.4506)
    w_new = w + (nw * (w_inf - w)) * r_wm - hww * (0.5 * dt / 200.0)
    s_new = s + ((0.5 + 0.5 * t_s) - s) * r_s
    return fast + slow - out, v_new, w_new, s_new


FAR_HALF, NEAR_HALF = -1, 1


def half_place(info_ref, half):
    flip = info_ref[FLIP]
    return (flip, flip) if half == FAR_HALF else (1 - flip, 1 - flip)


def half_kernel(kind, half, tiles, per_block, info_ref, *refs):
    side = info_ref[SIDE]
    sub = row_iota()
    own = tiles - 1
    index, outer = half_place(info_ref, half)
    if kind == "first":
        whole_ref, coeff_ref, outer_out, inner_out, gate_out = refs
        spots = [2 * index + outer, 2 * index + 1 - outer, 2 - index]
        reads = [lambda t, z=z: whole_ref[0, z, t] for z in spots]
    elif kind == "middle":
        *u_refs, gate_ref, coeff_ref, outer_out, inner_out, gate_out = refs
        reads = [lambda t, ref=ref: ref[t] for ref in u_refs]
    else:
        *u_refs, gate_ref, coeff_ref = refs[:5]
        out_ref = refs[-1]
        reads = [lambda t, ref=ref: ref[t] for ref in u_refs]
        place = [outer, 1 - outer]

    def one(local_tile, carry):
        tile = local_tile if kind != "last" else pl.program_id(0) * per_block + local_tile
        before, after = ring_neighbours(tile, tiles)
        mask_before, mask_after = edge_masks(tile, side, own)
        cur = [read(tile) for read in reads]
        prv = [read(before) * mask_before for read in reads]
        nxt = [read(after) * mask_after for read in reads]

        def coeff(index):
            return coeff_ref[index, local_tile]

        for plane in range(2):
            u = cur[plane]
            if plane == 0:
                around = cur[1]
                wide, wide_nxt, wide_prv = cur[1], nxt[1], prv[1]
            else:
                around = cur[0] + cur[2]
                wide, wide_nxt, wide_prv = cur[2] - cur[0], nxt[2] - nxt[0], prv[2] - prv[0]
            u_next = next_row(u, nxt[plane], sub)
            u_prev = prev_row(u, prv[plane], sub)
            tilt = coeff(C_ZY) * (next_row(wide, wide_nxt, sub) - prev_row(wide, wide_prv, sub))
            tall = u_next - u_prev
            to_left = coeff(C_XXR) * u + coeff(C_YXR) * tall
            to_right = coeff(C_XXL) * u - coeff(C_YXL) * tall
            if half == FAR_HALF:
                to_left += coeff(C_ZXR) * wide
                to_right -= coeff(C_ZXL) * wide
            else:
                to_left -= coeff(C_ZXR) * wide
                to_right += coeff(C_ZXL) * wide
            base = coeff(C_MID) * u + coeff(C_ZZ) * around + coeff(C_YY) * (u_next + u_prev)
            base = base + tilt if half == FAR_HALF else base - tilt
            base += left(to_left) + right(to_right)
            chunk = 256
            for start in range(0, 1024, chunk):
                lanes = slice(start, start + chunk)
                if kind == "first":
                    gates = [whole_ref[1 + g, spots[plane], tile, :, lanes] for g in range(3)]
                else:
                    gates = [gate_ref[g, plane, local_tile, :, lanes] for g in range(3)]
                u_add, *gates = ionic(u[:, lanes], *gates)
                u_new = base[:, lanes] + u_add
                if kind == "last":
                    for comp, value in enumerate([u_new] + gates):
                        out_ref[comp, place[plane], local_tile, :, lanes] = value
                else:
                    (outer_out, inner_out)[plane][tile, :, lanes] = u_new
                    for comp, value in enumerate(gates):
                        gate_out[comp, plane, tile, :, lanes] = value
        return carry

    lax.fori_loop(0, per_block, one, 0)


def half_costs(tiles, width):
    cells = 2 * tiles * 8 * width
    return cost(100 * cells, 40 * cells, 11 * cells)


def half_step(kind, half, info, arrays, coeffs):
    _, tiles, _, width = coeffs.shape
    vmem = pl.BlockSpec(memory_space=pltpu.VMEM)
    plane = jax.ShapeDtypeStruct((tiles, 8, width), jnp.float32)
    return pl.pallas_call(
        functools.partial(half_kernel, kind, half, tiles, tiles),
        in_specs=[pl.BlockSpec(memory_space=pltpu.SMEM)] + [vmem] * (len(arrays) + 1),
        out_specs=[vmem] * 3,
        out_shape=[plane, plane, jax.ShapeDtypeStruct((3, 2, tiles, 8, width), jnp.float32)],
        compiler_params=params(),
        cost_estimate=half_costs(tiles, width),
        name=kind + ("_far" if half == FAR_HALF else "_near"),
    )(info, *arrays, coeffs)


def half_last(half, info, arrays, coeffs, states=None):
    _, tiles, _, width = coeffs.shape
    per_block = 2
    whole = pl.BlockSpec((tiles, 8, width), lambda i, info: (0, 0, 0))
    in_specs = [whole] * 3 + [
        pl.BlockSpec((3, 2, per_block, 8, width), lambda i, info: (0, 0, i, 0, 0)),
        pl.BlockSpec((10, per_block, 8, width), lambda i, info: (0, i, 0, 0)),
    ]
    operands = [*arrays, coeffs]
    aliases = {}
    if states is not None:
        in_specs.append(pl.BlockSpec(memory_space=pl.ANY))
        operands.append(states)
        aliases = {len(operands): 0}
    return pl.pallas_call(
        functools.partial(half_kernel, "last", half, tiles, per_block),
        grid_spec=pltpu.PrefetchScalarGridSpec(
            num_scalar_prefetch=1,
            grid=((tiles - 1) // per_block,),
            in_specs=in_specs,
            out_specs=pl.BlockSpec((4, 2, per_block, 8, width), lambda i, info: (0, half_place(info, half)[0], i, 0, 0)),
        ),
        out_shape=jax.ShapeDtypeStruct((4, 4, tiles - 1, 8, width), jnp.float32),
        input_output_aliases=aliases,
        compiler_params=params(),
        cost_estimate=half_costs(tiles, width),
        name="last" + ("_far" if half == FAR_HALF else "_near"),
    )(info, *operands)


def halo_terms(halo_ref, coeff_ref, tile, tiles, side, sub, half):
    before, after = ring_neighbours(tile, tiles)
    mask_before, mask_after = edge_masks(tile, side, tiles - 1)
    cur = halo_ref[tile]
    up = next_row(cur, halo_ref[after] * mask_after, sub)
    down = prev_row(cur, halo_ref[before] * mask_before, sub)
    cross = coeff_ref[C_ZY, tile] * (up - down)
    cross += left(coeff_ref[C_ZXR, tile] * cur) - right(coeff_ref[C_ZXL, tile] * cur)
    total = coeff_ref[C_ZZ, tile] * cur
    return total - cross if half == FAR_HALF else total + cross


def halo_kernel(half, tiles, info_ref, outer_ref, halo_ref, coeff_ref, out_ref):
    side = info_ref[SIDE]
    sub = row_iota()

    def one(tile, carry):
        out_ref[tile] = outer_ref[tile] + halo_terms(halo_ref, coeff_ref, tile, tiles, side, sub, half)
        return carry

    def kept(tile, carry):
        out_ref[tile] = outer_ref[tile]
        return carry

    if half == NEAR_HALF:
        lax.fori_loop(0, tiles, one, 0)
    else:
        exists = info_ref[FAR] == 1

        @pl.when(exists)
        def _():
            lax.fori_loop(0, tiles, one, 0)

        @pl.when(jnp.logical_not(exists))
        def _():
            lax.fori_loop(0, tiles, kept, 0)


def halo_step(half, info, outer, halo, coeffs):
    tiles, _, width = outer.shape
    vmem = pl.BlockSpec(memory_space=pltpu.VMEM)
    cells = tiles * 8 * width
    return pl.pallas_call(
        functools.partial(halo_kernel, half, tiles),
        in_specs=[pl.BlockSpec(memory_space=pltpu.SMEM)] + [vmem] * 3,
        out_specs=vmem,
        out_shape=jax.ShapeDtypeStruct(outer.shape, jnp.float32),
        compiler_params=params(),
        cost_estimate=cost(15 * cells, 20 * cells),
        name="halo" + ("_far" if half == FAR_HALF else "_near"),
    )(info, outer, halo, coeffs)


def pair_matrix(width, scale):
    fine = lax.broadcasted_iota(jnp.int32, (width, width // 2), 0)
    coarse = lax.broadcasted_iota(jnp.int32, (width, width // 2), 1)
    return jnp.where((fine >> 1) == coarse, scale, 0.0)


def row_pairs(count, scale):
    coarse = lax.broadcasted_iota(jnp.int32, (count // 2, count), 0)
    fine = lax.broadcasted_iota(jnp.int32, (count // 2, count), 1)
    return jnp.where((fine >> 1) == coarse, scale, 0.0)


def dot(a, b):
    return jnp.dot(a, b, precision=HIGHEST, preferred_element_type=jnp.float32)


def pooled(field):
    rows, lanes = field.shape
    few = dot(row_pairs(rows, 0.5), field)
    pick = pair_matrix(256, 0.5)
    return jnp.concatenate([dot(few[:, at : at + 256], pick) for at in range(0, lanes, 256)], axis=1)


def finish_kernel(half, tiles, info_ref, part_ref, halo_ref, coeff_ref, tension_ref, *refs):
    if half == FAR_HALF:
        out_ref, tension_out, active_out = refs
    else:
        active_ref, _, out_ref, tension_out, active_out, facing_out = refs
    side = info_ref[SIDE]
    sub = row_iota()
    own = tiles - 1
    _, outer = half_place(info_ref, half)
    out_ref[0, 1 - outer] = part_ref[0, 1 - outer]

    def one(tile, carry):
        out_ref[0, outer, tile] = part_ref[0, outer, tile] + halo_terms(halo_ref, coeff_ref, tile, tiles, side, sub, half)
        return carry

    if half == NEAR_HALF:
        lax.fori_loop(0, own, one, 0)
    else:
        exists = info_ref[FAR] == 1

        @pl.when(exists)
        def _():
            lax.fori_loop(0, own, one, 0)

        @pl.when(jnp.logical_not(exists))
        def _():
            out_ref[0, outer] = part_ref[0, outer]

    both = 0.5 * (out_ref[0, 0] + out_ref[0, 1])
    mean = pooled(both.reshape(own * 8, both.shape[-1]))
    old = tension_ref[0]
    new = old + 0.5 * (mean - old)
    tension_out[0] = new
    if half == FAR_HALF:
        active_out[...] = pooled(0.5 * new)
    else:
        active_out[...] = active_ref[...] + pooled(0.5 * new)
        facing_out[...] = active_out[pl.ds(pl.multiple_of(8 * (1 - side), 8), 8), :]


def finish_half(half, info, part, halo, coeffs, tension, active=None, tension_next=None):
    tiles, _, width = halo.shape
    own = tiles - 1
    active_shape = (own * 2, width // 4)
    z_half = lambda info: half_place(info, half)[0]
    u_spec = pl.BlockSpec((1, 2, own, 8, width), lambda i, info: (0, z_half(info), 0, 0, 0))
    tension_spec = pl.BlockSpec((1,) + tension.shape[1:], lambda i, info: (z_half(info), 0, 0))
    active_spec = pl.BlockSpec(active_shape, lambda i, info: (0, 0))
    in_specs = [
        u_spec,
        pl.BlockSpec((tiles, 8, width), lambda i, info: (0, 0, 0)),
        pl.BlockSpec((4, tiles, 8, width), lambda i, info: (0, 0, 0, 0)),
        tension_spec,
    ]
    operands = [part, halo, coeffs, tension]
    out_specs = [u_spec, tension_spec, active_spec]
    out_shape = [
        jax.ShapeDtypeStruct(part.shape, jnp.float32),
        jax.ShapeDtypeStruct(tension.shape, jnp.float32),
        jax.ShapeDtypeStruct(active_shape, jnp.float32),
    ]
    aliases = {1: 0}
    if half == NEAR_HALF:
        in_specs += [active_spec, pl.BlockSpec(memory_space=pl.ANY)]
        operands += [active, tension_next]
        aliases[len(operands)] = 1
        out_specs.append(pl.BlockSpec((8, width // 4), lambda i, info: (0, 0)))
        out_shape.append(jax.ShapeDtypeStruct((8, width // 4), jnp.float32))
    cells = 2 * own * 8 * width
    return pl.pallas_call(
        functools.partial(finish_kernel, half, tiles),
        grid_spec=pltpu.PrefetchScalarGridSpec(num_scalar_prefetch=1, grid=(1,), in_specs=in_specs, out_specs=out_specs),
        out_shape=out_shape,
        input_output_aliases=aliases,
        compiler_params=params(),
        cost_estimate=cost(20 * cells, 20 * cells),
        name="finish" + ("_far" if half == FAR_HALF else "_near"),
    )(info, *operands)


REACH = 4
ROWS = 24


class Weights:
    def __init__(self, side, own, width):
        row = lax.broadcasted_iota(jnp.int32, (ROWS, width), 0)
        lane = lax.broadcasted_iota(jnp.int32, (ROWS, width), 1)
        self.next_y = jnp.where((row == own - 1) & (side == 1), 0.0, 1.0)
        self.prev_y = jnp.where((row == 0) & (side == 0), 0.0, 1.0)
        self.next_x = jnp.where(lane == width - 1, 0.0, 1.0)
        self.prev_x = jnp.where(lane == 0, 0.0, 1.0)


def up_y(val):
    return pltpu.roll(val, ROWS - 1, 0)


def down_y(val):
    return pltpu.roll(val, 1, 0)


def slope_z(below, mid, above):
    return 0.5 * (above - below)


def smooth_z(below, mid, above):
    return 0.75 * mid + 0.125 * (above + below)


def gradients(below, mid, above, k):
    slope = slope_z(below, mid, above)
    smooth = smooth_z(below, mid, above)
    slope_s = 0.75 * slope + 0.125 * (up_y(slope) * k.next_y + down_y(slope) * k.prev_y)
    ahead = up_y(smooth) * k.next_y
    behind = down_y(smooth) * k.prev_y
    smooth_s = 0.75 * smooth + 0.125 * (ahead + behind)
    smooth_d = 0.5 * (ahead - behind)

    def smooth_x(val):
        return 0.75 * val + 0.125 * (left(val) * k.next_x + right(val) * k.prev_x)

    return (
        smooth_x(slope_s),
        smooth_x(smooth_d),
        0.5 * (left(smooth_s) * k.next_x - right(smooth_s) * k.prev_x),
    )


def force(below, mid, above, k):
    p_z = slope_z(below[0], mid[0], above[0])
    p_y = smooth_z(below[1], mid[1], above[1])
    p_x = smooth_z(below[2], mid[2], above[2])
    small, half = 0.125 * p_z, 0.5 * p_y
    both = 0.75 * p_z + up_y(small + half) * k.next_y + down_y(small - half) * k.prev_y
    p_x = 0.75 * p_x + 0.125 * (up_y(p_x) * k.next_y + down_y(p_x) * k.prev_y)
    small, half = 0.125 * both, 0.5 * p_x
    return 0.75 * both + left(small + half) * k.next_x + right(small - half) * k.prev_x


def deformation(below, mid, above, k):
    deform = []
    for comp in range(3):
        row = list(gradients(below[comp], mid[comp], above[comp], k))
        row[comp] = row[comp] + 1.0
        deform.append(row)
    return deform


def passive_stress(deform):
    right_c = {}
    for a_pos, b_pos in PAIRS:
        right_c[a_pos, b_pos] = sum(deform[i_pos][a_pos] * deform[i_pos][b_pos] for i_pos in range(3))
    strain = {}
    for a_pos, b_pos in PAIRS:
        strain[a_pos, b_pos] = 0.5 * (right_c[a_pos, b_pos] - (1.0 if a_pos == b_pos else 0.0))
    trace = strain[0, 0] + strain[1, 1] + strain[2, 2]
    second = {}
    for a_pos, b_pos in PAIRS:
        entry = (2.0 * SHEAR) * strain[a_pos, b_pos]
        if a_pos == b_pos:
            entry = entry + LAME_FIRST * trace
        second[a_pos, b_pos] = entry
        second[b_pos, a_pos] = entry
    return second


def times(deform, second):
    return [
        [sum(deform[i_pos][b_pos] * second[b_pos, a_pos] for b_pos in range(3)) for a_pos in range(3)]
        for i_pos in range(3)
    ]


def metric(deform, fdir):
    def cofactor(i_pos, j_pos):
        i_next, i_last = (i_pos + 1) % 3, (i_pos + 2) % 3
        j_next, j_last = (j_pos + 1) % 3, (j_pos + 2) % 3
        return deform[i_next][j_next] * deform[i_last][j_last] - deform[i_next][j_last] * deform[i_last][j_next]

    cof = [[cofactor(i_pos, j_pos) for j_pos in range(3)] for i_pos in range(3)]
    det = deform[0][0] * cof[0][0] + deform[0][1] * cof[0][1] + deform[0][2] * cof[0][2]
    scale = 1.0 / det
    inv = [[cof[i_pos][j_pos] * scale for i_pos in range(3)] for j_pos in range(3)]
    along = [sum(inv[a_pos][i_pos] * fdir[i_pos] for i_pos in range(3)) for a_pos in range(3)]
    comps = []
    for a_pos, b_pos in PAIRS:
        inner = sum(inv[a_pos][i_pos] * inv[b_pos][i_pos] for i_pos in range(3))
        comps.append(SIGMA_TRANS * inner + (SIGMA_LONG - SIGMA_TRANS) * along[a_pos] * along[b_pos])
    return comps


def inside(slab, slabs, offset):
    spot = slab + offset
    return jnp.where((spot >= 0) & (spot < slabs), 1.0, 0.0)


class Planes:
    def __init__(self, field, slabs, reach):
        self.slabs, self.reach = slabs, reach
        self.parts = [field[None]]
        self.doubling = slabs in (1, 2, 4, 8)
        self.step = 1

    def round(self):
        if self.doubling:
            if self.step < self.slabs:
                held = jnp.concatenate(self.parts, axis=0) if len(self.parts) > 1 else self.parts[0]
                perm = [(i, i ^ self.step) for i in range(self.slabs)]
                self.parts.append(lax.ppermute(held, "slab", perm))
                self.step *= 2
        elif self.step == 1:
            for shift in self.shifts()[1:]:
                perm = [((i + shift) % self.slabs, i) for i in range(self.slabs)]
                self.parts.append(lax.ppermute(self.parts[0], "slab", perm))
            self.step = 0

    def shifts(self):
        return sorted({offset % self.slabs for offset in range(-self.reach, self.reach + 1)})

    def spot(self, slab, offset):
        if self.doubling:
            return slab ^ jnp.clip(slab + offset, 0, self.slabs - 1)
        return self.shifts().index(offset % self.slabs)


def fiber_table():
    index = jnp.arange(128, dtype=jnp.float32)
    theta = -1.0 + 2.0 * index / (NFIB - 1)
    tilt = 0.3 * jnp.sin(3.0 * index)
    return jnp.stack([jnp.sin(tilt), jnp.cos(tilt) * jnp.sin(theta), jnp.cos(tilt) * jnp.cos(theta)])


def facing_kernel(info_ref, *refs):
    out_ref = refs[-1]
    first = pl.multiple_of(8 * (1 - info_ref[SIDE]), 8)
    at = 0
    for ref in refs[:-1]:
        for pos in range(ref.shape[0]):
            for comp in range(ref.shape[1]):
                out_ref[at, comp] = ref[pos, comp, pl.ds(first, 8), :]
            at += 1


def facing_rows(info, fields):
    _, comps, _, width = fields[0].shape
    count = sum(field.shape[0] for field in fields)
    vmem = pl.BlockSpec(memory_space=pltpu.VMEM)
    return pl.pallas_call(
        facing_kernel,
        in_specs=[pl.BlockSpec(memory_space=pltpu.SMEM)] + [vmem] * len(fields),
        out_shape=jax.ShapeDtypeStruct((count, comps, 8, width), jnp.float32),
        compiler_params=params(),
        cost_estimate=cost(0, 600_000),
        name="facing",
    )(info, *fields)


def passive_kernel(planes, info_ref, table_ref, strip_ref, *refs):
    own_refs, (disp_out, stress_out, pull_out, disp_all, field) = refs[:-5], refs[-5:]
    slab, slabs = info_ref[SLAB], planes.slabs
    own, width = own_refs[0].shape[-2:]
    k = Weights(info_ref[SIDE], own, width)
    reach = REACH + 1

    at = 0
    for ref in own_refs:
        for pos in range(ref.shape[0]):
            for comp in range(ref.shape[1]):
                field[at, comp, :own] = ref[pos, comp]
                field[at, comp, own:] = strip_ref[at, comp]
            at += 1

    def plane(comp, offset):
        return field[planes.spot(slab, offset), comp]

    for offset in range(-reach, reach + 1):
        factor = inside(slab, slabs, offset)
        for comp in range(3):
            disp_all[comp, offset + reach] = plane(comp, offset) * factor

    tables = [jnp.broadcast_to(table_ref[comp : comp + 1], (8, 128)) for comp in range(3)]

    def direction(index, comp):
        index = index.astype(jnp.int32)
        rows = []
        for top in range(0, ROWS, 8):
            parts = [
                jnp.take_along_axis(tables[comp], index[top : top + 8, at : at + 128], axis=1, mode="promise_in_bounds")
                for at in range(0, width, 128)
            ]
            rows.append(jnp.concatenate(parts, axis=1))
        return jnp.concatenate(rows, axis=0)

    for step in range(2 * REACH + 1):
        offset = step - REACH
        below, mid, above = ([disp_all[comp, step + shift] for comp in range(3)] for shift in range(3))
        factor = inside(slab, slabs, offset)
        deform = deformation(below, mid, above, k)
        stress = times(deform, passive_stress(deform))
        index = plane(3, offset)
        fdir = [direction(index, comp) for comp in range(3)]
        for i_pos in range(3):
            pull = (ACTIVE_GAIN * factor) * sum(deform[i_pos][b_pos] * fdir[b_pos] for b_pos in range(3))
            for a_pos in range(3):
                stress_out[3 * i_pos + a_pos, step] = stress[i_pos][a_pos] * factor
                pull_out[3 * i_pos + a_pos, step] = pull * fdir[a_pos]
            disp_out[i_pos, step] = mid[i_pos]
            disp_out[3 + i_pos, step] = fdir[i_pos]


def passive_step(info, planes, strips):
    width = strips.shape[-1]
    count = 2 * REACH + 1
    shapes = [(6, count), (9, count), (9, count)]
    vmem = pl.BlockSpec(memory_space=pltpu.VMEM)
    return pl.pallas_call(
        functools.partial(passive_kernel, planes),
        in_specs=[pl.BlockSpec(memory_space=pltpu.SMEM)] + [vmem] * (2 + len(planes.parts)),
        out_shape=[jax.ShapeDtypeStruct((a, b, ROWS, width), jnp.float32) for a, b in shapes],
        scratch_shapes=[
            pltpu.VMEM((3, count + 2, ROWS, width), jnp.float32),
            pltpu.VMEM(strips.shape[:2] + (ROWS, width), jnp.float32),
        ],
        compiler_params=params(),
        cost_estimate=cost(400 * count * ROWS * width, 5_000_000),
        name="passive",
    )(info, fiber_table(), strips, *planes.parts)


def mechanics_kernel(planes, info_ref, disp_ref, stress_ref, pull_ref, *rest):
    active_refs, (disp_out, cond_out, d_one, p_two, active) = rest[:-5], rest[-5:]
    slab, side, slabs = info_ref[SLAB], info_ref[SIDE], planes.slabs
    own, width = disp_out.shape[-2:]
    k = Weights(side, own, width)

    at = 0
    for ref in active_refs:
        active[at : at + ref.shape[0]] = ref[...]
        at += ref.shape[0]

    def active_at(step):
        return active[planes.spot(slab, step - REACH)]

    for step in range(1, 2 * REACH):
        act = [active_at(step + shift) for shift in (-1, 0, 1)]
        factor = inside(slab, slabs, step - REACH)
        for i_pos in range(3):
            stress = [
                [stress_ref[3 * i_pos + a_pos, step + shift] + act[shift + 1] * pull_ref[3 * i_pos + a_pos, step + shift] for a_pos in range(3)]
                for shift in (-1, 0, 1)
            ]
            moved = disp_ref[i_pos, step] + MECH_RATE * force(stress[0], stress[1], stress[2], k)
            d_one[i_pos, step] = moved * factor

    for step in range(2, 2 * REACH - 1):
        disp = [[d_one[comp, step + shift] for comp in range(3)] for shift in (-1, 0, 1)]
        deform = deformation(disp[0], disp[1], disp[2], k)
        second = passive_stress(deform)
        fdir = [disp_ref[3 + comp, step] for comp in range(3)]
        gain = ACTIVE_GAIN * active_at(step)
        for a_pos, b_pos in PAIRS:
            entry = second[a_pos, b_pos] + gain * fdir[a_pos] * fdir[b_pos]
            second[a_pos, b_pos] = entry
            second[b_pos, a_pos] = entry
        stress = times(deform, second)
        factor = inside(slab, slabs, step - REACH)
        for i_pos in range(3):
            for a_pos in range(3):
                p_two[3 * i_pos + a_pos, step] = stress[i_pos][a_pos] * factor

    last = []
    for step in (REACH - 1, REACH, REACH + 1):
        factor = inside(slab, slabs, step - REACH)
        row = []
        for i_pos in range(3):
            stress = [[p_two[3 * i_pos + a_pos, step + shift] for a_pos in range(3)] for shift in (-1, 0, 1)]
            moved = d_one[i_pos, step] + MECH_RATE * force(stress[0], stress[1], stress[2], k)
            row.append(moved * factor)
        last.append(row)
    deform = deformation(last[0], last[1], last[2], k)
    comps = metric(deform, [disp_ref[3 + comp, REACH] for comp in range(3)])
    for i_pos in range(3):
        disp_out[i_pos, 0] = last[1][i_pos][:own]
    for pos, comp in enumerate(comps):
        cond_out[pos, 0] = comp[:own]


def mechanics_step(info, own, planes, window):
    width = planes.parts[0].shape[-1]
    count = 2 * REACH + 1
    held = sum(part.shape[0] for part in planes.parts)
    vmem = pl.BlockSpec(memory_space=pltpu.VMEM)
    return pl.pallas_call(
        functools.partial(mechanics_kernel, planes),
        in_specs=[pl.BlockSpec(memory_space=pltpu.SMEM)] + [vmem] * (3 + len(planes.parts)),
        out_shape=[
            jax.ShapeDtypeStruct((3, 1, own, width), jnp.float32),
            jax.ShapeDtypeStruct((6, 1, own, width), jnp.float32),
        ],
        scratch_shapes=[
            pltpu.VMEM((3, count, ROWS, width), jnp.float32),
            pltpu.VMEM((9, count, ROWS, width), jnp.float32),
            pltpu.VMEM((held, ROWS, width), jnp.float32),
        ],
        compiler_params=params(),
        cost_estimate=cost(400 * count * ROWS * width, 5_000_000),
        name="mechanics",
    )(info, *window, *planes.parts)


def tie(*arrays):
    return lax.optimization_barrier(arrays)


def on_device(states, cond, tension, fiber, disp):
    slabs = lax.axis_size("slab")
    slab, col = lax.axis_index("slab"), lax.axis_index("col")
    _, planes, rows, width = states.shape
    own = rows // 8
    flip = slab % 2
    far_exists = (slab > 0) & (slab < slabs - 1)
    info = jnp.stack([slab, col, flip, far_exists]).astype(jnp.int32)

    pairs = [(i, i ^ 1) for i in range(slabs)]
    others = [(i, i if i in (0, slabs - 1) else ((i + 1) ^ 1) - 1) for i in range(slabs)]
    cross_pairs = [(2 * i + c, 2 * j + 1 - c) for i, j in pairs for c in range(2)]
    cross_others = [(2 * i + c, 2 * j + 1 - c) for i, j in others for c in range(2)]
    swap = [(0, 1), (1, 0)]

    tiled = states.reshape(4, planes, own, 8, width)
    far, near, facing, far_rows, near_rows, cond_rows = pack(info, tiled, cond)
    far_halo = lax.ppermute(far, "slab", others)
    near_halo = lax.ppermute(near, "slab", pairs)
    strip = lax.ppermute(facing, "col", swap)
    cond_strip = lax.ppermute(cond_rows, "col", swap)
    far_strip = lax.ppermute(far_rows, ("slab", "col"), cross_others)
    near_strip = lax.ppermute(near_rows, ("slab", "col"), cross_pairs)
    fields = Planes(jnp.concatenate([disp[:, 0], fiber.astype(jnp.float32)], axis=0), slabs, REACH + 1)

    coeffs = fine_coeffs(info, cond, cond_strip)
    whole = jnp.concatenate([tiled, strip[:, :, None]], axis=2)
    far_halo = jnp.concatenate([far_halo, far_strip[None]], axis=0)
    near_halo = jnp.concatenate([near_halo, near_strip[None]], axis=0)
    fields.round()

    far_part, far_inner, far_gates = half_step("first", FAR_HALF, info, (whole,), coeffs)
    near_part, near_inner, near_gates = half_step("first", NEAR_HALF, info, (whole,), coeffs)
    for turn_index in range(1, SUB):
        last = turn_index == SUB - 1
        far = halo_step(FAR_HALF, info, far_part, far_halo, coeffs)
        far_halo = lax.ppermute(far, "slab", others)
        if not last:
            (near_part, *fields.parts) = tie(near_part, *fields.parts)
            fields.round()
        far_arrays = (far, far_inner, near_inner, far_gates)
        if last:
            part = half_last(FAR_HALF, info, far_arrays, coeffs)
        else:
            far_part, far_next, far_gates = half_step("middle", FAR_HALF, info, far_arrays, coeffs)
        near = halo_step(NEAR_HALF, info, near_part, near_halo, coeffs)
        near_halo = lax.ppermute(near, "slab", pairs)
        near_arrays = (near, near_inner, far_inner, near_gates)
        if last:
            part = half_last(NEAR_HALF, info, near_arrays, coeffs, part)
        else:
            near_part, near_inner, near_gates = half_step("middle", NEAR_HALF, info, near_arrays, coeffs)
            far_inner = far_next
    strips = lax.ppermute(facing_rows(info, fields.parts), "col", swap)
    part, tension_next, active = finish_half(FAR_HALF, info, part, far_halo, coeffs, tension)
    window = passive_step(info, fields, strips)
    states_next, tension_next, active, facing = finish_half(
        NEAR_HALF, info, part, near_halo, coeffs, tension, active, tension_next
    )
    active_strip = lax.ppermute(facing, "col", swap)
    actives = Planes(jnp.concatenate([active, active_strip], axis=0), slabs, REACH)
    for _ in range(3):
        actives.round()
    disp_next, cond_next = mechanics_step(info, disp.shape[2], actives, window)
    return (states_next.reshape(states.shape), tension_next, disp_next, cond_next)


def solution(mesh):
    in_specs = (
        P(None, ("grp", "slab"), "col", None),
        P(None, ("grp", "slab"), "col", None),
        P(("grp", "slab"), "col", None),
        P(("grp", "slab"), "col", None),
        P(None, ("grp", "slab"), "col", None),
    )
    out_specs = (
        P(None, ("grp", "slab"), "col", None),
        P(("grp", "slab"), "col", None),
        P(None, ("grp", "slab"), "col", None),
        P(None, ("grp", "slab"), "col", None),
    )
    return jax.shard_map(
        on_device, mesh=mesh, in_specs=in_specs, out_specs=out_specs, check_vma=False
    )
```

time: 139 us -> 99.7 us (0.72)
  waiting for transfers between devices: 37.5 us -> 11.8 us
  starting transfers between devices: 49.5 us -> 33.7 us
  Pallas kernels: 46.5 us -> 49.1 us
  other arithmetic: 3.05 us -> 0.77 us
  local copies, waits for them, and re-layouts: 1.37 us -> 3.1 us
    ppermute x26 -> x18, waiting for transfers between devices: 36.6 us -> 10.6 us  [the longest x4 6.32 us: on_device(): near_halo = lax.ppermute(near, 'slab', pairs)]
    ppermute x26 -> x18, starting transfers between devices: 49 us -> 33.2 us  [the longest x6 15.8 us: round(): self.parts.append(lax.ppermute(held, 'slab', perm))]
    unnamed x11 -> x12, local copies, waits for them, and re-layouts: 0.03 us -> 3.1 us
    pallas_call x10 -> x19, Pallas kernels: 43 us -> 45.6 us  [the longest x6 17.1 us: half_step(): pl.pallas_call(functools.partial(half_kernel, kind, half, tiles, tiles),...]
    select_n x3 -> x0, other arithmetic: 2.14 us -> none  [the longest x1 1.26 us: on_device(): facing = jnp.where(col == 0, tiled[:, :, own - 1], tiled[:, :, 0])]
  transfers between devices with their start and end apart: 28 -> 20, of which waited for: 9 -> 5; matrix products, arithmetic and copies ran while one was open for 2% -> 1% of each run, Pallas kernels for 22% -> 44%
where the time goes in v3:
time: 99.7 us; the launch traced here: 99.4 us
  Pallas kernels  49.1 us (49%)
  starting transfers between devices  33.7 us (34%)
  waiting for transfers between devices  11.8 us (12%)
  local copies, waits for them, and re-layouts  3.1 us (3%)
    pallas_call x6, Pallas kernels, half_step(): pl.pallas_call(functools.partial(half_kernel, kind, half, tiles, tiles),...  17.1 us
    ppermute x6, starting transfers between devices, round(): self.parts.append(lax.ppermute(held, 'slab', perm))  15.8 us
    ppermute x4, starting transfers between devices, on_device(): near_halo = lax.ppermute(near, 'slab', pairs)  10.6 us
    pallas_call x2, Pallas kernels, half_last(): pl.pallas_call(functools.partial(half_kernel, 'last', half, tiles, per_bl...  8.06 us
    pallas_call x2, Pallas kernels, finish_half(): pl.pallas_call(functools.partial(finish_kernel, half, tiles), grid_spec=p...  6.63 us
    ppermute x4, waiting for transfers between devices, on_device(): near_halo = lax.ppermute(near, 'slab', pairs)  6.32 us
    pallas_call x6, Pallas kernels, halo_step(): pl.pallas_call(functools.partial(halo_kernel, half, tiles), in_specs=[pl....  5.89 us
    pallas_call x1, Pallas kernels, mechanics_step(): pl.pallas_call(functools.partial(mechanics_kernel, planes), in_specs=[pl....  4.12 us
  transfers between devices with their start and end apart: 20, of which 5 were waited for; matrix products, arithmetic and copies ran while one was open for 1% of the time, Pallas kernels for 44%

profile of v3, /device:TPU:0, one launch (start us, length us, event | category | flops | bytes accessed | tf_op | source)
XLA Modules:
  0.0 99.4 jit_solution(10183176451629956100)
XLA Ops:
  0.7 2.2 %copy-done = f32[4,4,64,1024]{3,2,1,0:T(8,128)S(1)} copy-done((f32[4,4,64,1024]{3,2,1,0:T(8,128)S(1)}, f32[4,4,64,1024]{3,2,1,0:T(8,128)}, u32[]{:S(2)}) %copy-start) | copy-done | bytes 4194328
  6.4 6.5 %collective-permute-start.2 = (f32[1,4,16,256]{3,2,1,0:T(8,128)S(1)}, f32[1,4,16,256]{3,2,1,0:T(8,128)S(1)}, u32[]{:S(2)}, u32[]{:S(2)}) collective-permute-start(f32[1,4,16,256]{3,2,1,0:T(8,128)S(1)} %maximum_bitcast_fusion.refs_0_), channel_id=1, source_target_pairs={{0,2},{2,0},{4,6},{6,4},{8,10},{10,8},{12,14},{14,12},{1,3},{3,1},... | collective-permute-start | bytes 196616 | tf_op jit(solution)/shard_map/ppermute | solution.py:613
  13.0 3.0 %coeffs.1.refs_1_.coeff_ref.refs_4_ = f32[10,9,8,1024]{3,2,1,0:T(8,128)S(1)} custom-call(s32[4]{0:T(128)S(1)} %pad_add_fusion.info_ref, f32[6,1,16,256]{3,2,1,0:T(8,128)S(1)} %copy-done.3, f32[6,8,256]{2,1,0:T(8,128)S(1)} %collective-permute-done.1.strip_ref), custom_call_target="tpu_custom_call" | custom-call | flops 2000000 | bytes 3200000 | tf_op jit(solution)/shard_map/coeffs/pallas_call | solution.py:116
  15.9 3.4 %collective-permute-start.4 = (f32[8,1024]{1,0:T(8,128)S(1)}, f32[8,1024]{1,0:T(8,128)S(1)}, u32[]{:S(2)}, u32[]{:S(2)}) collective-permute-start(f32[8,1024]{1,0:T(8,128)S(1)} %get-tuple-element.52), channel_id=1, source_target_pairs={{0,3},{1,2},{2,1},{3,0},{4,7},{5,6},{6,5},{7,4},{8,11},{9,10},{10,... | collective-permute-start | bytes 98312 | tf_op jit(solution)/shard_map/ppermute | solution.py:841
  19.8 2.9 %first_far.1 = (f32[9,8,1024]{2,1,0:T(8,128)S(1)}, f32[9,8,1024]{2,1,0:T(8,128)S(1)}, f32[3,2,9,8,1024]{4,3,2,1,0:T(8,128)S(1)}) custom-call(s32[4]{0:T(128)S(1)} %pad_add_fusion.info_ref, f32[4,4,9,8,1024]{4,3,2,1,0:T(8,128)S(1)} %pad_maximum_fusion.refs_0_, f32[10,9,8,1024]{3,2,1,0:T(8,128)S(1)} %coeffs.1.refs_1_.coeff_ref.refs_4_), custom_call_target="tpu_custom_call" | custom-call | flops 14745600 | bytes 5898240 | tf_op jit(solution)/shard_map/first_far/pallas_call | solution.py:287
  25.1 2.9 %first_near.1 = (f32[9,8,1024]{2,1,0:T(8,128)S(1)}, f32[9,8,1024]{2,1,0:T(8,128)S(1)}, f32[3,2,9,8,1024]{4,3,2,1,0:T(8,128)S(1)}) custom-call(s32[4]{0:T(128)S(1)} %pad_add_fusion.info_ref, f32[4,4,9,8,1024]{4,3,2,1,0:T(8,128)S(1)} %pad_maximum_fusion.refs_0_, f32[10,9,8,1024]{3,2,1,0:T(8,128)S(1)} %coeffs.1.refs_1_.coeff_ref.refs_4_), custom_call_target="tpu_custom_call" | custom-call | flops 14745600 | bytes 5898240 | tf_op jit(solution)/shard_map/first_near/pallas_call | solution.py:287
  29.3 4.0 %collective-permute-start.6 = (f32[9,8,1024]{2,1,0:T(8,128)S(1)}, f32[9,8,1024]{2,1,0:T(8,128)S(1)}, u32[]{:S(2)}, u32[]{:S(2)}) collective-permute-start(f32[9,8,1024]{2,1,0:T(8,128)S(1)} %halo_near.3.refs_0_), channel_id=1, source_target_pairs={{0,2},{2,0},{4,6},{6,4},{8,10},{10,8},{12,14},{14,12},{1,3},{3,1},... | collective-permute-start | bytes 884744 | tf_op jit(solution)/shard_map/ppermute | solution.py:865
  35.0 2.8 %middle_far.2 = (f32[9,8,1024]{2,1,0:T(8,128)S(1)}, f32[9,8,1024]{2,1,0:T(8,128)S(1)}, f32[3,2,9,8,1024]{4,3,2,1,0:T(8,128)S(1)}) custom-call(s32[4]{0:T(128)S(1)} %pad_add_fusion.info_ref, f32[9,8,1024]{2,1,0:T(8,128)S(1)} %halo_far.3.refs_0_, f32[9,8,1024]{2,1,0:T(8,128)S(1)} %get-tuple-element.54.refs_2_.refs_1_, ...), custom_call_target="tpu_custom_call" | custom-call | flops 14745600 | bytes 5898240 | tf_op jit(solution)/shard_map/middle_far/pallas_call | solution.py:287
  39.2 2.9 %middle_near.2 = (f32[9,8,1024]{2,1,0:T(8,128)S(1)}, f32[9,8,1024]{2,1,0:T(8,128)S(1)}, f32[3,2,9,8,1024]{4,3,2,1,0:T(8,128)S(1)}) custom-call(s32[4]{0:T(128)S(1)} %pad_add_fusion.info_ref, f32[9,8,1024]{2,1,0:T(8,128)S(1)} %halo_near.3.refs_0_, f32[9,8,1024]{2,1,0:T(8,128)S(1)} %get-tuple-element.53.refs_1_.refs_2_, ...), custom_call_target="tpu_custom_call" | custom-call | flops 14745600 | bytes 5898240 | tf_op jit(solution)/shard_map/middle_near/pallas_call | solution.py:287
  43.4 4.0 %collective-permute-start.9 = (f32[9,8,1024]{2,1,0:T(8,128)S(1)}, f32[9,8,1024]{2,1,0:T(8,128)S(1)}, u32[]{:S(2)}, u32[]{:S(2)}) collective-permute-start(f32[9,8,1024]{2,1,0:T(8,128)S(1)} %halo_near.4.refs_0_), channel_id=1, source_target_pairs={{0,2},{2,0},{4,6},{6,4},{8,10},{10,8},{12,14},{14,12},{1,3},{3,1},... | collective-permute-start | bytes 884744 | tf_op jit(solution)/shard_map/ppermute | solution.py:865
  47.4 2.8 %middle_far.3 = (f32[9,8,1024]{2,1,0:T(8,128)S(1)}, f32[9,8,1024]{2,1,0:T(8,128)S(1)}, f32[3,2,9,8,1024]{4,3,2,1,0:T(8,128)S(1)}) custom-call(s32[4]{0:T(128)S(1)} %pad_add_fusion.info_ref, f32[9,8,1024]{2,1,0:T(8,128)S(1)} %halo_far.4.refs_0_, f32[9,8,1024]{2,1,0:T(8,128)S(1)} %get-tuple-element.65.refs_2_.refs_1_, ...), custom_call_target="tpu_custom_call" | custom-call | flops 14745600 | bytes 5898240 | tf_op jit(solution)/shard_map/middle_far/pallas_call | solution.py:287
  51.5 2.9 %middle_near.3 = (f32[9,8,1024]{2,1,0:T(8,128)S(1)}, f32[9,8,1024]{2,1,0:T(8,128)S(1)}, f32[3,2,9,8,1024]{4,3,2,1,0:T(8,128)S(1)}) custom-call(s32[4]{0:T(128)S(1)} %pad_add_fusion.info_ref, f32[9,8,1024]{2,1,0:T(8,128)S(1)} %halo_near.4.refs_0_, f32[9,8,1024]{2,1,0:T(8,128)S(1)} %get-tuple-element.60.refs_1_.refs_2_, ...), custom_call_target="tpu_custom_call" | custom-call | flops 14745600 | bytes 5898240 | tf_op jit(solution)/shard_map/middle_near/pallas_call | solution.py:287
  54.4 6.3 %collective-permute-done.9.halo_ref = f32[9,8,1024]{2,1,0:T(8,128)S(1)} collective-permute-done((f32[9,8,1024]{2,1,0:T(8,128)S(1)}, f32[9,8,1024]{2,1,0:T(8,128)S(1)}, u32[]{:S(2)}, u32[]{:S(2)}) %collective-permute-start.9) | collective-permute-done | bytes 294944 | tf_op jit(solution)/shard_map/ppermute | solution.py:865
  62.1 2.5 %collective-permute-start.13 = (f32[9,8,1024]{2,1,0:T(8,128)S(1)}, f32[9,8,1024]{2,1,0:T(8,128)S(1)}, u32[]{:S(2)}, u32[]{:S(2)}) collective-permute-start(f32[9,8,1024]{2,1,0:T(8,128)S(1)} %halo_near.5.refs_0_), channel_id=1, source_target_pairs={{0,2},{2,0},{4,6},{6,4},{8,10},{10,8},{12,14},{14,12},{1,3},{3,1},... | collective-permute-start | bytes 884744 | tf_op jit(solution)/shard_map/ppermute | solution.py:865
  65.2 4.0 %last_far.1.refs_5_ = f32[4,4,8,8,1024]{4,3,2,1,0:T(8,128)} custom-call(s32[4]{0:T(128)S(1)} %pad_add_fusion.info_ref, f32[9,8,1024]{2,1,0:T(8,128)S(1)} %halo_far.5.refs_0_, f32[9,8,1024]{2,1,0:T(8,128)S(1)} %get-tuple-element.71.refs_1_.refs_2_, f32[9,8,1024]{2,1,0:T(8,128)S(1)} %get-tuple-element.68.refs_2_.refs_1_, ...), custom_call_target="tpu_custom_call" | custom-call | flops 14745600 | bytes 5898240 | tf_op jit(solution)/shard_map/last_far/pallas_call | solution.py:312
  69.2 4.0 %last_near.1.part_ref = f32[4,4,8,8,1024]{4,3,2,1,0:T(8,128)} custom-call(s32[4]{0:T(128)S(1)} %pad_add_fusion.info_ref, f32[9,8,1024]{2,1,0:T(8,128)S(1)} %halo_near.5.refs_0_, f32[9,8,1024]{2,1,0:T(8,128)S(1)} %get-tuple-element.68.refs_2_.refs_1_, f32[9,8,1024]{2,1,0:T(8,128)S(1)} %get-tuple-element.71.refs_1_.refs_2_, ...), custom_call_target="tpu_custom_call", output_to_operand_aliasing={{}: (6, {})} | custom-call | flops 14745600 | bytes 5898240 | tf_op jit(solution)/shard_map/last_near/pallas_call | solution.py:312
  73.2 3.1 %finish_far.1 = (f32[4,4,8,8,1024]{4,3,2,1,0:T(8,128)}, f32[2,32,512]{2,1,0:T(8,128)}, f32[16,256]{1,0:T(8,128)S(1)}) custom-call(s32[4]{0:T(128)S(1)} %pad_add_fusion.info_ref, f32[4,4,8,8,1024]{4,3,2,1,0:T(8,128)} %last_near.1.part_ref, f32[9,8,1024]{2,1,0:T(8,128)S(1)} %collective-permute-done.12.halo_ref, ...), custom_call_target="tpu_custom_call", output_to_operand_aliasing={{0}: (1, {})} | custom-call | flops 2621440 | bytes 2621440 | tf_op jit(solution)/shard_map/finish_far/pallas_call | solution.py:473
  76.4 3.5 %finish_near.1 = (f32[4,4,8,8,1024]{4,3,2,1,0:T(8,128)}, f32[2,32,512]{2,1,0:T(8,128)}, f32[16,256]{1,0:T(8,128)S(1)}, f32[8,256]{1,0:T(8,128)S(1)}) custom-call(s32[4]{0:T(128)S(1)} %pad_add_fusion.info_ref, f32[4,4,8,8,1024]{4,3,2,1,0:T(8,128)} %get-tuple-element.75.part_ref, ...), custom_call_target="tpu_custom_call", output_to_operand_aliasing={{0}: (1, {}), {1}: (6, {})} | custom-call | flops 2621440 | bytes 2621440 | tf_op jit(solution)/shard_map/finish_near/pallas_call | solution.py:473
  81.0 2.3 %collective-permute-start.17 = (f32[1,24,256]{2,1,0:T(8,128)S(1)}, f32[1,24,256]{2,1,0:T(8,128)S(1)}, u32[]{:S(2)}, u32[]{:S(2)}) collective-permute-start(f32[1,24,256]{2,1,0:T(8,128)S(1)} %maximum_bitcast_fusion.1.rest_0_), channel_id=1, source_target_pairs={{0,2},{2,0},{4,6},{6,4},{8,10},{10,8},{12,14},{14,12},{1,3},{3,1},... | collective-permute-start | bytes 73736 | tf_op jit(solution)/shard_map/ppermute | solution.py:613
  85.2 1.9 %collective-permute-start.18 = (f32[2,24,256]{2,1,0:T(8,128)S(1)}, f32[2,24,256]{2,1,0:T(8,128)S(1)}, u32[]{:S(2)}, u32[]{:S(2)}) collective-permute-start(f32[2,24,256]{2,1,0:T(8,128)S(1)} %pad_maximum_fusion.6), channel_id=1, source_target_pairs={{0,4},{2,6},{4,0},{6,2},{8,12},{10,14},{12,8},{14,10},{1,5},{3,7},... | collective-permute-start | bytes 147464 | tf_op jit(solution)/shard_map/ppermute | solution.py:613
  87.1 2.1 %collective-permute-done.18.rest_2_ = f32[2,24,256]{2,1,0:T(8,128)S(1)} collective-permute-done((f32[2,24,256]{2,1,0:T(8,128)S(1)}, f32[2,24,256]{2,1,0:T(8,128)S(1)}, u32[]{:S(2)}, u32[]{:S(2)}) %collective-permute-start.18) | collective-permute-done | bytes 49184 | tf_op jit(solution)/shard_map/ppermute | solution.py:613
  89.3 3.0 %collective-permute-start.19 = (f32[4,24,256]{2,1,0:T(8,128)S(1)}, f32[4,24,256]{2,1,0:T(8,128)S(1)}, u32[]{:S(2)}, u32[]{:S(2)}) collective-permute-start(f32[4,24,256]{2,1,0:T(8,128)S(1)} %pad_maximum_fusion.5), channel_id=1, source_target_pairs={{0,8},{2,10},{4,12},{6,14},{8,0},{10,2},{12,4},{14,6},{1,9},{3,11}... | collective-permute-start | bytes 294920 | tf_op jit(solution)/shard_map/ppermute | solution.py:613
  92.2 3.0 %passive.1 = (f32[6,9,24,256]{3,2,1,0:T(8,128)S(1)}, f32[9,9,24,256]{3,2,1,0:T(8,128)S(1)}, f32[9,9,24,256]{3,2,1,0:T(8,128)S(1)}) custom-call(s32[4]{0:T(128)S(1)} %pad_add_fusion.info_ref, f32[3,128]{1,0:T(4,128)S(1)} %pad_maximum_fusion.7.table_ref, f32[8,4,8,256]{3,2,1,0:T(8,128)S(1)} %collective-permute-done.15.strip_ref, ...), custom_call_target="tpu_custom_call" | custom-call | flops 22118400 | bytes 5000000 | tf_op jit(solution)/shard_map/passive/pallas_call | solution.py:720
  95.2 4.1 %mechanics.1 = (f32[3,1,16,256]{3,2,1,0:T(8,128)}, f32[6,1,16,256]{3,2,1,0:T(8,128)}) custom-call(s32[4]{0:T(128)S(1)} %pad_add_fusion.info_ref, f32[6,9,24,256]{3,2,1,0:T(8,128)S(1)} %get-tuple-element.83.disp_ref, f32[9,9,24,256]{3,2,1,0:T(8,128)S(1)} %get-tuple-element.84.stress_ref, f32[9,9,24,256]{3,2,1,0:T(8,128)S(1)} %get-tuple-element.85.pull_ref, ...), custom_call_target="tpu_custom_call" | custom-call | flops 22118400 | bytes 5000000 | tf_op jit(solution)/shard_map/mechanics/pallas_call | solution.py:797
  (63 shorter events, 18.4 us)
Async XLA Ops:
  0.6 5.8 %copy-start.4 = (f32[3,1,16,256]{3,2,1,0:T(8,128)S(1)}, f32[3,1,16,256]{3,2,1,0:T(8,128)}, u32[]{:S(2)}) copy-start(f32[3,1,16,256]{3,2,1,0:T(8,128)} %param.9) | copy-start | bytes 147460
  3.8 2.6 %copy-start.5 = (s32[1,16,256]{2,1,0:T(8,128)S(1)}, s32[1,16,256]{2,1,0:T(8,128)}, u32[]{:S(2)}) copy-start(s32[1,16,256]{2,1,0:T(8,128)} %param.8) | copy-start | bytes 49156
  3.8 15.6 %copy-start.1 = (f32[4,4,64,1024]{3,2,1,0:T(8,128)S(1)}, f32[4,4,64,1024]{3,2,1,0:T(8,128)}, u32[]{:S(2)}) copy-start(f32[4,4,64,1024]{3,2,1,0:T(8,128)} %param.5) | copy-start | bytes 12582916
  4.6 14.8 %collective-permute-start = (f32[4,4,8,1024]{3,2,1,0:T(8,128)S(1)}, f32[4,4,8,1024]{3,2,1,0:T(8,128)S(1)}, u32[]{:S(2)}, u32[]{:S(2)}) collective-permute-start(f32[4,4,8,1024]{3,2,1,0:T(8,128)S(1)} %get-tuple-element.47), channel_id=1, source_target_pairs={{0,1},{1,0},{2,3},{3,2},{4,5},{5,4},{6,7},{7,6},{8,9},{9,8},{10,11... | collective-permute-start | bytes 1572872 | tf_op jit(solution)/shard_map/ppermute | solution.py:838
  5.1 14.2 %collective-permute-start.7 = (f32[8,8,1024]{2,1,0:T(8,128)S(1)}, f32[8,8,1024]{2,1,0:T(8,128)S(1)}, u32[]{:S(2)}, u32[]{:S(2)}) collective-permute-start(f32[8,8,1024]{2,1,0:T(8,128)S(1)} %get-tuple-element.62), channel_id=1, source_target_pairs={{0,0},{2,4},{4,2},{6,8},{8,6},{10,12},{12,10},{14,14},{1,1},{3,5},... | collective-permute-start | bytes 786440 | tf_op jit(solution)/shard_map/ppermute | solution.py:836
  5.8 7.1 %collective-permute-start.1 = (f32[6,8,256]{2,1,0:T(8,128)S(1)}, f32[6,8,256]{2,1,0:T(8,128)S(1)}, u32[]{:S(2)}, u32[]{:S(2)}) collective-permute-start(f32[6,8,256]{2,1,0:T(8,128)S(1)} %get-tuple-element.48), channel_id=1, source_target_pairs={{0,1},{1,0},{2,3},{3,2},{4,5},{5,4},{6,7},{7,6},{8,9},{9,8},{10,11... | collective-permute-start | bytes 147464 | tf_op jit(solution)/shard_map/ppermute | solution.py:839
  6.1 9.9 %collective-permute-start.8 = (f32[8,1024]{1,0:T(8,128)S(1)}, f32[8,1024]{1,0:T(8,128)S(1)}, u32[]{:S(2)}, u32[]{:S(2)}) collective-permute-start(f32[8,1024]{1,0:T(8,128)S(1)} %get-tuple-element.63), channel_id=1, source_target_pairs={{0,1},{1,0},{2,5},{3,4},{4,3},{5,2},{6,9},{7,8},{8,7},{9,6},{10,13... | collective-permute-start | bytes 98312 | tf_op jit(solution)/shard_map/ppermute | solution.py:840
  6.4 21.6 %collective-permute-start.2 = (f32[1,4,16,256]{3,2,1,0:T(8,128)S(1)}, f32[1,4,16,256]{3,2,1,0:T(8,128)S(1)}, u32[]{:S(2)}, u32[]{:S(2)}) collective-permute-start(f32[1,4,16,256]{3,2,1,0:T(8,128)S(1)} %maximum_bitcast_fusion.refs_0_), channel_id=1, source_target_pairs={{0,2},{2,0},{4,6},{6,4},{8,10},{10,8},{12,14},{14,12},{1,3},{3,1},... | collective-permute-start | bytes 196616 | tf_op jit(solution)/shard_map/ppermute | solution.py:613
  12.9 12.2 %collective-permute-start.3 = (f32[8,8,1024]{2,1,0:T(8,128)S(1)}, f32[8,8,1024]{2,1,0:T(8,128)S(1)}, u32[]{:S(2)}, u32[]{:S(2)}) collective-permute-start(f32[8,8,1024]{2,1,0:T(8,128)S(1)} %get-tuple-element.51), channel_id=1, source_target_pairs={{0,2},{2,0},{4,6},{6,4},{8,10},{10,8},{12,14},{14,12},{1,3},{3,1},... | collective-permute-start | bytes 786440 | tf_op jit(solution)/shard_map/ppermute | solution.py:837
  15.9 9.1 %collective-permute-start.4 = (f32[8,1024]{1,0:T(8,128)S(1)}, f32[8,1024]{1,0:T(8,128)S(1)}, u32[]{:S(2)}, u32[]{:S(2)}) collective-permute-start(f32[8,1024]{1,0:T(8,128)S(1)} %get-tuple-element.52), channel_id=1, source_target_pairs={{0,3},{1,2},{2,1},{3,0},{4,7},{5,6},{6,5},{7,4},{8,11},{9,10},{10,... | collective-permute-start | bytes 98312 | tf_op jit(solution)/shard_map/ppermute | solution.py:841
  23.3 14.6 %collective-permute-start.10 = (f32[9,8,1024]{2,1,0:T(8,128)S(1)}, f32[9,8,1024]{2,1,0:T(8,128)S(1)}, u32[]{:S(2)}, u32[]{:S(2)}) collective-permute-start(f32[9,8,1024]{2,1,0:T(8,128)S(1)} %halo_far.3.refs_0_), channel_id=1, source_target_pairs={{0,0},{2,4},{4,2},{6,8},{8,6},{10,12},{12,10},{14,14},{1,1},{3,5},... | collective-permute-start | bytes 884744 | tf_op jit(solution)/shard_map/ppermute | solution.py:855
  29.3 12.7 %collective-permute-start.6 = (f32[9,8,1024]{2,1,0:T(8,128)S(1)}, f32[9,8,1024]{2,1,0:T(8,128)S(1)}, u32[]{:S(2)}, u32[]{:S(2)}) collective-permute-start(f32[9,8,1024]{2,1,0:T(8,128)S(1)} %halo_near.3.refs_0_), channel_id=1, source_target_pairs={{0,2},{2,0},{4,6},{6,4},{8,10},{10,8},{12,14},{14,12},{1,3},{3,1},... | collective-permute-start | bytes 884744 | tf_op jit(solution)/shard_map/ppermute | solution.py:865
  33.4 8.7 %collective-permute-start.5 = (f32[2,4,16,256]{3,2,1,0:T(8,128)S(1)}, f32[2,4,16,256]{3,2,1,0:T(8,128)S(1)}, u32[]{:S(2)}, u32[]{:S(2)}) collective-permute-start(f32[2,4,16,256]{3,2,1,0:T(8,128)S(1)} %pad_maximum_fusion.4), channel_id=1, source_target_pairs={{0,4},{2,6},{4,0},{6,2},{8,12},{10,14},{12,8},{14,10},{1,5},{3,7},... | collective-permute-start | bytes 393224 | tf_op jit(solution)/shard_map/ppermute | solution.py:613
  38.5 11.7 %collective-permute-start.11 = (f32[9,8,1024]{2,1,0:T(8,128)S(1)}, f32[9,8,1024]{2,1,0:T(8,128)S(1)}, u32[]{:S(2)}, u32[]{:S(2)}) collective-permute-start(f32[9,8,1024]{2,1,0:T(8,128)S(1)} %halo_far.4.refs_0_), channel_id=1, source_target_pairs={{0,0},{2,4},{4,2},{6,8},{8,6},{10,12},{12,10},{14,14},{1,1},{3,5},... | collective-permute-start | bytes 884744 | tf_op jit(solution)/shard_map/ppermute | solution.py:855
  43.4 17.3 %collective-permute-start.9 = (f32[9,8,1024]{2,1,0:T(8,128)S(1)}, f32[9,8,1024]{2,1,0:T(8,128)S(1)}, u32[]{:S(2)}, u32[]{:S(2)}) collective-permute-start(f32[9,8,1024]{2,1,0:T(8,128)S(1)} %halo_near.4.refs_0_), channel_id=1, source_target_pairs={{0,2},{2,0},{4,6},{6,4},{8,10},{10,8},{12,14},{14,12},{1,3},{3,1},... | collective-permute-start | bytes 884744 | tf_op jit(solution)/shard_map/ppermute | solution.py:865
  50.9 22.4 %collective-permute-start.12 = (f32[9,8,1024]{2,1,0:T(8,128)S(1)}, f32[9,8,1024]{2,1,0:T(8,128)S(1)}, u32[]{:S(2)}, u32[]{:S(2)}) collective-permute-start(f32[9,8,1024]{2,1,0:T(8,128)S(1)} %halo_far.5.refs_0_), channel_id=1, source_target_pairs={{0,0},{2,4},{4,2},{6,8},{8,6},{10,12},{12,10},{14,14},{1,1},{3,5},... | collective-permute-start | bytes 884744 | tf_op jit(solution)/shard_map/ppermute | solution.py:855
  62.1 14.3 %collective-permute-start.13 = (f32[9,8,1024]{2,1,0:T(8,128)S(1)}, f32[9,8,1024]{2,1,0:T(8,128)S(1)}, u32[]{:S(2)}, u32[]{:S(2)}) collective-permute-start(f32[9,8,1024]{2,1,0:T(8,128)S(1)} %halo_near.5.refs_0_), channel_id=1, source_target_pairs={{0,2},{2,0},{4,6},{6,4},{8,10},{10,8},{12,14},{14,12},{1,3},{3,1},... | collective-permute-start | bytes 884744 | tf_op jit(solution)/shard_map/ppermute | solution.py:865
  64.6 18.8 %collective-permute-start.14 = (f32[4,4,16,256]{3,2,1,0:T(8,128)S(1)}, f32[4,4,16,256]{3,2,1,0:T(8,128)S(1)}, u32[]{:S(2)}, u32[]{:S(2)}) collective-permute-start(f32[4,4,16,256]{3,2,1,0:T(8,128)S(1)} %pad_maximum_fusion.3), channel_id=1, source_target_pairs={{0,8},{2,10},{4,12},{6,14},{8,0},{10,2},{12,4},{14,6},{1,9},{3,11}... | collective-permute-start | bytes 786440 | tf_op jit(solution)/shard_map/ppermute | solution.py:613
  69.2 4.0 %copy-start.2 = (f32[2,32,512]{2,1,0:T(8,128)S(1)}, f32[2,32,512]{2,1,0:T(8,128)}, u32[]{:S(2)}) copy-start(f32[2,32,512]{2,1,0:T(8,128)} %tension_ref.3) | copy-start | bytes 393220
  79.9 1.2 %collective-permute-start.16 = (f32[8,256]{1,0:T(8,128)S(1)}, f32[8,256]{1,0:T(8,128)S(1)}, u32[]{:S(2)}, u32[]{:S(2)}) collective-permute-start(f32[8,256]{1,0:T(8,128)S(1)} %get-tuple-element.87), channel_id=1, source_target_pairs={{0,1},{1,0},{2,3},{3,2},{4,5},{5,4},{6,7},{7,6},{8,9},{9,8},{10,11... | collective-permute-start | bytes 24584 | tf_op jit(solution)/shard_map/ppermute | solution.py:878
  81.0 4.1 %collective-permute-start.17 = (f32[1,24,256]{2,1,0:T(8,128)S(1)}, f32[1,24,256]{2,1,0:T(8,128)S(1)}, u32[]{:S(2)}, u32[]{:S(2)}) collective-permute-start(f32[1,24,256]{2,1,0:T(8,128)S(1)} %maximum_bitcast_fusion.1.rest_0_), channel_id=1, source_target_pairs={{0,2},{2,0},{4,6},{6,4},{8,10},{10,8},{12,14},{14,12},{1,3},{3,1},... | collective-permute-start | bytes 73736 | tf_op jit(solution)/shard_map/ppermute | solution.py:613
  84.0 8.2 %collective-permute-start.15 = (f32[8,4,8,256]{3,2,1,0:T(8,128)S(1)}, f32[8,4,8,256]{3,2,1,0:T(8,128)S(1)}, u32[]{:S(2)}, u32[]{:S(2)}) collective-permute-start(f32[8,4,8,256]{3,2,1,0:T(8,128)S(1)} %facing.1), channel_id=1, source_target_pairs={{0,1},{1,0},{2,3},{3,2},{4,5},{5,4},{6,7},{7,6},{8,9},{9,8},{10,11... | collective-permute-start | bytes 786440 | tf_op jit(solution)/shard_map/ppermute | solution.py:872
  85.2 4.1 %collective-permute-start.18 = (f32[2,24,256]{2,1,0:T(8,128)S(1)}, f32[2,24,256]{2,1,0:T(8,128)S(1)}, u32[]{:S(2)}, u32[]{:S(2)}) collective-permute-start(f32[2,24,256]{2,1,0:T(8,128)S(1)} %pad_maximum_fusion.6), channel_id=1, source_target_pairs={{0,4},{2,6},{4,0},{6,2},{8,12},{10,14},{12,8},{14,10},{1,5},{3,7},... | collective-permute-start | bytes 147464 | tf_op jit(solution)/shard_map/ppermute | solution.py:613
  89.3 6.0 %collective-permute-start.19 = (f32[4,24,256]{2,1,0:T(8,128)S(1)}, f32[4,24,256]{2,1,0:T(8,128)S(1)}, u32[]{:S(2)}, u32[]{:S(2)}) collective-permute-start(f32[4,24,256]{2,1,0:T(8,128)S(1)} %pad_maximum_fusion.5), channel_id=1, source_target_pairs={{0,8},{2,10},{4,12},{6,14},{8,0},{10,2},{12,4},{14,6},{1,9},{3,11}... | collective-permute-start | bytes 294920 | tf_op jit(solution)/shard_map/ppermute | solution.py:613
  (2 other events, 3.1 us)

commit v4 on v3

--- a/solution.py
+++ b/solution.py
@@ -123,17 +123,17 @@
     )(info, cond, strip)
 
 
-def pack_kernel(info_ref, states_ref, cond_ref, far_ref, near_ref, facing_ref, far_rows, near_rows, cond_rows, sems):
+def pack_kernel(info_ref, states_ref, cond_ref, far_ref, near_ref, edge_ref, facing_ref, cond_rows, sems):
     side, flip = info_ref[SIDE], info_ref[FLIP]
     planes, own = states_ref.shape[1:3]
     far, near = flip * (planes - 1), (1 - flip) * (planes - 1)
     edge = (1 - side) * (own - 1)
     half = pl.multiple_of(8 * (1 - side), 8)
     moves = [
+        (states_ref.at[0, far, edge], edge_ref.at[0]),
+        (states_ref.at[0, near, edge], edge_ref.at[1]),
         (states_ref.at[0, far], far_ref),
         (states_ref.at[0, near], near_ref),
-        (states_ref.at[0, far, edge], far_rows),
-        (states_ref.at[0, near, edge], near_rows),
         (states_ref.at[:, :, edge], facing_ref),
         (cond_ref.at[:, 0, pl.ds(half, 8), :], cond_rows),
     ]
@@ -146,15 +146,15 @@
 
 def pack(info, tiled, cond):
     comps, planes, own, _, width = tiled.shape
-    shapes = [(own, 8, width), (own, 8, width), (comps, planes, 8, width), (8, width), (8, width)]
+    shapes = [(own, 8, width), (own, 8, width), (2, 8, width), (comps, planes, 8, width)]
     shapes.append((cond.shape[0], 8, cond.shape[-1]))
     return pl.pallas_call(
         pack_kernel,
         in_specs=[pl.BlockSpec(memory_space=pltpu.SMEM)] + [pl.BlockSpec(memory_space=pltpu.HBM)] * 2,
         out_specs=[pl.BlockSpec(memory_space=pltpu.VMEM)] * len(shapes),
         out_shape=[jax.ShapeDtypeStruct(shape, jnp.float32) for shape in shapes],
-        scratch_shapes=[pltpu.SemaphoreType.DMA((len(shapes),))],
-        compiler_params=params(),
+        scratch_shapes=[pltpu.SemaphoreType.DMA((6,))],
+        compiler_params=pltpu.CompilerParams(vmem_limit_bytes=60 * 1024 * 1024),
         cost_estimate=cost(0, 2_500_000),
         name="pack",
     )(info, tiled, cond)
@@ -202,7 +202,7 @@
     return (flip, flip) if half == FAR_HALF else (1 - flip, 1 - flip)
 
 
-def half_kernel(kind, half, tiles, per_block, info_ref, *refs):
+def half_kernel(kind, half, tiles, info_ref, *refs):
     side = info_ref[SIDE]
     sub = row_iota()
     own = tiles - 1
@@ -211,17 +211,11 @@
         whole_ref, coeff_ref, outer_out, inner_out, gate_out = refs
         spots = [2 * index + outer, 2 * index + 1 - outer, 2 - index]
         reads = [lambda t, z=z: whole_ref[0, z, t] for z in spots]
-    elif kind == "middle":
+    else:
         *u_refs, gate_ref, coeff_ref, outer_out, inner_out, gate_out = refs
         reads = [lambda t, ref=ref: ref[t] for ref in u_refs]
-    else:
-        *u_refs, gate_ref, coeff_ref = refs[:5]
-        out_ref = refs[-1]
-        reads = [lambda t, ref=ref: ref[t] for ref in u_refs]
-        place = [outer, 1 - outer]
-
-    def one(local_tile, carry):
-        tile = local_tile if kind != "last" else pl.program_id(0) * per_block + local_tile
+
+    def diffused(tile):
         before, after = ring_neighbours(tile, tiles)
         mask_before, mask_after = edge_masks(tile, side, own)
         cur = [read(tile) for read in reads]
@@ -229,8 +223,9 @@
         nxt = [read(after) * mask_after for read in reads]
 
         def coeff(index):
-            return coeff_ref[index, local_tile]
-
+            return coeff_ref[index, tile]
+
+        bases = []
         for plane in range(2):
             u = cur[plane]
             if plane == 0:
@@ -253,114 +248,88 @@
                 to_right += coeff(C_ZXL) * wide
             base = coeff(C_MID) * u + coeff(C_ZZ) * around + coeff(C_YY) * (u_next + u_prev)
             base = base + tilt if half == FAR_HALF else base - tilt
-            base += left(to_left) + right(to_right)
-            chunk = 256
+            bases.append(base + left(to_left) + right(to_right))
+        return bases
+
+    def react(tile, bases):
+        chunk = 256
+        for plane in range(2):
             for start in range(0, 1024, chunk):
                 lanes = slice(start, start + chunk)
                 if kind == "first":
+                    u = whole_ref[0, spots[plane], tile, :, lanes]
                     gates = [whole_ref[1 + g, spots[plane], tile, :, lanes] for g in range(3)]
                 else:
-                    gates = [gate_ref[g, plane, local_tile, :, lanes] for g in range(3)]
-                u_add, *gates = ionic(u[:, lanes], *gates)
-                u_new = base[:, lanes] + u_add
-                if kind == "last":
-                    for comp, value in enumerate([u_new] + gates):
-                        out_ref[comp, place[plane], local_tile, :, lanes] = value
-                else:
-                    (outer_out, inner_out)[plane][tile, :, lanes] = u_new
-                    for comp, value in enumerate(gates):
-                        gate_out[comp, plane, tile, :, lanes] = value
+                    u = u_refs[plane][tile, :, lanes]
+                    gates = [gate_ref[g, plane, tile, :, lanes] for g in range(3)]
+                u_add, *gates = ionic(u, *gates)
+                (outer_out, inner_out)[plane][tile, :, lanes] = bases[plane][:, lanes] + u_add
+                for comp, value in enumerate(gates):
+                    gate_out[comp, plane, tile, :, lanes] = value
+
+    together = 2 if kind == "last" else 3
+
+    def some(step, carry):
+        numbers = [step * together + pos for pos in range(together)]
+        held = [diffused(tile) for tile in numbers]
+        for tile, bases in zip(numbers, held):
+            react(tile, bases)
         return carry
 
-    lax.fori_loop(0, per_block, one, 0)
-
-
-def half_costs(tiles, width):
-    cells = 2 * tiles * 8 * width
-    return cost(100 * cells, 40 * cells, 11 * cells)
+    lax.fori_loop(0, (own if kind == "last" else tiles) // together, some, 0)
 
 
 def half_step(kind, half, info, arrays, coeffs):
     _, tiles, _, width = coeffs.shape
     vmem = pl.BlockSpec(memory_space=pltpu.VMEM)
-    plane = jax.ShapeDtypeStruct((tiles, 8, width), jnp.float32)
+    kept = tiles - 1 if kind == "last" else tiles
+    plane = jax.ShapeDtypeStruct((kept, 8, width), jnp.float32)
+    cells = 2 * tiles * 8 * width
     return pl.pallas_call(
-        functools.partial(half_kernel, kind, half, tiles, tiles),
+        functools.partial(half_kernel, kind, half, tiles),
         in_specs=[pl.BlockSpec(memory_space=pltpu.SMEM)] + [vmem] * (len(arrays) + 1),
         out_specs=[vmem] * 3,
-        out_shape=[plane, plane, jax.ShapeDtypeStruct((3, 2, tiles, 8, width), jnp.float32)],
+        out_shape=[plane, plane, jax.ShapeDtypeStruct((3, 2, kept, 8, width), jnp.float32)],
         compiler_params=params(),
-        cost_estimate=half_costs(tiles, width),
+        cost_estimate=cost(100 * cells, 40 * cells, 11 * cells),
         name=kind + ("_far" if half == FAR_HALF else "_near"),
     )(info, *arrays, coeffs)
 
 
-def half_last(half, info, arrays, coeffs, states=None):
-    _, tiles, _, width = coeffs.shape
-    per_block = 2
-    whole = pl.BlockSpec((tiles, 8, width), lambda i, info: (0, 0, 0))
-    in_specs = [whole] * 3 + [
-        pl.BlockSpec((3, 2, per_block, 8, width), lambda i, info: (0, 0, i, 0, 0)),
-        pl.BlockSpec((10, per_block, 8, width), lambda i, info: (0, i, 0, 0)),
-    ]
-    operands = [*arrays, coeffs]
-    aliases = {}
-    if states is not None:
-        in_specs.append(pl.BlockSpec(memory_space=pl.ANY))
-        operands.append(states)
-        aliases = {len(operands): 0}
-    return pl.pallas_call(
-        functools.partial(half_kernel, "last", half, tiles, per_block),
-        grid_spec=pltpu.PrefetchScalarGridSpec(
-            num_scalar_prefetch=1,
-            grid=((tiles - 1) // per_block,),
-            in_specs=in_specs,
-            out_specs=pl.BlockSpec((4, 2, per_block, 8, width), lambda i, info: (0, half_place(info, half)[0], i, 0, 0)),
-        ),
-        out_shape=jax.ShapeDtypeStruct((4, 4, tiles - 1, 8, width), jnp.float32),
-        input_output_aliases=aliases,
-        compiler_params=params(),
-        cost_estimate=half_costs(tiles, width),
-        name="last" + ("_far" if half == FAR_HALF else "_near"),
-    )(info, *operands)
-
-
 def halo_terms(halo_ref, coeff_ref, tile, tiles, side, sub, half):
-    before, after = ring_neighbours(tile, tiles)
-    mask_before, mask_after = edge_masks(tile, side, tiles - 1)
-    cur = halo_ref[tile]
-    up = next_row(cur, halo_ref[after] * mask_after, sub)
-    down = prev_row(cur, halo_ref[before] * mask_before, sub)
-    cross = coeff_ref[C_ZY, tile] * (up - down)
+    before, after = (tile - 1) % tiles, (tile + 1) % tiles
+    cur, prv, nxt = halo_ref[tile], halo_ref[before], halo_ref[after]
+    if tile == 0:
+        prv = prv * jnp.where(side == 0, 0.0, 1.0)
+    if tile == tiles - 2:
+        nxt = nxt * jnp.where(side == 1, 0.0, 1.0)
+    cross = coeff_ref[C_ZY, tile] * (next_row(cur, nxt, sub) - prev_row(cur, prv, sub))
     cross += left(coeff_ref[C_ZXR, tile] * cur) - right(coeff_ref[C_ZXL, tile] * cur)
     total = coeff_ref[C_ZZ, tile] * cur
     return total - cross if half == FAR_HALF else total + cross
 
 
-def halo_kernel(half, tiles, info_ref, outer_ref, halo_ref, coeff_ref, out_ref):
+def add_halo(half, tiles, kept, info_ref, outer_ref, halo_ref, coeff_ref, out_ref):
     side = info_ref[SIDE]
     sub = row_iota()
 
-    def one(tile, carry):
-        out_ref[tile] = outer_ref[tile] + halo_terms(halo_ref, coeff_ref, tile, tiles, side, sub, half)
-        return carry
-
-    def kept(tile, carry):
-        out_ref[tile] = outer_ref[tile]
-        return carry
+    def fill():
+        for tile in range(kept):
+            out_ref[tile] = outer_ref[tile] + halo_terms(halo_ref, coeff_ref, tile, tiles, side, sub, half)
 
     if half == NEAR_HALF:
-        lax.fori_loop(0, tiles, one, 0)
+        fill()
     else:
         exists = info_ref[FAR] == 1
-
-        @pl.when(exists)
-        def _():
-            lax.fori_loop(0, tiles, one, 0)
+        pl.when(exists)(fill)
 
         @pl.when(jnp.logical_not(exists))
         def _():
-            lax.fori_loop(0, tiles, kept, 0)
+            out_ref[...] = outer_ref[...]
+
+
+def halo_kernel(half, tiles, info_ref, outer_ref, halo_ref, coeff_ref, out_ref):
+    add_halo(half, tiles, tiles, info_ref, outer_ref, halo_ref, coeff_ref, out_ref)
 
 
 def halo_step(half, info, outer, halo, coeffs):
@@ -378,102 +347,93 @@
     )(info, outer, halo, coeffs)
 
 
-def pair_matrix(width, scale):
-    fine = lax.broadcasted_iota(jnp.int32, (width, width // 2), 0)
-    coarse = lax.broadcasted_iota(jnp.int32, (width, width // 2), 1)
-    return jnp.where((fine >> 1) == coarse, scale, 0.0)
-
-
-def row_pairs(count, scale):
-    coarse = lax.broadcasted_iota(jnp.int32, (count // 2, count), 0)
-    fine = lax.broadcasted_iota(jnp.int32, (count // 2, count), 1)
-    return jnp.where((fine >> 1) == coarse, scale, 0.0)
-
-
-def dot(a, b):
-    return jnp.dot(a, b, precision=HIGHEST, preferred_element_type=jnp.float32)
-
-
-def pooled(field):
+def pooled(field, rows_ref):
     rows, lanes = field.shape
-    few = dot(row_pairs(rows, 0.5), field)
-    pick = pair_matrix(256, 0.5)
-    return jnp.concatenate([dot(few[:, at : at + 256], pick) for at in range(0, lanes, 256)], axis=1)
-
-
-def finish_kernel(half, tiles, info_ref, part_ref, halo_ref, coeff_ref, tension_ref, *refs):
+    fine = lax.broadcasted_iota(jnp.int32, (256, 128), 0)
+    coarse = lax.broadcasted_iota(jnp.int32, (256, 128), 1)
+    pick = jnp.where((fine >> 1) == coarse, 0.25, 0.0).astype(jnp.bfloat16)
+    few = []
+    for chunk in range(lanes // 128):
+        rows_ref[chunk, :rows] = field[:, 128 * chunk : 128 * chunk + 128]
+        even = rows_ref[chunk, pl.ds(0, rows // 2, stride=2), :]
+        few.append(even + rows_ref[chunk, pl.ds(1, rows // 2, stride=2), :])
+    pairs = [jnp.concatenate(few[pos : pos + 2], axis=1) for pos in range(0, len(few), 2)]
+    rest = jnp.concatenate(pairs, axis=0)
+    total = None
+    for _ in range(3):
+        part = rest.astype(jnp.bfloat16)
+        rest = rest - part.astype(jnp.float32)
+        mean = jnp.dot(part, pick, preferred_element_type=jnp.float32)
+        total = mean if total is None else total + mean
+    count = rows // 2
+    return jnp.concatenate([total[pos * count : (pos + 1) * count] for pos in range(len(pairs))], axis=1)
+
+
+def finish_kernel(half, tiles, info_ref, outer_ref, inner_ref, gate_ref, halo_ref, coeff_ref, tension_ref, *refs):
     if half == FAR_HALF:
-        out_ref, tension_out, active_out = refs
+        states_out, tension_out, active_out, u_ref, layer_ref, rows_ref, sems = refs
     else:
-        active_ref, _, out_ref, tension_out, active_out, facing_out = refs
-    side = info_ref[SIDE]
-    sub = row_iota()
+        active_ref, _, _, states_out, tension_out, active_out, facing_out, u_ref, layer_ref, rows_ref, sems = refs
+    index, outer = half_place(info_ref, half)
+    place = [2 * index + outer, 2 * index + 1 - outer]
+    moves = [(gate_ref.at[g, plane], states_out.at[1 + g, place[plane]]) for g in range(3) for plane in range(2)]
+    moves.append((inner_ref, states_out.at[0, place[1]]))
+    copies = [pltpu.make_async_copy(src, dst, sems.at[pos]) for pos, (src, dst) in enumerate(moves)]
+    for copy in copies:
+        copy.start()
     own = tiles - 1
-    _, outer = half_place(info_ref, half)
-    out_ref[0, 1 - outer] = part_ref[0, 1 - outer]
-
-    def one(tile, carry):
-        out_ref[0, outer, tile] = part_ref[0, outer, tile] + halo_terms(halo_ref, coeff_ref, tile, tiles, side, sub, half)
-        return carry
-
-    if half == NEAR_HALF:
-        lax.fori_loop(0, own, one, 0)
+    add_halo(half, tiles, own, info_ref, outer_ref, halo_ref, coeff_ref, u_ref)
+    copies.append(pltpu.make_async_copy(u_ref, states_out.at[0, place[0]], sems.at[len(moves)]))
+    copies[-1].start()
+    both = 0.5 * (u_ref[...] + inner_ref[...])
+    mean = pooled(both.reshape(own * 8, both.shape[-1]), rows_ref)
+    old = tension_ref[index]
+    new = old + 0.5 * (mean - old)
+    layer_ref[...] = new
+    copies.append(pltpu.make_async_copy(layer_ref, tension_out.at[index], sems.at[len(moves) + 1]))
+    copies[-1].start()
+    mean = pooled(0.5 * new, rows_ref)
+    if half == FAR_HALF:
+        active_out[...] = mean
     else:
-        exists = info_ref[FAR] == 1
-
-        @pl.when(exists)
-        def _():
-            lax.fori_loop(0, own, one, 0)
-
-        @pl.when(jnp.logical_not(exists))
-        def _():
-            out_ref[0, outer] = part_ref[0, outer]
-
-    both = 0.5 * (out_ref[0, 0] + out_ref[0, 1])
-    mean = pooled(both.reshape(own * 8, both.shape[-1]))
-    old = tension_ref[0]
-    new = old + 0.5 * (mean - old)
-    tension_out[0] = new
-    if half == FAR_HALF:
-        active_out[...] = pooled(0.5 * new)
-    else:
-        active_out[...] = active_ref[...] + pooled(0.5 * new)
-        facing_out[...] = active_out[pl.ds(pl.multiple_of(8 * (1 - side), 8), 8), :]
-
-
-def finish_half(half, info, part, halo, coeffs, tension, active=None, tension_next=None):
+        active_out[...] = active_ref[...] + mean
+        facing_out[...] = active_out[pl.ds(pl.multiple_of(8 * (1 - info_ref[SIDE]), 8), 8), :]
+    for copy in copies:
+        copy.wait()
+
+
+def finish_half(half, info, arrays, halo, coeffs, tension, active=None, states=None, tension_next=None):
     tiles, _, width = halo.shape
     own = tiles - 1
     active_shape = (own * 2, width // 4)
-    z_half = lambda info: half_place(info, half)[0]
-    u_spec = pl.BlockSpec((1, 2, own, 8, width), lambda i, info: (0, z_half(info), 0, 0, 0))
-    tension_spec = pl.BlockSpec((1,) + tension.shape[1:], lambda i, info: (z_half(info), 0, 0))
-    active_spec = pl.BlockSpec(active_shape, lambda i, info: (0, 0))
-    in_specs = [
-        u_spec,
-        pl.BlockSpec((tiles, 8, width), lambda i, info: (0, 0, 0)),
-        pl.BlockSpec((4, tiles, 8, width), lambda i, info: (0, 0, 0, 0)),
-        tension_spec,
-    ]
-    operands = [part, halo, coeffs, tension]
-    out_specs = [u_spec, tension_spec, active_spec]
+    vmem, hbm = pl.BlockSpec(memory_space=pltpu.VMEM), pl.BlockSpec(memory_space=pltpu.HBM)
+    in_specs = [pl.BlockSpec(memory_space=pltpu.SMEM)] + [vmem] * 6
+    operands = [*arrays, halo, coeffs, tension]
+    out_specs = [hbm, hbm, vmem]
     out_shape = [
-        jax.ShapeDtypeStruct(part.shape, jnp.float32),
+        jax.ShapeDtypeStruct((4, 4, own, 8, width), jnp.float32),
         jax.ShapeDtypeStruct(tension.shape, jnp.float32),
         jax.ShapeDtypeStruct(active_shape, jnp.float32),
     ]
-    aliases = {1: 0}
+    aliases = {}
     if half == NEAR_HALF:
-        in_specs += [active_spec, pl.BlockSpec(memory_space=pl.ANY)]
-        operands += [active, tension_next]
-        aliases[len(operands)] = 1
-        out_specs.append(pl.BlockSpec((8, width // 4), lambda i, info: (0, 0)))
+        in_specs += [vmem, hbm, hbm]
+        operands += [active, states, tension_next]
+        aliases = {8: 0, 9: 1}
+        out_specs.append(vmem)
         out_shape.append(jax.ShapeDtypeStruct((8, width // 4), jnp.float32))
     cells = 2 * own * 8 * width
     return pl.pallas_call(
         functools.partial(finish_kernel, half, tiles),
-        grid_spec=pltpu.PrefetchScalarGridSpec(num_scalar_prefetch=1, grid=(1,), in_specs=in_specs, out_specs=out_specs),
+        in_specs=in_specs,
+        out_specs=out_specs,
         out_shape=out_shape,
+        scratch_shapes=[
+            pltpu.VMEM((own, 8, width), jnp.float32),
+            pltpu.VMEM(tension.shape[1:], jnp.float32),
+            pltpu.VMEM((width // 128, own * 8, 128), jnp.float32),
+            pltpu.SemaphoreType.DMA((9,)),
+        ],
         input_output_aliases=aliases,
         compiler_params=params(),
         cost_estimate=cost(20 * cells, 20 * cells),
@@ -827,25 +787,21 @@
 
     pairs = [(i, i ^ 1) for i in range(slabs)]
     others = [(i, i if i in (0, slabs - 1) else ((i + 1) ^ 1) - 1) for i in range(slabs)]
-    cross_pairs = [(2 * i + c, 2 * j + 1 - c) for i, j in pairs for c in range(2)]
-    cross_others = [(2 * i + c, 2 * j + 1 - c) for i, j in others for c in range(2)]
     swap = [(0, 1), (1, 0)]
 
     tiled = states.reshape(4, planes, own, 8, width)
-    far, near, facing, far_rows, near_rows, cond_rows = pack(info, tiled, cond)
-    far_halo = lax.ppermute(far, "slab", others)
-    near_halo = lax.ppermute(near, "slab", pairs)
+    fields = Planes(jnp.concatenate([disp[:, 0], fiber.astype(jnp.float32)], axis=0), slabs, REACH + 1)
+    far, near, edges, facing, cond_rows = pack(info, tiled, cond)
+    edges = lax.ppermute(edges, "col", swap)
+    fields.round()
+    edges, *fields.parts = tie(edges, *fields.parts)
+    far_halo = lax.ppermute(jnp.concatenate([far, edges[:1]], axis=0), "slab", others)
+    near_halo = lax.ppermute(jnp.concatenate([near, edges[1:]], axis=0), "slab", pairs)
     strip = lax.ppermute(facing, "col", swap)
     cond_strip = lax.ppermute(cond_rows, "col", swap)
-    far_strip = lax.ppermute(far_rows, ("slab", "col"), cross_others)
-    near_strip = lax.ppermute(near_rows, ("slab", "col"), cross_pairs)
-    fields = Planes(jnp.concatenate([disp[:, 0], fiber.astype(jnp.float32)], axis=0), slabs, REACH + 1)
 
     coeffs = fine_coeffs(info, cond, cond_strip)
     whole = jnp.concatenate([tiled, strip[:, :, None]], axis=2)
-    far_halo = jnp.concatenate([far_halo, far_strip[None]], axis=0)
-    near_halo = jnp.concatenate([near_halo, near_strip[None]], axis=0)
-    fields.round()
 
     far_part, far_inner, far_gates = half_step("first", FAR_HALF, info, (whole,), coeffs)
     near_part, near_inner, near_gates = half_step("first", NEAR_HALF, info, (whole,), coeffs)
@@ -857,23 +813,20 @@
             (near_part, *fields.parts) = tie(near_part, *fields.parts)
             fields.round()
         far_arrays = (far, far_inner, near_inner, far_gates)
-        if last:
-            part = half_last(FAR_HALF, info, far_arrays, coeffs)
-        else:
-            far_part, far_next, far_gates = half_step("middle", FAR_HALF, info, far_arrays, coeffs)
+        kind = "last" if last else "middle"
+        far_part, far_next, far_gates = half_step(kind, FAR_HALF, info, far_arrays, coeffs)
         near = halo_step(NEAR_HALF, info, near_part, near_halo, coeffs)
         near_halo = lax.ppermute(near, "slab", pairs)
         near_arrays = (near, near_inner, far_inner, near_gates)
-        if last:
-            part = half_last(NEAR_HALF, info, near_arrays, coeffs, part)
-        else:
-            near_part, near_inner, near_gates = half_step("middle", NEAR_HALF, info, near_arrays, coeffs)
-            far_inner = far_next
+        near_part, near_inner, near_gates = half_step(kind, NEAR_HALF, info, near_arrays, coeffs)
+        far_inner = far_next
     strips = lax.ppermute(facing_rows(info, fields.parts), "col", swap)
-    part, tension_next, active = finish_half(FAR_HALF, info, part, far_halo, coeffs, tension)
+    far_arrays = (far_part, far_inner, far_gates)
+    near_arrays = (near_part, near_inner, near_gates)
+    states_next, tension_next, active = finish_half(FAR_HALF, info, far_arrays, far_halo, coeffs, tension)
     window = passive_step(info, fields, strips)
     states_next, tension_next, active, facing = finish_half(
-        NEAR_HALF, info, part, near_halo, coeffs, tension, active, tension_next
+        NEAR_HALF, info, near_arrays, near_halo, coeffs, tension, active, states_next, tension_next
     )
     active_strip = lax.ppermute(facing, "col", swap)
     actives = Planes(jnp.concatenate([active, active_strip], axis=0), slabs, REACH)

time: 99.7 us -> 95 us (0.953)
  Pallas kernels: 49.1 us -> 44.6 us
  starting transfers between devices: 33.7 us -> 37.4 us
  waiting for transfers between devices: 11.8 us -> 8.33 us
  local copies, waits for them, and re-layouts: 3.1 us -> 0.03 us
  other arithmetic: 0.77 us -> 3.4 us
    ppermute x4 -> x3, waiting for transfers between devices: 6.32 us -> 0.01 us  [on_device(): near_halo = lax.ppermute(near, 'slab', pairs)]
    ppermute x4 -> x3, starting transfers between devices: 10.6 us -> 16.6 us  [on_device(): near_halo = lax.ppermute(near, 'slab', pairs)]
    pallas_call x10, Pallas kernels: 31.8 us -> 26.9 us  [the longest x8 22.6 us: half_step(): pl.pallas_call(functools.partial(half_kernel, kind, half, tiles), in_spec...]
    ppermute x6, starting transfers between devices: 15.8 us -> 12.5 us  [round(): self.parts.append(lax.ppermute(held, 'slab', perm))]
    unnamed x12, local copies, waits for them, and re-layouts: 3.1 us -> 0.02 us
    ppermute x6, waiting for transfers between devices: 3.17 us -> 5.7 us  [round(): self.parts.append(lax.ppermute(held, 'slab', perm))]
    pallas_call x1, Pallas kernels: 0.78 us -> 3.08 us  [pack(): pl.pallas_call(pack_kernel, in_specs=[pl.BlockSpec(memory_space=pltpu.SME...]
    ppermute x2 -> x3, starting transfers between devices: 3.72 us -> 5.91 us  [the longest x1 4.58 us: on_device(): lax.ppermute(jnp.concatenate([near, edges[1:]], axis=0), 'slab', pairs)]
  transfers between devices with their start and end apart: 20 -> 19, of which waited for: 5 -> 6; matrix products, arithmetic and copies ran while one was open for 1% -> 3% of each run, Pallas kernels for 44% -> 39%
where the time goes in v4:
time: 95 us; the launch traced here: 94.7 us
  Pallas kernels  44.6 us (47%)
  starting transfers between devices  37.4 us (39%)
  waiting for transfers between devices  8.33 us (9%)
  other arithmetic  3.4 us (4%)
  between operations  0.99 us (1%)
    pallas_call x8, Pallas kernels, half_step(): pl.pallas_call(functools.partial(half_kernel, kind, half, tiles), in_spec...  22.6 us
    ppermute x3, starting transfers between devices, on_device(): near_halo = lax.ppermute(near, 'slab', pairs)  16.6 us
    ppermute x6, starting transfers between devices, round(): self.parts.append(lax.ppermute(held, 'slab', perm))  12.5 us
    ppermute x6, waiting for transfers between devices, round(): self.parts.append(lax.ppermute(held, 'slab', perm))  5.7 us
    ppermute x1, starting transfers between devices, on_device(): lax.ppermute(jnp.concatenate([near, edges[1:]], axis=0), 'slab', pairs)  4.58 us
    pallas_call x2, Pallas kernels, finish_half(): pl.pallas_call(functools.partial(finish_kernel, half, tiles), in_specs=in...  4.24 us
    pallas_call x1, Pallas kernels, mechanics_step(): pl.pallas_call(functools.partial(mechanics_kernel, planes), in_specs=[pl....  4.12 us
    pallas_call x6, Pallas kernels, halo_step(): pl.pallas_call(functools.partial(halo_kernel, half, tiles), in_specs=[pl....  4.02 us
  transfers between devices with their start and end apart: 19, of which 6 were waited for; matrix products, arithmetic and copies ran while one was open for 3% of the time, Pallas kernels for 39%

profile of v4, /device:TPU:0, one launch (start us, length us, event | category | flops | bytes accessed | tf_op | source)
XLA Modules:
  0.0 94.7 jit_solution(18366425212485288080)
XLA Ops:
  1.3 3.1 %pack.1 = (f32[8,8,1024]{2,1,0:T(8,128)}, f32[8,8,1024]{2,1,0:T(8,128)}, f32[2,8,1024]{2,1,0:T(8,128)}, f32[4,4,8,1024]{3,2,1,0:T(8,128)}, f32[6,8,256]{2,1,0:T(8,128)}) custom-call(s32[4]{0:T(128)} %pad_add_fusion.info_ref, f32[4,4,8,8,1024]{4,3,2,1,0:T(8,128)} %bitcast.12, f32[6,1,16,256]{3,2,1,0:T(8,128)} %cond_ref.3), custom_call_target="tpu_custom_call" | custom-call | bytes 2500000 | tf_op jit(solution)/shard_map/pack/pallas_call | solution.py:151
  4.9 2.6 %collective-permute-start.3 = (f32[1,4,16,256]{3,2,1,0:T(8,128)S(1)}, f32[1,4,16,256]{3,2,1,0:T(8,128)S(1)}, u32[]{:S(2)}, u32[]{:S(2)}) collective-permute-start(f32[1,4,16,256]{3,2,1,0:T(8,128)S(1)} %maximum_bitcast_fusion.refs_0_), channel_id=1, source_target_pairs={{0,2},{2,0},{4,6},{6,4},{8,10},{10,8},{12,14},{14,12},{1,3},{3,1},... | collective-permute-start | bytes 196616 | tf_op jit(solution)/shard_map/ppermute | solution.py:573
  7.7 2.5 %collective-permute-done.3.refs_1_ = f32[1,4,16,256]{3,2,1,0:T(8,128)S(1)} collective-permute-done((f32[1,4,16,256]{3,2,1,0:T(8,128)S(1)}, f32[1,4,16,256]{3,2,1,0:T(8,128)S(1)}, u32[]{:S(2)}, u32[]{:S(2)}) %collective-permute-start.3) | collective-permute-done | bytes 65568 | tf_op jit(solution)/shard_map/ppermute | solution.py:573
  13.2 4.6 %collective-permute-start.4 = (f32[9,8,1024]{2,1,0:T(8,128)S(1)}, f32[9,8,1024]{2,1,0:T(8,128)S(1)}, u32[]{:S(2)}, u32[]{:S(2)}) collective-permute-start(f32[9,8,1024]{2,1,0:T(8,128)S(1)} %pad_maximum_fusion.1), channel_id=1, source_target_pairs={{0,2},{2,0},{4,6},{6,4},{8,10},{10,8},{12,14},{14,12},{1,3},{3,1},... | collective-permute-start | bytes 884744 | tf_op jit(solution)/shard_map/ppermute | solution.py:799
  19.2 3.0 %coeffs.1.refs_1_.coeff_ref.refs_4_ = f32[10,9,8,1024]{3,2,1,0:T(8,128)S(1)} custom-call(s32[4]{0:T(128)S(1)} %copy-done.2, f32[6,1,16,256]{3,2,1,0:T(8,128)S(1)} %copy-done.1, f32[6,8,256]{2,1,0:T(8,128)S(1)} %collective-permute-done.1.strip_ref), custom_call_target="tpu_custom_call" | custom-call | flops 2000000 | bytes 3200000 | tf_op jit(solution)/shard_map/coeffs/pallas_call | solution.py:116
  22.6 2.9 %first_far.1 = (f32[9,8,1024]{2,1,0:T(8,128)S(1)}, f32[9,8,1024]{2,1,0:T(8,128)S(1)}, f32[3,2,9,8,1024]{4,3,2,1,0:T(8,128)S(1)}) custom-call(s32[4]{0:T(128)S(1)} %copy-done.2, f32[4,4,9,8,1024]{4,3,2,1,0:T(8,128)S(1)} %pad_maximum_fusion.refs_0_, f32[10,9,8,1024]{3,2,1,0:T(8,128)S(1)} %coeffs.1.refs_1_.coeff_ref.refs_4_), custom_call_target="tpu_custom_call" | custom-call | flops 14745600 | bytes 5898240 | tf_op jit(solution)/shard_map/first_far/pallas_call | solution.py:288
  26.8 2.9 %first_near.1 = (f32[9,8,1024]{2,1,0:T(8,128)S(1)}, f32[9,8,1024]{2,1,0:T(8,128)S(1)}, f32[3,2,9,8,1024]{4,3,2,1,0:T(8,128)S(1)}) custom-call(s32[4]{0:T(128)S(1)} %copy-done.2, f32[4,4,9,8,1024]{4,3,2,1,0:T(8,128)S(1)} %pad_maximum_fusion.refs_0_, f32[10,9,8,1024]{3,2,1,0:T(8,128)S(1)} %coeffs.1.refs_1_.coeff_ref.refs_4_), custom_call_target="tpu_custom_call" | custom-call | flops 14745600 | bytes 5898240 | tf_op jit(solution)/shard_map/first_near/pallas_call | solution.py:288
  30.5 4.5 %collective-permute-start.6 = (f32[9,8,1024]{2,1,0:T(8,128)S(1)}, f32[9,8,1024]{2,1,0:T(8,128)S(1)}, u32[]{:S(2)}, u32[]{:S(2)}) collective-permute-start(f32[9,8,1024]{2,1,0:T(8,128)S(1)} %halo_near.3.refs_0_), channel_id=1, source_target_pairs={{0,2},{2,0},{4,6},{6,4},{8,10},{10,8},{12,14},{14,12},{1,3},{3,1},... | collective-permute-start | bytes 884744 | tf_op jit(solution)/shard_map/ppermute | solution.py:819
  36.7 2.9 %middle_far.2 = (f32[9,8,1024]{2,1,0:T(8,128)S(1)}, f32[9,8,1024]{2,1,0:T(8,128)S(1)}, f32[3,2,9,8,1024]{4,3,2,1,0:T(8,128)S(1)}) custom-call(s32[4]{0:T(128)S(1)} %copy-done.2, f32[9,8,1024]{2,1,0:T(8,128)S(1)} %halo_far.3.refs_0_, f32[9,8,1024]{2,1,0:T(8,128)S(1)} %get-tuple-element.65.refs_2_.refs_1_, ...), custom_call_target="tpu_custom_call" | custom-call | flops 14745600 | bytes 5898240 | tf_op jit(solution)/shard_map/middle_far/pallas_call | solution.py:288
  40.9 2.9 %middle_near.2 = (f32[9,8,1024]{2,1,0:T(8,128)S(1)}, f32[9,8,1024]{2,1,0:T(8,128)S(1)}, f32[3,2,9,8,1024]{4,3,2,1,0:T(8,128)S(1)}) custom-call(s32[4]{0:T(128)S(1)} %copy-done.2, f32[9,8,1024]{2,1,0:T(8,128)S(1)} %halo_near.3.refs_0_, f32[9,8,1024]{2,1,0:T(8,128)S(1)} %get-tuple-element.64.refs_1_.refs_2_, ...), custom_call_target="tpu_custom_call" | custom-call | flops 14745600 | bytes 5898240 | tf_op jit(solution)/shard_map/middle_near/pallas_call | solution.py:288
  44.6 3.9 %collective-permute-start.8 = (f32[9,8,1024]{2,1,0:T(8,128)S(1)}, f32[9,8,1024]{2,1,0:T(8,128)S(1)}, u32[]{:S(2)}, u32[]{:S(2)}) collective-permute-start(f32[9,8,1024]{2,1,0:T(8,128)S(1)} %halo_near.4.refs_0_), channel_id=1, source_target_pairs={{0,2},{2,0},{4,6},{6,4},{8,10},{10,8},{12,14},{14,12},{1,3},{3,1},... | collective-permute-start | bytes 884744 | tf_op jit(solution)/shard_map/ppermute | solution.py:819
  48.5 2.9 %middle_far.3 = (f32[9,8,1024]{2,1,0:T(8,128)S(1)}, f32[9,8,1024]{2,1,0:T(8,128)S(1)}, f32[3,2,9,8,1024]{4,3,2,1,0:T(8,128)S(1)}) custom-call(s32[4]{0:T(128)S(1)} %copy-done.2, f32[9,8,1024]{2,1,0:T(8,128)S(1)} %halo_far.4.refs_0_, f32[9,8,1024]{2,1,0:T(8,128)S(1)} %get-tuple-element.75.refs_2_.refs_1_, ...), custom_call_target="tpu_custom_call" | custom-call | flops 14745600 | bytes 5898240 | tf_op jit(solution)/shard_map/middle_far/pallas_call | solution.py:288
  52.6 2.9 %middle_near.3 = (f32[9,8,1024]{2,1,0:T(8,128)S(1)}, f32[9,8,1024]{2,1,0:T(8,128)S(1)}, f32[3,2,9,8,1024]{4,3,2,1,0:T(8,128)S(1)}) custom-call(s32[4]{0:T(128)S(1)} %copy-done.2, f32[9,8,1024]{2,1,0:T(8,128)S(1)} %halo_near.4.refs_0_, f32[9,8,1024]{2,1,0:T(8,128)S(1)} %get-tuple-element.71.refs_1_.refs_2_, ...), custom_call_target="tpu_custom_call" | custom-call | flops 14745600 | bytes 5898240 | tf_op jit(solution)/shard_map/middle_near/pallas_call | solution.py:288
  56.3 8.1 %collective-permute-start.10 = (f32[9,8,1024]{2,1,0:T(8,128)S(1)}, f32[9,8,1024]{2,1,0:T(8,128)S(1)}, u32[]{:S(2)}, u32[]{:S(2)}) collective-permute-start(f32[9,8,1024]{2,1,0:T(8,128)S(1)} %halo_near.5.refs_0_), channel_id=1, source_target_pairs={{0,2},{2,0},{4,6},{6,4},{8,10},{10,8},{12,14},{14,12},{1,3},{3,1},... | collective-permute-start | bytes 884744 | tf_op jit(solution)/shard_map/ppermute | solution.py:819
  65.7 2.6 %last_far.1 = (f32[8,8,1024]{2,1,0:T(8,128)S(1)}, f32[8,8,1024]{2,1,0:T(8,128)S(1)}, f32[3,2,8,8,1024]{4,3,2,1,0:T(8,128)S(1)}) custom-call(s32[4]{0:T(128)S(1)} %copy-done.2, f32[9,8,1024]{2,1,0:T(8,128)S(1)} %halo_far.5.refs_0_, f32[9,8,1024]{2,1,0:T(8,128)S(1)} %get-tuple-element.81.refs_2_.refs_1_, f32[9,8,1024]{2,1,0:T(8,128)S(1)} %get-tuple-element.78.refs_1_.refs_2_, ...), custom_call_target="tpu_custom_call" | custom-call | flops 14745600 | bytes 5898240 | tf_op jit(solution)/shard_map/last_far/pallas_call | solution.py:288
  68.4 2.6 %last_near.1 = (f32[8,8,1024]{2,1,0:T(8,128)S(1)}, f32[8,8,1024]{2,1,0:T(8,128)S(1)}, f32[3,2,8,8,1024]{4,3,2,1,0:T(8,128)S(1)}) custom-call(s32[4]{0:T(128)S(1)} %copy-done.2, f32[9,8,1024]{2,1,0:T(8,128)S(1)} %halo_near.5.refs_0_, f32[9,8,1024]{2,1,0:T(8,128)S(1)} %get-tuple-element.78.refs_1_.refs_2_, ...), custom_call_target="tpu_custom_call" | custom-call | flops 14745600 | bytes 5898240 | tf_op jit(solution)/shard_map/last_near/pallas_call | solution.py:288
  71.0 1.9 %finish_far.1 = (f32[4,4,8,8,1024]{4,3,2,1,0:T(8,128)}, f32[2,32,512]{2,1,0:T(8,128)}, f32[16,256]{1,0:T(8,128)S(1)}) custom-call(s32[4]{0:T(128)S(1)} %copy-done.2, f32[8,8,1024]{2,1,0:T(8,128)S(1)} %get-tuple-element.88.outer_ref, f32[8,8,1024]{2,1,0:T(8,128)S(1)} %get-tuple-element.89.inner_ref, f32[3,2,8,8,1024]{4,3,2,1,0:T(8,128)S(1)} %get-tuple-element.90.gate_ref, ...), custom_call_target="tpu_custom_call" | custom-call | flops 2621440 | bytes 2621440 | tf_op jit(solution)/shard_map/finish_far/pallas_call | solution.py:426
  73.0 2.3 %finish_near.1 = (f32[4,4,8,8,1024]{4,3,2,1,0:T(8,128)}, f32[2,32,512]{2,1,0:T(8,128)}, f32[16,256]{1,0:T(8,128)S(1)}, f32[8,256]{1,0:T(8,128)S(1)}) custom-call(s32[4]{0:T(128)S(1)} %copy-done.2, f32[8,8,1024]{2,1,0:T(8,128)S(1)} %get-tuple-element.83.outer_ref, ...), custom_call_target="tpu_custom_call", output_to_operand_aliasing={{0}: (8, {}), {1}: (9, {})} | custom-call | flops 2621440 | bytes 2621440 | tf_op jit(solution)/shard_map/finish_near/pallas_call | solution.py:426
  76.5 1.9 %collective-permute-start.16 = (f32[1,24,256]{2,1,0:T(8,128)S(1)}, f32[1,24,256]{2,1,0:T(8,128)S(1)}, u32[]{:S(2)}, u32[]{:S(2)}) collective-permute-start(f32[1,24,256]{2,1,0:T(8,128)S(1)} %maximum_bitcast_fusion.1.rest_0_), channel_id=1, source_target_pairs={{0,2},{2,0},{4,6},{6,4},{8,10},{10,8},{12,14},{14,12},{1,3},{3,1},... | collective-permute-start | bytes 73736 | tf_op jit(solution)/shard_map/ppermute | solution.py:573
  80.4 2.1 %collective-permute-start.17 = (f32[2,24,256]{2,1,0:T(8,128)S(1)}, f32[2,24,256]{2,1,0:T(8,128)S(1)}, u32[]{:S(2)}, u32[]{:S(2)}) collective-permute-start(f32[2,24,256]{2,1,0:T(8,128)S(1)} %pad_maximum_fusion.6), channel_id=1, source_target_pairs={{0,4},{2,6},{4,0},{6,2},{8,12},{10,14},{12,8},{14,10},{1,5},{3,7},... | collective-permute-start | bytes 147464 | tf_op jit(solution)/shard_map/ppermute | solution.py:573
  82.6 2.0 %collective-permute-done.17.rest_2_ = f32[2,24,256]{2,1,0:T(8,128)S(1)} collective-permute-done((f32[2,24,256]{2,1,0:T(8,128)S(1)}, f32[2,24,256]{2,1,0:T(8,128)S(1)}, u32[]{:S(2)}, u32[]{:S(2)}) %collective-permute-start.17) | collective-permute-done | bytes 49184 | tf_op jit(solution)/shard_map/ppermute | solution.py:573
  84.5 3.1 %collective-permute-start.18 = (f32[4,24,256]{2,1,0:T(8,128)S(1)}, f32[4,24,256]{2,1,0:T(8,128)S(1)}, u32[]{:S(2)}, u32[]{:S(2)}) collective-permute-start(f32[4,24,256]{2,1,0:T(8,128)S(1)} %pad_maximum_fusion.5), channel_id=1, source_target_pairs={{0,8},{2,10},{4,12},{6,14},{8,0},{10,2},{12,4},{14,6},{1,9},{3,11}... | collective-permute-start | bytes 294920 | tf_op jit(solution)/shard_map/ppermute | solution.py:573
  87.6 3.0 %passive.1 = (f32[6,9,24,256]{3,2,1,0:T(8,128)S(1)}, f32[9,9,24,256]{3,2,1,0:T(8,128)S(1)}, f32[9,9,24,256]{3,2,1,0:T(8,128)S(1)}) custom-call(s32[4]{0:T(128)S(1)} %copy-done.2, f32[3,128]{1,0:T(4,128)S(1)} %pad_maximum_fusion.7.table_ref, f32[8,4,8,256]{3,2,1,0:T(8,128)S(1)} %collective-permute-done.14.strip_ref, ...), custom_call_target="tpu_custom_call" | custom-call | flops 22118400 | bytes 5000000 | tf_op jit(solution)/shard_map/passive/pallas_call | solution.py:680
  90.6 4.1 %mechanics.1 = (f32[3,1,16,256]{3,2,1,0:T(8,128)}, f32[6,1,16,256]{3,2,1,0:T(8,128)}) custom-call(s32[4]{0:T(128)S(1)} %copy-done.2, f32[6,9,24,256]{3,2,1,0:T(8,128)S(1)} %get-tuple-element.99.disp_ref, f32[9,9,24,256]{3,2,1,0:T(8,128)S(1)} %get-tuple-element.100.stress_ref, f32[9,9,24,256]{3,2,1,0:T(8,128)S(1)} %get-tuple-element.101.pull_ref, ...), custom_call_target="tpu_custom_call" | custom-call | flops 22118400 | bytes 5000000 | tf_op jit(solution)/shard_map/mechanics/pallas_call | solution.py:757
  (62 shorter events, 18.4 us)
Async XLA Ops:
  1.3 3.6 %copy-start.5 = (s32[1,16,256]{2,1,0:T(8,128)S(1)}, s32[1,16,256]{2,1,0:T(8,128)}, u32[]{:S(2)}) copy-start(s32[1,16,256]{2,1,0:T(8,128)} %param.8) | copy-start | bytes 49156
  1.3 3.6 %copy-start.4 = (f32[3,1,16,256]{3,2,1,0:T(8,128)S(1)}, f32[3,1,16,256]{3,2,1,0:T(8,128)}, u32[]{:S(2)}) copy-start(f32[3,1,16,256]{3,2,1,0:T(8,128)} %param.9) | copy-start | bytes 147460
  1.3 17.9 %copy-start.1 = (f32[6,1,16,256]{3,2,1,0:T(8,128)S(1)}, f32[6,1,16,256]{3,2,1,0:T(8,128)}, u32[]{:S(2)}) copy-start(f32[6,1,16,256]{3,2,1,0:T(8,128)} %cond_ref.3) | copy-start | bytes 294916
  1.3 17.9 %copy-start.2 = (s32[4]{0:T(128)S(1)}, s32[4]{0:T(128)}, u32[]{:S(2)}) copy-start(s32[4]{0:T(128)} %pad_add_fusion.info_ref) | copy-start | bytes 52
  4.4 3.3 %collective-permute-start.2 = (f32[2,8,1024]{2,1,0:T(8,128)}, f32[2,8,1024]{2,1,0:T(8,128)S(1)}, u32[]{:S(2)}, u32[]{:S(2)}) collective-permute-start(f32[2,8,1024]{2,1,0:T(8,128)} %get-tuple-element.58), channel_id=1, source_target_pairs={{0,1},{1,0},{2,3},{3,2},{4,5},{5,4},{6,7},{7,6},{8,9},{9,8},{10,11... | collective-permute-start | bytes 196616 | tf_op jit(solution)/shard_map/ppermute | solution.py:795
  4.9 5.3 %collective-permute-start.3 = (f32[1,4,16,256]{3,2,1,0:T(8,128)S(1)}, f32[1,4,16,256]{3,2,1,0:T(8,128)S(1)}, u32[]{:S(2)}, u32[]{:S(2)}) collective-permute-start(f32[1,4,16,256]{3,2,1,0:T(8,128)S(1)} %maximum_bitcast_fusion.refs_0_), channel_id=1, source_target_pairs={{0,2},{2,0},{4,6},{6,4},{8,10},{10,8},{12,14},{14,12},{1,3},{3,1},... | collective-permute-start | bytes 196616 | tf_op jit(solution)/shard_map/ppermute | solution.py:573
  7.5 14.7 %collective-permute-start = (f32[4,4,8,1024]{3,2,1,0:T(8,128)}, f32[4,4,8,1024]{3,2,1,0:T(8,128)S(1)}, u32[]{:S(2)}, u32[]{:S(2)}) collective-permute-start(f32[4,4,8,1024]{3,2,1,0:T(8,128)} %get-tuple-element.55), channel_id=1, source_target_pairs={{0,1},{1,0},{2,3},{3,2},{4,5},{5,4},{6,7},{7,6},{8,9},{9,8},{10,11... | collective-permute-start | bytes 1572872 | tf_op jit(solution)/shard_map/ppermute | solution.py:800
  10.3 11.9 %copy-start.3 = (f32[4,4,64,1024]{3,2,1,0:T(8,128)S(1)}, f32[4,4,64,1024]{3,2,1,0:T(8,128)}, u32[]{:S(2)}) copy-start(f32[4,4,64,1024]{3,2,1,0:T(8,128)} %param.5) | copy-start | bytes 12582916
  11.4 14.1 %collective-permute-start.7 = (f32[9,8,1024]{2,1,0:T(8,128)S(1)}, f32[9,8,1024]{2,1,0:T(8,128)S(1)}, u32[]{:S(2)}, u32[]{:S(2)}) collective-permute-start(f32[9,8,1024]{2,1,0:T(8,128)S(1)} %pad_maximum_fusion.2), channel_id=1, source_target_pairs={{0,0},{2,4},{4,2},{6,8},{8,6},{10,12},{12,10},{14,14},{1,1},{3,5},... | collective-permute-start | bytes 884744 | tf_op jit(solution)/shard_map/ppermute | solution.py:798
  13.2 16.5 %collective-permute-start.4 = (f32[9,8,1024]{2,1,0:T(8,128)S(1)}, f32[9,8,1024]{2,1,0:T(8,128)S(1)}, u32[]{:S(2)}, u32[]{:S(2)}) collective-permute-start(f32[9,8,1024]{2,1,0:T(8,128)S(1)} %pad_maximum_fusion.1), channel_id=1, source_target_pairs={{0,2},{2,0},{4,6},{6,4},{8,10},{10,8},{12,14},{14,12},{1,3},{3,1},... | collective-permute-start | bytes 884744 | tf_op jit(solution)/shard_map/ppermute | solution.py:799
  17.8 1.4 %collective-permute-start.1 = (f32[6,8,256]{2,1,0:T(8,128)}, f32[6,8,256]{2,1,0:T(8,128)S(1)}, u32[]{:S(2)}, u32[]{:S(2)}) collective-permute-start(f32[6,8,256]{2,1,0:T(8,128)} %get-tuple-element.56), channel_id=1, source_target_pairs={{0,1},{1,0},{2,3},{3,2},{4,5},{5,4},{6,7},{7,6},{8,9},{9,8},{10,11... | collective-permute-start | bytes 147464 | tf_op jit(solution)/shard_map/ppermute | solution.py:801
  26.1 13.5 %collective-permute-start.9 = (f32[9,8,1024]{2,1,0:T(8,128)S(1)}, f32[9,8,1024]{2,1,0:T(8,128)S(1)}, u32[]{:S(2)}, u32[]{:S(2)}) collective-permute-start(f32[9,8,1024]{2,1,0:T(8,128)S(1)} %halo_far.3.refs_0_), channel_id=1, source_target_pairs={{0,0},{2,4},{4,2},{6,8},{8,6},{10,12},{12,10},{14,14},{1,1},{3,5},... | collective-permute-start | bytes 884744 | tf_op jit(solution)/shard_map/ppermute | solution.py:811
  30.5 13.3 %collective-permute-start.6 = (f32[9,8,1024]{2,1,0:T(8,128)S(1)}, f32[9,8,1024]{2,1,0:T(8,128)S(1)}, u32[]{:S(2)}, u32[]{:S(2)}) collective-permute-start(f32[9,8,1024]{2,1,0:T(8,128)S(1)} %halo_near.3.refs_0_), channel_id=1, source_target_pairs={{0,2},{2,0},{4,6},{6,4},{8,10},{10,8},{12,14},{14,12},{1,3},{3,1},... | collective-permute-start | bytes 884744 | tf_op jit(solution)/shard_map/ppermute | solution.py:819
  35.1 8.7 %collective-permute-start.5 = (f32[2,4,16,256]{3,2,1,0:T(8,128)S(1)}, f32[2,4,16,256]{3,2,1,0:T(8,128)S(1)}, u32[]{:S(2)}, u32[]{:S(2)}) collective-permute-start(f32[2,4,16,256]{3,2,1,0:T(8,128)S(1)} %pad_maximum_fusion.4), channel_id=1, source_target_pairs={{0,4},{2,6},{4,0},{6,2},{8,12},{10,14},{12,8},{14,10},{1,5},{3,7},... | collective-permute-start | bytes 393224 | tf_op jit(solution)/shard_map/ppermute | solution.py:573
  40.2 11.2 %collective-permute-start.11 = (f32[9,8,1024]{2,1,0:T(8,128)S(1)}, f32[9,8,1024]{2,1,0:T(8,128)S(1)}, u32[]{:S(2)}, u32[]{:S(2)}) collective-permute-start(f32[9,8,1024]{2,1,0:T(8,128)S(1)} %halo_far.4.refs_0_), channel_id=1, source_target_pairs={{0,0},{2,4},{4,2},{6,8},{8,6},{10,12},{12,10},{14,14},{1,1},{3,5},... | collective-permute-start | bytes 884744 | tf_op jit(solution)/shard_map/ppermute | solution.py:811
  44.6 11.0 %collective-permute-start.8 = (f32[9,8,1024]{2,1,0:T(8,128)S(1)}, f32[9,8,1024]{2,1,0:T(8,128)S(1)}, u32[]{:S(2)}, u32[]{:S(2)}) collective-permute-start(f32[9,8,1024]{2,1,0:T(8,128)S(1)} %halo_near.4.refs_0_), channel_id=1, source_target_pairs={{0,2},{2,0},{4,6},{6,4},{8,10},{10,8},{12,14},{14,12},{1,3},{3,1},... | collective-permute-start | bytes 884744 | tf_op jit(solution)/shard_map/ppermute | solution.py:819
  52.0 19.0 %collective-permute-start.12 = (f32[9,8,1024]{2,1,0:T(8,128)S(1)}, f32[9,8,1024]{2,1,0:T(8,128)S(1)}, u32[]{:S(2)}, u32[]{:S(2)}) collective-permute-start(f32[9,8,1024]{2,1,0:T(8,128)S(1)} %halo_far.5.refs_0_), channel_id=1, source_target_pairs={{0,0},{2,4},{4,2},{6,8},{8,6},{10,12},{12,10},{14,14},{1,1},{3,5},... | collective-permute-start | bytes 884744 | tf_op jit(solution)/shard_map/ppermute | solution.py:811
  56.3 16.6 %collective-permute-start.10 = (f32[9,8,1024]{2,1,0:T(8,128)S(1)}, f32[9,8,1024]{2,1,0:T(8,128)S(1)}, u32[]{:S(2)}, u32[]{:S(2)}) collective-permute-start(f32[9,8,1024]{2,1,0:T(8,128)S(1)} %halo_near.5.refs_0_), channel_id=1, source_target_pairs={{0,2},{2,0},{4,6},{6,4},{8,10},{10,8},{12,14},{14,12},{1,3},{3,1},... | collective-permute-start | bytes 884744 | tf_op jit(solution)/shard_map/ppermute | solution.py:819
  64.5 15.1 %collective-permute-start.13 = (f32[4,4,16,256]{3,2,1,0:T(8,128)S(1)}, f32[4,4,16,256]{3,2,1,0:T(8,128)S(1)}, u32[]{:S(2)}, u32[]{:S(2)}) collective-permute-start(f32[4,4,16,256]{3,2,1,0:T(8,128)S(1)} %pad_maximum_fusion.3), channel_id=1, source_target_pairs={{0,8},{2,10},{4,12},{6,14},{8,0},{10,2},{12,4},{14,6},{1,9},{3,11}... | collective-permute-start | bytes 786440 | tf_op jit(solution)/shard_map/ppermute | solution.py:573
  75.3 1.2 %collective-permute-start.15 = (f32[8,256]{1,0:T(8,128)S(1)}, f32[8,256]{1,0:T(8,128)S(1)}, u32[]{:S(2)}, u32[]{:S(2)}) collective-permute-start(f32[8,256]{1,0:T(8,128)S(1)} %get-tuple-element.103), channel_id=1, source_target_pairs={{0,1},{1,0},{2,3},{3,2},{4,5},{5,4},{6,7},{7,6},{8,9},{9,8},{10,11... | collective-permute-start | bytes 24584 | tf_op jit(solution)/shard_map/ppermute | solution.py:831
  76.5 3.8 %collective-permute-start.16 = (f32[1,24,256]{2,1,0:T(8,128)S(1)}, f32[1,24,256]{2,1,0:T(8,128)S(1)}, u32[]{:S(2)}, u32[]{:S(2)}) collective-permute-start(f32[1,24,256]{2,1,0:T(8,128)S(1)} %maximum_bitcast_fusion.1.rest_0_), channel_id=1, source_target_pairs={{0,2},{2,0},{4,6},{6,4},{8,10},{10,8},{12,14},{14,12},{1,3},{3,1},... | collective-permute-start | bytes 73736 | tf_op jit(solution)/shard_map/ppermute | solution.py:573
  80.2 7.4 %collective-permute-start.14 = (f32[8,4,8,256]{3,2,1,0:T(8,128)S(1)}, f32[8,4,8,256]{3,2,1,0:T(8,128)S(1)}, u32[]{:S(2)}, u32[]{:S(2)}) collective-permute-start(f32[8,4,8,256]{3,2,1,0:T(8,128)S(1)} %facing.1), channel_id=1, source_target_pairs={{0,1},{1,0},{2,3},{3,2},{4,5},{5,4},{6,7},{7,6},{8,9},{9,8},{10,11... | collective-permute-start | bytes 786440 | tf_op jit(solution)/shard_map/ppermute | solution.py:823
  80.4 4.2 %collective-permute-start.17 = (f32[2,24,256]{2,1,0:T(8,128)S(1)}, f32[2,24,256]{2,1,0:T(8,128)S(1)}, u32[]{:S(2)}, u32[]{:S(2)}) collective-permute-start(f32[2,24,256]{2,1,0:T(8,128)S(1)} %pad_maximum_fusion.6), channel_id=1, source_target_pairs={{0,4},{2,6},{4,0},{6,2},{8,12},{10,14},{12,8},{14,10},{1,5},{3,7},... | collective-permute-start | bytes 147464 | tf_op jit(solution)/shard_map/ppermute | solution.py:573
  84.5 6.0 %collective-permute-start.18 = (f32[4,24,256]{2,1,0:T(8,128)S(1)}, f32[4,24,256]{2,1,0:T(8,128)S(1)}, u32[]{:S(2)}, u32[]{:S(2)}) collective-permute-start(f32[4,24,256]{2,1,0:T(8,128)S(1)} %pad_maximum_fusion.5), channel_id=1, source_target_pairs={{0,8},{2,10},{4,12},{6,14},{8,0},{10,2},{12,4},{14,6},{1,9},{3,11}... | collective-permute-start | bytes 294920 | tf_op jit(solution)/shard_map/ppermute | solution.py:573
  (1 other events, 2.7 us)

commit v5 on v4

--- a/solution.py
+++ b/solution.py
@@ -123,41 +123,98 @@
     )(info, cond, strip)
 
 
-def pack_kernel(info_ref, states_ref, cond_ref, far_ref, near_ref, edge_ref, facing_ref, cond_rows, sems):
-    side, flip = info_ref[SIDE], info_ref[FLIP]
+SENT, FIELD = 17, 4
+
+
+def packed_strip(strip, side):
+    half = strip.shape[-1] // 2
+    low, high = strip[:, :half], strip[:, half:]
+    sub = lax.broadcasted_iota(jnp.int32, low.shape, 0)
+    first = jnp.where(side == 0, low, pltpu.roll(low, 4, 0))
+    second = jnp.where(side == 0, pltpu.roll(high, 4, 0), high)
+    return jnp.where(sub < 4, first, second)
+
+
+def store_sent(ref, tile, tiles, value, side):
+    half = value.shape[-1] // 2
+    if tile < tiles - 1:
+        ref[tile] = value[:, :half]
+        ref[tiles - 1 + tile] = value[:, half:]
+    else:
+        ref[2 * tile] = packed_strip(value, side)
+
+
+def load_sent(ref, tile, tiles, side):
+    if tile < tiles - 1:
+        return jnp.concatenate([ref[tile], ref[tiles - 1 + tile]], axis=1)
+    packed = ref[2 * tile]
+    turned = pltpu.roll(packed, 4, 0)
+    return jnp.concatenate([jnp.where(side == 0, packed, turned), jnp.where(side == 0, turned, packed)], axis=1)
+
+
+SMEM = pl.BlockSpec(memory_space=pltpu.SMEM)
+VMEM = pl.BlockSpec(memory_space=pltpu.VMEM)
+
+
+def shape_of(*shape):
+    return jax.ShapeDtypeStruct(shape, jnp.float32)
+
+
+def facing_kernel(info_ref, states_ref, cond_ref, edge_ref, facing_ref, cond_rows):
+    flip, side = info_ref[FLIP], info_ref[SIDE]
+    comps, planes, own = states_ref.shape[:3]
+    edge = (1 - side) * (own - 1)
+    edge_ref[0] = states_ref[0, flip * (planes - 1), edge]
+    edge_ref[1] = states_ref[0, (1 - flip) * (planes - 1), edge]
+    for comp in range(comps):
+        for plane in range(planes):
+            facing_ref[comp, plane] = states_ref[comp, plane, edge]
+    first = pl.multiple_of(8 * (1 - side), 8)
+    for comp in range(cond_ref.shape[0]):
+        cond_rows[comp] = cond_ref[comp, 0, pl.ds(first, 8), :]
+
+
+def sends_kernel(info_ref, edge_ref, states_ref, disp_ref, fiber_ref, far_ref, near_ref):
+    flip, side = info_ref[FLIP], info_ref[SIDE]
     planes, own = states_ref.shape[1:3]
-    far, near = flip * (planes - 1), (1 - flip) * (planes - 1)
-    edge = (1 - side) * (own - 1)
-    half = pl.multiple_of(8 * (1 - side), 8)
-    moves = [
-        (states_ref.at[0, far, edge], edge_ref.at[0]),
-        (states_ref.at[0, near, edge], edge_ref.at[1]),
-        (states_ref.at[0, far], far_ref),
-        (states_ref.at[0, near], near_ref),
-        (states_ref.at[:, :, edge], facing_ref),
-        (cond_ref.at[:, 0, pl.ds(half, 8), :], cond_rows),
-    ]
-    copies = [pltpu.make_async_copy(src, dst, sems.at[pos]) for pos, (src, dst) in enumerate(moves)]
-    for copy in copies:
-        copy.start()
-    for copy in copies:
-        copy.wait()
-
-
-def pack(info, tiled, cond):
-    comps, planes, own, _, width = tiled.shape
-    shapes = [(own, 8, width), (own, 8, width), (2, 8, width), (comps, planes, 8, width)]
-    shapes.append((cond.shape[0], 8, cond.shape[-1]))
+    for pos, (ref, plane) in enumerate([(far_ref, flip * (planes - 1)), (near_ref, (1 - flip) * (planes - 1))]):
+        for tile in range(own):
+            store_sent(ref, tile, own + 1, states_ref[0, plane, tile], side)
+        store_sent(ref, own, own + 1, edge_ref[pos], side)
+    for comp in range(3):
+        near_ref[SENT + comp] = jnp.concatenate([disp_ref[comp, 0, :8], disp_ref[comp, 0, 8:]], axis=1)
+    index = fiber_ref[0].astype(jnp.float32)
+    near_ref[SENT + 3] = jnp.concatenate([index[:8], index[8:]], axis=1)
+
+
+def facing_parts(info, tiled, cond):
+    comps, planes, _, _, width = tiled.shape
     return pl.pallas_call(
-        pack_kernel,
-        in_specs=[pl.BlockSpec(memory_space=pltpu.SMEM)] + [pl.BlockSpec(memory_space=pltpu.HBM)] * 2,
-        out_specs=[pl.BlockSpec(memory_space=pltpu.VMEM)] * len(shapes),
-        out_shape=[jax.ShapeDtypeStruct(shape, jnp.float32) for shape in shapes],
-        scratch_shapes=[pltpu.SemaphoreType.DMA((6,))],
-        compiler_params=pltpu.CompilerParams(vmem_limit_bytes=60 * 1024 * 1024),
-        cost_estimate=cost(0, 2_500_000),
-        name="pack",
+        facing_kernel,
+        in_specs=[SMEM, VMEM, VMEM],
+        out_specs=[VMEM] * 3,
+        out_shape=[
+            shape_of(2, 8, width),
+            shape_of(comps, planes, 8, width),
+            shape_of(cond.shape[0], 8, cond.shape[-1]),
+        ],
+        compiler_params=params(),
+        cost_estimate=cost(0, 1_200_000),
+        name="facing_parts",
     )(info, tiled, cond)
+
+
+def first_sends(info, edges, tiled, disp, fiber):
+    width = tiled.shape[-1]
+    return pl.pallas_call(
+        sends_kernel,
+        in_specs=[SMEM] + [VMEM] * 4,
+        out_specs=[VMEM] * 2,
+        out_shape=[shape_of(SENT, 8, width // 2), shape_of(SENT + FIELD, 8, width // 2)],
+        compiler_params=params(),
+        cost_estimate=cost(0, 1_200_000),
+        name="sends",
+    )(info, edges, tiled, disp, fiber)
 
 
 def fraction(val):
@@ -298,7 +355,7 @@
 
 def halo_terms(halo_ref, coeff_ref, tile, tiles, side, sub, half):
     before, after = (tile - 1) % tiles, (tile + 1) % tiles
-    cur, prv, nxt = halo_ref[tile], halo_ref[before], halo_ref[after]
+    cur, prv, nxt = (load_sent(halo_ref, at, tiles, side) for at in (tile, before, after))
     if tile == 0:
         prv = prv * jnp.where(side == 0, 0.0, 1.0)
     if tile == tiles - 2:
@@ -309,27 +366,29 @@
     return total - cross if half == FAR_HALF else total + cross
 
 
-def add_halo(half, tiles, kept, info_ref, outer_ref, halo_ref, coeff_ref, out_ref):
+def add_halo(half, tiles, kept, info_ref, outer_ref, halo_ref, coeff_ref, out_ref, sent_ref=None):
     side = info_ref[SIDE]
     sub = row_iota()
 
-    def fill():
+    def fill(beyond=True):
         for tile in range(kept):
-            out_ref[tile] = outer_ref[tile] + halo_terms(halo_ref, coeff_ref, tile, tiles, side, sub, half)
+            value = outer_ref[tile]
+            if beyond:
+                value += halo_terms(halo_ref, coeff_ref, tile, tiles, side, sub, half)
+            out_ref[tile] = value
+            if sent_ref is not None:
+                store_sent(sent_ref, tile, tiles, value, side)
 
     if half == NEAR_HALF:
         fill()
     else:
         exists = info_ref[FAR] == 1
         pl.when(exists)(fill)
-
-        @pl.when(jnp.logical_not(exists))
-        def _():
-            out_ref[...] = outer_ref[...]
-
-
-def halo_kernel(half, tiles, info_ref, outer_ref, halo_ref, coeff_ref, out_ref):
-    add_halo(half, tiles, tiles, info_ref, outer_ref, halo_ref, coeff_ref, out_ref)
+        pl.when(jnp.logical_not(exists))(functools.partial(fill, False))
+
+
+def halo_kernel(half, tiles, info_ref, outer_ref, halo_ref, coeff_ref, out_ref, sent_ref):
+    add_halo(half, tiles, tiles, info_ref, outer_ref, halo_ref, coeff_ref, out_ref, sent_ref)
 
 
 def halo_step(half, info, outer, halo, coeffs):
@@ -339,8 +398,8 @@
     return pl.pallas_call(
         functools.partial(halo_kernel, half, tiles),
         in_specs=[pl.BlockSpec(memory_space=pltpu.SMEM)] + [vmem] * 3,
-        out_specs=vmem,
-        out_shape=jax.ShapeDtypeStruct(outer.shape, jnp.float32),
+        out_specs=[vmem, vmem],
+        out_shape=[shape_of(*outer.shape), shape_of(SENT, 8, width // 2)],
         compiler_params=params(),
         cost_estimate=cost(15 * cells, 20 * cells),
         name="halo" + ("_far" if half == FAR_HALF else "_near"),
@@ -403,7 +462,7 @@
 
 
 def finish_half(half, info, arrays, halo, coeffs, tension, active=None, states=None, tension_next=None):
-    tiles, _, width = halo.shape
+    _, tiles, _, width = coeffs.shape
     own = tiles - 1
     active_shape = (own * 2, width // 4)
     vmem, hbm = pl.BlockSpec(memory_space=pltpu.VMEM), pl.BlockSpec(memory_space=pltpu.HBM)
@@ -559,11 +618,14 @@
 
 
 class Planes:
-    def __init__(self, field, slabs, reach):
+    def __init__(self, field, slabs, reach, from_pair=None):
         self.slabs, self.reach = slabs, reach
         self.parts = [field[None]]
-        self.doubling = slabs in (1, 2, 4, 8)
+        self.doubling = slabs in (2, 4, 8)
         self.step = 1
+        if self.doubling and from_pair is not None:
+            self.parts.append(from_pair[None])
+            self.step = 2
 
     def round(self):
         if self.doubling:
@@ -594,14 +656,16 @@
     return jnp.stack([jnp.sin(tilt), jnp.cos(tilt) * jnp.sin(theta), jnp.cos(tilt) * jnp.cos(theta)])
 
 
-def facing_kernel(info_ref, *refs):
+def facing_fields_kernel(info_ref, *refs):
     out_ref = refs[-1]
-    first = pl.multiple_of(8 * (1 - info_ref[SIDE]), 8)
+    upper_side = info_ref[SIDE] == 0
     at = 0
     for ref in refs[:-1]:
         for pos in range(ref.shape[0]):
             for comp in range(ref.shape[1]):
-                out_ref[at, comp] = ref[pos, comp, pl.ds(first, 8), :]
+                both = ref[pos, comp]
+                half = both.shape[-1] // 2
+                out_ref[at, comp] = jnp.where(upper_side, both[:, half:], both[:, :half])
             at += 1
 
 
@@ -610,9 +674,9 @@
     count = sum(field.shape[0] for field in fields)
     vmem = pl.BlockSpec(memory_space=pltpu.VMEM)
     return pl.pallas_call(
-        facing_kernel,
+        facing_fields_kernel,
         in_specs=[pl.BlockSpec(memory_space=pltpu.SMEM)] + [vmem] * len(fields),
-        out_shape=jax.ShapeDtypeStruct((count, comps, 8, width), jnp.float32),
+        out_shape=shape_of(count, comps, 8, width // 2),
         compiler_params=params(),
         cost_estimate=cost(0, 600_000),
         name="facing",
@@ -622,7 +686,8 @@
 def passive_kernel(planes, info_ref, table_ref, strip_ref, *refs):
     own_refs, (disp_out, stress_out, pull_out, disp_all, field) = refs[:-5], refs[-5:]
     slab, slabs = info_ref[SLAB], planes.slabs
-    own, width = own_refs[0].shape[-2:]
+    width = strip_ref.shape[-1]
+    own = ROWS - 8
     k = Weights(info_ref[SIDE], own, width)
     reach = REACH + 1
 
@@ -630,8 +695,8 @@
     for ref in own_refs:
         for pos in range(ref.shape[0]):
             for comp in range(ref.shape[1]):
-                field[at, comp, :own] = ref[pos, comp]
-                field[at, comp, own:] = strip_ref[at, comp]
+                both = ref[pos, comp]
+                field[at, comp] = jnp.concatenate([both[:, :width], both[:, width:], strip_ref[at, comp]], axis=0)
             at += 1
 
     def plane(comp, offset):
@@ -790,15 +855,14 @@
     swap = [(0, 1), (1, 0)]
 
     tiled = states.reshape(4, planes, own, 8, width)
-    fields = Planes(jnp.concatenate([disp[:, 0], fiber.astype(jnp.float32)], axis=0), slabs, REACH + 1)
-    far, near, edges, facing, cond_rows = pack(info, tiled, cond)
+    edges, facing, cond_rows = facing_parts(info, tiled, cond)
     edges = lax.ppermute(edges, "col", swap)
-    fields.round()
-    edges, *fields.parts = tie(edges, *fields.parts)
-    far_halo = lax.ppermute(jnp.concatenate([far, edges[:1]], axis=0), "slab", others)
-    near_halo = lax.ppermute(jnp.concatenate([near, edges[1:]], axis=0), "slab", pairs)
+    cond_strip = lax.ppermute(cond_rows, "col", swap)
     strip = lax.ppermute(facing, "col", swap)
-    cond_strip = lax.ppermute(cond_rows, "col", swap)
+    far, near = first_sends(info, edges, tiled, disp, fiber)
+    far_halo = lax.ppermute(far, "slab", others)
+    near_halo = lax.ppermute(near, "slab", pairs)
+    fields = Planes(near[SENT:], slabs, REACH + 1, near_halo[SENT:])
 
     coeffs = fine_coeffs(info, cond, cond_strip)
     whole = jnp.concatenate([tiled, strip[:, :, None]], axis=2)
@@ -807,16 +871,16 @@
     near_part, near_inner, near_gates = half_step("first", NEAR_HALF, info, (whole,), coeffs)
     for turn_index in range(1, SUB):
         last = turn_index == SUB - 1
-        far = halo_step(FAR_HALF, info, far_part, far_halo, coeffs)
-        far_halo = lax.ppermute(far, "slab", others)
-        if not last:
-            (near_part, *fields.parts) = tie(near_part, *fields.parts)
-            fields.round()
+        far, far_send = halo_step(FAR_HALF, info, far_part, far_halo, coeffs)
+        far_halo = lax.ppermute(far_send, "slab", others)
         far_arrays = (far, far_inner, near_inner, far_gates)
         kind = "last" if last else "middle"
         far_part, far_next, far_gates = half_step(kind, FAR_HALF, info, far_arrays, coeffs)
-        near = halo_step(NEAR_HALF, info, near_part, near_halo, coeffs)
-        near_halo = lax.ppermute(near, "slab", pairs)
+        near, near_send = halo_step(NEAR_HALF, info, near_part, near_halo, coeffs)
+        near_halo = lax.ppermute(near_send, "slab", pairs)
+        if not last:
+            near, *fields.parts = tie(near, *fields.parts)
+            fields.round()
         near_arrays = (near, near_inner, far_inner, near_gates)
         near_part, near_inner, near_gates = half_step(kind, NEAR_HALF, info, near_arrays, coeffs)
         far_inner = far_next

time: 95 us -> 96.4 us (1.015)
  waiting for transfers between devices: 8.33 us -> 19.7 us
  starting transfers between devices: 37.4 us -> 28.7 us
  local copies, waits for them, and re-layouts: 0.03 us -> 3.11 us
  other arithmetic: 3.4 us -> 1.02 us
  Pallas kernels: 44.6 us -> 42.7 us
    ppermute x2 -> x6, starting transfers between devices: 5.39 us -> 19.8 us  [the longest x3 17.7 us: on_device(): near_halo = lax.ppermute(near_send, 'slab', pairs)]
    ppermute x3 -> x1, starting transfers between devices: 16.6 us -> 2.92 us  [on_device(): near_halo = lax.ppermute(near, 'slab', pairs)]
    ppermute x6 -> x5, waiting for transfers between devices: 5.7 us -> 14.9 us  [round(): self.parts.append(lax.ppermute(held, 'slab', perm))]
    ppermute x6 -> x5, starting transfers between devices: 12.5 us -> 4.41 us  [round(): self.parts.append(lax.ppermute(held, 'slab', perm))]
    unnamed x12 -> x14, local copies, waits for them, and re-layouts: 0.02 us -> 3.1 us
    concatenate x2 -> x0, other arithmetic: 2.09 us -> none  [the longest x1 1.12 us: on_device(): jnp.concatenate([far, edges[:1]], axis=0)]
    pallas_call x2 -> x3, Pallas kernels: 3.64 us -> 1.74 us  [the longest x1 0.59 us: facing_parts(): pl.pallas_call(facing_kernel, in_specs=[SMEM, VMEM, VMEM], out_specs=[VME...]
    ppermute x3 -> x1, waiting for transfers between devices: 0.01 us -> 1.55 us  [on_device(): near_halo = lax.ppermute(near, 'slab', pairs)]
  transfers between devices with their start and end apart: 19 -> 18, of which waited for: 6 -> 8; matrix products, arithmetic and copies ran while one was open for 3% -> 1% of each run, Pallas kernels for 39% -> 40%
where the time goes in v5:
time: 96.4 us; the launch traced here: 96.1 us
  Pallas kernels  42.7 us (44%)
  starting transfers between devices  28.7 us (30%)
  waiting for transfers between devices  19.7 us (20%)
  local copies, waits for them, and re-layouts  3.11 us (3%)
  other arithmetic  1.02 us (1%)
  between operations  0.98 us (1%)
    pallas_call x8, Pallas kernels, half_step(): pl.pallas_call(functools.partial(half_kernel, kind, half, tiles), in_spec...  22.6 us
    ppermute x3, starting transfers between devices, on_device(): near_halo = lax.ppermute(near_send, 'slab', pairs)  17.7 us
    ppermute x5, waiting for transfers between devices, round(): self.parts.append(lax.ppermute(held, 'slab', perm))  14.9 us
    ppermute x5, starting transfers between devices, round(): self.parts.append(lax.ppermute(held, 'slab', perm))  4.41 us
    pallas_call x2, Pallas kernels, finish_half(): pl.pallas_call(functools.partial(finish_kernel, half, tiles), in_specs=in...  4.24 us
    pallas_call x1, Pallas kernels, mechanics_step(): pl.pallas_call(functools.partial(mechanics_kernel, planes), in_specs=[pl....  4.11 us
    pallas_call x6, Pallas kernels, halo_step(): pl.pallas_call(functools.partial(halo_kernel, half, tiles), in_specs=[pl....  4.07 us
    unnamed x14, local copies, waits for them, and re-layouts  3.1 us
  transfers between devices with their start and end apart: 18, of which 8 were waited for; matrix products, arithmetic and copies ran while one was open for 1% of the time, Pallas kernels for 40%

profile of v5, /device:TPU:0, one launch (start us, length us, event | category | flops | bytes accessed | tf_op | source)
XLA Modules:
  0.0 96.1 jit_solution(4053130988784748258)
XLA Ops:
  0.7 2.2 %copy-done = f32[4,4,64,1024]{3,2,1,0:T(8,128)S(1)} copy-done((f32[4,4,64,1024]{3,2,1,0:T(8,128)S(1)}, f32[4,4,64,1024]{3,2,1,0:T(8,128)}, u32[]{:S(2)}) %copy-start) | copy-done | bytes 4194328
  7.2 2.9 %collective-permute-start.3 = (f32[21,8,512]{2,1,0:T(8,128)S(1)}, f32[21,8,512]{2,1,0:T(8,128)S(1)}, u32[]{:S(2)}, u32[]{:S(2)}) collective-permute-start(f32[21,8,512]{2,1,0:T(8,128)S(1)} %get-tuple-element.68), channel_id=1, source_target_pairs={{0,2},{2,0},{4,6},{6,4},{8,10},{10,8},{12,14},{14,12},{1,3},{3,1},... | collective-permute-start | bytes 1032200 | tf_op jit(solution)/shard_map/ppermute | solution.py:864
  11.3 3.0 %coeffs.1.refs_1_.coeff_ref.refs_4_ = f32[10,9,8,1024]{3,2,1,0:T(8,128)S(1)} custom-call(s32[4]{0:T(128)S(1)} %pad_add_fusion.info_ref, f32[6,1,16,256]{3,2,1,0:T(8,128)S(1)} %copy-done.4, f32[6,8,256]{2,1,0:T(8,128)S(1)} %collective-permute-done.1.strip_ref), custom_call_target="tpu_custom_call" | custom-call | flops 2000000 | bytes 3200000 | tf_op jit(solution)/shard_map/coeffs/pallas_call | solution.py:116
  15.0 2.9 %first_far.1 = (f32[9,8,1024]{2,1,0:T(8,128)S(1)}, f32[9,8,1024]{2,1,0:T(8,128)S(1)}, f32[3,2,9,8,1024]{4,3,2,1,0:T(8,128)S(1)}) custom-call(s32[4]{0:T(128)S(1)} %pad_add_fusion.info_ref, f32[4,4,9,8,1024]{4,3,2,1,0:T(8,128)S(1)} %pad_maximum_fusion.refs_0_, f32[10,9,8,1024]{3,2,1,0:T(8,128)S(1)} %coeffs.1.refs_1_.coeff_ref.refs_4_), custom_call_target="tpu_custom_call" | custom-call | flops 14745600 | bytes 5898240 | tf_op jit(solution)/shard_map/first_far/pallas_call | solution.py:345
  19.2 2.9 %first_near.1 = (f32[9,8,1024]{2,1,0:T(8,128)S(1)}, f32[9,8,1024]{2,1,0:T(8,128)S(1)}, f32[3,2,9,8,1024]{4,3,2,1,0:T(8,128)S(1)}) custom-call(s32[4]{0:T(128)S(1)} %pad_add_fusion.info_ref, f32[4,4,9,8,1024]{4,3,2,1,0:T(8,128)S(1)} %pad_maximum_fusion.refs_0_, f32[10,9,8,1024]{3,2,1,0:T(8,128)S(1)} %coeffs.1.refs_1_.coeff_ref.refs_4_), custom_call_target="tpu_custom_call" | custom-call | flops 14745600 | bytes 5898240 | tf_op jit(solution)/shard_map/first_near/pallas_call | solution.py:345
  22.1 1.5 %collective-permute-done.3.halo_ref = f32[21,8,512]{2,1,0:T(8,128)S(1)} collective-permute-done((f32[21,8,512]{2,1,0:T(8,128)S(1)}, f32[21,8,512]{2,1,0:T(8,128)S(1)}, u32[]{:S(2)}, u32[]{:S(2)}) %collective-permute-start.3) | collective-permute-done | bytes 344096 | tf_op jit(solution)/shard_map/ppermute | solution.py:864
  24.4 7.1 %collective-permute-start.4 = (f32[17,8,512]{2,1,0:T(8,128)S(1)}, f32[17,8,512]{2,1,0:T(8,128)S(1)}, u32[]{:S(2)}, u32[]{:S(2)}) collective-permute-start(f32[17,8,512]{2,1,0:T(8,128)S(1)} %get-tuple-element.75), channel_id=1, source_target_pairs={{0,2},{2,0},{4,6},{6,4},{8,10},{10,8},{12,14},{14,12},{1,3},{3,1},... | collective-permute-start | bytes 835592 | tf_op jit(solution)/shard_map/ppermute | solution.py:880
  31.6 2.9 %middle_far.2 = (f32[9,8,1024]{2,1,0:T(8,128)S(1)}, f32[9,8,1024]{2,1,0:T(8,128)S(1)}, f32[3,2,9,8,1024]{4,3,2,1,0:T(8,128)S(1)}) custom-call(s32[4]{0:T(128)S(1)} %pad_add_fusion.info_ref, f32[9,8,1024]{2,1,0:T(8,128)S(1)} %get-tuple-element.83.refs_0_, f32[9,8,1024]{2,1,0:T(8,128)S(1)} %get-tuple-element.72.refs_2_.refs_1_, ...), custom_call_target="tpu_custom_call" | custom-call | flops 14745600 | bytes 5898240 | tf_op jit(solution)/shard_map/middle_far/pallas_call | solution.py:345
  35.7 2.9 %middle_near.2 = (f32[9,8,1024]{2,1,0:T(8,128)S(1)}, f32[9,8,1024]{2,1,0:T(8,128)S(1)}, f32[3,2,9,8,1024]{4,3,2,1,0:T(8,128)S(1)}) custom-call(s32[4]{0:T(128)S(1)} %pad_add_fusion.info_ref, f32[9,8,1024]{2,1,0:T(8,128)S(1)} %get-tuple-element.70.refs_0_, f32[9,8,1024]{2,1,0:T(8,128)S(1)} %get-tuple-element.71.refs_1_.refs_2_, ...), custom_call_target="tpu_custom_call" | custom-call | flops 14745600 | bytes 5898240 | tf_op jit(solution)/shard_map/middle_near/pallas_call | solution.py:345
  39.4 7.7 %collective-permute-start.7 = (f32[17,8,512]{2,1,0:T(8,128)S(1)}, f32[17,8,512]{2,1,0:T(8,128)S(1)}, u32[]{:S(2)}, u32[]{:S(2)}) collective-permute-start(f32[17,8,512]{2,1,0:T(8,128)S(1)} %get-tuple-element.88), channel_id=1, source_target_pairs={{0,2},{2,0},{4,6},{6,4},{8,10},{10,8},{12,14},{14,12},{1,3},{3,1},... | collective-permute-start | bytes 835592 | tf_op jit(solution)/shard_map/ppermute | solution.py:880
  47.2 5.0 %collective-permute-done.5.refs_2_ = f32[2,4,8,512]{3,2,1,0:T(8,128)S(1)} collective-permute-done((f32[2,4,8,512]{3,2,1,0:T(8,128)S(1)}, f32[2,4,8,512]{3,2,1,0:T(8,128)S(1)}, u32[]{:S(2)}, u32[]{:S(2)}) %collective-permute-start.5) | collective-permute-done | bytes 131104 | tf_op jit(solution)/shard_map/ppermute | solution.py:635
  52.1 2.9 %middle_far.3 = (f32[9,8,1024]{2,1,0:T(8,128)S(1)}, f32[9,8,1024]{2,1,0:T(8,128)S(1)}, f32[3,2,9,8,1024]{4,3,2,1,0:T(8,128)S(1)}) custom-call(s32[4]{0:T(128)S(1)} %pad_add_fusion.info_ref, f32[9,8,1024]{2,1,0:T(8,128)S(1)} %get-tuple-element.93.refs_0_, f32[9,8,1024]{2,1,0:T(8,128)S(1)} %get-tuple-element.85.refs_2_.refs_1_, ...), custom_call_target="tpu_custom_call" | custom-call | flops 14745600 | bytes 5898240 | tf_op jit(solution)/shard_map/middle_far/pallas_call | solution.py:345
  56.3 2.9 %middle_near.3 = (f32[9,8,1024]{2,1,0:T(8,128)S(1)}, f32[9,8,1024]{2,1,0:T(8,128)S(1)}, f32[3,2,9,8,1024]{4,3,2,1,0:T(8,128)S(1)}) custom-call(s32[4]{0:T(128)S(1)} %pad_add_fusion.info_ref, f32[9,8,1024]{2,1,0:T(8,128)S(1)} %get-tuple-element.79.refs_0_, f32[9,8,1024]{2,1,0:T(8,128)S(1)} %get-tuple-element.80.refs_1_.refs_2_, ...), custom_call_target="tpu_custom_call" | custom-call | flops 14745600 | bytes 5898240 | tf_op jit(solution)/shard_map/middle_near/pallas_call | solution.py:345
  60.0 3.0 %collective-permute-start.9 = (f32[17,8,512]{2,1,0:T(8,128)S(1)}, f32[17,8,512]{2,1,0:T(8,128)S(1)}, u32[]{:S(2)}, u32[]{:S(2)}) collective-permute-start(f32[17,8,512]{2,1,0:T(8,128)S(1)} %get-tuple-element.100), channel_id=1, source_target_pairs={{0,2},{2,0},{4,6},{6,4},{8,10},{10,8},{12,14},{14,12},{1,3},{3,1},... | collective-permute-start | bytes 835592 | tf_op jit(solution)/shard_map/ppermute | solution.py:880
  63.0 4.2 %collective-permute-start.12 = (f32[4,4,8,512]{3,2,1,0:T(8,128)S(1)}, f32[4,4,8,512]{3,2,1,0:T(8,128)S(1)}, u32[]{:S(2)}, u32[]{:S(2)}) collective-permute-start(f32[4,4,8,512]{3,2,1,0:T(8,128)S(1)} %pad_maximum_fusion.1), channel_id=1, source_target_pairs={{0,8},{2,10},{4,12},{6,14},{8,0},{10,2},{12,4},{14,6},{1,9},{3,11}... | collective-permute-start | bytes 786440 | tf_op jit(solution)/shard_map/ppermute | solution.py:635
  67.2 2.6 %last_far.1 = (f32[8,8,1024]{2,1,0:T(8,128)S(1)}, f32[8,8,1024]{2,1,0:T(8,128)S(1)}, f32[3,2,8,8,1024]{4,3,2,1,0:T(8,128)S(1)}) custom-call(s32[4]{0:T(128)S(1)} %pad_add_fusion.info_ref, f32[9,8,1024]{2,1,0:T(8,128)S(1)} %get-tuple-element.103.refs_0_, f32[9,8,1024]{2,1,0:T(8,128)S(1)} %get-tuple-element.95.refs_2_.refs_1_, ...), custom_call_target="tpu_custom_call" | custom-call | flops 14745600 | bytes 5898240 | tf_op jit(solution)/shard_map/last_far/pallas_call | solution.py:345
  69.9 2.6 %last_near.1 = (f32[8,8,1024]{2,1,0:T(8,128)S(1)}, f32[8,8,1024]{2,1,0:T(8,128)S(1)}, f32[3,2,8,8,1024]{4,3,2,1,0:T(8,128)S(1)}) custom-call(s32[4]{0:T(128)S(1)} %pad_add_fusion.info_ref, f32[9,8,1024]{2,1,0:T(8,128)S(1)} %get-tuple-element.89.refs_0_, f32[9,8,1024]{2,1,0:T(8,128)S(1)} %get-tuple-element.90.refs_1_.refs_2_, ...), custom_call_target="tpu_custom_call" | custom-call | flops 14745600 | bytes 5898240 | tf_op jit(solution)/shard_map/last_near/pallas_call | solution.py:345
  72.5 1.9 %finish_far.1 = (f32[4,4,8,8,1024]{4,3,2,1,0:T(8,128)}, f32[2,32,512]{2,1,0:T(8,128)}, f32[16,256]{1,0:T(8,128)S(1)}) custom-call(s32[4]{0:T(128)S(1)} %pad_add_fusion.info_ref, f32[8,8,1024]{2,1,0:T(8,128)S(1)} %get-tuple-element.105.outer_ref, f32[8,8,1024]{2,1,0:T(8,128)S(1)} %get-tuple-element.106.inner_ref, ...), custom_call_target="tpu_custom_call" | custom-call | flops 2621440 | bytes 2621440 | tf_op jit(solution)/shard_map/finish_far/pallas_call | solution.py:485
  74.5 2.3 %finish_near.1 = (f32[4,4,8,8,1024]{4,3,2,1,0:T(8,128)}, f32[2,32,512]{2,1,0:T(8,128)}, f32[16,256]{1,0:T(8,128)S(1)}, f32[8,256]{1,0:T(8,128)S(1)}) custom-call(s32[4]{0:T(128)S(1)} %pad_add_fusion.info_ref, f32[8,8,1024]{2,1,0:T(8,128)S(1)} %get-tuple-element.97.outer_ref, ...), custom_call_target="tpu_custom_call", output_to_operand_aliasing={{0}: (8, {}), {1}: (9, {})} | custom-call | flops 2621440 | bytes 2621440 | tf_op jit(solution)/shard_map/finish_near/pallas_call | solution.py:485
  78.9 2.9 %collective-permute-done.15.rest_1_ = f32[1,24,256]{2,1,0:T(8,128)S(1)} collective-permute-done((f32[1,24,256]{2,1,0:T(8,128)S(1)}, f32[1,24,256]{2,1,0:T(8,128)S(1)}, u32[]{:S(2)}, u32[]{:S(2)}) %collective-permute-start.15) | collective-permute-done | bytes 24608 | tf_op jit(solution)/shard_map/ppermute | solution.py:635
  82.0 4.0 %collective-permute-done.16.rest_2_ = f32[2,24,256]{2,1,0:T(8,128)S(1)} collective-permute-done((f32[2,24,256]{2,1,0:T(8,128)S(1)}, f32[2,24,256]{2,1,0:T(8,128)S(1)}, u32[]{:S(2)}, u32[]{:S(2)}) %collective-permute-start.16) | collective-permute-done | bytes 49184 | tf_op jit(solution)/shard_map/ppermute | solution.py:635
  86.1 3.0 %passive.1 = (f32[6,9,24,256]{3,2,1,0:T(8,128)S(1)}, f32[9,9,24,256]{3,2,1,0:T(8,128)S(1)}, f32[9,9,24,256]{3,2,1,0:T(8,128)S(1)}) custom-call(s32[4]{0:T(128)S(1)} %pad_add_fusion.info_ref, f32[3,128]{1,0:T(4,128)S(1)} %pad_maximum_fusion.5.table_ref, f32[8,4,8,256]{3,2,1,0:T(8,128)S(1)} %collective-permute-done.13.strip_ref, ...), custom_call_target="tpu_custom_call" | custom-call | flops 22118400 | bytes 5000000 | tf_op jit(solution)/shard_map/passive/pallas_call | solution.py:745
  89.0 3.0 %collective-permute-done.17.rest_3_ = f32[4,24,256]{2,1,0:T(8,128)S(1)} collective-permute-done((f32[4,24,256]{2,1,0:T(8,128)S(1)}, f32[4,24,256]{2,1,0:T(8,128)S(1)}, u32[]{:S(2)}, u32[]{:S(2)}) %collective-permute-start.17) | collective-permute-done | bytes 98336 | tf_op jit(solution)/shard_map/ppermute | solution.py:635
  92.0 4.1 %mechanics.1 = (f32[3,1,16,256]{3,2,1,0:T(8,128)}, f32[6,1,16,256]{3,2,1,0:T(8,128)}) custom-call(s32[4]{0:T(128)S(1)} %pad_add_fusion.info_ref, f32[6,9,24,256]{3,2,1,0:T(8,128)S(1)} %get-tuple-element.117.disp_ref, f32[9,9,24,256]{3,2,1,0:T(8,128)S(1)} %get-tuple-element.118.stress_ref, f32[9,9,24,256]{3,2,1,0:T(8,128)S(1)} %get-tuple-element.119.pull_ref, ...), custom_call_target="tpu_custom_call" | custom-call | flops 22118400 | bytes 5000000 | tf_op jit(solution)/shard_map/mechanics/pallas_call | solution.py:822
  (60 shorter events, 14.8 us)
Async XLA Ops:
  0.7 2.2 %copy-start = (f32[4,4,64,1024]{3,2,1,0:T(8,128)S(1)}, f32[4,4,64,1024]{3,2,1,0:T(8,128)}, u32[]{:S(2)}) copy-start(f32[4,4,64,1024]{3,2,1,0:T(8,128)} %param.5) | copy-start | bytes 12582916
  3.8 2.8 %copy-start.5 = (f32[3,1,16,256]{3,2,1,0:T(8,128)S(1)}, f32[3,1,16,256]{3,2,1,0:T(8,128)}, u32[]{:S(2)}) copy-start(f32[3,1,16,256]{3,2,1,0:T(8,128)} %disp_ref.1) | copy-start | bytes 147460
  3.8 2.8 %copy-start.6 = (s32[1,16,256]{2,1,0:T(8,128)S(1)}, s32[1,16,256]{2,1,0:T(8,128)}, u32[]{:S(2)}) copy-start(s32[1,16,256]{2,1,0:T(8,128)} %fiber_ref.1) | copy-start | bytes 49156
  4.4 9.9 %collective-permute-start = (f32[4,4,8,1024]{3,2,1,0:T(8,128)S(1)}, f32[4,4,8,1024]{3,2,1,0:T(8,128)S(1)}, u32[]{:S(2)}, u32[]{:S(2)}) collective-permute-start(f32[4,4,8,1024]{3,2,1,0:T(8,128)S(1)} %get-tuple-element.64), channel_id=1, source_target_pairs={{0,1},{1,0},{2,3},{3,2},{4,5},{5,4},{6,7},{7,6},{8,9},{9,8},{10,11... | collective-permute-start | bytes 1572872 | tf_op jit(solution)/shard_map/ppermute | solution.py:861
  4.9 6.4 %copy-start.4 = (f32[6,1,16,256]{3,2,1,0:T(8,128)S(1)}, f32[6,1,16,256]{3,2,1,0:T(8,128)}, u32[]{:S(2)}) copy-start(f32[6,1,16,256]{3,2,1,0:T(8,128)} %cond_ref.3) | copy-start | bytes 294916
  4.9 1.6 %collective-permute-start.2 = (f32[2,8,1024]{2,1,0:T(8,128)S(1)}, f32[2,8,1024]{2,1,0:T(8,128)S(1)}, u32[]{:S(2)}, u32[]{:S(2)}) collective-permute-start(f32[2,8,1024]{2,1,0:T(8,128)S(1)} %get-tuple-element.67), channel_id=1, source_target_pairs={{0,1},{1,0},{2,3},{3,2},{4,5},{5,4},{6,7},{7,6},{8,9},{9,8},{10,11... | collective-permute-start | bytes 196616 | tf_op jit(solution)/shard_map/ppermute | solution.py:859
  6.6 7.7 %copy-start.1 = (f32[4,4,64,1024]{3,2,1,0:T(8,128)S(1)}, f32[4,4,64,1024]{3,2,1,0:T(8,128)}, u32[]{:S(2)}) copy-start(f32[4,4,64,1024]{3,2,1,0:T(8,128)} %param.5) | copy-start | bytes 12582916
  7.2 16.5 %collective-permute-start.3 = (f32[21,8,512]{2,1,0:T(8,128)S(1)}, f32[21,8,512]{2,1,0:T(8,128)S(1)}, u32[]{:S(2)}, u32[]{:S(2)}) collective-permute-start(f32[21,8,512]{2,1,0:T(8,128)S(1)} %get-tuple-element.68), channel_id=1, source_target_pairs={{0,2},{2,0},{4,6},{6,4},{8,10},{10,8},{12,14},{14,12},{1,3},{3,1},... | collective-permute-start | bytes 1032200 | tf_op jit(solution)/shard_map/ppermute | solution.py:864
  10.1 1.2 %collective-permute-start.1 = (f32[6,8,256]{2,1,0:T(8,128)S(1)}, f32[6,8,256]{2,1,0:T(8,128)S(1)}, u32[]{:S(2)}, u32[]{:S(2)}) collective-permute-start(f32[6,8,256]{2,1,0:T(8,128)S(1)} %get-tuple-element.65), channel_id=1, source_target_pairs={{0,1},{1,0},{2,3},{3,2},{4,5},{5,4},{6,7},{7,6},{8,9},{9,8},{10,11... | collective-permute-start | bytes 147464 | tf_op jit(solution)/shard_map/ppermute | solution.py:860
  10.1 7.8 %collective-permute-start.6 = (f32[17,8,512]{2,1,0:T(8,128)S(1)}, f32[17,8,512]{2,1,0:T(8,128)S(1)}, u32[]{:S(2)}, u32[]{:S(2)}) collective-permute-start(f32[17,8,512]{2,1,0:T(8,128)S(1)} %get-tuple-element.82), channel_id=1, source_target_pairs={{0,0},{2,4},{4,2},{6,8},{8,6},{10,12},{12,10},{14,14},{1,1},{3,5},... | collective-permute-start | bytes 835592 | tf_op jit(solution)/shard_map/ppermute | solution.py:863
  18.5 15.9 %collective-permute-start.8 = (f32[17,8,512]{2,1,0:T(8,128)S(1)}, f32[17,8,512]{2,1,0:T(8,128)S(1)}, u32[]{:S(2)}, u32[]{:S(2)}) collective-permute-start(f32[17,8,512]{2,1,0:T(8,128)S(1)} %get-tuple-element.92), channel_id=1, source_target_pairs={{0,0},{2,4},{4,2},{6,8},{8,6},{10,12},{12,10},{14,14},{1,1},{3,5},... | collective-permute-start | bytes 835592 | tf_op jit(solution)/shard_map/ppermute | solution.py:875
  24.4 14.2 %collective-permute-start.4 = (f32[17,8,512]{2,1,0:T(8,128)S(1)}, f32[17,8,512]{2,1,0:T(8,128)S(1)}, u32[]{:S(2)}, u32[]{:S(2)}) collective-permute-start(f32[17,8,512]{2,1,0:T(8,128)S(1)} %get-tuple-element.75), channel_id=1, source_target_pairs={{0,2},{2,0},{4,6},{6,4},{8,10},{10,8},{12,14},{14,12},{1,3},{3,1},... | collective-permute-start | bytes 835592 | tf_op jit(solution)/shard_map/ppermute | solution.py:880
  35.1 20.0 %collective-permute-start.10 = (f32[17,8,512]{2,1,0:T(8,128)S(1)}, f32[17,8,512]{2,1,0:T(8,128)S(1)}, u32[]{:S(2)}, u32[]{:S(2)}) collective-permute-start(f32[17,8,512]{2,1,0:T(8,128)S(1)} %get-tuple-element.102), channel_id=1, source_target_pairs={{0,0},{2,4},{4,2},{6,8},{8,6},{10,12},{12,10},{14,14},{1,1},{3,5},... | collective-permute-start | bytes 835592 | tf_op jit(solution)/shard_map/ppermute | solution.py:875
  39.4 19.8 %collective-permute-start.7 = (f32[17,8,512]{2,1,0:T(8,128)S(1)}, f32[17,8,512]{2,1,0:T(8,128)S(1)}, u32[]{:S(2)}, u32[]{:S(2)}) collective-permute-start(f32[17,8,512]{2,1,0:T(8,128)S(1)} %get-tuple-element.88), channel_id=1, source_target_pairs={{0,2},{2,0},{4,6},{6,4},{8,10},{10,8},{12,14},{14,12},{1,3},{3,1},... | collective-permute-start | bytes 835592 | tf_op jit(solution)/shard_map/ppermute | solution.py:880
  47.1 5.0 %collective-permute-start.5 = (f32[2,4,8,512]{3,2,1,0:T(8,128)S(1)}, f32[2,4,8,512]{3,2,1,0:T(8,128)S(1)}, u32[]{:S(2)}, u32[]{:S(2)}) collective-permute-start(f32[2,4,8,512]{3,2,1,0:T(8,128)S(1)} %pad_maximum_fusion.2), channel_id=1, source_target_pairs={{0,4},{2,6},{4,0},{6,2},{8,12},{10,14},{12,8},{14,10},{1,5},{3,7},... | collective-permute-start | bytes 393224 | tf_op jit(solution)/shard_map/ppermute | solution.py:635
  55.6 16.9 %collective-permute-start.11 = (f32[17,8,512]{2,1,0:T(8,128)S(1)}, f32[17,8,512]{2,1,0:T(8,128)S(1)}, u32[]{:S(2)}, u32[]{:S(2)}) collective-permute-start(f32[17,8,512]{2,1,0:T(8,128)S(1)} %get-tuple-element.108), channel_id=1, source_target_pairs={{0,0},{2,4},{4,2},{6,8},{8,6},{10,12},{12,10},{14,14},{1,1},{3,5},... | collective-permute-start | bytes 835592 | tf_op jit(solution)/shard_map/ppermute | solution.py:875
  60.0 14.5 %collective-permute-start.9 = (f32[17,8,512]{2,1,0:T(8,128)S(1)}, f32[17,8,512]{2,1,0:T(8,128)S(1)}, u32[]{:S(2)}, u32[]{:S(2)}) collective-permute-start(f32[17,8,512]{2,1,0:T(8,128)S(1)} %get-tuple-element.100), channel_id=1, source_target_pairs={{0,2},{2,0},{4,6},{6,4},{8,10},{10,8},{12,14},{14,12},{1,3},{3,1},... | collective-permute-start | bytes 835592 | tf_op jit(solution)/shard_map/ppermute | solution.py:880
  63.0 15.1 %collective-permute-start.12 = (f32[4,4,8,512]{3,2,1,0:T(8,128)S(1)}, f32[4,4,8,512]{3,2,1,0:T(8,128)S(1)}, u32[]{:S(2)}, u32[]{:S(2)}) collective-permute-start(f32[4,4,8,512]{3,2,1,0:T(8,128)S(1)} %pad_maximum_fusion.1), channel_id=1, source_target_pairs={{0,8},{2,10},{4,12},{6,14},{8,0},{10,2},{12,4},{14,6},{1,9},{3,11}... | collective-permute-start | bytes 786440 | tf_op jit(solution)/shard_map/ppermute | solution.py:635
  69.8 2.7 %copy-start.2 = (f32[2,32,512]{2,1,0:T(8,128)S(1)}, f32[2,32,512]{2,1,0:T(8,128)}, u32[]{:S(2)}) copy-start(f32[2,32,512]{2,1,0:T(8,128)} %tension_ref.3) | copy-start | bytes 393220
  76.8 1.2 %collective-permute-start.14 = (f32[8,256]{1,0:T(8,128)S(1)}, f32[8,256]{1,0:T(8,128)S(1)}, u32[]{:S(2)}, u32[]{:S(2)}) collective-permute-start(f32[8,256]{1,0:T(8,128)S(1)} %get-tuple-element.121), channel_id=1, source_target_pairs={{0,1},{1,0},{2,3},{3,2},{4,5},{5,4},{6,7},{7,6},{8,9},{9,8},{10,11... | collective-permute-start | bytes 24584 | tf_op jit(solution)/shard_map/ppermute | solution.py:895
  78.0 3.8 %collective-permute-start.15 = (f32[1,24,256]{2,1,0:T(8,128)S(1)}, f32[1,24,256]{2,1,0:T(8,128)S(1)}, u32[]{:S(2)}, u32[]{:S(2)}) collective-permute-start(f32[1,24,256]{2,1,0:T(8,128)S(1)} %maximum_bitcast_fusion.rest_0_), channel_id=1, source_target_pairs={{0,2},{2,0},{4,6},{6,4},{8,10},{10,8},{12,14},{14,12},{1,3},{3,1},... | collective-permute-start | bytes 73736 | tf_op jit(solution)/shard_map/ppermute | solution.py:635
  78.7 7.3 %collective-permute-start.13 = (f32[8,4,8,256]{3,2,1,0:T(8,128)S(1)}, f32[8,4,8,256]{3,2,1,0:T(8,128)S(1)}, u32[]{:S(2)}, u32[]{:S(2)}) collective-permute-start(f32[8,4,8,256]{3,2,1,0:T(8,128)S(1)} %facing.1), channel_id=1, source_target_pairs={{0,1},{1,0},{2,3},{3,2},{4,5},{5,4},{6,7},{7,6},{8,9},{9,8},{10,11... | collective-permute-start | bytes 786440 | tf_op jit(solution)/shard_map/ppermute | solution.py:887
  81.9 4.1 %collective-permute-start.16 = (f32[2,24,256]{2,1,0:T(8,128)S(1)}, f32[2,24,256]{2,1,0:T(8,128)S(1)}, u32[]{:S(2)}, u32[]{:S(2)}) collective-permute-start(f32[2,24,256]{2,1,0:T(8,128)S(1)} %pad_maximum_fusion.4), channel_id=1, source_target_pairs={{0,4},{2,6},{4,0},{6,2},{8,12},{10,14},{12,8},{14,10},{1,5},{3,7},... | collective-permute-start | bytes 147464 | tf_op jit(solution)/shard_map/ppermute | solution.py:635
  86.0 6.1 %collective-permute-start.17 = (f32[4,24,256]{2,1,0:T(8,128)S(1)}, f32[4,24,256]{2,1,0:T(8,128)S(1)}, u32[]{:S(2)}, u32[]{:S(2)}) collective-permute-start(f32[4,24,256]{2,1,0:T(8,128)S(1)} %pad_maximum_fusion.3), channel_id=1, source_target_pairs={{0,8},{2,10},{4,12},{6,14},{8,0},{10,2},{12,4},{14,6},{1,9},{3,11}... | collective-permute-start | bytes 294920 | tf_op jit(solution)/shard_map/ppermute | solution.py:635
  (1 other events, 0.9 us)

commit v6 on v5

--- a/solution.py
+++ b/solution.py
@@ -174,17 +174,35 @@
         cond_rows[comp] = cond_ref[comp, 0, pl.ds(first, 8), :]
 
 
-def sends_kernel(info_ref, edge_ref, states_ref, disp_ref, fiber_ref, far_ref, near_ref):
+def field_kernel(disp_ref, fiber_ref, field_ref):
+    for comp in range(3):
+        field_ref[comp] = jnp.concatenate([disp_ref[comp, 0, :8], disp_ref[comp, 0, 8:]], axis=1)
+    index = fiber_ref[0].astype(jnp.float32)
+    field_ref[3] = jnp.concatenate([index[:8], index[8:]], axis=1)
+
+
+def own_field(disp, fiber):
+    return pl.pallas_call(
+        field_kernel,
+        in_specs=[VMEM] * 2,
+        out_specs=VMEM,
+        out_shape=shape_of(FIELD, 8, 2 * disp.shape[-1]),
+        compiler_params=params(),
+        cost_estimate=cost(0, 130_000),
+        name="own_field",
+    )(disp, fiber)
+
+
+def sends_kernel(info_ref, edge_ref, states_ref, *refs):
+    field_refs, (far_ref, near_ref) = refs[:-2], refs[-2:]
     flip, side = info_ref[FLIP], info_ref[SIDE]
     planes, own = states_ref.shape[1:3]
     for pos, (ref, plane) in enumerate([(far_ref, flip * (planes - 1)), (near_ref, (1 - flip) * (planes - 1))]):
         for tile in range(own):
             store_sent(ref, tile, own + 1, states_ref[0, plane, tile], side)
         store_sent(ref, own, own + 1, edge_ref[pos], side)
-    for comp in range(3):
-        near_ref[SENT + comp] = jnp.concatenate([disp_ref[comp, 0, :8], disp_ref[comp, 0, 8:]], axis=1)
-    index = fiber_ref[0].astype(jnp.float32)
-    near_ref[SENT + 3] = jnp.concatenate([index[:8], index[8:]], axis=1)
+    for pos, ref in enumerate(field_refs):
+        near_ref[SENT + FIELD * pos : SENT + FIELD * (pos + 1)] = ref[0]
 
 
 def facing_parts(info, tiled, cond):
@@ -204,17 +222,17 @@
     )(info, tiled, cond)
 
 
-def first_sends(info, edges, tiled, disp, fiber):
+def first_sends(info, edges, tiled, fields):
     width = tiled.shape[-1]
     return pl.pallas_call(
         sends_kernel,
-        in_specs=[SMEM] + [VMEM] * 4,
+        in_specs=[SMEM] + [VMEM] * (2 + len(fields)),
         out_specs=[VMEM] * 2,
-        out_shape=[shape_of(SENT, 8, width // 2), shape_of(SENT + FIELD, 8, width // 2)],
+        out_shape=[shape_of(SENT, 8, width // 2), shape_of(SENT + FIELD * len(fields), 8, width // 2)],
         compiler_params=params(),
         cost_estimate=cost(0, 1_200_000),
         name="sends",
-    )(info, edges, tiled, disp, fiber)
+    )(info, edges, tiled, *fields)
 
 
 def fraction(val):
@@ -428,29 +446,37 @@
     return jnp.concatenate([total[pos * count : (pos + 1) * count] for pos in range(len(pairs))], axis=1)
 
 
-def finish_kernel(half, tiles, info_ref, outer_ref, inner_ref, gate_ref, halo_ref, coeff_ref, tension_ref, *refs):
+def finish_kernel(half, tiles, info_ref, outer_ref, inner_ref, halo_ref, coeff_ref, tension_ref, *refs):
     if half == FAR_HALF:
+        gate_ref, near_inner_ref, near_gate_ref, *refs = refs
         states_out, tension_out, active_out, u_ref, layer_ref, rows_ref, sems = refs
+        moves = []
+        for which, inners, gates in ((FAR_HALF, inner_ref, gate_ref), (NEAR_HALF, near_inner_ref, near_gate_ref)):
+            index, outer = half_place(info_ref, which)
+            place = [2 * index + outer, 2 * index + 1 - outer]
+            moves += [(gates.at[g, plane], states_out.at[1 + g, place[plane]]) for g in range(3) for plane in range(2)]
+            moves.append((inners, states_out.at[0, place[1]]))
     else:
         active_ref, _, _, states_out, tension_out, active_out, facing_out, u_ref, layer_ref, rows_ref, sems = refs
+        moves = []
+    copies = []
+
+    def start(src, dst):
+        copies.append(pltpu.make_async_copy(src, dst, sems.at[len(copies)]))
+        copies[-1].start()
+
+    for src, dst in moves:
+        start(src, dst)
     index, outer = half_place(info_ref, half)
-    place = [2 * index + outer, 2 * index + 1 - outer]
-    moves = [(gate_ref.at[g, plane], states_out.at[1 + g, place[plane]]) for g in range(3) for plane in range(2)]
-    moves.append((inner_ref, states_out.at[0, place[1]]))
-    copies = [pltpu.make_async_copy(src, dst, sems.at[pos]) for pos, (src, dst) in enumerate(moves)]
-    for copy in copies:
-        copy.start()
     own = tiles - 1
     add_halo(half, tiles, own, info_ref, outer_ref, halo_ref, coeff_ref, u_ref)
-    copies.append(pltpu.make_async_copy(u_ref, states_out.at[0, place[0]], sems.at[len(moves)]))
-    copies[-1].start()
+    start(u_ref, states_out.at[0, 2 * index + outer])
     both = 0.5 * (u_ref[...] + inner_ref[...])
     mean = pooled(both.reshape(own * 8, both.shape[-1]), rows_ref)
     old = tension_ref[index]
     new = old + 0.5 * (mean - old)
     layer_ref[...] = new
-    copies.append(pltpu.make_async_copy(layer_ref, tension_out.at[index], sems.at[len(moves) + 1]))
-    copies[-1].start()
+    start(layer_ref, tension_out.at[index])
     mean = pooled(0.5 * new, rows_ref)
     if half == FAR_HALF:
         active_out[...] = mean
@@ -461,26 +487,21 @@
         copy.wait()
 
 
-def finish_half(half, info, arrays, halo, coeffs, tension, active=None, states=None, tension_next=None):
+def finish_half(half, info, outer, inner, halo, coeffs, tension, others):
     _, tiles, _, width = coeffs.shape
     own = tiles - 1
     active_shape = (own * 2, width // 4)
-    vmem, hbm = pl.BlockSpec(memory_space=pltpu.VMEM), pl.BlockSpec(memory_space=pltpu.HBM)
-    in_specs = [pl.BlockSpec(memory_space=pltpu.SMEM)] + [vmem] * 6
-    operands = [*arrays, halo, coeffs, tension]
-    out_specs = [hbm, hbm, vmem]
-    out_shape = [
-        jax.ShapeDtypeStruct((4, 4, own, 8, width), jnp.float32),
-        jax.ShapeDtypeStruct(tension.shape, jnp.float32),
-        jax.ShapeDtypeStruct(active_shape, jnp.float32),
-    ]
+    hbm = pl.BlockSpec(memory_space=pltpu.HBM)
+    out_specs = [hbm, hbm, VMEM]
+    out_shape = [shape_of(4, 4, own, 8, width), shape_of(*tension.shape), shape_of(*active_shape)]
     aliases = {}
-    if half == NEAR_HALF:
-        in_specs += [vmem, hbm, hbm]
-        operands += [active, states, tension_next]
-        aliases = {8: 0, 9: 1}
-        out_specs.append(vmem)
-        out_shape.append(jax.ShapeDtypeStruct((8, width // 4), jnp.float32))
+    if half == FAR_HALF:
+        in_specs = [SMEM] + [VMEM] * 8
+    else:
+        in_specs = [SMEM] + [VMEM] * 6 + [hbm, hbm]
+        aliases = {7: 0, 8: 1}
+        out_specs.append(VMEM)
+        out_shape.append(shape_of(8, width // 4))
     cells = 2 * own * 8 * width
     return pl.pallas_call(
         functools.partial(finish_kernel, half, tiles),
@@ -491,13 +512,13 @@
             pltpu.VMEM((own, 8, width), jnp.float32),
             pltpu.VMEM(tension.shape[1:], jnp.float32),
             pltpu.VMEM((width // 128, own * 8, 128), jnp.float32),
-            pltpu.SemaphoreType.DMA((9,)),
+            pltpu.SemaphoreType.DMA((16 if half == FAR_HALF else 2,)),
         ],
         input_output_aliases=aliases,
         compiler_params=params(),
         cost_estimate=cost(20 * cells, 20 * cells),
         name="finish" + ("_far" if half == FAR_HALF else "_near"),
-    )(info, *operands)
+    )(info, outer, inner, halo, coeffs, tension, *others)
 
 
 REACH = 4
@@ -618,34 +639,34 @@
 
 
 class Planes:
-    def __init__(self, field, slabs, reach, from_pair=None):
-        self.slabs, self.reach = slabs, reach
+    def __init__(self, field, slabs, reach, order):
+        self.slabs, self.reach, self.order = slabs, reach, order
         self.parts = [field[None]]
-        self.doubling = slabs in (2, 4, 8)
-        self.step = 1
-        if self.doubling and from_pair is not None:
-            self.parts.append(from_pair[None])
-            self.step = 2
+        self.doubling = slabs == 8
+        self.rounds = 0
 
     def round(self):
         if self.doubling:
-            if self.step < self.slabs:
-                held = jnp.concatenate(self.parts, axis=0) if len(self.parts) > 1 else self.parts[0]
-                perm = [(i, i ^ self.step) for i in range(self.slabs)]
-                self.parts.append(lax.ppermute(held, "slab", perm))
-                self.step *= 2
-        elif self.step == 1:
+            held = jnp.concatenate(self.parts, axis=0) if len(self.parts) > 1 else self.parts[0]
+            perm = [(i, i ^ self.order[self.rounds]) for i in range(self.slabs)]
+            self.take(lax.ppermute(held, "slab", perm))
+        elif self.rounds == 0:
             for shift in self.shifts()[1:]:
                 perm = [((i + shift) % self.slabs, i) for i in range(self.slabs)]
-                self.parts.append(lax.ppermute(self.parts[0], "slab", perm))
-            self.step = 0
+                self.take(lax.ppermute(self.parts[0], "slab", perm))
+
+    def take(self, part):
+        self.parts.append(part)
+        self.rounds += 1
 
     def shifts(self):
         return sorted({offset % self.slabs for offset in range(-self.reach, self.reach + 1)})
 
     def spot(self, slab, offset):
         if self.doubling:
-            return slab ^ jnp.clip(slab + offset, 0, self.slabs - 1)
+            apart = slab ^ jnp.clip(slab + offset, 0, self.slabs - 1)
+            bits = [(apart & step) // step for step in self.order]
+            return bits[0] + 2 * bits[1] + 4 * bits[2]
         return self.shifts().index(offset % self.slabs)
 
 
@@ -855,20 +876,24 @@
     swap = [(0, 1), (1, 0)]
 
     tiled = states.reshape(4, planes, own, 8, width)
+    fields = Planes(own_field(disp, fiber), slabs, REACH + 1, (1, 4, 2))
     edges, facing, cond_rows = facing_parts(info, tiled, cond)
     edges = lax.ppermute(edges, "col", swap)
     cond_strip = lax.ppermute(cond_rows, "col", swap)
     strip = lax.ppermute(facing, "col", swap)
-    far, near = first_sends(info, edges, tiled, disp, fiber)
+    carried = fields.parts if fields.doubling else []
+    far, near = first_sends(info, edges, tiled, carried)
     far_halo = lax.ppermute(far, "slab", others)
     near_halo = lax.ppermute(near, "slab", pairs)
-    fields = Planes(near[SENT:], slabs, REACH + 1, near_halo[SENT:])
 
     coeffs = fine_coeffs(info, cond, cond_strip)
     whole = jnp.concatenate([tiled, strip[:, :, None]], axis=2)
 
     far_part, far_inner, far_gates = half_step("first", FAR_HALF, info, (whole,), coeffs)
     near_part, near_inner, near_gates = half_step("first", NEAR_HALF, info, (whole,), coeffs)
+    if fields.doubling:
+        near_part, near_halo = tie(near_part, near_halo)
+        fields.take(near_halo[SENT:][None])
     for turn_index in range(1, SUB):
         last = turn_index == SUB - 1
         far, far_send = halo_step(FAR_HALF, info, far_part, far_halo, coeffs)
@@ -876,24 +901,25 @@
         far_arrays = (far, far_inner, near_inner, far_gates)
         kind = "last" if last else "middle"
         far_part, far_next, far_gates = half_step(kind, FAR_HALF, info, far_arrays, coeffs)
+        if turn_index >= 2:
+            near_part, *fields.parts = tie(near_part, *fields.parts)
         near, near_send = halo_step(NEAR_HALF, info, near_part, near_halo, coeffs)
         near_halo = lax.ppermute(near_send, "slab", pairs)
         if not last:
-            near, *fields.parts = tie(near, *fields.parts)
             fields.round()
         near_arrays = (near, near_inner, far_inner, near_gates)
         near_part, near_inner, near_gates = half_step(kind, NEAR_HALF, info, near_arrays, coeffs)
         far_inner = far_next
     strips = lax.ppermute(facing_rows(info, fields.parts), "col", swap)
-    far_arrays = (far_part, far_inner, far_gates)
-    near_arrays = (near_part, near_inner, near_gates)
-    states_next, tension_next, active = finish_half(FAR_HALF, info, far_arrays, far_halo, coeffs, tension)
+    states_next, tension_next, active = finish_half(
+        FAR_HALF, info, far_part, far_inner, far_halo, coeffs, tension, (far_gates, near_inner, near_gates)
+    )
     window = passive_step(info, fields, strips)
     states_next, tension_next, active, facing = finish_half(
-        NEAR_HALF, info, near_arrays, near_halo, coeffs, tension, active, states_next, tension_next
+        NEAR_HALF, info, near_part, near_inner, near_halo, coeffs, tension, (active, states_next, tension_next)
     )
     active_strip = lax.ppermute(facing, "col", swap)
-    actives = Planes(jnp.concatenate([active, active_strip], axis=0), slabs, REACH)
+    actives = Planes(jnp.concatenate([active, active_strip], axis=0), slabs, REACH, (4, 1, 2))
     for _ in range(3):
         actives.round()
     disp_next, cond_next = mechanics_step(info, disp.shape[2], actives, window)

time: 96.4 us -> 92.3 us (0.957)
  waiting for transfers between devices: 19.7 us -> 13.2 us
  starting transfers between devices: 28.7 us -> 31 us
    ppermute x5, starting transfers between devices: 4.41 us -> 13 us  [round(): self.take(lax.ppermute(held, 'slab', perm))]
    ppermute x5, waiting for transfers between devices: 14.9 us -> 7.33 us  [round(): self.take(lax.ppermute(held, 'slab', perm))]
    ppermute x3, starting transfers between devices: 17.7 us -> 11.6 us  [on_device(): near_halo = lax.ppermute(near_send, 'slab', pairs)]
    ppermute x3, waiting for transfers between devices: 0.01 us -> 1.05 us  [on_device(): near_halo = lax.ppermute(near_send, 'slab', pairs)]
where the time goes in v6:
time: 92.3 us; the launch traced here: 92 us
  Pallas kernels  42.8 us (46%)
  starting transfers between devices  31 us (34%)
  waiting for transfers between devices  13.2 us (14%)
  local copies, waits for them, and re-layouts  3.11 us (3%)
  other arithmetic  1.02 us (1%)
  between operations  0.96 us (1%)
    pallas_call x8, Pallas kernels, half_step(): pl.pallas_call(functools.partial(half_kernel, kind, half, tiles), in_spec...  22.6 us
    ppermute x5, starting transfers between devices, round(): self.take(lax.ppermute(held, 'slab', perm))  13 us
    ppermute x3, starting transfers between devices, on_device(): near_halo = lax.ppermute(near_send, 'slab', pairs)  11.6 us
    ppermute x5, waiting for transfers between devices, round(): self.take(lax.ppermute(held, 'slab', perm))  7.33 us
    pallas_call x2, Pallas kernels, finish_half(): pl.pallas_call(functools.partial(finish_kernel, half, tiles), in_specs=in...  4.26 us
    pallas_call x1, Pallas kernels, mechanics_step(): pl.pallas_call(functools.partial(mechanics_kernel, planes), in_specs=[pl....  4.14 us
    pallas_call x6, Pallas kernels, halo_step(): pl.pallas_call(functools.partial(halo_kernel, half, tiles), in_specs=[pl....  4.07 us
    unnamed x14, local copies, waits for them, and re-layouts  3.1 us
  transfers between devices with their start and end apart: 18, of which 8 were waited for; matrix products, arithmetic and copies ran while one was open for 1% of the time, Pallas kernels for 40%

profile of v6, /device:TPU:0, one launch (start us, length us, event | category | flops | bytes accessed | tf_op | source)
XLA Modules:
  0.0 92.0 jit_solution(9864728943884747587)
XLA Ops:
  0.7 2.2 %copy-done = f32[4,4,64,1024]{3,2,1,0:T(8,128)S(1)} copy-done((f32[4,4,64,1024]{3,2,1,0:T(8,128)S(1)}, f32[4,4,64,1024]{3,2,1,0:T(8,128)}, u32[]{:S(2)}) %copy-start) | copy-done | bytes 4194328
  7.2 2.9 %collective-permute-start.3 = (f32[21,8,512]{2,1,0:T(8,128)S(1)}, f32[21,8,512]{2,1,0:T(8,128)S(1)}, u32[]{:S(2)}, u32[]{:S(2)}) collective-permute-start(f32[21,8,512]{2,1,0:T(8,128)S(1)} %get-tuple-element.72), channel_id=1, source_target_pairs={{0,2},{2,0},{4,6},{6,4},{8,10},{10,8},{12,14},{14,12},{1,3},{3,1},... | collective-permute-start | bytes 1032200 | tf_op jit(solution)/shard_map/ppermute | solution.py:887
  11.3 3.0 %coeffs.1.refs_1_.coeff_ref.refs_4_ = f32[10,9,8,1024]{3,2,1,0:T(8,128)S(1)} custom-call(s32[4]{0:T(128)S(1)} %pad_add_fusion.info_ref, f32[6,1,16,256]{3,2,1,0:T(8,128)S(1)} %copy-done.4, f32[6,8,256]{2,1,0:T(8,128)S(1)} %collective-permute-done.1.strip_ref), custom_call_target="tpu_custom_call" | custom-call | flops 2000000 | bytes 3200000 | tf_op jit(solution)/shard_map/coeffs/pallas_call | solution.py:116
  15.0 2.9 %first_far.1 = (f32[9,8,1024]{2,1,0:T(8,128)S(1)}, f32[9,8,1024]{2,1,0:T(8,128)S(1)}, f32[3,2,9,8,1024]{4,3,2,1,0:T(8,128)S(1)}) custom-call(s32[4]{0:T(128)S(1)} %pad_add_fusion.info_ref, f32[4,4,9,8,1024]{4,3,2,1,0:T(8,128)S(1)} %pad_maximum_fusion.refs_0_, f32[10,9,8,1024]{3,2,1,0:T(8,128)S(1)} %coeffs.1.refs_1_.coeff_ref.refs_4_), custom_call_target="tpu_custom_call" | custom-call | flops 14745600 | bytes 5898240 | tf_op jit(solution)/shard_map/first_far/pallas_call | solution.py:363
  19.2 2.9 %first_near.1 = (f32[9,8,1024]{2,1,0:T(8,128)S(1)}, f32[9,8,1024]{2,1,0:T(8,128)S(1)}, f32[3,2,9,8,1024]{4,3,2,1,0:T(8,128)S(1)}) custom-call(s32[4]{0:T(128)S(1)} %pad_add_fusion.info_ref, f32[4,4,9,8,1024]{4,3,2,1,0:T(8,128)S(1)} %pad_maximum_fusion.refs_0_, f32[10,9,8,1024]{3,2,1,0:T(8,128)S(1)} %coeffs.1.refs_1_.coeff_ref.refs_4_), custom_call_target="tpu_custom_call" | custom-call | flops 14745600 | bytes 5898240 | tf_op jit(solution)/shard_map/first_near/pallas_call | solution.py:363
  24.4 7.1 %collective-permute-start.5 = (f32[17,8,512]{2,1,0:T(8,128)S(1)}, f32[17,8,512]{2,1,0:T(8,128)S(1)}, u32[]{:S(2)}, u32[]{:S(2)}) collective-permute-start(f32[17,8,512]{2,1,0:T(8,128)S(1)} %get-tuple-element.81), channel_id=1, source_target_pairs={{0,2},{2,0},{4,6},{6,4},{8,10},{10,8},{12,14},{14,12},{1,3},{3,1},... | collective-permute-start | bytes 835592 | tf_op jit(solution)/shard_map/ppermute | solution.py:907
  31.6 2.7 %collective-permute-start.4 = (f32[2,4,8,512]{3,2,1,0:T(8,128)S(1)}, f32[2,4,8,512]{3,2,1,0:T(8,128)S(1)}, u32[]{:S(2)}, u32[]{:S(2)}) collective-permute-start(f32[2,4,8,512]{3,2,1,0:T(8,128)S(1)} %pad_maximum_fusion.2), channel_id=1, source_target_pairs={{0,8},{2,10},{4,12},{6,14},{8,0},{10,2},{12,4},{14,6},{1,9},{3,11}... | collective-permute-start | bytes 393224 | tf_op jit(solution)/shard_map/ppermute | solution.py:652
  34.2 2.9 %middle_far.2 = (f32[9,8,1024]{2,1,0:T(8,128)S(1)}, f32[9,8,1024]{2,1,0:T(8,128)S(1)}, f32[3,2,9,8,1024]{4,3,2,1,0:T(8,128)S(1)}) custom-call(s32[4]{0:T(128)S(1)} %pad_add_fusion.info_ref, f32[9,8,1024]{2,1,0:T(8,128)S(1)} %get-tuple-element.86.refs_0_, f32[9,8,1024]{2,1,0:T(8,128)S(1)} %get-tuple-element.77.refs_2_.refs_1_, ...), custom_call_target="tpu_custom_call" | custom-call | flops 14745600 | bytes 5898240 | tf_op jit(solution)/shard_map/middle_far/pallas_call | solution.py:363
  37.1 2.9 %middle_near.2 = (f32[9,8,1024]{2,1,0:T(8,128)S(1)}, f32[9,8,1024]{2,1,0:T(8,128)S(1)}, f32[3,2,9,8,1024]{4,3,2,1,0:T(8,128)S(1)}) custom-call(s32[4]{0:T(128)S(1)} %pad_add_fusion.info_ref, f32[9,8,1024]{2,1,0:T(8,128)S(1)} %get-tuple-element.75.refs_0_, f32[9,8,1024]{2,1,0:T(8,128)S(1)} %get-tuple-element.76.refs_1_.refs_2_, ...), custom_call_target="tpu_custom_call" | custom-call | flops 14745600 | bytes 5898240 | tf_op jit(solution)/shard_map/middle_near/pallas_call | solution.py:363
  42.1 2.0 %collective-permute-start.8 = (f32[17,8,512]{2,1,0:T(8,128)S(1)}, f32[17,8,512]{2,1,0:T(8,128)S(1)}, u32[]{:S(2)}, u32[]{:S(2)}) collective-permute-start(f32[17,8,512]{2,1,0:T(8,128)S(1)} %get-tuple-element.95), channel_id=1, source_target_pairs={{0,2},{2,0},{4,6},{6,4},{8,10},{10,8},{12,14},{14,12},{1,3},{3,1},... | collective-permute-start | bytes 835592 | tf_op jit(solution)/shard_map/ppermute | solution.py:907
  44.1 1.9 %collective-permute-start.7 = (f32[4,4,8,512]{3,2,1,0:T(8,128)S(1)}, f32[4,4,8,512]{3,2,1,0:T(8,128)S(1)}, u32[]{:S(2)}, u32[]{:S(2)}) collective-permute-start(f32[4,4,8,512]{3,2,1,0:T(8,128)S(1)} %pad_maximum_fusion.1), channel_id=1, source_target_pairs={{0,4},{2,6},{4,0},{6,2},{8,12},{10,14},{12,8},{14,10},{1,5},{3,7},... | collective-permute-start | bytes 786440 | tf_op jit(solution)/shard_map/ppermute | solution.py:652
  46.0 2.9 %middle_far.3 = (f32[9,8,1024]{2,1,0:T(8,128)S(1)}, f32[9,8,1024]{2,1,0:T(8,128)S(1)}, f32[3,2,9,8,1024]{4,3,2,1,0:T(8,128)S(1)}) custom-call(s32[4]{0:T(128)S(1)} %pad_add_fusion.info_ref, f32[9,8,1024]{2,1,0:T(8,128)S(1)} %get-tuple-element.100.refs_0_, f32[9,8,1024]{2,1,0:T(8,128)S(1)} %get-tuple-element.88.refs_2_.refs_1_, ...), custom_call_target="tpu_custom_call" | custom-call | flops 14745600 | bytes 5898240 | tf_op jit(solution)/shard_map/middle_far/pallas_call | solution.py:363
  50.2 2.9 %middle_near.3 = (f32[9,8,1024]{2,1,0:T(8,128)S(1)}, f32[9,8,1024]{2,1,0:T(8,128)S(1)}, f32[3,2,9,8,1024]{4,3,2,1,0:T(8,128)S(1)}) custom-call(s32[4]{0:T(128)S(1)} %pad_add_fusion.info_ref, f32[9,8,1024]{2,1,0:T(8,128)S(1)} %get-tuple-element.82.refs_0_, f32[9,8,1024]{2,1,0:T(8,128)S(1)} %get-tuple-element.83.refs_1_.refs_2_, ...), custom_call_target="tpu_custom_call" | custom-call | flops 14745600 | bytes 5898240 | tf_op jit(solution)/shard_map/middle_near/pallas_call | solution.py:363
  53.1 3.6 %collective-permute-done.7.refs_3_ = f32[4,4,8,512]{3,2,1,0:T(8,128)S(1)} collective-permute-done((f32[4,4,8,512]{3,2,1,0:T(8,128)S(1)}, f32[4,4,8,512]{3,2,1,0:T(8,128)S(1)}, u32[]{:S(2)}, u32[]{:S(2)}) %collective-permute-start.7) | collective-permute-done | bytes 262176 | tf_op jit(solution)/shard_map/ppermute | solution.py:652
  58.6 2.5 %collective-permute-start.10 = (f32[17,8,512]{2,1,0:T(8,128)S(1)}, f32[17,8,512]{2,1,0:T(8,128)S(1)}, u32[]{:S(2)}, u32[]{:S(2)}) collective-permute-start(f32[17,8,512]{2,1,0:T(8,128)S(1)} %get-tuple-element.106), channel_id=1, source_target_pairs={{0,2},{2,0},{4,6},{6,4},{8,10},{10,8},{12,14},{14,12},{1,3},{3,1},... | collective-permute-start | bytes 835592 | tf_op jit(solution)/shard_map/ppermute | solution.py:907
  61.1 2.6 %last_far.1 = (f32[8,8,1024]{2,1,0:T(8,128)S(1)}, f32[8,8,1024]{2,1,0:T(8,128)S(1)}, f32[3,2,8,8,1024]{4,3,2,1,0:T(8,128)S(1)}) custom-call(s32[4]{0:T(128)S(1)} %pad_add_fusion.info_ref, f32[9,8,1024]{2,1,0:T(8,128)S(1)} %get-tuple-element.109.refs_0_, f32[9,8,1024]{2,1,0:T(8,128)S(1)} %get-tuple-element.102.refs_2_.refs_1_, ...), custom_call_target="tpu_custom_call" | custom-call | flops 14745600 | bytes 5898240 | tf_op jit(solution)/shard_map/last_far/pallas_call | solution.py:363
  63.7 2.6 %last_near.1 = (f32[8,8,1024]{2,1,0:T(8,128)S(1)}, f32[8,8,1024]{2,1,0:T(8,128)S(1)}, f32[3,2,8,8,1024]{4,3,2,1,0:T(8,128)S(1)}) custom-call(s32[4]{0:T(128)S(1)} %pad_add_fusion.info_ref, f32[9,8,1024]{2,1,0:T(8,128)S(1)} %get-tuple-element.96.refs_0_, f32[9,8,1024]{2,1,0:T(8,128)S(1)} %get-tuple-element.97.refs_1_.refs_2_, ...), custom_call_target="tpu_custom_call" | custom-call | flops 14745600 | bytes 5898240 | tf_op jit(solution)/shard_map/last_near/pallas_call | solution.py:363
  66.4 2.6 %finish_far.1 = (f32[4,4,8,8,1024]{4,3,2,1,0:T(8,128)}, f32[2,32,512]{2,1,0:T(8,128)}, f32[16,256]{1,0:T(8,128)S(1)}) custom-call(s32[4]{0:T(128)S(1)} %pad_add_fusion.info_ref, f32[8,8,1024]{2,1,0:T(8,128)S(1)} %get-tuple-element.111.outer_ref, f32[8,8,1024]{2,1,0:T(8,128)S(1)} %get-tuple-element.112.inner_ref, ...), custom_call_target="tpu_custom_call" | custom-call | flops 2621440 | bytes 2621440 | tf_op jit(solution)/shard_map/finish_far/pallas_call | solution.py:506
  69.0 1.6 %finish_near.1 = (f32[4,4,8,8,1024]{4,3,2,1,0:T(8,128)}, f32[2,32,512]{2,1,0:T(8,128)}, f32[16,256]{1,0:T(8,128)S(1)}, f32[8,256]{1,0:T(8,128)S(1)}) custom-call(s32[4]{0:T(128)S(1)} %pad_add_fusion.info_ref, f32[8,8,1024]{2,1,0:T(8,128)S(1)} %get-tuple-element.104.outer_ref, ...), custom_call_target="tpu_custom_call", output_to_operand_aliasing={{0}: (7, {}), {1}: (8, {})} | custom-call | flops 2621440 | bytes 2621440 | tf_op jit(solution)/shard_map/finish_near/pallas_call | solution.py:506
  71.9 3.7 %collective-permute-start.15 = (f32[1,24,256]{2,1,0:T(8,128)S(1)}, f32[1,24,256]{2,1,0:T(8,128)S(1)}, u32[]{:S(2)}, u32[]{:S(2)}) collective-permute-start(f32[1,24,256]{2,1,0:T(8,128)S(1)} %maximum_bitcast_fusion.rest_0_), channel_id=1, source_target_pairs={{0,8},{2,10},{4,12},{6,14},{8,0},{10,2},{12,4},{14,6},{1,9},{3,11}... | collective-permute-start | bytes 73736 | tf_op jit(solution)/shard_map/ppermute | solution.py:652
  78.9 2.6 %collective-permute-done.16.rest_2_ = f32[2,24,256]{2,1,0:T(8,128)S(1)} collective-permute-done((f32[2,24,256]{2,1,0:T(8,128)S(1)}, f32[2,24,256]{2,1,0:T(8,128)S(1)}, u32[]{:S(2)}, u32[]{:S(2)}) %collective-permute-start.16) | collective-permute-done | bytes 49184 | tf_op jit(solution)/shard_map/ppermute | solution.py:652
  81.5 3.4 %collective-permute-start.17 = (f32[4,24,256]{2,1,0:T(8,128)S(1)}, f32[4,24,256]{2,1,0:T(8,128)S(1)}, u32[]{:S(2)}, u32[]{:S(2)}) collective-permute-start(f32[4,24,256]{2,1,0:T(8,128)S(1)} %pad_maximum_fusion.3), channel_id=1, source_target_pairs={{0,4},{2,6},{4,0},{6,2},{8,12},{10,14},{12,8},{14,10},{1,5},{3,7},... | collective-permute-start | bytes 294920 | tf_op jit(solution)/shard_map/ppermute | solution.py:652
  84.9 3.0 %passive.1 = (f32[6,9,24,256]{3,2,1,0:T(8,128)S(1)}, f32[9,9,24,256]{3,2,1,0:T(8,128)S(1)}, f32[9,9,24,256]{3,2,1,0:T(8,128)S(1)}) custom-call(s32[4]{0:T(128)S(1)} %pad_add_fusion.info_ref, f32[3,128]{1,0:T(4,128)S(1)} %pad_maximum_fusion.5.table_ref, f32[8,4,8,256]{3,2,1,0:T(8,128)S(1)} %collective-permute-done.13.strip_ref, ...), custom_call_target="tpu_custom_call" | custom-call | flops 22118400 | bytes 5000000 | tf_op jit(solution)/shard_map/passive/pallas_call | solution.py:766
  87.9 4.1 %mechanics.1 = (f32[3,1,16,256]{3,2,1,0:T(8,128)}, f32[6,1,16,256]{3,2,1,0:T(8,128)}) custom-call(s32[4]{0:T(128)S(1)} %pad_add_fusion.info_ref, f32[6,9,24,256]{3,2,1,0:T(8,128)S(1)} %get-tuple-element.125.disp_ref, f32[9,9,24,256]{3,2,1,0:T(8,128)S(1)} %get-tuple-element.126.stress_ref, f32[9,9,24,256]{3,2,1,0:T(8,128)S(1)} %get-tuple-element.127.pull_ref, ...), custom_call_target="tpu_custom_call" | custom-call | flops 22118400 | bytes 5000000 | tf_op jit(solution)/shard_map/mechanics/pallas_call | solution.py:843
  (60 shorter events, 19.5 us)
Async XLA Ops:
  0.7 2.2 %copy-start = (f32[4,4,64,1024]{3,2,1,0:T(8,128)S(1)}, f32[4,4,64,1024]{3,2,1,0:T(8,128)}, u32[]{:S(2)}) copy-start(f32[4,4,64,1024]{3,2,1,0:T(8,128)} %param.5) | copy-start | bytes 12582916
  3.8 1.2 %copy-start.5 = (f32[3,1,16,256]{3,2,1,0:T(8,128)S(1)}, f32[3,1,16,256]{3,2,1,0:T(8,128)}, u32[]{:S(2)}) copy-start(f32[3,1,16,256]{3,2,1,0:T(8,128)} %disp_ref.1) | copy-start | bytes 147460
  3.8 1.2 %copy-start.6 = (s32[1,16,256]{2,1,0:T(8,128)S(1)}, s32[1,16,256]{2,1,0:T(8,128)}, u32[]{:S(2)}) copy-start(s32[1,16,256]{2,1,0:T(8,128)} %fiber_ref.1) | copy-start | bytes 49156
  3.8 2.7 %copy-start.1 = (f32[4,4,64,1024]{3,2,1,0:T(8,128)S(1)}, f32[4,4,64,1024]{3,2,1,0:T(8,128)}, u32[]{:S(2)}) copy-start(f32[4,4,64,1024]{3,2,1,0:T(8,128)} %param.5) | copy-start | bytes 12582916
  4.4 9.9 %collective-permute-start = (f32[4,4,8,1024]{3,2,1,0:T(8,128)S(1)}, f32[4,4,8,1024]{3,2,1,0:T(8,128)S(1)}, u32[]{:S(2)}, u32[]{:S(2)}) collective-permute-start(f32[4,4,8,1024]{3,2,1,0:T(8,128)S(1)} %get-tuple-element.68), channel_id=1, source_target_pairs={{0,1},{1,0},{2,3},{3,2},{4,5},{5,4},{6,7},{7,6},{8,9},{9,8},{10,11... | collective-permute-start | bytes 1572872 | tf_op jit(solution)/shard_map/ppermute | solution.py:883
  4.9 1.6 %collective-permute-start.2 = (f32[2,8,1024]{2,1,0:T(8,128)S(1)}, f32[2,8,1024]{2,1,0:T(8,128)S(1)}, u32[]{:S(2)}, u32[]{:S(2)}) collective-permute-start(f32[2,8,1024]{2,1,0:T(8,128)S(1)} %get-tuple-element.71), channel_id=1, source_target_pairs={{0,1},{1,0},{2,3},{3,2},{4,5},{5,4},{6,7},{7,6},{8,9},{9,8},{10,11... | collective-permute-start | bytes 196616 | tf_op jit(solution)/shard_map/ppermute | solution.py:881
  6.6 4.8 %copy-start.4 = (f32[6,1,16,256]{3,2,1,0:T(8,128)S(1)}, f32[6,1,16,256]{3,2,1,0:T(8,128)}, u32[]{:S(2)}) copy-start(f32[6,1,16,256]{3,2,1,0:T(8,128)} %cond_ref.3) | copy-start | bytes 294916
  7.2 16.5 %collective-permute-start.3 = (f32[21,8,512]{2,1,0:T(8,128)S(1)}, f32[21,8,512]{2,1,0:T(8,128)S(1)}, u32[]{:S(2)}, u32[]{:S(2)}) collective-permute-start(f32[21,8,512]{2,1,0:T(8,128)S(1)} %get-tuple-element.72), channel_id=1, source_target_pairs={{0,2},{2,0},{4,6},{6,4},{8,10},{10,8},{12,14},{14,12},{1,3},{3,1},... | collective-permute-start | bytes 1032200 | tf_op jit(solution)/shard_map/ppermute | solution.py:887
  10.1 1.2 %collective-permute-start.1 = (f32[6,8,256]{2,1,0:T(8,128)S(1)}, f32[6,8,256]{2,1,0:T(8,128)S(1)}, u32[]{:S(2)}, u32[]{:S(2)}) collective-permute-start(f32[6,8,256]{2,1,0:T(8,128)S(1)} %get-tuple-element.69), channel_id=1, source_target_pairs={{0,1},{1,0},{2,3},{3,2},{4,5},{5,4},{6,7},{7,6},{8,9},{9,8},{10,11... | collective-permute-start | bytes 147464 | tf_op jit(solution)/shard_map/ppermute | solution.py:882
  10.1 7.8 %collective-permute-start.6 = (f32[17,8,512]{2,1,0:T(8,128)S(1)}, f32[17,8,512]{2,1,0:T(8,128)S(1)}, u32[]{:S(2)}, u32[]{:S(2)}) collective-permute-start(f32[17,8,512]{2,1,0:T(8,128)S(1)} %get-tuple-element.85), channel_id=1, source_target_pairs={{0,0},{2,4},{4,2},{6,8},{8,6},{10,12},{12,10},{14,14},{1,1},{3,5},... | collective-permute-start | bytes 835592 | tf_op jit(solution)/shard_map/ppermute | solution.py:886
  18.5 21.5 %collective-permute-start.9 = (f32[17,8,512]{2,1,0:T(8,128)S(1)}, f32[17,8,512]{2,1,0:T(8,128)S(1)}, u32[]{:S(2)}, u32[]{:S(2)}) collective-permute-start(f32[17,8,512]{2,1,0:T(8,128)S(1)} %get-tuple-element.99), channel_id=1, source_target_pairs={{0,0},{2,4},{4,2},{6,8},{8,6},{10,12},{12,10},{14,14},{1,1},{3,5},... | collective-permute-start | bytes 835592 | tf_op jit(solution)/shard_map/ppermute | solution.py:900
  24.4 16.9 %collective-permute-start.5 = (f32[17,8,512]{2,1,0:T(8,128)S(1)}, f32[17,8,512]{2,1,0:T(8,128)S(1)}, u32[]{:S(2)}, u32[]{:S(2)}) collective-permute-start(f32[17,8,512]{2,1,0:T(8,128)S(1)} %get-tuple-element.81), channel_id=1, source_target_pairs={{0,2},{2,0},{4,6},{6,4},{8,10},{10,8},{12,14},{14,12},{1,3},{3,1},... | collective-permute-start | bytes 835592 | tf_op jit(solution)/shard_map/ppermute | solution.py:907
  31.6 8.4 %collective-permute-start.4 = (f32[2,4,8,512]{3,2,1,0:T(8,128)S(1)}, f32[2,4,8,512]{3,2,1,0:T(8,128)S(1)}, u32[]{:S(2)}, u32[]{:S(2)}) collective-permute-start(f32[2,4,8,512]{3,2,1,0:T(8,128)S(1)} %pad_maximum_fusion.2), channel_id=1, source_target_pairs={{0,8},{2,10},{4,12},{6,14},{8,0},{10,2},{12,4},{14,6},{1,9},{3,11}... | collective-permute-start | bytes 393224 | tf_op jit(solution)/shard_map/ppermute | solution.py:652
  40.6 8.3 %collective-permute-start.11 = (f32[17,8,512]{2,1,0:T(8,128)S(1)}, f32[17,8,512]{2,1,0:T(8,128)S(1)}, u32[]{:S(2)}, u32[]{:S(2)}) collective-permute-start(f32[17,8,512]{2,1,0:T(8,128)S(1)} %get-tuple-element.108), channel_id=1, source_target_pairs={{0,0},{2,4},{4,2},{6,8},{8,6},{10,12},{12,10},{14,14},{1,1},{3,5},... | collective-permute-start | bytes 835592 | tf_op jit(solution)/shard_map/ppermute | solution.py:900
  42.1 15.7 %collective-permute-start.8 = (f32[17,8,512]{2,1,0:T(8,128)S(1)}, f32[17,8,512]{2,1,0:T(8,128)S(1)}, u32[]{:S(2)}, u32[]{:S(2)}) collective-permute-start(f32[17,8,512]{2,1,0:T(8,128)S(1)} %get-tuple-element.95), channel_id=1, source_target_pairs={{0,2},{2,0},{4,6},{6,4},{8,10},{10,8},{12,14},{14,12},{1,3},{3,1},... | collective-permute-start | bytes 835592 | tf_op jit(solution)/shard_map/ppermute | solution.py:907
  44.1 12.6 %collective-permute-start.7 = (f32[4,4,8,512]{3,2,1,0:T(8,128)S(1)}, f32[4,4,8,512]{3,2,1,0:T(8,128)S(1)}, u32[]{:S(2)}, u32[]{:S(2)}) collective-permute-start(f32[4,4,8,512]{3,2,1,0:T(8,128)S(1)} %pad_maximum_fusion.1), channel_id=1, source_target_pairs={{0,4},{2,6},{4,0},{6,2},{8,12},{10,14},{12,8},{14,10},{1,5},{3,7},... | collective-permute-start | bytes 786440 | tf_op jit(solution)/shard_map/ppermute | solution.py:652
  49.5 16.8 %collective-permute-start.12 = (f32[17,8,512]{2,1,0:T(8,128)S(1)}, f32[17,8,512]{2,1,0:T(8,128)S(1)}, u32[]{:S(2)}, u32[]{:S(2)}) collective-permute-start(f32[17,8,512]{2,1,0:T(8,128)S(1)} %get-tuple-element.113), channel_id=1, source_target_pairs={{0,0},{2,4},{4,2},{6,8},{8,6},{10,12},{12,10},{14,14},{1,1},{3,5},... | collective-permute-start | bytes 835592 | tf_op jit(solution)/shard_map/ppermute | solution.py:900
  58.6 10.4 %collective-permute-start.10 = (f32[17,8,512]{2,1,0:T(8,128)S(1)}, f32[17,8,512]{2,1,0:T(8,128)S(1)}, u32[]{:S(2)}, u32[]{:S(2)}) collective-permute-start(f32[17,8,512]{2,1,0:T(8,128)S(1)} %get-tuple-element.106), channel_id=1, source_target_pairs={{0,2},{2,0},{4,6},{6,4},{8,10},{10,8},{12,14},{14,12},{1,3},{3,1},... | collective-permute-start | bytes 835592 | tf_op jit(solution)/shard_map/ppermute | solution.py:907
  63.7 2.7 %copy-start.2 = (f32[2,32,512]{2,1,0:T(8,128)S(1)}, f32[2,32,512]{2,1,0:T(8,128)}, u32[]{:S(2)}) copy-start(f32[2,32,512]{2,1,0:T(8,128)} %tension_ref.3) | copy-start | bytes 393220
  70.7 1.2 %collective-permute-start.14 = (f32[8,256]{1,0:T(8,128)S(1)}, f32[8,256]{1,0:T(8,128)S(1)}, u32[]{:S(2)}, u32[]{:S(2)}) collective-permute-start(f32[8,256]{1,0:T(8,128)S(1)} %get-tuple-element.129), channel_id=1, source_target_pairs={{0,1},{1,0},{2,3},{3,2},{4,5},{5,4},{6,7},{7,6},{8,9},{9,8},{10,11... | collective-permute-start | bytes 24584 | tf_op jit(solution)/shard_map/ppermute | solution.py:921
  71.9 5.5 %collective-permute-start.15 = (f32[1,24,256]{2,1,0:T(8,128)S(1)}, f32[1,24,256]{2,1,0:T(8,128)S(1)}, u32[]{:S(2)}, u32[]{:S(2)}) collective-permute-start(f32[1,24,256]{2,1,0:T(8,128)S(1)} %maximum_bitcast_fusion.rest_0_), channel_id=1, source_target_pairs={{0,8},{2,10},{4,12},{6,14},{8,0},{10,2},{12,4},{14,6},{1,9},{3,11}... | collective-permute-start | bytes 73736 | tf_op jit(solution)/shard_map/ppermute | solution.py:652
  76.3 8.6 %collective-permute-start.13 = (f32[8,4,8,256]{3,2,1,0:T(8,128)S(1)}, f32[8,4,8,256]{3,2,1,0:T(8,128)S(1)}, u32[]{:S(2)}, u32[]{:S(2)}) collective-permute-start(f32[8,4,8,256]{3,2,1,0:T(8,128)S(1)} %facing.1), channel_id=1, source_target_pairs={{0,1},{1,0},{2,3},{3,2},{4,5},{5,4},{6,7},{7,6},{8,9},{9,8},{10,11... | collective-permute-start | bytes 786440 | tf_op jit(solution)/shard_map/ppermute | solution.py:913
  77.4 4.1 %collective-permute-start.16 = (f32[2,24,256]{2,1,0:T(8,128)S(1)}, f32[2,24,256]{2,1,0:T(8,128)S(1)}, u32[]{:S(2)}, u32[]{:S(2)}) collective-permute-start(f32[2,24,256]{2,1,0:T(8,128)S(1)} %pad_maximum_fusion.4), channel_id=1, source_target_pairs={{0,2},{2,0},{4,6},{6,4},{8,10},{10,8},{12,14},{14,12},{1,3},{3,1},... | collective-permute-start | bytes 147464 | tf_op jit(solution)/shard_map/ppermute | solution.py:652
  81.5 6.4 %collective-permute-start.17 = (f32[4,24,256]{2,1,0:T(8,128)S(1)}, f32[4,24,256]{2,1,0:T(8,128)S(1)}, u32[]{:S(2)}, u32[]{:S(2)}) collective-permute-start(f32[4,24,256]{2,1,0:T(8,128)S(1)} %pad_maximum_fusion.3), channel_id=1, source_target_pairs={{0,4},{2,6},{4,0},{6,2},{8,12},{10,14},{12,8},{14,10},{1,5},{3,7},... | collective-permute-start | bytes 294920 | tf_op jit(solution)/shard_map/ppermute | solution.py:652
  (1 other events, 0.9 us)

commit v7 on v6

--- a/solution.py
+++ b/solution.py
@@ -24,7 +24,6 @@
 
 SLAB, SIDE, FLIP, FAR = range(4)
 
-HIGHEST = lax.Precision.HIGHEST
 LIMIT = 40 * 1024 * 1024
 
 
@@ -66,6 +65,16 @@
     before = jnp.where(tile == 0, tiles - 1, tile - 1)
     after = jnp.where(tile == tiles - 1, 0, tile + 1)
     return before, after
+
+
+def split_dot(rest, pick):
+    total = None
+    for _ in range(3):
+        part = rest.astype(jnp.bfloat16)
+        rest = rest - part.astype(jnp.float32)
+        product = jnp.dot(part, pick, preferred_element_type=jnp.float32)
+        total = product if total is None else total + product
+    return total
 
 
 def coeff_kernel(info_ref, cond_ref, strip_ref, out_ref):
@@ -73,41 +82,43 @@
     turn = jnp.where(info_ref[FLIP] == 1, -0.5, 0.5)
     upper_side = info_ref[SIDE] == 0
     fine = 4 * width
-    mech = lax.broadcasted_iota(jnp.int32, (width, fine), 0)
-    cell = lax.broadcasted_iota(jnp.int32, (width, fine), 1)
+    apart = lax.broadcasted_iota(jnp.int32, (width, fine), 1) - 4 * lax.broadcasted_iota(jnp.int32, (width, fine), 0)
     own = rows // 2
-    block = rows + 8
-    sub = lax.broadcasted_iota(jnp.int32, (8, fine), 0)
-
-    def spread(comps, shift):
-        pick = jnp.where(mech == ((cell + shift) >> 2), 1.0, 0.0)
-        flat = jnp.concatenate([part for comp in comps for part in (cond_ref[comp, 0], strip_ref[comp])], axis=0)
-        wide = jnp.dot(flat, pick, precision=HIGHEST, preferred_element_type=jnp.float32)
-        return [wide[pos * block : (pos + 1) * block] for pos in range(len(comps))]
-
-    def both(first, second):
-        return jnp.where(sub < 4, jnp.broadcast_to(first, (8, fine)), jnp.broadcast_to(second, (8, fine)))
-
-    def store(index, wide):
-        for tile in range(own):
-            out_ref[index, tile] = both(wide[2 * tile : 2 * tile + 1], wide[2 * tile + 1 : 2 * tile + 2])
-        head = both(wide[rows : rows + 1], wide[rows + 1 : rows + 2])
-        tail = both(wide[block - 2 : block - 1], wide[block - 1 : block])
-        out_ref[index, own] = jnp.where(upper_side, head, tail)
-
-    zz, yy, xx, zy = spread((0, 1, 2, 3), 0)
-    store(C_ZZ, zz)
-    store(C_YY, yy)
-    store(C_MID, 1.0 - 2.0 * (zz + yy + xx))
-    store(C_ZY, turn * zy)
-    xx, zx, yx = spread((2, 4, 5), -1)
-    store(C_XXR, xx)
-    store(C_ZXR, turn * zx)
-    store(C_YXR, 0.5 * yx)
-    xx, zx, yx = spread((2, 4, 5), 1)
-    store(C_XXL, xx)
-    store(C_ZXL, turn * zx)
-    store(C_YXL, 0.5 * yx)
+    sub = lax.broadcasted_iota(jnp.int32, (8, width), 0)
+
+    def tall(val):
+        tiles = []
+        for row in range(0, val.shape[0], 2):
+            first, second = (jnp.broadcast_to(val[at : at + 1], (8, width)) for at in (row, row + 1))
+            tiles.append(jnp.where(sub < 4, first, second))
+        return tiles
+
+    comps = []
+    for comp in range(6):
+        strip = tall(strip_ref[comp])
+        comps.append(tall(cond_ref[comp, 0]) + [jnp.where(upper_side, strip[0], strip[-1])])
+
+    def spread(names, shift):
+        pick = jnp.where((apart >= -shift) & (apart < 4 - shift), 1.0, 0.0).astype(jnp.bfloat16)
+        return split_dot(jnp.concatenate([tile for name in names for tile in comps[name]], axis=0), pick)
+
+    def store(index, wide, place, factor):
+        for tile in range(own + 1):
+            at = 8 * (place * (own + 1) + tile)
+            out_ref[index, tile] = wide[at : at + 8] if factor is None else factor * wide[at : at + 8]
+
+    wide = spread((0, 1, 3, 2), 0)
+    store(C_ZZ, wide, 0, None)
+    store(C_YY, wide, 1, None)
+    store(C_ZY, wide, 2, turn)
+    for tile in range(own + 1):
+        zz, yy, xx = (wide[8 * (place * (own + 1) + tile) :][:8] for place in (0, 1, 3))
+        out_ref[C_MID, tile] = 1.0 - 2.0 * (zz + yy + xx)
+    for shift, (name_xx, name_zx, name_yx) in ((-1, (C_XXR, C_ZXR, C_YXR)), (1, (C_XXL, C_ZXL, C_YXL))):
+        wide = spread((2, 4, 5), shift)
+        store(name_xx, wide, 0, None)
+        store(name_zx, wide, 1, turn)
+        store(name_yx, wide, 2, 0.5)
 
 
 def fine_coeffs(info, cond, strip):
@@ -193,16 +204,13 @@
     )(disp, fiber)
 
 
-def sends_kernel(info_ref, edge_ref, states_ref, *refs):
-    field_refs, (far_ref, near_ref) = refs[:-2], refs[-2:]
+def sends_kernel(info_ref, edge_ref, states_ref, far_ref, near_ref):
     flip, side = info_ref[FLIP], info_ref[SIDE]
     planes, own = states_ref.shape[1:3]
     for pos, (ref, plane) in enumerate([(far_ref, flip * (planes - 1)), (near_ref, (1 - flip) * (planes - 1))]):
         for tile in range(own):
             store_sent(ref, tile, own + 1, states_ref[0, plane, tile], side)
         store_sent(ref, own, own + 1, edge_ref[pos], side)
-    for pos, ref in enumerate(field_refs):
-        near_ref[SENT + FIELD * pos : SENT + FIELD * (pos + 1)] = ref[0]
 
 
 def facing_parts(info, tiled, cond):
@@ -222,17 +230,17 @@
     )(info, tiled, cond)
 
 
-def first_sends(info, edges, tiled, fields):
+def first_sends(info, edges, tiled):
     width = tiled.shape[-1]
     return pl.pallas_call(
         sends_kernel,
-        in_specs=[SMEM] + [VMEM] * (2 + len(fields)),
+        in_specs=[SMEM] + [VMEM] * 2,
         out_specs=[VMEM] * 2,
-        out_shape=[shape_of(SENT, 8, width // 2), shape_of(SENT + FIELD * len(fields), 8, width // 2)],
+        out_shape=[shape_of(SENT, 8, width // 2)] * 2,
         compiler_params=params(),
         cost_estimate=cost(0, 1_200_000),
         name="sends",
-    )(info, edges, tiled, *fields)
+    )(info, edges, tiled)
 
 
 def fraction(val):
@@ -411,12 +419,11 @@
 
 def halo_step(half, info, outer, halo, coeffs):
     tiles, _, width = outer.shape
-    vmem = pl.BlockSpec(memory_space=pltpu.VMEM)
     cells = tiles * 8 * width
     return pl.pallas_call(
         functools.partial(halo_kernel, half, tiles),
-        in_specs=[pl.BlockSpec(memory_space=pltpu.SMEM)] + [vmem] * 3,
-        out_specs=[vmem, vmem],
+        in_specs=[SMEM] + [VMEM] * 3,
+        out_specs=[VMEM] * 2,
         out_shape=[shape_of(*outer.shape), shape_of(SENT, 8, width // 2)],
         compiler_params=params(),
         cost_estimate=cost(15 * cells, 20 * cells),
@@ -435,13 +442,7 @@
         even = rows_ref[chunk, pl.ds(0, rows // 2, stride=2), :]
         few.append(even + rows_ref[chunk, pl.ds(1, rows // 2, stride=2), :])
     pairs = [jnp.concatenate(few[pos : pos + 2], axis=1) for pos in range(0, len(few), 2)]
-    rest = jnp.concatenate(pairs, axis=0)
-    total = None
-    for _ in range(3):
-        part = rest.astype(jnp.bfloat16)
-        rest = rest - part.astype(jnp.float32)
-        mean = jnp.dot(part, pick, preferred_element_type=jnp.float32)
-        total = mean if total is None else total + mean
+    total = split_dot(jnp.concatenate(pairs, axis=0), pick)
     count = rows // 2
     return jnp.concatenate([total[pos * count : (pos + 1) * count] for pos in range(len(pairs))], axis=1)
 
@@ -881,35 +882,30 @@
     edges = lax.ppermute(edges, "col", swap)
     cond_strip = lax.ppermute(cond_rows, "col", swap)
     strip = lax.ppermute(facing, "col", swap)
-    carried = fields.parts if fields.doubling else []
-    far, near = first_sends(info, edges, tiled, carried)
+    far, near = first_sends(info, edges, tiled)
     far_halo = lax.ppermute(far, "slab", others)
     near_halo = lax.ppermute(near, "slab", pairs)
-
     coeffs = fine_coeffs(info, cond, cond_strip)
     whole = jnp.concatenate([tiled, strip[:, :, None]], axis=2)
 
     far_part, far_inner, far_gates = half_step("first", FAR_HALF, info, (whole,), coeffs)
-    near_part, near_inner, near_gates = half_step("first", NEAR_HALF, info, (whole,), coeffs)
-    if fields.doubling:
-        near_part, near_halo = tie(near_part, near_halo)
-        fields.take(near_halo[SENT:][None])
+    near_kind, near_arrays = "first", (whole,)
     for turn_index in range(1, SUB):
         last = turn_index == SUB - 1
+        kind = "last" if last else "middle"
         far, far_send = halo_step(FAR_HALF, info, far_part, far_halo, coeffs)
+        far_send, *near_arrays = tie(far_send, *near_arrays)
+        near_part, near_inner, near_gates = half_step(near_kind, NEAR_HALF, info, near_arrays, coeffs)
         far_halo = lax.ppermute(far_send, "slab", others)
-        far_arrays = (far, far_inner, near_inner, far_gates)
-        kind = "last" if last else "middle"
-        far_part, far_next, far_gates = half_step(kind, FAR_HALF, info, far_arrays, coeffs)
-        if turn_index >= 2:
-            near_part, *fields.parts = tie(near_part, *fields.parts)
+        far_part, far_next, far_gates = half_step(kind, FAR_HALF, info, (far, far_inner, near_inner, far_gates), coeffs)
+        if last:
+            near_part, far_part, *fields.parts = tie(near_part, far_part, *fields.parts)
         near, near_send = halo_step(NEAR_HALF, info, near_part, near_halo, coeffs)
         near_halo = lax.ppermute(near_send, "slab", pairs)
-        if not last:
-            fields.round()
-        near_arrays = (near, near_inner, far_inner, near_gates)
-        near_part, near_inner, near_gates = half_step(kind, NEAR_HALF, info, near_arrays, coeffs)
+        fields.round()
+        near_kind, near_arrays = kind, (near, near_inner, far_inner, near_gates)
         far_inner = far_next
+    near_part, near_inner, near_gates = half_step(near_kind, NEAR_HALF, info, near_arrays, coeffs)
     strips = lax.ppermute(facing_rows(info, fields.parts), "col", swap)
     states_next, tension_next, active = finish_half(
         FAR_HALF, info, far_part, far_inner, far_halo, coeffs, tension, (far_gates, near_inner, near_gates)

time: 92.3 us -> 91.1 us (0.987)
  starting transfers between devices: 31 us -> 28.9 us
  waiting for transfers between devices: 13.2 us -> 14.9 us
    ppermute x1, waiting for transfers between devices: 1.55 us -> 7.37 us  [on_device(): near_halo = lax.ppermute(near, 'slab', pairs)]
    ppermute x5 -> x6, starting transfers between devices: 13 us -> 9.04 us  [round(): self.take(lax.ppermute(held, 'slab', perm))]
    ppermute x1, starting transfers between devices: 2.92 us -> 5.7 us  [on_device(): near_halo = lax.ppermute(near, 'slab', pairs)]
    ppermute x5 -> x6, waiting for transfers between devices: 7.33 us -> 4.94 us  [round(): self.take(lax.ppermute(held, 'slab', perm))]
    ppermute x3, starting transfers between devices: 11.6 us -> 10.2 us  [on_device(): near_halo = lax.ppermute(near_send, 'slab', pairs)]
  transfers between devices with their start and end apart: 18 -> 19, of which waited for: 8 -> 7; matrix products, arithmetic and copies ran while one was open for 1% -> 1% of each run, Pallas kernels for 40% -> 41%
where the time goes in v7:
time: 91.1 us; the launch traced here: 90.9 us
  Pallas kernels  42 us (46%)
  starting transfers between devices  28.9 us (32%)
  waiting for transfers between devices  14.9 us (16%)
  local copies, waits for them, and re-layouts  3.11 us (3%)
  other arithmetic  1.01 us (1%)
  between operations  0.98 us (1%)
    pallas_call x8, Pallas kernels, half_step(): pl.pallas_call(functools.partial(half_kernel, kind, half, tiles), in_spec...  22.6 us
    ppermute x3, starting transfers between devices, on_device(): near_halo = lax.ppermute(near_send, 'slab', pairs)  10.2 us
    ppermute x6, starting transfers between devices, round(): self.take(lax.ppermute(held, 'slab', perm))  9.04 us
    ppermute x1, waiting for transfers between devices, on_device(): near_halo = lax.ppermute(near, 'slab', pairs)  7.37 us
    ppermute x1, starting transfers between devices, on_device(): near_halo = lax.ppermute(near, 'slab', pairs)  5.7 us
    ppermute x6, waiting for transfers between devices, round(): self.take(lax.ppermute(held, 'slab', perm))  4.94 us
    pallas_call x2, Pallas kernels, finish_half(): pl.pallas_call(functools.partial(finish_kernel, half, tiles), in_specs=in...  4.26 us
    pallas_call x1, Pallas kernels, mechanics_step(): pl.pallas_call(functools.partial(mechanics_kernel, planes), in_specs=[pl....  4.14 us
  transfers between devices with their start and end apart: 19, of which 7 were waited for; matrix products, arithmetic and copies ran while one was open for 1% of the time, Pallas kernels for 41%

profile of v7, /device:TPU:0, one launch (start us, length us, event | category | flops | bytes accessed | tf_op | source)
XLA Modules:
  0.0 90.9 jit_solution(7038320952344937802)
XLA Ops:
  0.7 2.2 %copy-done = f32[4,4,64,1024]{3,2,1,0:T(8,128)S(1)} copy-done((f32[4,4,64,1024]{3,2,1,0:T(8,128)S(1)}, f32[4,4,64,1024]{3,2,1,0:T(8,128)}, u32[]{:S(2)}) %copy-start) | copy-done | bytes 4194328
  8.0 5.7 %collective-permute-start.5 = (f32[17,8,512]{2,1,0:T(8,128)S(1)}, f32[17,8,512]{2,1,0:T(8,128)S(1)}, u32[]{:S(2)}, u32[]{:S(2)}) collective-permute-start(f32[17,8,512]{2,1,0:T(8,128)S(1)} %get-tuple-element.91), channel_id=1, source_target_pairs={{0,2},{2,0},{4,6},{6,4},{8,10},{10,8},{12,14},{14,12},{1,3},{3,1},... | collective-permute-start | bytes 835592 | tf_op jit(solution)/shard_map/ppermute | solution.py:887
  13.7 2.2 %coeffs.1.refs_1_.coeff_ref.refs_4_ = f32[10,9,8,1024]{3,2,1,0:T(8,128)S(1)} custom-call(s32[4]{0:T(128)S(1)} %pad_add_fusion.info_ref, f32[6,1,16,256]{3,2,1,0:T(8,128)S(1)} %copy-done.4, f32[6,8,256]{2,1,0:T(8,128)S(1)} %collective-permute-done.1.strip_ref), custom_call_target="tpu_custom_call" | custom-call | flops 2000000 | bytes 3200000 | tf_op jit(solution)/shard_map/coeffs/pallas_call | solution.py:127
  16.6 2.9 %first_far.1 = (f32[9,8,1024]{2,1,0:T(8,128)S(1)}, f32[9,8,1024]{2,1,0:T(8,128)S(1)}, f32[3,2,9,8,1024]{4,3,2,1,0:T(8,128)S(1)}) custom-call(s32[4]{0:T(128)S(1)} %pad_add_fusion.info_ref, f32[4,4,9,8,1024]{4,3,2,1,0:T(8,128)S(1)} %pad_maximum_fusion.refs_0_, f32[10,9,8,1024]{3,2,1,0:T(8,128)S(1)} %coeffs.1.refs_1_.coeff_ref.refs_4_), custom_call_target="tpu_custom_call" | custom-call | flops 14745600 | bytes 5898240 | tf_op jit(solution)/shard_map/first_far/pallas_call | solution.py:371
  20.8 2.9 %first_near.1 = (f32[9,8,1024]{2,1,0:T(8,128)S(1)}, f32[9,8,1024]{2,1,0:T(8,128)S(1)}, f32[3,2,9,8,1024]{4,3,2,1,0:T(8,128)S(1)}) custom-call(s32[4]{0:T(128)S(1)} %pad_add_fusion.info_ref, f32[4,4,9,8,1024]{4,3,2,1,0:T(8,128)S(1)} %pad_maximum_fusion.refs_0_, f32[10,9,8,1024]{3,2,1,0:T(8,128)S(1)} %coeffs.1.refs_1_.coeff_ref.refs_4_), custom_call_target="tpu_custom_call" | custom-call | flops 14745600 | bytes 5898240 | tf_op jit(solution)/shard_map/first_near/pallas_call | solution.py:371
  23.7 7.4 %collective-permute-done.5.halo_ref = f32[17,8,512]{2,1,0:T(8,128)S(1)} collective-permute-done((f32[17,8,512]{2,1,0:T(8,128)S(1)}, f32[17,8,512]{2,1,0:T(8,128)S(1)}, u32[]{:S(2)}, u32[]{:S(2)}) %collective-permute-start.5) | collective-permute-done | bytes 278560 | tf_op jit(solution)/shard_map/ppermute | solution.py:887
  31.9 2.5 %collective-permute-start.7 = (f32[17,8,512]{2,1,0:T(8,128)S(1)}, f32[17,8,512]{2,1,0:T(8,128)S(1)}, u32[]{:S(2)}, u32[]{:S(2)}) collective-permute-start(f32[17,8,512]{2,1,0:T(8,128)S(1)} %get-tuple-element.104), channel_id=1, source_target_pairs={{0,2},{2,0},{4,6},{6,4},{8,10},{10,8},{12,14},{14,12},{1,3},{3,1},... | collective-permute-start | bytes 835592 | tf_op jit(solution)/shard_map/ppermute | solution.py:904
  34.5 2.9 %middle_far.2 = (f32[9,8,1024]{2,1,0:T(8,128)S(1)}, f32[9,8,1024]{2,1,0:T(8,128)S(1)}, f32[3,2,9,8,1024]{4,3,2,1,0:T(8,128)S(1)}) custom-call(s32[4]{0:T(128)S(1)} %pad_add_fusion.info_ref, f32[9,8,1024]{2,1,0:T(8,128)S(1)} %get-tuple-element.79.refs_0_, f32[9,8,1024]{2,1,0:T(8,128)S(1)} %get-tuple-element.96.refs_1_.refs_2_, ...), custom_call_target="tpu_custom_call" | custom-call | flops 14745600 | bytes 5898240 | tf_op jit(solution)/shard_map/middle_far/pallas_call | solution.py:371
  38.7 2.9 %middle_near.2 = (f32[9,8,1024]{2,1,0:T(8,128)S(1)}, f32[9,8,1024]{2,1,0:T(8,128)S(1)}, f32[3,2,9,8,1024]{4,3,2,1,0:T(8,128)S(1)}) custom-call(s32[4]{0:T(128)S(1)} %pad_add_fusion.info_ref, f32[9,8,1024]{2,1,0:T(8,128)S(1)} %get-tuple-element.94.refs_0_, f32[9,8,1024]{2,1,0:T(8,128)S(1)} %get-tuple-element.95.refs_2_.refs_1_, ...), custom_call_target="tpu_custom_call" | custom-call | flops 14745600 | bytes 5898240 | tf_op jit(solution)/shard_map/middle_near/pallas_call | solution.py:371
  42.6 4.8 %collective-permute-start.10 = (f32[17,8,512]{2,1,0:T(8,128)S(1)}, f32[17,8,512]{2,1,0:T(8,128)S(1)}, u32[]{:S(2)}, u32[]{:S(2)}) collective-permute-start(f32[17,8,512]{2,1,0:T(8,128)S(1)} %get-tuple-element.118), channel_id=1, source_target_pairs={{0,2},{2,0},{4,6},{6,4},{8,10},{10,8},{12,14},{14,12},{1,3},{3,1},... | collective-permute-start | bytes 835592 | tf_op jit(solution)/shard_map/ppermute | solution.py:904
  47.4 2.7 %collective-permute-start.9 = (f32[2,4,8,512]{3,2,1,0:T(8,128)S(1)}, f32[2,4,8,512]{3,2,1,0:T(8,128)S(1)}, u32[]{:S(2)}, u32[]{:S(2)}) collective-permute-start(f32[2,4,8,512]{3,2,1,0:T(8,128)S(1)} %pad_maximum_fusion.2), channel_id=1, source_target_pairs={{0,8},{2,10},{4,12},{6,14},{8,0},{10,2},{12,4},{14,6},{1,9},{3,11}... | collective-permute-start | bytes 393224 | tf_op jit(solution)/shard_map/ppermute | solution.py:653
  50.1 2.9 %middle_far.3 = (f32[9,8,1024]{2,1,0:T(8,128)S(1)}, f32[9,8,1024]{2,1,0:T(8,128)S(1)}, f32[3,2,9,8,1024]{4,3,2,1,0:T(8,128)S(1)}) custom-call(s32[4]{0:T(128)S(1)} %pad_add_fusion.info_ref, f32[9,8,1024]{2,1,0:T(8,128)S(1)} %get-tuple-element.87.refs_0_, f32[9,8,1024]{2,1,0:T(8,128)S(1)} %get-tuple-element.109.refs_1_.refs_2_, ...), custom_call_target="tpu_custom_call" | custom-call | flops 14745600 | bytes 5898240 | tf_op jit(solution)/shard_map/middle_far/pallas_call | solution.py:371
  54.3 2.9 %middle_near.3 = (f32[9,8,1024]{2,1,0:T(8,128)S(1)}, f32[9,8,1024]{2,1,0:T(8,128)S(1)}, f32[3,2,9,8,1024]{4,3,2,1,0:T(8,128)S(1)}) custom-call(s32[4]{0:T(128)S(1)} %pad_add_fusion.info_ref, f32[9,8,1024]{2,1,0:T(8,128)S(1)} %get-tuple-element.107.refs_0_, f32[9,8,1024]{2,1,0:T(8,128)S(1)} %get-tuple-element.108.refs_2_.refs_1_, ...), custom_call_target="tpu_custom_call" | custom-call | flops 14745600 | bytes 5898240 | tf_op jit(solution)/shard_map/middle_near/pallas_call | solution.py:371
  57.2 2.6 %last_far.1 = (f32[8,8,1024]{2,1,0:T(8,128)S(1)}, f32[8,8,1024]{2,1,0:T(8,128)S(1)}, f32[3,2,8,8,1024]{4,3,2,1,0:T(8,128)S(1)}) custom-call(s32[4]{0:T(128)S(1)} %pad_add_fusion.info_ref, f32[9,8,1024]{2,1,0:T(8,128)S(1)} %get-tuple-element.112.refs_0_, f32[9,8,1024]{2,1,0:T(8,128)S(1)} %get-tuple-element.113.refs_1_.refs_2_, ...), custom_call_target="tpu_custom_call" | custom-call | flops 14745600 | bytes 5898240 | tf_op jit(solution)/shard_map/last_far/pallas_call | solution.py:371
  60.6 2.9 %collective-permute-start.11 = (f32[17,8,512]{2,1,0:T(8,128)S(1)}, f32[17,8,512]{2,1,0:T(8,128)S(1)}, u32[]{:S(2)}, u32[]{:S(2)}) collective-permute-start(f32[17,8,512]{2,1,0:T(8,128)S(1)} %get-tuple-element.123), channel_id=1, source_target_pairs={{0,2},{2,0},{4,6},{6,4},{8,10},{10,8},{12,14},{14,12},{1,3},{3,1},... | collective-permute-start | bytes 835592 | tf_op jit(solution)/shard_map/ppermute | solution.py:904
  64.5 2.6 %last_near.1 = (f32[8,8,1024]{2,1,0:T(8,128)S(1)}, f32[8,8,1024]{2,1,0:T(8,128)S(1)}, f32[3,2,8,8,1024]{4,3,2,1,0:T(8,128)S(1)}) custom-call(s32[4]{0:T(128)S(1)} %pad_add_fusion.info_ref, f32[9,8,1024]{2,1,0:T(8,128)S(1)} %get-tuple-element.119.refs_0_, f32[9,8,1024]{2,1,0:T(8,128)S(1)} %get-tuple-element.114.refs_2_.refs_1_, ...), custom_call_target="tpu_custom_call" | custom-call | flops 14745600 | bytes 5898240 | tf_op jit(solution)/shard_map/last_near/pallas_call | solution.py:371
  67.2 2.6 %finish_far.1 = (f32[4,4,8,8,1024]{4,3,2,1,0:T(8,128)}, f32[2,32,512]{2,1,0:T(8,128)}, f32[16,256]{1,0:T(8,128)S(1)}) custom-call(s32[4]{0:T(128)S(1)} %pad_add_fusion.info_ref, f32[8,8,1024]{2,1,0:T(8,128)S(1)} %get-tuple-element.124.outer_ref, f32[8,8,1024]{2,1,0:T(8,128)S(1)} %get-tuple-element.125.inner_ref, ...), custom_call_target="tpu_custom_call" | custom-call | flops 2621440 | bytes 2621440 | tf_op jit(solution)/shard_map/finish_far/pallas_call | solution.py:507
  69.8 1.6 %finish_near.1 = (f32[4,4,8,8,1024]{4,3,2,1,0:T(8,128)}, f32[2,32,512]{2,1,0:T(8,128)}, f32[16,256]{1,0:T(8,128)S(1)}, f32[8,256]{1,0:T(8,128)S(1)}) custom-call(s32[4]{0:T(128)S(1)} %pad_add_fusion.info_ref, f32[8,8,1024]{2,1,0:T(8,128)S(1)} %get-tuple-element.121.outer_ref, ...), custom_call_target="tpu_custom_call", output_to_operand_aliasing={{0}: (7, {}), {1}: (8, {})} | custom-call | flops 2621440 | bytes 2621440 | tf_op jit(solution)/shard_map/finish_near/pallas_call | solution.py:507
  72.7 3.2 %collective-permute-start.16 = (f32[1,24,256]{2,1,0:T(8,128)S(1)}, f32[1,24,256]{2,1,0:T(8,128)S(1)}, u32[]{:S(2)}, u32[]{:S(2)}) collective-permute-start(f32[1,24,256]{2,1,0:T(8,128)S(1)} %maximum_bitcast_fusion.rest_0_), channel_id=1, source_target_pairs={{0,8},{2,10},{4,12},{6,14},{8,0},{10,2},{12,4},{14,6},{1,9},{3,11}... | collective-permute-start | bytes 73736 | tf_op jit(solution)/shard_map/ppermute | solution.py:653
  76.7 1.3 %collective-permute-done.16.rest_1_ = f32[1,24,256]{2,1,0:T(8,128)S(1)} collective-permute-done((f32[1,24,256]{2,1,0:T(8,128)S(1)}, f32[1,24,256]{2,1,0:T(8,128)S(1)}, u32[]{:S(2)}, u32[]{:S(2)}) %collective-permute-start.16) | collective-permute-done | bytes 24608 | tf_op jit(solution)/shard_map/ppermute | solution.py:653
  78.0 1.5 %collective-permute-start.17 = (f32[2,24,256]{2,1,0:T(8,128)S(1)}, f32[2,24,256]{2,1,0:T(8,128)S(1)}, u32[]{:S(2)}, u32[]{:S(2)}) collective-permute-start(f32[2,24,256]{2,1,0:T(8,128)S(1)} %pad_maximum_fusion.4), channel_id=1, source_target_pairs={{0,2},{2,0},{4,6},{6,4},{8,10},{10,8},{12,14},{14,12},{1,3},{3,1},... | collective-permute-start | bytes 147464 | tf_op jit(solution)/shard_map/ppermute | solution.py:653
  79.6 2.5 %collective-permute-done.17.rest_2_ = f32[2,24,256]{2,1,0:T(8,128)S(1)} collective-permute-done((f32[2,24,256]{2,1,0:T(8,128)S(1)}, f32[2,24,256]{2,1,0:T(8,128)S(1)}, u32[]{:S(2)}, u32[]{:S(2)}) %collective-permute-start.17) | collective-permute-done | bytes 49184 | tf_op jit(solution)/shard_map/ppermute | solution.py:653
  82.7 3.0 %passive.1 = (f32[6,9,24,256]{3,2,1,0:T(8,128)S(1)}, f32[9,9,24,256]{3,2,1,0:T(8,128)S(1)}, f32[9,9,24,256]{3,2,1,0:T(8,128)S(1)}) custom-call(s32[4]{0:T(128)S(1)} %pad_add_fusion.info_ref, f32[3,128]{1,0:T(4,128)S(1)} %pad_maximum_fusion.5.table_ref, f32[8,4,8,256]{3,2,1,0:T(8,128)S(1)} %collective-permute-done.14.strip_ref, ...), custom_call_target="tpu_custom_call" | custom-call | flops 22118400 | bytes 5000000 | tf_op jit(solution)/shard_map/passive/pallas_call | solution.py:767
  86.8 4.1 %mechanics.1 = (f32[3,1,16,256]{3,2,1,0:T(8,128)}, f32[6,1,16,256]{3,2,1,0:T(8,128)}) custom-call(s32[4]{0:T(128)S(1)} %pad_add_fusion.info_ref, f32[6,9,24,256]{3,2,1,0:T(8,128)S(1)} %get-tuple-element.137.disp_ref, f32[9,9,24,256]{3,2,1,0:T(8,128)S(1)} %get-tuple-element.138.stress_ref, f32[9,9,24,256]{3,2,1,0:T(8,128)S(1)} %get-tuple-element.139.pull_ref, ...), custom_call_target="tpu_custom_call" | custom-call | flops 22118400 | bytes 5000000 | tf_op jit(solution)/shard_map/mechanics/pallas_call | solution.py:844
  (61 shorter events, 17.1 us)
Async XLA Ops:
  4.4 11.5 %collective-permute-start = (f32[4,4,8,1024]{3,2,1,0:T(8,128)S(1)}, f32[4,4,8,1024]{3,2,1,0:T(8,128)S(1)}, u32[]{:S(2)}, u32[]{:S(2)}) collective-permute-start(f32[4,4,8,1024]{3,2,1,0:T(8,128)S(1)} %get-tuple-element.74), channel_id=1, source_target_pairs={{0,1},{1,0},{2,3},{3,2},{4,5},{5,4},{6,7},{7,6},{8,9},{9,8},{10,11... | collective-permute-start | bytes 1572872 | tf_op jit(solution)/shard_map/ppermute | solution.py:884
  4.9 1.6 %collective-permute-start.2 = (f32[2,8,1024]{2,1,0:T(8,128)S(1)}, f32[2,8,1024]{2,1,0:T(8,128)S(1)}, u32[]{:S(2)}, u32[]{:S(2)}) collective-permute-start(f32[2,8,1024]{2,1,0:T(8,128)S(1)} %get-tuple-element.77), channel_id=1, source_target_pairs={{0,1},{1,0},{2,3},{3,2},{4,5},{5,4},{6,7},{7,6},{8,9},{9,8},{10,11... | collective-permute-start | bytes 196616 | tf_op jit(solution)/shard_map/ppermute | solution.py:882
  5.0 8.7 %copy-start.4 = (f32[6,1,16,256]{3,2,1,0:T(8,128)S(1)}, f32[6,1,16,256]{3,2,1,0:T(8,128)}, u32[]{:S(2)}) copy-start(f32[6,1,16,256]{3,2,1,0:T(8,128)} %cond_ref.3) | copy-start | bytes 294916
  5.0 8.7 %collective-permute-start.1 = (f32[6,8,256]{2,1,0:T(8,128)S(1)}, f32[6,8,256]{2,1,0:T(8,128)S(1)}, u32[]{:S(2)}, u32[]{:S(2)}) collective-permute-start(f32[6,8,256]{2,1,0:T(8,128)S(1)} %get-tuple-element.75), channel_id=1, source_target_pairs={{0,1},{1,0},{2,3},{3,2},{4,5},{5,4},{6,7},{7,6},{8,9},{9,8},{10,11... | collective-permute-start | bytes 147464 | tf_op jit(solution)/shard_map/ppermute | solution.py:883
  6.6 9.3 %copy-start.1 = (f32[4,4,64,1024]{3,2,1,0:T(8,128)S(1)}, f32[4,4,64,1024]{3,2,1,0:T(8,128)}, u32[]{:S(2)}) copy-start(f32[4,4,64,1024]{3,2,1,0:T(8,128)} %param.5) | copy-start | bytes 12582916
  7.1 12.4 %collective-permute-start.3 = (f32[17,8,512]{2,1,0:T(8,128)S(1)}, f32[17,8,512]{2,1,0:T(8,128)S(1)}, u32[]{:S(2)}, u32[]{:S(2)}) collective-permute-start(f32[17,8,512]{2,1,0:T(8,128)S(1)} %get-tuple-element.78), channel_id=1, source_target_pairs={{0,0},{2,4},{4,2},{6,8},{8,6},{10,12},{12,10},{14,14},{1,1},{3,5},... | collective-permute-start | bytes 835592 | tf_op jit(solution)/shard_map/ppermute | solution.py:886
  8.0 23.2 %collective-permute-start.5 = (f32[17,8,512]{2,1,0:T(8,128)S(1)}, f32[17,8,512]{2,1,0:T(8,128)S(1)}, u32[]{:S(2)}, u32[]{:S(2)}) collective-permute-start(f32[17,8,512]{2,1,0:T(8,128)S(1)} %get-tuple-element.91), channel_id=1, source_target_pairs={{0,2},{2,0},{4,6},{6,4},{8,10},{10,8},{12,14},{14,12},{1,3},{3,1},... | collective-permute-start | bytes 835592 | tf_op jit(solution)/shard_map/ppermute | solution.py:887
  20.1 17.3 %collective-permute-start.4 = (f32[17,8,512]{2,1,0:T(8,128)S(1)}, f32[17,8,512]{2,1,0:T(8,128)S(1)}, u32[]{:S(2)}, u32[]{:S(2)}) collective-permute-start(f32[17,8,512]{2,1,0:T(8,128)S(1)} %get-tuple-element.86), channel_id=1, source_target_pairs={{0,0},{2,4},{4,2},{6,8},{8,6},{10,12},{12,10},{14,14},{1,1},{3,5},... | collective-permute-start | bytes 835592 | tf_op jit(solution)/shard_map/ppermute | solution.py:899
  23.7 10.7 %copy-start.5 = (f32[3,1,16,256]{3,2,1,0:T(8,128)S(1)}, f32[3,1,16,256]{3,2,1,0:T(8,128)}, u32[]{:S(2)}) copy-start(f32[3,1,16,256]{3,2,1,0:T(8,128)} %disp_ref.1) | copy-start | bytes 147460
  23.7 10.7 %copy-start.6 = (s32[1,16,256]{2,1,0:T(8,128)S(1)}, s32[1,16,256]{2,1,0:T(8,128)}, u32[]{:S(2)}) copy-start(s32[1,16,256]{2,1,0:T(8,128)} %fiber_ref.1) | copy-start | bytes 49156
  31.9 10.0 %collective-permute-start.7 = (f32[17,8,512]{2,1,0:T(8,128)S(1)}, f32[17,8,512]{2,1,0:T(8,128)S(1)}, u32[]{:S(2)}, u32[]{:S(2)}) collective-permute-start(f32[17,8,512]{2,1,0:T(8,128)S(1)} %get-tuple-element.104), channel_id=1, source_target_pairs={{0,2},{2,0},{4,6},{6,4},{8,10},{10,8},{12,14},{14,12},{1,3},{3,1},... | collective-permute-start | bytes 835592 | tf_op jit(solution)/shard_map/ppermute | solution.py:904
  34.4 13.0 %collective-permute-start.8 = (f32[1,4,8,512]{3,2,1,0:T(8,128)S(1)}, f32[1,4,8,512]{3,2,1,0:T(8,128)S(1)}, u32[]{:S(2)}, u32[]{:S(2)}) collective-permute-start(f32[1,4,8,512]{3,2,1,0:T(8,128)S(1)} %bitcast.13), channel_id=1, source_target_pairs={{0,2},{2,0},{4,6},{6,4},{8,10},{10,8},{12,14},{14,12},{1,3},{3,1},... | collective-permute-start | bytes 196616 | tf_op jit(solution)/shard_map/ppermute | solution.py:653
  38.0 15.0 %collective-permute-start.6 = (f32[17,8,512]{2,1,0:T(8,128)S(1)}, f32[17,8,512]{2,1,0:T(8,128)S(1)}, u32[]{:S(2)}, u32[]{:S(2)}) collective-permute-start(f32[17,8,512]{2,1,0:T(8,128)S(1)} %get-tuple-element.101), channel_id=1, source_target_pairs={{0,0},{2,4},{4,2},{6,8},{8,6},{10,12},{12,10},{14,14},{1,1},{3,5},... | collective-permute-start | bytes 835592 | tf_op jit(solution)/shard_map/ppermute | solution.py:899
  42.6 17.2 %collective-permute-start.10 = (f32[17,8,512]{2,1,0:T(8,128)S(1)}, f32[17,8,512]{2,1,0:T(8,128)S(1)}, u32[]{:S(2)}, u32[]{:S(2)}) collective-permute-start(f32[17,8,512]{2,1,0:T(8,128)S(1)} %get-tuple-element.118), channel_id=1, source_target_pairs={{0,2},{2,0},{4,6},{6,4},{8,10},{10,8},{12,14},{14,12},{1,3},{3,1},... | collective-permute-start | bytes 835592 | tf_op jit(solution)/shard_map/ppermute | solution.py:904
  47.4 12.4 %collective-permute-start.9 = (f32[2,4,8,512]{3,2,1,0:T(8,128)S(1)}, f32[2,4,8,512]{3,2,1,0:T(8,128)S(1)}, u32[]{:S(2)}, u32[]{:S(2)}) collective-permute-start(f32[2,4,8,512]{3,2,1,0:T(8,128)S(1)} %pad_maximum_fusion.2), channel_id=1, source_target_pairs={{0,8},{2,10},{4,12},{6,14},{8,0},{10,2},{12,4},{14,6},{1,9},{3,11}... | collective-permute-start | bytes 393224 | tf_op jit(solution)/shard_map/ppermute | solution.py:653
  53.6 13.6 %collective-permute-start.12 = (f32[17,8,512]{2,1,0:T(8,128)S(1)}, f32[17,8,512]{2,1,0:T(8,128)S(1)}, u32[]{:S(2)}, u32[]{:S(2)}) collective-permute-start(f32[17,8,512]{2,1,0:T(8,128)S(1)} %get-tuple-element.126), channel_id=1, source_target_pairs={{0,0},{2,4},{4,2},{6,8},{8,6},{10,12},{12,10},{14,14},{1,1},{3,5},... | collective-permute-start | bytes 835592 | tf_op jit(solution)/shard_map/ppermute | solution.py:899
  60.6 9.2 %collective-permute-start.11 = (f32[17,8,512]{2,1,0:T(8,128)S(1)}, f32[17,8,512]{2,1,0:T(8,128)S(1)}, u32[]{:S(2)}, u32[]{:S(2)}) collective-permute-start(f32[17,8,512]{2,1,0:T(8,128)S(1)} %get-tuple-element.123), channel_id=1, source_target_pairs={{0,2},{2,0},{4,6},{6,4},{8,10},{10,8},{12,14},{14,12},{1,3},{3,1},... | collective-permute-start | bytes 835592 | tf_op jit(solution)/shard_map/ppermute | solution.py:904
  63.5 12.5 %collective-permute-start.13 = (f32[4,4,8,512]{3,2,1,0:T(8,128)S(1)}, f32[4,4,8,512]{3,2,1,0:T(8,128)S(1)}, u32[]{:S(2)}, u32[]{:S(2)}) collective-permute-start(f32[4,4,8,512]{3,2,1,0:T(8,128)S(1)} %pad_maximum_fusion.1), channel_id=1, source_target_pairs={{0,4},{2,6},{4,0},{6,2},{8,12},{10,14},{12,8},{14,10},{1,5},{3,7},... | collective-permute-start | bytes 786440 | tf_op jit(solution)/shard_map/ppermute | solution.py:653
  64.5 2.6 %copy-start.2 = (f32[2,32,512]{2,1,0:T(8,128)S(1)}, f32[2,32,512]{2,1,0:T(8,128)}, u32[]{:S(2)}) copy-start(f32[2,32,512]{2,1,0:T(8,128)} %tension_ref.3) | copy-start | bytes 393220
  71.5 1.2 %collective-permute-start.15 = (f32[8,256]{1,0:T(8,128)S(1)}, f32[8,256]{1,0:T(8,128)S(1)}, u32[]{:S(2)}, u32[]{:S(2)}) collective-permute-start(f32[8,256]{1,0:T(8,128)S(1)} %get-tuple-element.141), channel_id=1, source_target_pairs={{0,1},{1,0},{2,3},{3,2},{4,5},{5,4},{6,7},{7,6},{8,9},{9,8},{10,11... | collective-permute-start | bytes 24584 | tf_op jit(solution)/shard_map/ppermute | solution.py:917
  72.7 5.3 %collective-permute-start.16 = (f32[1,24,256]{2,1,0:T(8,128)S(1)}, f32[1,24,256]{2,1,0:T(8,128)S(1)}, u32[]{:S(2)}, u32[]{:S(2)}) collective-permute-start(f32[1,24,256]{2,1,0:T(8,128)S(1)} %maximum_bitcast_fusion.rest_0_), channel_id=1, source_target_pairs={{0,8},{2,10},{4,12},{6,14},{8,0},{10,2},{12,4},{14,6},{1,9},{3,11}... | collective-permute-start | bytes 73736 | tf_op jit(solution)/shard_map/ppermute | solution.py:653
  76.6 6.1 %collective-permute-start.14 = (f32[8,4,8,256]{3,2,1,0:T(8,128)S(1)}, f32[8,4,8,256]{3,2,1,0:T(8,128)S(1)}, u32[]{:S(2)}, u32[]{:S(2)}) collective-permute-start(f32[8,4,8,256]{3,2,1,0:T(8,128)S(1)} %facing.1), channel_id=1, source_target_pairs={{0,1},{1,0},{2,3},{3,2},{4,5},{5,4},{6,7},{7,6},{8,9},{9,8},{10,11... | collective-permute-start | bytes 786440 | tf_op jit(solution)/shard_map/ppermute | solution.py:909
  78.0 4.1 %collective-permute-start.17 = (f32[2,24,256]{2,1,0:T(8,128)S(1)}, f32[2,24,256]{2,1,0:T(8,128)S(1)}, u32[]{:S(2)}, u32[]{:S(2)}) collective-permute-start(f32[2,24,256]{2,1,0:T(8,128)S(1)} %pad_maximum_fusion.4), channel_id=1, source_target_pairs={{0,2},{2,0},{4,6},{6,4},{8,10},{10,8},{12,14},{14,12},{1,3},{3,1},... | collective-permute-start | bytes 147464 | tf_op jit(solution)/shard_map/ppermute | solution.py:653
  82.1 4.7 %collective-permute-start.18 = (f32[4,24,256]{2,1,0:T(8,128)S(1)}, f32[4,24,256]{2,1,0:T(8,128)S(1)}, u32[]{:S(2)}, u32[]{:S(2)}) collective-permute-start(f32[4,24,256]{2,1,0:T(8,128)S(1)} %pad_maximum_fusion.3), channel_id=1, source_target_pairs={{0,4},{2,6},{4,0},{6,2},{8,12},{10,14},{12,8},{14,10},{1,5},{3,7},... | collective-permute-start | bytes 294920 | tf_op jit(solution)/shard_map/ppermute | solution.py:653
  (2 other events, 3.1 us)

commit v8 on v7

--- a/solution.py
+++ b/solution.py
@@ -171,12 +171,18 @@
     return jax.ShapeDtypeStruct(shape, jnp.float32)
 
 
-def facing_kernel(info_ref, states_ref, cond_ref, edge_ref, facing_ref, cond_rows):
+def edges_kernel(info_ref, u_ref, edge_ref):
     flip, side = info_ref[FLIP], info_ref[SIDE]
+    planes, own = u_ref.shape[:2]
+    edge = (1 - side) * (own - 1)
+    edge_ref[0] = u_ref[flip * (planes - 1), edge]
+    edge_ref[1] = u_ref[(1 - flip) * (planes - 1), edge]
+
+
+def facing_kernel(info_ref, states_ref, cond_ref, facing_ref, cond_rows):
+    side = info_ref[SIDE]
     comps, planes, own = states_ref.shape[:3]
     edge = (1 - side) * (own - 1)
-    edge_ref[0] = states_ref[0, flip * (planes - 1), edge]
-    edge_ref[1] = states_ref[0, (1 - flip) * (planes - 1), edge]
     for comp in range(comps):
         for plane in range(planes):
             facing_ref[comp, plane] = states_ref[comp, plane, edge]
@@ -185,6 +191,18 @@
         cond_rows[comp] = cond_ref[comp, 0, pl.ds(first, 8), :]
 
 
+def edge_rows(info, u):
+    return pl.pallas_call(
+        edges_kernel,
+        in_specs=[SMEM, VMEM],
+        out_specs=VMEM,
+        out_shape=shape_of(2, 8, u.shape[-1]),
+        compiler_params=params(),
+        cost_estimate=cost(0, 130_000),
+        name="edges",
+    )(info, u)
+
+
 def field_kernel(disp_ref, fiber_ref, field_ref):
     for comp in range(3):
         field_ref[comp] = jnp.concatenate([disp_ref[comp, 0, :8], disp_ref[comp, 0, 8:]], axis=1)
@@ -204,12 +222,12 @@
     )(disp, fiber)
 
 
-def sends_kernel(info_ref, edge_ref, states_ref, far_ref, near_ref):
+def sends_kernel(info_ref, edge_ref, u_ref, far_ref, near_ref):
     flip, side = info_ref[FLIP], info_ref[SIDE]
-    planes, own = states_ref.shape[1:3]
+    planes, own = u_ref.shape[:2]
     for pos, (ref, plane) in enumerate([(far_ref, flip * (planes - 1)), (near_ref, (1 - flip) * (planes - 1))]):
         for tile in range(own):
-            store_sent(ref, tile, own + 1, states_ref[0, plane, tile], side)
+            store_sent(ref, tile, own + 1, u_ref[plane, tile], side)
         store_sent(ref, own, own + 1, edge_ref[pos], side)
 
 
@@ -218,9 +236,8 @@
     return pl.pallas_call(
         facing_kernel,
         in_specs=[SMEM, VMEM, VMEM],
-        out_specs=[VMEM] * 3,
+        out_specs=[VMEM] * 2,
         out_shape=[
-            shape_of(2, 8, width),
             shape_of(comps, planes, 8, width),
             shape_of(cond.shape[0], 8, cond.shape[-1]),
         ],
@@ -230,8 +247,8 @@
     )(info, tiled, cond)
 
 
-def first_sends(info, edges, tiled):
-    width = tiled.shape[-1]
+def first_sends(info, edges, u):
+    width = u.shape[-1]
     return pl.pallas_call(
         sends_kernel,
         in_specs=[SMEM] + [VMEM] * 2,
@@ -240,7 +257,7 @@
         compiler_params=params(),
         cost_estimate=cost(0, 1_200_000),
         name="sends",
-    )(info, edges, tiled)
+    )(info, edges, u)
 
 
 def fraction(val):
@@ -878,13 +895,14 @@
 
     tiled = states.reshape(4, planes, own, 8, width)
     fields = Planes(own_field(disp, fiber), slabs, REACH + 1, (1, 4, 2))
-    edges, facing, cond_rows = facing_parts(info, tiled, cond)
-    edges = lax.ppermute(edges, "col", swap)
+    edges = lax.ppermute(edge_rows(info, tiled[0]), "col", swap)
+    far, near = first_sends(info, edges, tiled[0])
+    late_info, far, near = tie(info, far, near)
+    far_halo = lax.ppermute(far, "slab", others)
+    near_halo = lax.ppermute(near, "slab", pairs)
+    facing, cond_rows = facing_parts(late_info, tiled, cond)
     cond_strip = lax.ppermute(cond_rows, "col", swap)
     strip = lax.ppermute(facing, "col", swap)
-    far, near = first_sends(info, edges, tiled)
-    far_halo = lax.ppermute(far, "slab", others)
-    near_halo = lax.ppermute(near, "slab", pairs)
     coeffs = fine_coeffs(info, cond, cond_strip)
     whole = jnp.concatenate([tiled, strip[:, :, None]], axis=2)
 

time: 91.1 us -> 91.9 us (level)
    squeeze x0 -> x1, local copies, waits for them, and re-layouts: none -> 1.36 us  [on_device(): edges = lax.ppermute(edge_rows(info, tiled[0]), 'col', swap)]
    unnamed x14 -> x12, local copies, waits for them, and re-layouts: 3.11 us -> 2.21 us
  transfers between devices with their start and end apart: 19 -> 19, of which waited for: 7 -> 7; matrix products, arithmetic and copies ran while one was open for 1% -> 1% of each run, Pallas kernels for 41% -> 40%
where the time goes in v8:
time: 91.9 us; the launch traced here: 91.7 us
  Pallas kernels  42.1 us (46%)
  starting transfers between devices  29 us (32%)
  waiting for transfers between devices  15.1 us (16%)
  local copies, waits for them, and re-layouts  3.57 us (4%)
  other arithmetic  1.02 us (1%)
  between operations  1.02 us (1%)
    pallas_call x8, Pallas kernels, half_step(): pl.pallas_call(functools.partial(half_kernel, kind, half, tiles), in_spec...  22.2 us
    ppermute x3, starting transfers between devices, on_device(): near_halo = lax.ppermute(near_send, 'slab', pairs)  10.1 us
    ppermute x6, starting transfers between devices, round(): self.take(lax.ppermute(held, 'slab', perm))  9.13 us
    ppermute x1, waiting for transfers between devices, on_device(): near_halo = lax.ppermute(near, 'slab', pairs)  7.65 us
    ppermute x1, starting transfers between devices, on_device(): near_halo = lax.ppermute(near, 'slab', pairs)  5.68 us
    ppermute x6, waiting for transfers between devices, round(): self.take(lax.ppermute(held, 'slab', perm))  5.01 us
    pallas_call x2, Pallas kernels, finish_half(): pl.pallas_call(functools.partial(finish_kernel, half, tiles), in_specs=in...  4.26 us
    pallas_call x6, Pallas kernels, halo_step(): pl.pallas_call(functools.partial(halo_kernel, half, tiles), in_specs=[SME...  4.1 us
  transfers between devices with their start and end apart: 19, of which 7 were waited for; matrix products, arithmetic and copies ran while one was open for 1% of the time, Pallas kernels for 40%

profile of v8, /device:TPU:0, one launch (start us, length us, event | category | flops | bytes accessed | tf_op | source)
XLA Modules:
  0.0 91.7 jit_solution(6671804288012980006)
XLA Ops:
  0.7 1.4 %slice_bitcast_fusion.u_ref = f32[4,8,8,1024]{3,2,1,0:T(8,128)S(1)} fusion(f32[4,4,64,1024]{3,2,1,0:T(8,128)} %param.5), kind=kLoop, calls=%fused_computation.1 | loop fusion | bytes 2097152 | tf_op jit(solution)/shard_map/squeeze | solution.py:898
  4.7 2.2 %copy-done = f32[4,4,64,1024]{3,2,1,0:T(8,128)S(1)} copy-done((f32[4,4,64,1024]{3,2,1,0:T(8,128)S(1)}, f32[4,4,64,1024]{3,2,1,0:T(8,128)}, u32[]{:S(2)}) %copy-start) | copy-done | bytes 4194328
  8.9 5.7 %collective-permute-start.5 = (f32[17,8,512]{2,1,0:T(8,128)S(1)}, f32[17,8,512]{2,1,0:T(8,128)S(1)}, u32[]{:S(2)}, u32[]{:S(2)}) collective-permute-start(f32[17,8,512]{2,1,0:T(8,128)S(1)} %get-tuple-element.95), channel_id=1, source_target_pairs={{0,2},{2,0},{4,6},{6,4},{8,10},{10,8},{12,14},{14,12},{1,3},{3,1},... | collective-permute-start | bytes 835592 | tf_op jit(solution)/shard_map/ppermute | solution.py:902
  14.5 2.2 %coeffs.1.refs_1_.coeff_ref.refs_4_ = f32[10,9,8,1024]{3,2,1,0:T(8,128)S(1)} custom-call(s32[4]{0:T(128)S(1)} %pad_add_fusion.info_ref, f32[6,1,16,256]{3,2,1,0:T(8,128)S(1)} %copy-done.3, f32[6,8,256]{2,1,0:T(8,128)S(1)} %collective-permute-done.2.strip_ref), custom_call_target="tpu_custom_call" | custom-call | flops 2000000 | bytes 3200000 | tf_op jit(solution)/shard_map/coeffs/pallas_call | solution.py:127
  17.5 2.8 %first_far.1 = (f32[9,8,1024]{2,1,0:T(8,128)S(1)}, f32[9,8,1024]{2,1,0:T(8,128)S(1)}, f32[3,2,9,8,1024]{4,3,2,1,0:T(8,128)S(1)}) custom-call(s32[4]{0:T(128)S(1)} %pad_add_fusion.info_ref, f32[4,4,9,8,1024]{4,3,2,1,0:T(8,128)S(1)} %pad_maximum_fusion.refs_0_, f32[10,9,8,1024]{3,2,1,0:T(8,128)S(1)} %coeffs.1.refs_1_.coeff_ref.refs_4_), custom_call_target="tpu_custom_call" | custom-call | flops 14745600 | bytes 5898240 | tf_op jit(solution)/shard_map/first_far/pallas_call | solution.py:388
  21.6 2.8 %first_near.1 = (f32[9,8,1024]{2,1,0:T(8,128)S(1)}, f32[9,8,1024]{2,1,0:T(8,128)S(1)}, f32[3,2,9,8,1024]{4,3,2,1,0:T(8,128)S(1)}) custom-call(s32[4]{0:T(128)S(1)} %pad_add_fusion.info_ref, f32[4,4,9,8,1024]{4,3,2,1,0:T(8,128)S(1)} %pad_maximum_fusion.refs_0_, f32[10,9,8,1024]{3,2,1,0:T(8,128)S(1)} %coeffs.1.refs_1_.coeff_ref.refs_4_), custom_call_target="tpu_custom_call" | custom-call | flops 14745600 | bytes 5898240 | tf_op jit(solution)/shard_map/first_near/pallas_call | solution.py:388
  24.4 7.6 %collective-permute-done.5.halo_ref = f32[17,8,512]{2,1,0:T(8,128)S(1)} collective-permute-done((f32[17,8,512]{2,1,0:T(8,128)S(1)}, f32[17,8,512]{2,1,0:T(8,128)S(1)}, u32[]{:S(2)}, u32[]{:S(2)}) %collective-permute-start.5) | collective-permute-done | bytes 278560 | tf_op jit(solution)/shard_map/ppermute | solution.py:902
  32.8 2.5 %collective-permute-start.7 = (f32[17,8,512]{2,1,0:T(8,128)S(1)}, f32[17,8,512]{2,1,0:T(8,128)S(1)}, u32[]{:S(2)}, u32[]{:S(2)}) collective-permute-start(f32[17,8,512]{2,1,0:T(8,128)S(1)} %get-tuple-element.108), channel_id=1, source_target_pairs={{0,2},{2,0},{4,6},{6,4},{8,10},{10,8},{12,14},{14,12},{1,3},{3,1},... | collective-permute-start | bytes 835592 | tf_op jit(solution)/shard_map/ppermute | solution.py:922
  35.4 2.9 %middle_far.2 = (f32[9,8,1024]{2,1,0:T(8,128)S(1)}, f32[9,8,1024]{2,1,0:T(8,128)S(1)}, f32[3,2,9,8,1024]{4,3,2,1,0:T(8,128)S(1)}) custom-call(s32[4]{0:T(128)S(1)} %pad_add_fusion.info_ref, f32[9,8,1024]{2,1,0:T(8,128)S(1)} %get-tuple-element.83.refs_0_, f32[9,8,1024]{2,1,0:T(8,128)S(1)} %get-tuple-element.100.refs_1_.refs_2_, ...), custom_call_target="tpu_custom_call" | custom-call | flops 14745600 | bytes 5898240 | tf_op jit(solution)/shard_map/middle_far/pallas_call | solution.py:388
  39.6 2.8 %middle_near.2 = (f32[9,8,1024]{2,1,0:T(8,128)S(1)}, f32[9,8,1024]{2,1,0:T(8,128)S(1)}, f32[3,2,9,8,1024]{4,3,2,1,0:T(8,128)S(1)}) custom-call(s32[4]{0:T(128)S(1)} %pad_add_fusion.info_ref, f32[9,8,1024]{2,1,0:T(8,128)S(1)} %get-tuple-element.98.refs_0_, f32[9,8,1024]{2,1,0:T(8,128)S(1)} %get-tuple-element.99.refs_2_.refs_1_, ...), custom_call_target="tpu_custom_call" | custom-call | flops 14745600 | bytes 5898240 | tf_op jit(solution)/shard_map/middle_near/pallas_call | solution.py:388
  43.5 4.7 %collective-permute-start.10 = (f32[17,8,512]{2,1,0:T(8,128)S(1)}, f32[17,8,512]{2,1,0:T(8,128)S(1)}, u32[]{:S(2)}, u32[]{:S(2)}) collective-permute-start(f32[17,8,512]{2,1,0:T(8,128)S(1)} %get-tuple-element.122), channel_id=1, source_target_pairs={{0,2},{2,0},{4,6},{6,4},{8,10},{10,8},{12,14},{14,12},{1,3},{3,1},... | collective-permute-start | bytes 835592 | tf_op jit(solution)/shard_map/ppermute | solution.py:922
  48.3 2.7 %collective-permute-start.9 = (f32[2,4,8,512]{3,2,1,0:T(8,128)S(1)}, f32[2,4,8,512]{3,2,1,0:T(8,128)S(1)}, u32[]{:S(2)}, u32[]{:S(2)}) collective-permute-start(f32[2,4,8,512]{3,2,1,0:T(8,128)S(1)} %pad_maximum_fusion.2), channel_id=1, source_target_pairs={{0,8},{2,10},{4,12},{6,14},{8,0},{10,2},{12,4},{14,6},{1,9},{3,11}... | collective-permute-start | bytes 393224 | tf_op jit(solution)/shard_map/ppermute | solution.py:670
  50.9 2.9 %middle_far.3 = (f32[9,8,1024]{2,1,0:T(8,128)S(1)}, f32[9,8,1024]{2,1,0:T(8,128)S(1)}, f32[3,2,9,8,1024]{4,3,2,1,0:T(8,128)S(1)}) custom-call(s32[4]{0:T(128)S(1)} %pad_add_fusion.info_ref, f32[9,8,1024]{2,1,0:T(8,128)S(1)} %get-tuple-element.91.refs_0_, f32[9,8,1024]{2,1,0:T(8,128)S(1)} %get-tuple-element.113.refs_1_.refs_2_, ...), custom_call_target="tpu_custom_call" | custom-call | flops 14745600 | bytes 5898240 | tf_op jit(solution)/shard_map/middle_far/pallas_call | solution.py:388
  55.1 2.9 %middle_near.3 = (f32[9,8,1024]{2,1,0:T(8,128)S(1)}, f32[9,8,1024]{2,1,0:T(8,128)S(1)}, f32[3,2,9,8,1024]{4,3,2,1,0:T(8,128)S(1)}) custom-call(s32[4]{0:T(128)S(1)} %pad_add_fusion.info_ref, f32[9,8,1024]{2,1,0:T(8,128)S(1)} %get-tuple-element.111.refs_0_, f32[9,8,1024]{2,1,0:T(8,128)S(1)} %get-tuple-element.112.refs_2_.refs_1_, ...), custom_call_target="tpu_custom_call" | custom-call | flops 14745600 | bytes 5898240 | tf_op jit(solution)/shard_map/middle_near/pallas_call | solution.py:388
  58.0 2.6 %last_far.1 = (f32[8,8,1024]{2,1,0:T(8,128)S(1)}, f32[8,8,1024]{2,1,0:T(8,128)S(1)}, f32[3,2,8,8,1024]{4,3,2,1,0:T(8,128)S(1)}) custom-call(s32[4]{0:T(128)S(1)} %pad_add_fusion.info_ref, f32[9,8,1024]{2,1,0:T(8,128)S(1)} %get-tuple-element.116.refs_0_, f32[9,8,1024]{2,1,0:T(8,128)S(1)} %get-tuple-element.117.refs_1_.refs_2_, ...), custom_call_target="tpu_custom_call" | custom-call | flops 14745600 | bytes 5898240 | tf_op jit(solution)/shard_map/last_far/pallas_call | solution.py:388
  61.4 2.9 %collective-permute-start.11 = (f32[17,8,512]{2,1,0:T(8,128)S(1)}, f32[17,8,512]{2,1,0:T(8,128)S(1)}, u32[]{:S(2)}, u32[]{:S(2)}) collective-permute-start(f32[17,8,512]{2,1,0:T(8,128)S(1)} %get-tuple-element.127), channel_id=1, source_target_pairs={{0,2},{2,0},{4,6},{6,4},{8,10},{10,8},{12,14},{14,12},{1,3},{3,1},... | collective-permute-start | bytes 835592 | tf_op jit(solution)/shard_map/ppermute | solution.py:922
  65.3 2.6 %last_near.1 = (f32[8,8,1024]{2,1,0:T(8,128)S(1)}, f32[8,8,1024]{2,1,0:T(8,128)S(1)}, f32[3,2,8,8,1024]{4,3,2,1,0:T(8,128)S(1)}) custom-call(s32[4]{0:T(128)S(1)} %pad_add_fusion.info_ref, f32[9,8,1024]{2,1,0:T(8,128)S(1)} %get-tuple-element.123.refs_0_, f32[9,8,1024]{2,1,0:T(8,128)S(1)} %get-tuple-element.118.refs_2_.refs_1_, ...), custom_call_target="tpu_custom_call" | custom-call | flops 14745600 | bytes 5898240 | tf_op jit(solution)/shard_map/last_near/pallas_call | solution.py:388
  68.0 2.6 %finish_far.1 = (f32[4,4,8,8,1024]{4,3,2,1,0:T(8,128)}, f32[2,32,512]{2,1,0:T(8,128)}, f32[16,256]{1,0:T(8,128)S(1)}) custom-call(s32[4]{0:T(128)S(1)} %pad_add_fusion.info_ref, f32[8,8,1024]{2,1,0:T(8,128)S(1)} %get-tuple-element.128.outer_ref, f32[8,8,1024]{2,1,0:T(8,128)S(1)} %get-tuple-element.129.inner_ref, ...), custom_call_target="tpu_custom_call" | custom-call | flops 2621440 | bytes 2621440 | tf_op jit(solution)/shard_map/finish_far/pallas_call | solution.py:524
  70.6 1.7 %finish_near.1 = (f32[4,4,8,8,1024]{4,3,2,1,0:T(8,128)}, f32[2,32,512]{2,1,0:T(8,128)}, f32[16,256]{1,0:T(8,128)S(1)}, f32[8,256]{1,0:T(8,128)S(1)}) custom-call(s32[4]{0:T(128)S(1)} %pad_add_fusion.info_ref, f32[8,8,1024]{2,1,0:T(8,128)S(1)} %get-tuple-element.125.outer_ref, ...), custom_call_target="tpu_custom_call", output_to_operand_aliasing={{0}: (7, {}), {1}: (8, {})} | custom-call | flops 2621440 | bytes 2621440 | tf_op jit(solution)/shard_map/finish_near/pallas_call | solution.py:524
  73.5 3.4 %collective-permute-start.16 = (f32[1,24,256]{2,1,0:T(8,128)S(1)}, f32[1,24,256]{2,1,0:T(8,128)S(1)}, u32[]{:S(2)}, u32[]{:S(2)}) collective-permute-start(f32[1,24,256]{2,1,0:T(8,128)S(1)} %maximum_bitcast_fusion.rest_0_), channel_id=1, source_target_pairs={{0,8},{2,10},{4,12},{6,14},{8,0},{10,2},{12,4},{14,6},{1,9},{3,11}... | collective-permute-start | bytes 73736 | tf_op jit(solution)/shard_map/ppermute | solution.py:670
  78.9 1.5 %collective-permute-start.17 = (f32[2,24,256]{2,1,0:T(8,128)S(1)}, f32[2,24,256]{2,1,0:T(8,128)S(1)}, u32[]{:S(2)}, u32[]{:S(2)}) collective-permute-start(f32[2,24,256]{2,1,0:T(8,128)S(1)} %pad_maximum_fusion.4), channel_id=1, source_target_pairs={{0,2},{2,0},{4,6},{6,4},{8,10},{10,8},{12,14},{14,12},{1,3},{3,1},... | collective-permute-start | bytes 147464 | tf_op jit(solution)/shard_map/ppermute | solution.py:670
  80.5 2.5 %collective-permute-done.17.rest_2_ = f32[2,24,256]{2,1,0:T(8,128)S(1)} collective-permute-done((f32[2,24,256]{2,1,0:T(8,128)S(1)}, f32[2,24,256]{2,1,0:T(8,128)S(1)}, u32[]{:S(2)}, u32[]{:S(2)}) %collective-permute-start.17) | collective-permute-done | bytes 49184 | tf_op jit(solution)/shard_map/ppermute | solution.py:670
  83.5 3.0 %passive.1 = (f32[6,9,24,256]{3,2,1,0:T(8,128)S(1)}, f32[9,9,24,256]{3,2,1,0:T(8,128)S(1)}, f32[9,9,24,256]{3,2,1,0:T(8,128)S(1)}) custom-call(s32[4]{0:T(128)S(1)} %pad_add_fusion.info_ref, f32[3,128]{1,0:T(4,128)S(1)} %pad_maximum_fusion.5.table_ref, f32[8,4,8,256]{3,2,1,0:T(8,128)S(1)} %collective-permute-done.14.strip_ref, ...), custom_call_target="tpu_custom_call" | custom-call | flops 22118400 | bytes 5000000 | tf_op jit(solution)/shard_map/passive/pallas_call | solution.py:784
  87.7 4.0 %mechanics.1 = (f32[3,1,16,256]{3,2,1,0:T(8,128)}, f32[6,1,16,256]{3,2,1,0:T(8,128)}) custom-call(s32[4]{0:T(128)S(1)} %pad_add_fusion.info_ref, f32[6,9,24,256]{3,2,1,0:T(8,128)S(1)} %get-tuple-element.141.disp_ref, f32[9,9,24,256]{3,2,1,0:T(8,128)S(1)} %get-tuple-element.142.stress_ref, f32[9,9,24,256]{3,2,1,0:T(8,128)S(1)} %get-tuple-element.143.pull_ref, ...), custom_call_target="tpu_custom_call" | custom-call | flops 22118400 | bytes 5000000 | tf_op jit(solution)/shard_map/mechanics/pallas_call | solution.py:861
  (61 shorter events, 18.1 us)
Async XLA Ops:
  0.6 4.0 %copy-start.3 = (f32[6,1,16,256]{3,2,1,0:T(8,128)S(1)}, f32[6,1,16,256]{3,2,1,0:T(8,128)}, u32[]{:S(2)}) copy-start(f32[6,1,16,256]{3,2,1,0:T(8,128)} %cond_ref.3) | copy-start | bytes 294916
  2.7 1.4 %collective-permute-start = (f32[2,8,1024]{2,1,0:T(8,128)S(1)}, f32[2,8,1024]{2,1,0:T(8,128)S(1)}, u32[]{:S(2)}, u32[]{:S(2)}) collective-permute-start(f32[2,8,1024]{2,1,0:T(8,128)S(1)} %edges.1), channel_id=1, source_target_pairs={{0,1},{1,0},{2,3},{3,2},{4,5},{5,4},{6,7},{7,6},{8,9},{9,8},{10,11... | collective-permute-start | bytes 196616 | tf_op jit(solution)/shard_map/ppermute | solution.py:898
  6.9 9.9 %copy-start.1 = (f32[4,4,64,1024]{3,2,1,0:T(8,128)S(1)}, f32[4,4,64,1024]{3,2,1,0:T(8,128)}, u32[]{:S(2)}) copy-start(f32[4,4,64,1024]{3,2,1,0:T(8,128)} %param.5) | copy-start | bytes 12582916
  7.5 9.3 %collective-permute-start.1 = (f32[4,4,8,1024]{3,2,1,0:T(8,128)S(1)}, f32[4,4,8,1024]{3,2,1,0:T(8,128)S(1)}, u32[]{:S(2)}, u32[]{:S(2)}) collective-permute-start(f32[4,4,8,1024]{3,2,1,0:T(8,128)S(1)} %get-tuple-element.79), channel_id=1, source_target_pairs={{0,1},{1,0},{2,3},{3,2},{4,5},{5,4},{6,7},{7,6},{8,9},{9,8},{10,11... | collective-permute-start | bytes 1572872 | tf_op jit(solution)/shard_map/ppermute | solution.py:905
  7.9 6.6 %collective-permute-start.2 = (f32[6,8,256]{2,1,0:T(8,128)S(1)}, f32[6,8,256]{2,1,0:T(8,128)S(1)}, u32[]{:S(2)}, u32[]{:S(2)}) collective-permute-start(f32[6,8,256]{2,1,0:T(8,128)S(1)} %get-tuple-element.80), channel_id=1, source_target_pairs={{0,1},{1,0},{2,3},{3,2},{4,5},{5,4},{6,7},{7,6},{8,9},{9,8},{10,11... | collective-permute-start | bytes 147464 | tf_op jit(solution)/shard_map/ppermute | solution.py:904
  8.1 12.2 %collective-permute-start.3 = (f32[17,8,512]{2,1,0:T(8,128)S(1)}, f32[17,8,512]{2,1,0:T(8,128)S(1)}, u32[]{:S(2)}, u32[]{:S(2)}) collective-permute-start(f32[17,8,512]{2,1,0:T(8,128)S(1)} %get-tuple-element.82), channel_id=1, source_target_pairs={{0,0},{2,4},{4,2},{6,8},{8,6},{10,12},{12,10},{14,14},{1,1},{3,5},... | collective-permute-start | bytes 835592 | tf_op jit(solution)/shard_map/ppermute | solution.py:901
  8.9 23.2 %collective-permute-start.5 = (f32[17,8,512]{2,1,0:T(8,128)S(1)}, f32[17,8,512]{2,1,0:T(8,128)S(1)}, u32[]{:S(2)}, u32[]{:S(2)}) collective-permute-start(f32[17,8,512]{2,1,0:T(8,128)S(1)} %get-tuple-element.95), channel_id=1, source_target_pairs={{0,2},{2,0},{4,6},{6,4},{8,10},{10,8},{12,14},{14,12},{1,3},{3,1},... | collective-permute-start | bytes 835592 | tf_op jit(solution)/shard_map/ppermute | solution.py:902
  20.9 17.4 %collective-permute-start.4 = (f32[17,8,512]{2,1,0:T(8,128)S(1)}, f32[17,8,512]{2,1,0:T(8,128)S(1)}, u32[]{:S(2)}, u32[]{:S(2)}) collective-permute-start(f32[17,8,512]{2,1,0:T(8,128)S(1)} %get-tuple-element.90), channel_id=1, source_target_pairs={{0,0},{2,4},{4,2},{6,8},{8,6},{10,12},{12,10},{14,14},{1,1},{3,5},... | collective-permute-start | bytes 835592 | tf_op jit(solution)/shard_map/ppermute | solution.py:917
  24.3 11.0 %copy-start.4 = (f32[3,1,16,256]{3,2,1,0:T(8,128)S(1)}, f32[3,1,16,256]{3,2,1,0:T(8,128)}, u32[]{:S(2)}) copy-start(f32[3,1,16,256]{3,2,1,0:T(8,128)} %disp_ref.1) | copy-start | bytes 147460
  24.4 11.0 %copy-start.5 = (s32[1,16,256]{2,1,0:T(8,128)S(1)}, s32[1,16,256]{2,1,0:T(8,128)}, u32[]{:S(2)}) copy-start(s32[1,16,256]{2,1,0:T(8,128)} %fiber_ref.1) | copy-start | bytes 49156
  32.8 10.0 %collective-permute-start.7 = (f32[17,8,512]{2,1,0:T(8,128)S(1)}, f32[17,8,512]{2,1,0:T(8,128)S(1)}, u32[]{:S(2)}, u32[]{:S(2)}) collective-permute-start(f32[17,8,512]{2,1,0:T(8,128)S(1)} %get-tuple-element.108), channel_id=1, source_target_pairs={{0,2},{2,0},{4,6},{6,4},{8,10},{10,8},{12,14},{14,12},{1,3},{3,1},... | collective-permute-start | bytes 835592 | tf_op jit(solution)/shard_map/ppermute | solution.py:922
  35.3 12.9 %collective-permute-start.8 = (f32[1,4,8,512]{3,2,1,0:T(8,128)S(1)}, f32[1,4,8,512]{3,2,1,0:T(8,128)S(1)}, u32[]{:S(2)}, u32[]{:S(2)}) collective-permute-start(f32[1,4,8,512]{3,2,1,0:T(8,128)S(1)} %bitcast.14), channel_id=1, source_target_pairs={{0,2},{2,0},{4,6},{6,4},{8,10},{10,8},{12,14},{14,12},{1,3},{3,1},... | collective-permute-start | bytes 196616 | tf_op jit(solution)/shard_map/ppermute | solution.py:670
  38.9 14.9 %collective-permute-start.6 = (f32[17,8,512]{2,1,0:T(8,128)S(1)}, f32[17,8,512]{2,1,0:T(8,128)S(1)}, u32[]{:S(2)}, u32[]{:S(2)}) collective-permute-start(f32[17,8,512]{2,1,0:T(8,128)S(1)} %get-tuple-element.105), channel_id=1, source_target_pairs={{0,0},{2,4},{4,2},{6,8},{8,6},{10,12},{12,10},{14,14},{1,1},{3,5},... | collective-permute-start | bytes 835592 | tf_op jit(solution)/shard_map/ppermute | solution.py:917
  43.5 17.1 %collective-permute-start.10 = (f32[17,8,512]{2,1,0:T(8,128)S(1)}, f32[17,8,512]{2,1,0:T(8,128)S(1)}, u32[]{:S(2)}, u32[]{:S(2)}) collective-permute-start(f32[17,8,512]{2,1,0:T(8,128)S(1)} %get-tuple-element.122), channel_id=1, source_target_pairs={{0,2},{2,0},{4,6},{6,4},{8,10},{10,8},{12,14},{14,12},{1,3},{3,1},... | collective-permute-start | bytes 835592 | tf_op jit(solution)/shard_map/ppermute | solution.py:922
  48.3 12.3 %collective-permute-start.9 = (f32[2,4,8,512]{3,2,1,0:T(8,128)S(1)}, f32[2,4,8,512]{3,2,1,0:T(8,128)S(1)}, u32[]{:S(2)}, u32[]{:S(2)}) collective-permute-start(f32[2,4,8,512]{3,2,1,0:T(8,128)S(1)} %pad_maximum_fusion.2), channel_id=1, source_target_pairs={{0,8},{2,10},{4,12},{6,14},{8,0},{10,2},{12,4},{14,6},{1,9},{3,11}... | collective-permute-start | bytes 393224 | tf_op jit(solution)/shard_map/ppermute | solution.py:670
  54.4 13.5 %collective-permute-start.12 = (f32[17,8,512]{2,1,0:T(8,128)S(1)}, f32[17,8,512]{2,1,0:T(8,128)S(1)}, u32[]{:S(2)}, u32[]{:S(2)}) collective-permute-start(f32[17,8,512]{2,1,0:T(8,128)S(1)} %get-tuple-element.130), channel_id=1, source_target_pairs={{0,0},{2,4},{4,2},{6,8},{8,6},{10,12},{12,10},{14,14},{1,1},{3,5},... | collective-permute-start | bytes 835592 | tf_op jit(solution)/shard_map/ppermute | solution.py:917
  61.4 9.2 %collective-permute-start.11 = (f32[17,8,512]{2,1,0:T(8,128)S(1)}, f32[17,8,512]{2,1,0:T(8,128)S(1)}, u32[]{:S(2)}, u32[]{:S(2)}) collective-permute-start(f32[17,8,512]{2,1,0:T(8,128)S(1)} %get-tuple-element.127), channel_id=1, source_target_pairs={{0,2},{2,0},{4,6},{6,4},{8,10},{10,8},{12,14},{14,12},{1,3},{3,1},... | collective-permute-start | bytes 835592 | tf_op jit(solution)/shard_map/ppermute | solution.py:922
  64.3 12.6 %collective-permute-start.13 = (f32[4,4,8,512]{3,2,1,0:T(8,128)S(1)}, f32[4,4,8,512]{3,2,1,0:T(8,128)S(1)}, u32[]{:S(2)}, u32[]{:S(2)}) collective-permute-start(f32[4,4,8,512]{3,2,1,0:T(8,128)S(1)} %pad_maximum_fusion.1), channel_id=1, source_target_pairs={{0,4},{2,6},{4,0},{6,2},{8,12},{10,14},{12,8},{14,10},{1,5},{3,7},... | collective-permute-start | bytes 786440 | tf_op jit(solution)/shard_map/ppermute | solution.py:670
  65.3 2.6 %copy-start.2 = (f32[2,32,512]{2,1,0:T(8,128)S(1)}, f32[2,32,512]{2,1,0:T(8,128)}, u32[]{:S(2)}) copy-start(f32[2,32,512]{2,1,0:T(8,128)} %tension_ref.3) | copy-start | bytes 393220
  72.2 1.2 %collective-permute-start.15 = (f32[8,256]{1,0:T(8,128)S(1)}, f32[8,256]{1,0:T(8,128)S(1)}, u32[]{:S(2)}, u32[]{:S(2)}) collective-permute-start(f32[8,256]{1,0:T(8,128)S(1)} %get-tuple-element.145), channel_id=1, source_target_pairs={{0,1},{1,0},{2,3},{3,2},{4,5},{5,4},{6,7},{7,6},{8,9},{9,8},{10,11... | collective-permute-start | bytes 24584 | tf_op jit(solution)/shard_map/ppermute | solution.py:935
  73.5 5.4 %collective-permute-start.16 = (f32[1,24,256]{2,1,0:T(8,128)S(1)}, f32[1,24,256]{2,1,0:T(8,128)S(1)}, u32[]{:S(2)}, u32[]{:S(2)}) collective-permute-start(f32[1,24,256]{2,1,0:T(8,128)S(1)} %maximum_bitcast_fusion.rest_0_), channel_id=1, source_target_pairs={{0,8},{2,10},{4,12},{6,14},{8,0},{10,2},{12,4},{14,6},{1,9},{3,11}... | collective-permute-start | bytes 73736 | tf_op jit(solution)/shard_map/ppermute | solution.py:670
  77.5 6.0 %collective-permute-start.14 = (f32[8,4,8,256]{3,2,1,0:T(8,128)S(1)}, f32[8,4,8,256]{3,2,1,0:T(8,128)S(1)}, u32[]{:S(2)}, u32[]{:S(2)}) collective-permute-start(f32[8,4,8,256]{3,2,1,0:T(8,128)S(1)} %facing.1), channel_id=1, source_target_pairs={{0,1},{1,0},{2,3},{3,2},{4,5},{5,4},{6,7},{7,6},{8,9},{9,8},{10,11... | collective-permute-start | bytes 786440 | tf_op jit(solution)/shard_map/ppermute | solution.py:927
  78.9 4.1 %collective-permute-start.17 = (f32[2,24,256]{2,1,0:T(8,128)S(1)}, f32[2,24,256]{2,1,0:T(8,128)S(1)}, u32[]{:S(2)}, u32[]{:S(2)}) collective-permute-start(f32[2,24,256]{2,1,0:T(8,128)S(1)} %pad_maximum_fusion.4), channel_id=1, source_target_pairs={{0,2},{2,0},{4,6},{6,4},{8,10},{10,8},{12,14},{14,12},{1,3},{3,1},... | collective-permute-start | bytes 147464 | tf_op jit(solution)/shard_map/ppermute | solution.py:670
  83.0 4.7 %collective-permute-start.18 = (f32[4,24,256]{2,1,0:T(8,128)S(1)}, f32[4,24,256]{2,1,0:T(8,128)S(1)}, u32[]{:S(2)}, u32[]{:S(2)}) collective-permute-start(f32[4,24,256]{2,1,0:T(8,128)S(1)} %pad_maximum_fusion.3), channel_id=1, source_target_pairs={{0,4},{2,6},{4,0},{6,2},{8,12},{10,14},{12,8},{14,10},{1,5},{3,7},... | collective-permute-start | bytes 294920 | tf_op jit(solution)/shard_map/ppermute | solution.py:670
  (1 other events, 2.2 us)

commit v9 on v7

--- a/solution.py
+++ b/solution.py
@@ -171,7 +171,13 @@
     return jax.ShapeDtypeStruct(shape, jnp.float32)
 
 
-def facing_kernel(info_ref, states_ref, cond_ref, edge_ref, facing_ref, cond_rows):
+def cond_rows_kernel(info_ref, cond_ref, cond_rows):
+    first = pl.multiple_of(8 * (1 - info_ref[SIDE]), 8)
+    for comp in range(cond_ref.shape[0]):
+        cond_rows[comp] = cond_ref[comp, 0, pl.ds(first, 8), :]
+
+
+def facing_kernel(info_ref, states_ref, edge_ref, facing_ref):
     flip, side = info_ref[FLIP], info_ref[SIDE]
     comps, planes, own = states_ref.shape[:3]
     edge = (1 - side) * (own - 1)
@@ -180,9 +186,6 @@
     for comp in range(comps):
         for plane in range(planes):
             facing_ref[comp, plane] = states_ref[comp, plane, edge]
-    first = pl.multiple_of(8 * (1 - side), 8)
-    for comp in range(cond_ref.shape[0]):
-        cond_rows[comp] = cond_ref[comp, 0, pl.ds(first, 8), :]
 
 
 def field_kernel(disp_ref, fiber_ref, field_ref):
@@ -213,21 +216,29 @@
         store_sent(ref, own, own + 1, edge_ref[pos], side)
 
 
-def facing_parts(info, tiled, cond):
+def facing_parts(info, tiled):
     comps, planes, _, _, width = tiled.shape
     return pl.pallas_call(
         facing_kernel,
-        in_specs=[SMEM, VMEM, VMEM],
-        out_specs=[VMEM] * 3,
-        out_shape=[
-            shape_of(2, 8, width),
-            shape_of(comps, planes, 8, width),
-            shape_of(cond.shape[0], 8, cond.shape[-1]),
-        ],
+        in_specs=[SMEM, VMEM],
+        out_specs=[VMEM] * 2,
+        out_shape=[shape_of(2, 8, width), shape_of(comps, planes, 8, width)],
         compiler_params=params(),
         cost_estimate=cost(0, 1_200_000),
         name="facing_parts",
-    )(info, tiled, cond)
+    )(info, tiled)
+
+
+def facing_cond(info, cond):
+    return pl.pallas_call(
+        cond_rows_kernel,
+        in_specs=[SMEM, VMEM],
+        out_specs=VMEM,
+        out_shape=shape_of(cond.shape[0], 8, cond.shape[-1]),
+        compiler_params=params(),
+        cost_estimate=cost(0, 100_000),
+        name="facing_cond",
+    )(info, cond)
 
 
 def first_sends(info, edges, tiled):
@@ -878,9 +889,9 @@
 
     tiled = states.reshape(4, planes, own, 8, width)
     fields = Planes(own_field(disp, fiber), slabs, REACH + 1, (1, 4, 2))
-    edges, facing, cond_rows = facing_parts(info, tiled, cond)
+    edges, facing = facing_parts(info, tiled)
     edges = lax.ppermute(edges, "col", swap)
-    cond_strip = lax.ppermute(cond_rows, "col", swap)
+    cond_strip = lax.ppermute(facing_cond(info, cond), "col", swap)
     strip = lax.ppermute(facing, "col", swap)
     far, near = first_sends(info, edges, tiled)
     far_halo = lax.ppermute(far, "slab", others)

time: 91.1 us -> 89.7 us (0.985)
  waiting for transfers between devices: 14.9 us -> 11.4 us
  starting transfers between devices: 28.9 us -> 30.3 us
    ppermute x1, waiting for transfers between devices: 7.37 us -> 1.87 us  [on_device(): near_halo = lax.ppermute(near, 'slab', pairs)]
    ppermute x3, starting transfers between devices: 10.2 us -> 13 us  [on_device(): near_halo = lax.ppermute(near_send, 'slab', pairs)]
    ppermute x6, waiting for transfers between devices: 4.94 us -> 7.36 us  [round(): self.take(lax.ppermute(held, 'slab', perm))]
    ppermute x1, waiting for transfers between devices: 1.12 us -> 0.01 us  [on_device(): edges = lax.ppermute(edges, 'col', swap)]
    ppermute x6, starting transfers between devices: 9.04 us -> 8 us  [round(): self.take(lax.ppermute(held, 'slab', perm))]
    unnamed x14 -> x12, local copies, waits for them, and re-layouts: 3.11 us -> 3.17 us
  transfers between devices with their start and end apart: 19 -> 19, of which waited for: 7 -> 7; matrix products, arithmetic and copies ran while one was open for 1% -> 1% of each run, Pallas kernels for 41% -> 42%
where the time goes in v9:
time: 89.7 us; the launch traced here: 89.5 us
  Pallas kernels  42.5 us (47%)
  starting transfers between devices  30.3 us (34%)
  waiting for transfers between devices  11.4 us (13%)
  local copies, waits for them, and re-layouts  3.17 us (4%)
  other arithmetic  1.02 us (1%)
  between operations  0.99 us (1%)
    pallas_call x8, Pallas kernels, half_step(): pl.pallas_call(functools.partial(half_kernel, kind, half, tiles), in_spec...  22.6 us
    ppermute x3, starting transfers between devices, on_device(): near_halo = lax.ppermute(near_send, 'slab', pairs)  13 us
    ppermute x6, starting transfers between devices, round(): self.take(lax.ppermute(held, 'slab', perm))  8 us
    ppermute x6, waiting for transfers between devices, round(): self.take(lax.ppermute(held, 'slab', perm))  7.36 us
    ppermute x1, starting transfers between devices, on_device(): near_halo = lax.ppermute(near, 'slab', pairs)  5.36 us
    pallas_call x2, Pallas kernels, finish_half(): pl.pallas_call(functools.partial(finish_kernel, half, tiles), in_specs=in...  4.25 us
    pallas_call x1, Pallas kernels, mechanics_step(): pl.pallas_call(functools.partial(mechanics_kernel, planes), in_specs=[pl....  4.14 us
    pallas_call x6, Pallas kernels, halo_step(): pl.pallas_call(functools.partial(halo_kernel, half, tiles), in_specs=[SME...  4.07 us
  transfers between devices with their start and end apart: 19, of which 7 were waited for; matrix products, arithmetic and copies ran while one was open for 1% of the time, Pallas kernels for 42%

profile of v9, /device:TPU:0, one launch (start us, length us, event | category | flops | bytes accessed | tf_op | source)
XLA Modules:
  0.0 89.5 jit_solution(9455953557755369708)
XLA Ops:
  0.7 2.2 %copy-done = f32[4,4,64,1024]{3,2,1,0:T(8,128)S(1)} copy-done((f32[4,4,64,1024]{3,2,1,0:T(8,128)S(1)}, f32[4,4,64,1024]{3,2,1,0:T(8,128)}, u32[]{:S(2)}) %copy-start) | copy-done | bytes 4194328
  7.4 5.4 %collective-permute-start.5 = (f32[17,8,512]{2,1,0:T(8,128)S(1)}, f32[17,8,512]{2,1,0:T(8,128)S(1)}, u32[]{:S(2)}, u32[]{:S(2)}) collective-permute-start(f32[17,8,512]{2,1,0:T(8,128)S(1)} %get-tuple-element.89), channel_id=1, source_target_pairs={{0,2},{2,0},{4,6},{6,4},{8,10},{10,8},{12,14},{14,12},{1,3},{3,1},... | collective-permute-start | bytes 835592 | tf_op jit(solution)/shard_map/ppermute | solution.py:898
  12.8 2.2 %coeffs.1.refs_1_.coeff_ref.refs_4_ = f32[10,9,8,1024]{3,2,1,0:T(8,128)S(1)} custom-call(s32[4]{0:T(128)S(1)} %pad_add_fusion.info_ref, f32[6,1,16,256]{3,2,1,0:T(8,128)S(1)} %copy-done.3, f32[6,8,256]{2,1,0:T(8,128)S(1)} %collective-permute-done.1.strip_ref), custom_call_target="tpu_custom_call" | custom-call | flops 2000000 | bytes 3200000 | tf_op jit(solution)/shard_map/coeffs/pallas_call | solution.py:127
  15.7 2.9 %first_far.1 = (f32[9,8,1024]{2,1,0:T(8,128)S(1)}, f32[9,8,1024]{2,1,0:T(8,128)S(1)}, f32[3,2,9,8,1024]{4,3,2,1,0:T(8,128)S(1)}) custom-call(s32[4]{0:T(128)S(1)} %pad_add_fusion.info_ref, f32[4,4,9,8,1024]{4,3,2,1,0:T(8,128)S(1)} %pad_maximum_fusion.refs_0_, f32[10,9,8,1024]{3,2,1,0:T(8,128)S(1)} %coeffs.1.refs_1_.coeff_ref.refs_4_), custom_call_target="tpu_custom_call" | custom-call | flops 14745600 | bytes 5898240 | tf_op jit(solution)/shard_map/first_far/pallas_call | solution.py:382
  19.9 2.9 %first_near.1 = (f32[9,8,1024]{2,1,0:T(8,128)S(1)}, f32[9,8,1024]{2,1,0:T(8,128)S(1)}, f32[3,2,9,8,1024]{4,3,2,1,0:T(8,128)S(1)}) custom-call(s32[4]{0:T(128)S(1)} %pad_add_fusion.info_ref, f32[4,4,9,8,1024]{4,3,2,1,0:T(8,128)S(1)} %pad_maximum_fusion.refs_0_, f32[10,9,8,1024]{3,2,1,0:T(8,128)S(1)} %coeffs.1.refs_1_.coeff_ref.refs_4_), custom_call_target="tpu_custom_call" | custom-call | flops 14745600 | bytes 5898240 | tf_op jit(solution)/shard_map/first_near/pallas_call | solution.py:382
  22.9 1.9 %collective-permute-done.5.halo_ref = f32[17,8,512]{2,1,0:T(8,128)S(1)} collective-permute-done((f32[17,8,512]{2,1,0:T(8,128)S(1)}, f32[17,8,512]{2,1,0:T(8,128)S(1)}, u32[]{:S(2)}, u32[]{:S(2)}) %collective-permute-start.5) | collective-permute-done | bytes 278560 | tf_op jit(solution)/shard_map/ppermute | solution.py:898
  25.5 3.7 %collective-permute-start.7 = (f32[17,8,512]{2,1,0:T(8,128)S(1)}, f32[17,8,512]{2,1,0:T(8,128)S(1)}, u32[]{:S(2)}, u32[]{:S(2)}) collective-permute-start(f32[17,8,512]{2,1,0:T(8,128)S(1)} %get-tuple-element.102), channel_id=1, source_target_pairs={{0,2},{2,0},{4,6},{6,4},{8,10},{10,8},{12,14},{14,12},{1,3},{3,1},... | collective-permute-start | bytes 835592 | tf_op jit(solution)/shard_map/ppermute | solution.py:915
  29.3 2.9 %middle_far.2 = (f32[9,8,1024]{2,1,0:T(8,128)S(1)}, f32[9,8,1024]{2,1,0:T(8,128)S(1)}, f32[3,2,9,8,1024]{4,3,2,1,0:T(8,128)S(1)}) custom-call(s32[4]{0:T(128)S(1)} %pad_add_fusion.info_ref, f32[9,8,1024]{2,1,0:T(8,128)S(1)} %get-tuple-element.77.refs_0_, f32[9,8,1024]{2,1,0:T(8,128)S(1)} %get-tuple-element.94.refs_1_.refs_2_, ...), custom_call_target="tpu_custom_call" | custom-call | flops 14745600 | bytes 5898240 | tf_op jit(solution)/shard_map/middle_far/pallas_call | solution.py:382
  33.5 2.9 %middle_near.2 = (f32[9,8,1024]{2,1,0:T(8,128)S(1)}, f32[9,8,1024]{2,1,0:T(8,128)S(1)}, f32[3,2,9,8,1024]{4,3,2,1,0:T(8,128)S(1)}) custom-call(s32[4]{0:T(128)S(1)} %pad_add_fusion.info_ref, f32[9,8,1024]{2,1,0:T(8,128)S(1)} %get-tuple-element.92.refs_0_, f32[9,8,1024]{2,1,0:T(8,128)S(1)} %get-tuple-element.93.refs_2_.refs_1_, ...), custom_call_target="tpu_custom_call" | custom-call | flops 14745600 | bytes 5898240 | tf_op jit(solution)/shard_map/middle_near/pallas_call | solution.py:382
  37.3 4.8 %collective-permute-start.10 = (f32[17,8,512]{2,1,0:T(8,128)S(1)}, f32[17,8,512]{2,1,0:T(8,128)S(1)}, u32[]{:S(2)}, u32[]{:S(2)}) collective-permute-start(f32[17,8,512]{2,1,0:T(8,128)S(1)} %get-tuple-element.116), channel_id=1, source_target_pairs={{0,2},{2,0},{4,6},{6,4},{8,10},{10,8},{12,14},{14,12},{1,3},{3,1},... | collective-permute-start | bytes 835592 | tf_op jit(solution)/shard_map/ppermute | solution.py:915
  42.1 1.8 %collective-permute-done.8.refs_1_ = f32[1,4,8,512]{3,2,1,0:T(8,128)S(1)} collective-permute-done((f32[1,4,8,512]{3,2,1,0:T(8,128)S(1)}, f32[1,4,8,512]{3,2,1,0:T(8,128)S(1)}, u32[]{:S(2)}, u32[]{:S(2)}) %collective-permute-start.8) | collective-permute-done | bytes 65568 | tf_op jit(solution)/shard_map/ppermute | solution.py:664
  43.9 3.6 %collective-permute-start.9 = (f32[2,4,8,512]{3,2,1,0:T(8,128)S(1)}, f32[2,4,8,512]{3,2,1,0:T(8,128)S(1)}, u32[]{:S(2)}, u32[]{:S(2)}) collective-permute-start(f32[2,4,8,512]{3,2,1,0:T(8,128)S(1)} %pad_maximum_fusion.2), channel_id=1, source_target_pairs={{0,8},{2,10},{4,12},{6,14},{8,0},{10,2},{12,4},{14,6},{1,9},{3,11}... | collective-permute-start | bytes 393224 | tf_op jit(solution)/shard_map/ppermute | solution.py:664
  47.6 2.9 %middle_far.3 = (f32[9,8,1024]{2,1,0:T(8,128)S(1)}, f32[9,8,1024]{2,1,0:T(8,128)S(1)}, f32[3,2,9,8,1024]{4,3,2,1,0:T(8,128)S(1)}) custom-call(s32[4]{0:T(128)S(1)} %pad_add_fusion.info_ref, f32[9,8,1024]{2,1,0:T(8,128)S(1)} %get-tuple-element.85.refs_0_, f32[9,8,1024]{2,1,0:T(8,128)S(1)} %get-tuple-element.107.refs_1_.refs_2_, ...), custom_call_target="tpu_custom_call" | custom-call | flops 14745600 | bytes 5898240 | tf_op jit(solution)/shard_map/middle_far/pallas_call | solution.py:382
  51.8 2.9 %middle_near.3 = (f32[9,8,1024]{2,1,0:T(8,128)S(1)}, f32[9,8,1024]{2,1,0:T(8,128)S(1)}, f32[3,2,9,8,1024]{4,3,2,1,0:T(8,128)S(1)}) custom-call(s32[4]{0:T(128)S(1)} %pad_add_fusion.info_ref, f32[9,8,1024]{2,1,0:T(8,128)S(1)} %get-tuple-element.105.refs_0_, f32[9,8,1024]{2,1,0:T(8,128)S(1)} %get-tuple-element.106.refs_2_.refs_1_, ...), custom_call_target="tpu_custom_call" | custom-call | flops 14745600 | bytes 5898240 | tf_op jit(solution)/shard_map/middle_near/pallas_call | solution.py:382
  54.7 2.6 %last_far.1 = (f32[8,8,1024]{2,1,0:T(8,128)S(1)}, f32[8,8,1024]{2,1,0:T(8,128)S(1)}, f32[3,2,8,8,1024]{4,3,2,1,0:T(8,128)S(1)}) custom-call(s32[4]{0:T(128)S(1)} %pad_add_fusion.info_ref, f32[9,8,1024]{2,1,0:T(8,128)S(1)} %get-tuple-element.110.refs_0_, f32[9,8,1024]{2,1,0:T(8,128)S(1)} %get-tuple-element.111.refs_1_.refs_2_, ...), custom_call_target="tpu_custom_call" | custom-call | flops 14745600 | bytes 5898240 | tf_op jit(solution)/shard_map/last_far/pallas_call | solution.py:382
  58.1 4.5 %collective-permute-start.11 = (f32[17,8,512]{2,1,0:T(8,128)S(1)}, f32[17,8,512]{2,1,0:T(8,128)S(1)}, u32[]{:S(2)}, u32[]{:S(2)}) collective-permute-start(f32[17,8,512]{2,1,0:T(8,128)S(1)} %get-tuple-element.121), channel_id=1, source_target_pairs={{0,2},{2,0},{4,6},{6,4},{8,10},{10,8},{12,14},{14,12},{1,3},{3,1},... | collective-permute-start | bytes 835592 | tf_op jit(solution)/shard_map/ppermute | solution.py:915
  62.7 2.6 %last_near.1 = (f32[8,8,1024]{2,1,0:T(8,128)S(1)}, f32[8,8,1024]{2,1,0:T(8,128)S(1)}, f32[3,2,8,8,1024]{4,3,2,1,0:T(8,128)S(1)}) custom-call(s32[4]{0:T(128)S(1)} %pad_add_fusion.info_ref, f32[9,8,1024]{2,1,0:T(8,128)S(1)} %get-tuple-element.117.refs_0_, f32[9,8,1024]{2,1,0:T(8,128)S(1)} %get-tuple-element.112.refs_2_.refs_1_, ...), custom_call_target="tpu_custom_call" | custom-call | flops 14745600 | bytes 5898240 | tf_op jit(solution)/shard_map/last_near/pallas_call | solution.py:382
  65.4 2.6 %finish_far.1 = (f32[4,4,8,8,1024]{4,3,2,1,0:T(8,128)}, f32[2,32,512]{2,1,0:T(8,128)}, f32[16,256]{1,0:T(8,128)S(1)}) custom-call(s32[4]{0:T(128)S(1)} %pad_add_fusion.info_ref, f32[8,8,1024]{2,1,0:T(8,128)S(1)} %get-tuple-element.122.outer_ref, f32[8,8,1024]{2,1,0:T(8,128)S(1)} %get-tuple-element.123.inner_ref, ...), custom_call_target="tpu_custom_call" | custom-call | flops 2621440 | bytes 2621440 | tf_op jit(solution)/shard_map/finish_far/pallas_call | solution.py:518
  73.3 3.2 %collective-permute-done.16.rest_1_ = f32[1,24,256]{2,1,0:T(8,128)S(1)} collective-permute-done((f32[1,24,256]{2,1,0:T(8,128)S(1)}, f32[1,24,256]{2,1,0:T(8,128)S(1)}, u32[]{:S(2)}, u32[]{:S(2)}) %collective-permute-start.16) | collective-permute-done | bytes 24608 | tf_op jit(solution)/shard_map/ppermute | solution.py:664
  76.5 1.7 %collective-permute-start.17 = (f32[2,24,256]{2,1,0:T(8,128)S(1)}, f32[2,24,256]{2,1,0:T(8,128)S(1)}, u32[]{:S(2)}, u32[]{:S(2)}) collective-permute-start(f32[2,24,256]{2,1,0:T(8,128)S(1)} %pad_maximum_fusion.4), channel_id=1, source_target_pairs={{0,2},{2,0},{4,6},{6,4},{8,10},{10,8},{12,14},{14,12},{1,3},{3,1},... | collective-permute-start | bytes 147464 | tf_op jit(solution)/shard_map/ppermute | solution.py:664
  78.4 2.3 %collective-permute-done.17.rest_2_ = f32[2,24,256]{2,1,0:T(8,128)S(1)} collective-permute-done((f32[2,24,256]{2,1,0:T(8,128)S(1)}, f32[2,24,256]{2,1,0:T(8,128)S(1)}, u32[]{:S(2)}, u32[]{:S(2)}) %collective-permute-start.17) | collective-permute-done | bytes 49184 | tf_op jit(solution)/shard_map/ppermute | solution.py:664
  80.6 1.7 %collective-permute-start.18 = (f32[4,24,256]{2,1,0:T(8,128)S(1)}, f32[4,24,256]{2,1,0:T(8,128)S(1)}, u32[]{:S(2)}, u32[]{:S(2)}) collective-permute-start(f32[4,24,256]{2,1,0:T(8,128)S(1)} %pad_maximum_fusion.3), channel_id=1, source_target_pairs={{0,4},{2,6},{4,0},{6,2},{8,12},{10,14},{12,8},{14,10},{1,5},{3,7},... | collective-permute-start | bytes 294920 | tf_op jit(solution)/shard_map/ppermute | solution.py:664
  82.4 3.0 %passive.1 = (f32[6,9,24,256]{3,2,1,0:T(8,128)S(1)}, f32[9,9,24,256]{3,2,1,0:T(8,128)S(1)}, f32[9,9,24,256]{3,2,1,0:T(8,128)S(1)}) custom-call(s32[4]{0:T(128)S(1)} %pad_add_fusion.info_ref, f32[3,128]{1,0:T(4,128)S(1)} %pad_maximum_fusion.5.table_ref, f32[8,4,8,256]{3,2,1,0:T(8,128)S(1)} %collective-permute-done.14.strip_ref, ...), custom_call_target="tpu_custom_call" | custom-call | flops 22118400 | bytes 5000000 | tf_op jit(solution)/shard_map/passive/pallas_call | solution.py:778
  85.4 4.1 %mechanics.1 = (f32[3,1,16,256]{3,2,1,0:T(8,128)}, f32[6,1,16,256]{3,2,1,0:T(8,128)}) custom-call(s32[4]{0:T(128)S(1)} %pad_add_fusion.info_ref, f32[6,9,24,256]{3,2,1,0:T(8,128)S(1)} %get-tuple-element.135.disp_ref, f32[9,9,24,256]{3,2,1,0:T(8,128)S(1)} %get-tuple-element.136.stress_ref, f32[9,9,24,256]{3,2,1,0:T(8,128)S(1)} %get-tuple-element.137.pull_ref, ...), custom_call_target="tpu_custom_call" | custom-call | flops 22118400 | bytes 5000000 | tf_op jit(solution)/shard_map/mechanics/pallas_call | solution.py:855
  (60 shorter events, 17.1 us)
Async XLA Ops:
  0.7 2.2 %copy-start = (f32[4,4,64,1024]{3,2,1,0:T(8,128)S(1)}, f32[4,4,64,1024]{3,2,1,0:T(8,128)}, u32[]{:S(2)}) copy-start(f32[4,4,64,1024]{3,2,1,0:T(8,128)} %param.5) | copy-start | bytes 12582916
  2.9 3.2 %copy-start.1 = (f32[4,4,64,1024]{3,2,1,0:T(8,128)S(1)}, f32[4,4,64,1024]{3,2,1,0:T(8,128)}, u32[]{:S(2)}) copy-start(f32[4,4,64,1024]{3,2,1,0:T(8,128)} %param.5) | copy-start | bytes 12582916
  3.5 11.5 %collective-permute-start = (f32[4,4,8,1024]{3,2,1,0:T(8,128)S(1)}, f32[4,4,8,1024]{3,2,1,0:T(8,128)S(1)}, u32[]{:S(2)}, u32[]{:S(2)}) collective-permute-start(f32[4,4,8,1024]{3,2,1,0:T(8,128)S(1)} %get-tuple-element.73), channel_id=1, source_target_pairs={{0,1},{1,0},{2,3},{3,2},{4,5},{5,4},{6,7},{7,6},{8,9},{9,8},{10,11... | collective-permute-start | bytes 1572872 | tf_op jit(solution)/shard_map/ppermute | solution.py:895
  4.0 2.1 %collective-permute-start.2 = (f32[2,8,1024]{2,1,0:T(8,128)S(1)}, f32[2,8,1024]{2,1,0:T(8,128)S(1)}, u32[]{:S(2)}, u32[]{:S(2)}) collective-permute-start(f32[2,8,1024]{2,1,0:T(8,128)S(1)} %get-tuple-element.75), channel_id=1, source_target_pairs={{0,1},{1,0},{2,3},{3,2},{4,5},{5,4},{6,7},{7,6},{8,9},{9,8},{10,11... | collective-permute-start | bytes 196616 | tf_op jit(solution)/shard_map/ppermute | solution.py:893
  5.6 7.2 %collective-permute-start.1 = (f32[6,8,256]{2,1,0:T(8,128)S(1)}, f32[6,8,256]{2,1,0:T(8,128)S(1)}, u32[]{:S(2)}, u32[]{:S(2)}) collective-permute-start(f32[6,8,256]{2,1,0:T(8,128)S(1)} %facing_cond.1), channel_id=1, source_target_pairs={{0,1},{1,0},{2,3},{3,2},{4,5},{5,4},{6,7},{7,6},{8,9},{9,8},{10,11... | collective-permute-start | bytes 147464 | tf_op jit(solution)/shard_map/ppermute | solution.py:894
  6.7 11.9 %collective-permute-start.3 = (f32[17,8,512]{2,1,0:T(8,128)S(1)}, f32[17,8,512]{2,1,0:T(8,128)S(1)}, u32[]{:S(2)}, u32[]{:S(2)}) collective-permute-start(f32[17,8,512]{2,1,0:T(8,128)S(1)} %get-tuple-element.76), channel_id=1, source_target_pairs={{0,0},{2,4},{4,2},{6,8},{8,6},{10,12},{12,10},{14,14},{1,1},{3,5},... | collective-permute-start | bytes 835592 | tf_op jit(solution)/shard_map/ppermute | solution.py:897
  7.4 17.3 %collective-permute-start.5 = (f32[17,8,512]{2,1,0:T(8,128)S(1)}, f32[17,8,512]{2,1,0:T(8,128)S(1)}, u32[]{:S(2)}, u32[]{:S(2)}) collective-permute-start(f32[17,8,512]{2,1,0:T(8,128)S(1)} %get-tuple-element.89), channel_id=1, source_target_pairs={{0,2},{2,0},{4,6},{6,4},{8,10},{10,8},{12,14},{14,12},{1,3},{3,1},... | collective-permute-start | bytes 835592 | tf_op jit(solution)/shard_map/ppermute | solution.py:898
  19.2 13.0 %collective-permute-start.4 = (f32[17,8,512]{2,1,0:T(8,128)S(1)}, f32[17,8,512]{2,1,0:T(8,128)S(1)}, u32[]{:S(2)}, u32[]{:S(2)}) collective-permute-start(f32[17,8,512]{2,1,0:T(8,128)S(1)} %get-tuple-element.84), channel_id=1, source_target_pairs={{0,0},{2,4},{4,2},{6,8},{8,6},{10,12},{12,10},{14,14},{1,1},{3,5},... | collective-permute-start | bytes 835592 | tf_op jit(solution)/shard_map/ppermute | solution.py:910
  22.8 6.4 %copy-start.4 = (f32[3,1,16,256]{3,2,1,0:T(8,128)S(1)}, f32[3,1,16,256]{3,2,1,0:T(8,128)}, u32[]{:S(2)}) copy-start(f32[3,1,16,256]{3,2,1,0:T(8,128)} %disp_ref.1) | copy-start | bytes 147460
  22.8 6.4 %copy-start.5 = (s32[1,16,256]{2,1,0:T(8,128)S(1)}, s32[1,16,256]{2,1,0:T(8,128)}, u32[]{:S(2)}) copy-start(s32[1,16,256]{2,1,0:T(8,128)} %fiber_ref.1) | copy-start | bytes 49156
  25.5 11.0 %collective-permute-start.7 = (f32[17,8,512]{2,1,0:T(8,128)S(1)}, f32[17,8,512]{2,1,0:T(8,128)S(1)}, u32[]{:S(2)}, u32[]{:S(2)}) collective-permute-start(f32[17,8,512]{2,1,0:T(8,128)S(1)} %get-tuple-element.102), channel_id=1, source_target_pairs={{0,2},{2,0},{4,6},{6,4},{8,10},{10,8},{12,14},{14,12},{1,3},{3,1},... | collective-permute-start | bytes 835592 | tf_op jit(solution)/shard_map/ppermute | solution.py:915
  29.2 14.7 %collective-permute-start.8 = (f32[1,4,8,512]{3,2,1,0:T(8,128)S(1)}, f32[1,4,8,512]{3,2,1,0:T(8,128)S(1)}, u32[]{:S(2)}, u32[]{:S(2)}) collective-permute-start(f32[1,4,8,512]{3,2,1,0:T(8,128)S(1)} %bitcast.13), channel_id=1, source_target_pairs={{0,2},{2,0},{4,6},{6,4},{8,10},{10,8},{12,14},{14,12},{1,3},{3,1},... | collective-permute-start | bytes 196616 | tf_op jit(solution)/shard_map/ppermute | solution.py:664
  32.8 17.6 %collective-permute-start.6 = (f32[17,8,512]{2,1,0:T(8,128)S(1)}, f32[17,8,512]{2,1,0:T(8,128)S(1)}, u32[]{:S(2)}, u32[]{:S(2)}) collective-permute-start(f32[17,8,512]{2,1,0:T(8,128)S(1)} %get-tuple-element.99), channel_id=1, source_target_pairs={{0,0},{2,4},{4,2},{6,8},{8,6},{10,12},{12,10},{14,14},{1,1},{3,5},... | collective-permute-start | bytes 835592 | tf_op jit(solution)/shard_map/ppermute | solution.py:910
  37.3 20.0 %collective-permute-start.10 = (f32[17,8,512]{2,1,0:T(8,128)S(1)}, f32[17,8,512]{2,1,0:T(8,128)S(1)}, u32[]{:S(2)}, u32[]{:S(2)}) collective-permute-start(f32[17,8,512]{2,1,0:T(8,128)S(1)} %get-tuple-element.116), channel_id=1, source_target_pairs={{0,2},{2,0},{4,6},{6,4},{8,10},{10,8},{12,14},{14,12},{1,3},{3,1},... | collective-permute-start | bytes 835592 | tf_op jit(solution)/shard_map/ppermute | solution.py:915
  43.9 13.4 %collective-permute-start.9 = (f32[2,4,8,512]{3,2,1,0:T(8,128)S(1)}, f32[2,4,8,512]{3,2,1,0:T(8,128)S(1)}, u32[]{:S(2)}, u32[]{:S(2)}) collective-permute-start(f32[2,4,8,512]{3,2,1,0:T(8,128)S(1)} %pad_maximum_fusion.2), channel_id=1, source_target_pairs={{0,8},{2,10},{4,12},{6,14},{8,0},{10,2},{12,4},{14,6},{1,9},{3,11}... | collective-permute-start | bytes 393224 | tf_op jit(solution)/shard_map/ppermute | solution.py:664
  51.1 14.3 %collective-permute-start.12 = (f32[17,8,512]{2,1,0:T(8,128)S(1)}, f32[17,8,512]{2,1,0:T(8,128)S(1)}, u32[]{:S(2)}, u32[]{:S(2)}) collective-permute-start(f32[17,8,512]{2,1,0:T(8,128)S(1)} %get-tuple-element.124), channel_id=1, source_target_pairs={{0,0},{2,4},{4,2},{6,8},{8,6},{10,12},{12,10},{14,14},{1,1},{3,5},... | collective-permute-start | bytes 835592 | tf_op jit(solution)/shard_map/ppermute | solution.py:910
  58.1 10.8 %collective-permute-start.11 = (f32[17,8,512]{2,1,0:T(8,128)S(1)}, f32[17,8,512]{2,1,0:T(8,128)S(1)}, u32[]{:S(2)}, u32[]{:S(2)}) collective-permute-start(f32[17,8,512]{2,1,0:T(8,128)S(1)} %get-tuple-element.121), channel_id=1, source_target_pairs={{0,2},{2,0},{4,6},{6,4},{8,10},{10,8},{12,14},{14,12},{1,3},{3,1},... | collective-permute-start | bytes 835592 | tf_op jit(solution)/shard_map/ppermute | solution.py:915
  62.6 10.0 %collective-permute-start.13 = (f32[4,4,8,512]{3,2,1,0:T(8,128)S(1)}, f32[4,4,8,512]{3,2,1,0:T(8,128)S(1)}, u32[]{:S(2)}, u32[]{:S(2)}) collective-permute-start(f32[4,4,8,512]{3,2,1,0:T(8,128)S(1)} %pad_maximum_fusion.1), channel_id=1, source_target_pairs={{0,4},{2,6},{4,0},{6,2},{8,12},{10,14},{12,8},{14,10},{1,5},{3,7},... | collective-permute-start | bytes 786440 | tf_op jit(solution)/shard_map/ppermute | solution.py:664
  62.7 2.7 %copy-start.2 = (f32[2,32,512]{2,1,0:T(8,128)S(1)}, f32[2,32,512]{2,1,0:T(8,128)}, u32[]{:S(2)}) copy-start(f32[2,32,512]{2,1,0:T(8,128)} %tension_ref.3) | copy-start | bytes 393220
  70.6 1.2 %collective-permute-start.15 = (f32[8,256]{1,0:T(8,128)S(1)}, f32[8,256]{1,0:T(8,128)S(1)}, u32[]{:S(2)}, u32[]{:S(2)}) collective-permute-start(f32[8,256]{1,0:T(8,128)S(1)} %get-tuple-element.139), channel_id=1, source_target_pairs={{0,1},{1,0},{2,3},{3,2},{4,5},{5,4},{6,7},{7,6},{8,9},{9,8},{10,11... | collective-permute-start | bytes 24584 | tf_op jit(solution)/shard_map/ppermute | solution.py:928
  71.8 4.7 %collective-permute-start.16 = (f32[1,24,256]{2,1,0:T(8,128)S(1)}, f32[1,24,256]{2,1,0:T(8,128)S(1)}, u32[]{:S(2)}, u32[]{:S(2)}) collective-permute-start(f32[1,24,256]{2,1,0:T(8,128)S(1)} %maximum_bitcast_fusion.rest_0_), channel_id=1, source_target_pairs={{0,8},{2,10},{4,12},{6,14},{8,0},{10,2},{12,4},{14,6},{1,9},{3,11}... | collective-permute-start | bytes 73736 | tf_op jit(solution)/shard_map/ppermute | solution.py:664
  73.2 9.2 %collective-permute-start.14 = (f32[8,4,8,256]{3,2,1,0:T(8,128)S(1)}, f32[8,4,8,256]{3,2,1,0:T(8,128)S(1)}, u32[]{:S(2)}, u32[]{:S(2)}) collective-permute-start(f32[8,4,8,256]{3,2,1,0:T(8,128)S(1)} %facing.1), channel_id=1, source_target_pairs={{0,1},{1,0},{2,3},{3,2},{4,5},{5,4},{6,7},{7,6},{8,9},{9,8},{10,11... | collective-permute-start | bytes 786440 | tf_op jit(solution)/shard_map/ppermute | solution.py:920
  76.5 4.1 %collective-permute-start.17 = (f32[2,24,256]{2,1,0:T(8,128)S(1)}, f32[2,24,256]{2,1,0:T(8,128)S(1)}, u32[]{:S(2)}, u32[]{:S(2)}) collective-permute-start(f32[2,24,256]{2,1,0:T(8,128)S(1)} %pad_maximum_fusion.4), channel_id=1, source_target_pairs={{0,2},{2,0},{4,6},{6,4},{8,10},{10,8},{12,14},{14,12},{1,3},{3,1},... | collective-permute-start | bytes 147464 | tf_op jit(solution)/shard_map/ppermute | solution.py:664
  80.6 4.7 %collective-permute-start.18 = (f32[4,24,256]{2,1,0:T(8,128)S(1)}, f32[4,24,256]{2,1,0:T(8,128)S(1)}, u32[]{:S(2)}, u32[]{:S(2)}) collective-permute-start(f32[4,24,256]{2,1,0:T(8,128)S(1)} %pad_maximum_fusion.3), channel_id=1, source_target_pairs={{0,4},{2,6},{4,0},{6,2},{8,12},{10,14},{12,8},{14,10},{1,5},{3,7},... | collective-permute-start | bytes 294920 | tf_op jit(solution)/shard_map/ppermute | solution.py:664
  (1 other events, 1.0 us)
